TPU v7x, 512 devices: a whole 4x8x8 slice. The times are simulated.
512 devices in a mesh: dp: 32 (over z, y_lo), tensor: 16 (over y_hi, x, core).
Axes of the slice: x: 4, y: 8 (y_hi: 2, y_lo: 4; y = y_hi * 4 + y_lo), z: 8, core: 2. Of those that a mesh axis runs over, the one named last changes fastest.
Arguments:
- states: bfloat16 [8192, 8192], P('dp'), may hold values from -6 to 6
- query_weight: bfloat16 [8192, 4096], P('tensor', 'dp'), may hold values from -0.0625 to 0.0625
- key_matrix: bfloat16 [8192, 512], P('tensor', 'dp'), may hold values from -0.0625 to 0.0625
- value_matrix: bfloat16 [8192, 512], P('tensor', 'dp'), may hold values from -0.0625 to 0.0625
- block_mask: int32 [128, 4], P('dp'), may hold values from 0 to 1, as said below
- risk_weight: float32 [128], P('dp'), may hold values from -1 to 1
- upstream: bfloat16 [8192, 4096], P('dp', 'tensor'), may hold values from -1.5 to 1.5
Outputs:
- attn_out: bfloat16 [8192, 4096], P('dp', 'tensor')
- grad_query: float32 [8192, 4096], P('dp', 'tensor')
Inputs may be any that keep to these rules, and one draw needn't show every extreme that they name: `block_mask`: within each group of 4 blocks, row b is 1 exactly at the blocks on the path from the root of b's tree to b, b included; every ancestor has a lower index than its descendants.
All inputs are finite; a program needn't handle non-finite values.
Results may differ from a plain program's by a relative error of at most 0.03.
Values may be sent and summed in bfloat16 or wider, within the bound.
No kernel may reach another device: no remote copies, remote signals or barrier semaphores. Data moves between devices by JAX's collectives and lax.ppermute only.
A program may use at most 128 MiB of HBM per device.

v0:
```python
import math

import jax
import jax.numpy as jnp
import numpy as np
from jax import lax
from jax.sharding import PartitionSpec as P

LOCAL_QUERY_HEADS = 32
LOCAL_KEY_HEADS = 4
HEAD_DIMENSION = 128
BS = 64


def apply_rotary(vector, cosine_lookup, sine_lookup):
    halves = vector.shape[-1] // 2
    first_half = vector[..., :halves]
    second_half = vector[..., halves:]
    return (
        vector * cosine_lookup + jnp.concatenate([-second_half, first_half], axis=-1) * sine_lookup
    )


def unrotate(vector, cosine_lookup, sine_lookup):
    halves = vector.shape[-1] // 2
    first_half = vector[..., :halves]
    second_half = vector[..., halves:]
    return (
        vector * cosine_lookup + jnp.concatenate([second_half, -first_half], axis=-1) * sine_lookup
    )


def shards(states, query_weight, key_matrix, value_matrix, block_mask, risk_weight, upstream):
    tensor_size = lax.axis_size("tensor")
    dp_size = lax.axis_size("dp")
    sequence_length = states.shape[0]
    model_width = states.shape[1]
    per_dev = LOCAL_QUERY_HEADS // tensor_size
    heads_per_group = LOCAL_QUERY_HEADS // LOCAL_KEY_HEADS
    kv_dev = max(1, per_dev // heads_per_group)
    thin_rows = model_width // (tensor_size * dp_size)
    sharers = 1
    col_width = kv_dev * HEAD_DIMENSION // sharers
    column_rows = []
    for target in range(tensor_size):
        first_head = target * per_dev // heads_per_group
        full_cols = [
            (first_head + extra) * HEAD_DIMENSION + inner
            for extra in range(kv_dev)
            for inner in range(HEAD_DIMENSION)
        ]
        portion = target % sharers
        column_rows.append(full_cols[portion * col_width : (portion + 1) * col_width])
    column_table = np.array(column_rows, dtype=np.int32)

    def pair_buffer(row_block):
        picked = row_block[:, column_table]
        return picked.reshape(row_block.shape[0], tensor_size, col_width)

    token_grid = states.reshape(sequence_length, tensor_size, dp_size, thin_rows)
    pair_rows = (
        lax.all_to_all(key_matrix, "dp", split_axis=0, concat_axis=1, tiled=True),
        lax.all_to_all(value_matrix, "dp", split_axis=0, concat_axis=1, tiled=True),
    )
    query_cols = lax.all_gather(query_weight, "dp", axis=1, tiled=True)
    arrived = (
        lax.all_to_all(
            query_cols.reshape(query_cols.shape[0], tensor_size, per_dev * HEAD_DIMENSION),
            "tensor",
            split_axis=1,
            concat_axis=0,
            tiled=True,
        ),
        lax.all_to_all(
            pair_buffer(pair_rows[0]), "tensor", split_axis=1, concat_axis=0, tiled=True
        ),
        lax.all_to_all(
            pair_buffer(pair_rows[1]), "tensor", split_axis=1, concat_axis=0, tiled=True
        ),
    )
    query_full, key_part, value_part = tuple(
        (item.reshape(item.shape[0], item.shape[2]) for item in arrived)
    )
    q_lin = jnp.dot(states, query_full, preferred_element_type=jnp.float32)
    pieces = (
        lax.all_gather(key_part, "dp", axis=0, tiled=True),
        lax.all_gather(value_part, "dp", axis=0, tiled=True),
    )
    columns = token_grid.transpose(0, 2, 1, 3).reshape(sequence_length, pieces[0].shape[0])
    key_linear = jnp.dot(columns, pieces[0], preferred_element_type=jnp.float32)
    value_linear = jnp.dot(columns, pieces[1], preferred_element_type=jnp.float32)
    scaling = 1.0 / math.sqrt(HEAD_DIMENSION)
    depths = jnp.sum(block_mask, axis=1) - 1
    offsets = jnp.arange(BS, dtype=jnp.int32)
    places = (depths[:, None] * BS + offsets[None, :]).reshape(sequence_length)
    frequency = jnp.exp(
        -math.log(1000000.0)
        * jnp.arange(HEAD_DIMENSION // 2, dtype=jnp.float32)
        * 2.0
        / HEAD_DIMENSION
    )
    angles = places.astype(jnp.float32)[:, None] * frequency[None, :]
    cosine_lookup = jnp.concatenate([jnp.cos(angles), jnp.cos(angles)], axis=-1)[:, None, :]
    sine_lookup = jnp.concatenate([jnp.sin(angles), jnp.sin(angles)], axis=-1)[:, None, :]
    queries = (
        apply_rotary(
            q_lin.reshape(sequence_length, per_dev, HEAD_DIMENSION), cosine_lookup, sine_lookup
        )
        * scaling
    ).astype(jnp.bfloat16)
    rotated_keys = apply_rotary(
        key_linear.reshape(sequence_length, kv_dev, HEAD_DIMENSION), cosine_lookup, sine_lookup
    ).astype(jnp.bfloat16)
    projected_values = value_linear.reshape(sequence_length, kv_dev, HEAD_DIMENSION).astype(
        jnp.bfloat16
    )
    head_map = np.arange(per_dev) // heads_per_group
    key_heads = rotated_keys[:, head_map]
    value_heads = projected_values[:, head_map]
    scores = jnp.einsum("qhd,khd->hqk", queries, key_heads, preferred_element_type=jnp.float32)
    position = jnp.arange(sequence_length, dtype=jnp.int32)
    blocks = position // BS
    wide_mask = jnp.repeat(jnp.repeat(block_mask, BS, axis=0), BS, axis=1) > 0
    visible = wide_mask & (
        (blocks[:, None] != blocks[None, :]) | (position[:, None] >= position[None, :])
    )
    raised = jnp.exp(jnp.where(visible[None], scores, -jnp.inf))
    attend = raised / jnp.sum(raised, axis=-1, keepdims=True)
    attend_b = attend.astype(jnp.bfloat16)
    mixed = jnp.einsum("hqk,khd->qhd", attend_b, value_heads, preferred_element_type=jnp.float32)
    attn_out = mixed.reshape(sequence_length, per_dev * HEAD_DIMENSION).astype(jnp.bfloat16)
    token_risk = jnp.repeat(risk_weight, BS)
    weighted = (
        (upstream.astype(jnp.float32) * token_risk[:, None])
        .astype(jnp.bfloat16)
        .reshape(sequence_length, per_dev, HEAD_DIMENSION)
    )
    pressure = jnp.einsum("qhd,khd->hqk", weighted, value_heads, preferred_element_type=jnp.float32)
    centre = jnp.sum(attend * pressure, axis=-1, keepdims=True)
    slope = (attend * (pressure - centre)).astype(jnp.bfloat16)
    dq_rot = (
        jnp.einsum("hqk,khd->qhd", slope, key_heads, preferred_element_type=jnp.float32) * scaling
    )
    dq_rows = (
        unrotate(dq_rot, cosine_lookup, sine_lookup)
        .reshape(sequence_length, per_dev * HEAD_DIMENSION)
        .astype(jnp.bfloat16)
    )
    columns = states
    grad_query = lax.psum_scatter(
        lax.dot_general(
            columns, dq_rows, (((0,), (0,)), ((), ())), preferred_element_type=jnp.float32
        ).astype(jnp.bfloat16),
        "dp",
        scatter_dimension=0,
        tiled=True,
    ).astype(jnp.float32)
    return (attn_out, grad_query)


def solution(mesh):
    in_specs = (
        P("dp", None),
        P("tensor", "dp"),
        P("tensor", "dp"),
        P("tensor", "dp"),
        P("dp", None),
        P("dp"),
        P("dp", "tensor"),
    )
    out_specs = (P("dp", "tensor"), P("dp", "tensor"))
    return jax.shard_map(shards, mesh=mesh, in_specs=in_specs, out_specs=out_specs, check_vma=False)
```

profile of v0, /device:TPU:6, one launch (start us, length us, event | category | flops | bytes accessed | tf_op | source)
XLA Modules:
  0.0 774.1 jit_solution(15821695000008231698)
XLA Ops:
  7.2 1.7 copy.68
  8.9 0.9 all_to_all.61
  9.8 0.7 reshape.190
  10.6 13.7 %all-to-all-start = ((bf16[32,2,128]{2,1,0:T(2,128)(2,1)}), bf16[32,2,128]{2,1,0:T(2,128)(2,1)S(1)}, u32[]{:S(2)}, u32[]{:S(2)}) async-start(bf16[32,2,128]{2,1,0:T(2,128)(2,1)} %reshape.190), calls=%async_computation | async-start | bytes 32768 | tf_op jit(solution)/shard_map/all_to_all | solution.py:63
  24.4 0.7 broadcast_clamp_fusion
  25.1 9.3 %all-to-all-done = bf16[32,2,128]{2,1,0:T(2,128)(2,1)S(1)} async-done(((bf16[32,2,128]{2,1,0:T(2,128)(2,1)}), bf16[32,2,128]{2,1,0:T(2,128)(2,1)S(1)}, u32[]{:S(2)}, u32[]{:S(2)}) %all-to-all-start) | async-done | bytes 16416 | tf_op jit(solution)/shard_map/all_to_all | solution.py:63
  34.4 0.1 reshape.191
  34.5 6.2 gather_fusion
  40.7 0.2 copy.63
  40.9 16.0 %all_to_all.83 = bf16[16,16,128]{2,0,1:T(8,128)(2,1)} all-to-all(bf16[16,16,128]{2,0,1:T(8,128)(2,1)S(1)} %bitcast.102), channel_id=1, replica_groups=mesh['dp'=32,'tensor'=16] {'tensor'}, dimensions={1} | all-to-all | bytes 131072 | tf_op jit(solution)/shard_map/all_to_all | solution.py:77
  56.9 0.9 all_to_all.71
  57.8 0.1 reshape.192
  58.0 13.7 %all_to_all.84 = bf16[32,2,128]{2,1,0:T(2,128)(2,1)S(1)} all-to-all(bf16[32,2,128]{2,1,0:T(2,128)(2,1)S(1)} %reshape.192), channel_id=1, replica_groups=mesh['dp'=32,'tensor'=16] {'dp'}, dimensions={0} | all-to-all | bytes 32768 | tf_op jit(solution)/shard_map/all_to_all | solution.py:62
  71.7 0.1 reshape.193
  71.8 6.2 gather_fusion.1
  78.0 0.8 copy.72
  78.8 5.1 all-to-all-start.4
  83.9 101.0 %all-gather.6.cloned.1.call-done = bf16[512,4096]{0,1:T(8,128)(2,1)} async-done(((bf16[512,128]{0,1:T(8,128)(2,1)}), bf16[512,4096]{0,1:T(8,128)(2,1)}) %all-gather.6.cloned.1.call-update) | async-done | bytes 4194320 | tf_op jit(solution)/shard_map/all_gather | solution.py:65
  184.9 6.4 copy.69
  191.3 0.6 copy-done
  191.9 8.0 %all-to-all-start.2 = ((bf16[512,16,256]{2,0,1:T(8,128)(2,1)}), bf16[512,16,256]{2,0,1:T(8,128)(2,1)}, u32[]{:S(2)}, u32[]{:S(2)}) async-start(bf16[512,16,256]{2,0,1:T(8,128)(2,1)} %copy.69), calls=%async_computation.2 | async-start | bytes 8388608 | tf_op jit(solution)/shard_map/all_to_all | solution.py:67
  200.0 0.7 all-gather.8.cloned.1.call-update
  200.8 0.1 copy.67
  200.9 0.1 broadcast_in_dim.48
  201.0 0.1 gt.20
  201.1 0.1 reduce_sum.27
  201.3 0.1 convert_element_type.68
  201.4 6.4 copy.64
  207.7 4.7 copy.65
  212.5 0.1 mul.101
  212.6 0.1 fusion.15
  212.8 0.3 multiply_cosine_fusion
  213.1 188.9 %all-gather.4.cloned.1.call-done = bf16[8192,128]{1,0:T(8,128)(2,1)} async-done(((bf16[256,128]{1,0:T(8,128)(2,1)}), bf16[8192,128]{1,0:T(8,128)(2,1)}) %all-gather.4.cloned.1.call-update) | async-done | bytes 2097168 | tf_op jit(solution)/shard_map/all_gather | solution.py:87
  402.0 3.8 fusion.4
  405.8 0.1 copy.66
  405.9 161.7 %all-gather.8.cloned.1.call-done = bf16[8192,128]{1,0:T(8,128)(2,1)} async-done(((bf16[256,128]{1,0:T(8,128)(2,1)}), bf16[8192,128]{1,0:T(8,128)(2,1)}) %all-gather.8.cloned.1.call-update) | async-done | bytes 2097168 | tf_op jit(solution)/shard_map/all_gather | solution.py:86
  567.6 3.7 fusion.36
  571.3 0.3 fusion.18
  571.6 6.4 copy.70
  578.0 4.7 fusion.1
  582.8 0.3 fusion.3
  583.1 0.2 multiply_reduce_fusion
  583.2 0.3 broadcast_multiply_fusion
  583.6 5.4 fusion
  589.0 0.3 convolution_convert_fusion.1
  589.3 0.8 copy.79
  590.1 175.8 %reduce-scatter.2.cloned.1.call-done = bf16[256,256]{0,1:T(8,128)(2,1)} async-done(((bf16[8192,256]{0,1:T(8,128)(2,1)}), bf16[256,256]{0,1:T(8,128)(2,1)}) %reduce-scatter.2.cloned.1.call-update) | async-done | bytes 131088 | tf_op jit(solution)/shard_map/reduce_scatter | solution.py:150
  765.9 1.7 copy.80
  (29 shorter events, 0.6 us)
Async XLA Ops:
  7.2 177.7 %all-gather.6.cloned.1.call-start = ((), (), s32[]{:S(2)}) async-start(), calls=%async_computation.7 | async-start | bytes 4325376 | tf_op jit(solution)/shard_map/all_gather | solution.py:65
  10.6 23.8 %all-to-all-start = ((bf16[32,2,128]{2,1,0:T(2,128)(2,1)}), bf16[32,2,128]{2,1,0:T(2,128)(2,1)S(1)}, u32[]{:S(2)}, u32[]{:S(2)}) async-start(bf16[32,2,128]{2,1,0:T(2,128)(2,1)} %reshape.190), calls=%async_computation | async-start | bytes 32768 | tf_op jit(solution)/shard_map/all_to_all | solution.py:63
  24.3 377.6 %all-gather.4.cloned.1.call-start = ((), (), s32[]{:S(2)}) async-start(), calls=%async_computation.6 | async-start | bytes 2162688 | tf_op jit(solution)/shard_map/all_gather | solution.py:87
  78.8 112.5 %all-to-all-start.4 = ((bf16[16,16,128]{2,0,1:T(8,128)(2,1)}), bf16[16,16,128]{2,0,1:T(8,128)(2,1)S(1)}, u32[]{:S(2)}, u32[]{:S(2)}) async-start(bf16[16,16,128]{2,0,1:T(8,128)(2,1)} %bitcast.22), calls=%async_computation.4 | async-start | bytes 131072 | tf_op jit(solution)/shard_map/all_to_all | solution.py:74
  191.3 9.5 %copy-start.2 = (s32[4,4]{1,0:T(4,128)S(1)}, s32[4,4]{1,0:T(4,128)}, u32[]{:S(2)}) copy-start(s32[4,4]{1,0:T(4,128)} %param.17) | copy-start | bytes 196
  191.3 0.6 copy-start
  191.9 379.7 %all-to-all-start.2 = ((bf16[512,16,256]{2,0,1:T(8,128)(2,1)}), bf16[512,16,256]{2,0,1:T(8,128)(2,1)}, u32[]{:S(2)}, u32[]{:S(2)}) async-start(bf16[512,16,256]{2,0,1:T(8,128)(2,1)} %copy.69), calls=%async_computation.2 | async-start | bytes 8388608 | tf_op jit(solution)/shard_map/all_to_all | solution.py:67
  200.0 367.6 %all-gather.8.cloned.1.call-start = ((), (), s32[]{:S(2)}) async-start(), calls=%async_computation.8 | async-start | bytes 2162688 | tf_op jit(solution)/shard_map/all_gather | solution.py:86
  200.7 565.1 %reduce-scatter.2.cloned.1.call-start = ((), (), s32[]{:S(2)}) async-start(), calls=%async_computation.9 | async-start | bytes 4325376 | tf_op jit(solution)/shard_map/reduce_scatter | solution.py:150
  207.7 4.7 copy-start.3
  405.8 165.6 %copy-start.1 = (bf16[256,256]{1,0:T(8,128)(2,1)S(1)}, bf16[256,256]{1,0:T(8,128)(2,1)}, u32[]{:S(2)}) copy-start(bf16[256,256]{1,0:T(8,128)(2,1)} %param.19) | copy-start | bytes 393220
Sparse Core Ops, SparseCore 0:
  10.7 174.1 all-gather.5
  187.0 214.9 all-gather.3
  404.6 162.9 all-gather.7
  589.2 176.6 reduce-scatter.1
where the time goes:
time: 775 us; the launch traced here: 774 us
  waiting for transfers between devices  637 us (82%)
  local copies, waits for them, and re-layouts  45.6 us (6%)
  blocking collectives  29.6 us (4%)
  starting transfers between devices  27 us (3%)
  matrix products  18.7 us (2%)
  between operations  14 us (2%)
    all_gather x1, waiting for transfers between devices, shards(): lax.all_gather(value_part, 'dp', axis=0, tiled=True)  189 us
    reduce_scatter x1, waiting for transfers between devices, shards(): lax.psum_scatter(lax.dot_general(columns, dq_rows, (((0,), (0,)), ((), ()...  176 us
    all_gather x1, waiting for transfers between devices, shards(): lax.all_gather(key_part, 'dp', axis=0, tiled=True)  162 us
    all_gather x1, waiting for transfers between devices, shards(): query_cols = lax.all_gather(query_weight, 'dp', axis=1, tiled=True)  101 us
    all_to_all x1, blocking collectives, shards(): lax.all_to_all(pair_buffer(pair_rows[1]), 'tensor', split_axis=1, concat_...  16 us
  transfers between devices with their start and end apart: 7, of which 5 were waited for; matrix products, arithmetic and copies ran while one was open for 6% of the time, Pallas kernels for 0%

commit v1 on v0

v1 whole, which is shorter than its diff:
```python
import math

import jax
import jax.numpy as jnp
from jax import lax
from jax.experimental import pallas as pl
from jax.experimental.pallas import tpu as pltpu
from jax.sharding import Mesh
from jax.sharding import PartitionSpec as P

HEAD = 128
BS = 64
TOK = 256
AXES = ("z", "yl", "yh", "xh", "xb", "c")
SIZES = (8, 4, 2, 2, 2, 2)
F32 = jnp.float32
BF16 = jnp.bfloat16
VMEM_LIMIT = 48 * 1024 * 1024


def params():
    return pltpu.CompilerParams(vmem_limit_bytes=VMEM_LIMIT)


def home_pairs(turn):
    pairs = []
    for z in range(8):
        for yl in range(4):
            for t in range(16):
                half = (yl % 2) ^ turn
                block = 2 * t + half
                owner = (4 * z + yl) // 2
                pairs.append(((4 * z + yl) * 16 + t, block * 16 + owner))
    return pairs


def swap(value, axis, size, offset):
    return lax.ppermute(value, axis, [(i, i ^ offset) for i in range(size)])


def cut_kernel(where_ref, states_ref, one_ref, two_ref, three_ref, sems):
    core, lane = where_ref[0], where_ref[1]
    copies = []
    for number, out in enumerate((one_ref, two_ref, three_ref)):
        other = lane ^ (number + 1)
        for part in range(4):
            start = pl.multiple_of((4 * core + part) * 1024 + other * 256, 256)
            copies.append(
                pltpu.make_async_copy(
                    states_ref.at[:, pl.ds(start, 256)],
                    out.at[:, pl.ds(256 * part, 256)],
                    sems.at[number * 4 + part],
                )
            )
    for copy in copies:
        copy.start()
    for copy in copies:
        copy.wait()


def cut(where, states):
    shape = jax.ShapeDtypeStruct((TOK, 1024), BF16)
    return pl.pallas_call(
        cut_kernel,
        out_shape=(shape,) * 3,
        in_specs=[pl.BlockSpec(memory_space=pltpu.SMEM), pl.BlockSpec(memory_space=pl.ANY)],
        out_specs=(pl.BlockSpec(memory_space=pl.ANY),) * 3,
        scratch_shapes=[pltpu.SemaphoreType.DMA((12,))],
        compiler_params=params(),
        name="cut_states",
    )(where, states)


def z_block(step, where):
    return 4 * (where[0] ^ (step // 4)) + step % 4


def token_specs():
    own = pl.BlockSpec((TOK, 256), lambda i, w: (0, 4 * z_block(i, w) + w[1]))
    near = [pl.BlockSpec((TOK, 256), lambda i, w: (0, jnp.minimum(i, 3)))] * 3
    far = pl.BlockSpec((3, TOK, 256), lambda i, w: (0, 0, jnp.maximum(i - 4, 0)))
    return [own, *near, far]


def project_kernel(where_ref, own, n1, n2, n3, far, weights, own_out, o1, o2, o3, q_acc, kv_acc):
    step = pl.program_id(0)

    @pl.when(step == 0)
    def _():
        q_acc[...] = jnp.zeros_like(q_acc)
        kv_acc[...] = jnp.zeros_like(kv_acc)

    w_q = jnp.concatenate([weights[0, 0, :256, :], weights[0, 1, :256, :]], axis=1)
    w_kv = []
    for chunk in range(2):
        base = 256 + 32 * chunk
        w_kv.append(
            jnp.concatenate(
                [
                    weights[0, 0, base : base + 16, :],
                    weights[0, 1, base : base + 16, :],
                    weights[0, 0, base + 16 : base + 32, :],
                    weights[0, 1, base + 16 : base + 32, :],
                ],
                axis=0,
            )
        )
    w_kv = jnp.concatenate(w_kv, axis=1)

    def add(tokens):
        for j, x in enumerate(tokens):
            rows = pl.ds(j * TOK, TOK)
            q_acc[rows, :] += jnp.dot(x, w_q, preferred_element_type=F32)
            kv_acc[rows, :] += lax.dot_general(
                x, w_kv, (((1,), (1,)), ((), ())), preferred_element_type=F32
            )

    @pl.when(step < 4)
    def _():
        add((own[...], n1[...], n2[...], n3[...]))

    @pl.when(step >= 4)
    def _():
        add((own[...], far[0], far[1], far[2]))

    @pl.when(step == 7)
    def _():
        for j, out in enumerate((own_out, o1, o2, o3)):
            rows = pl.ds(j * TOK, TOK)
            out[:256, :] = q_acc[rows, :].astype(out.dtype)
            out[256:, :] = kv_acc[rows, :].T.astype(out.dtype)


def project(where, states, near, far, weights):
    full = pl.BlockSpec((320, 256), lambda i, w: (0, 0))
    return pl.pallas_call(
        project_kernel,
        out_shape=(
            jax.ShapeDtypeStruct((320, 256), F32),
            jax.ShapeDtypeStruct((320, 256), BF16),
            jax.ShapeDtypeStruct((320, 256), BF16),
            jax.ShapeDtypeStruct((320, 256), BF16),
        ),
        grid_spec=pltpu.PrefetchScalarGridSpec(
            num_scalar_prefetch=1,
            grid=(8,),
            in_specs=[
                *token_specs(),
                pl.BlockSpec((1, 2, 320, 128), lambda i, w: (z_block(i, w), 0, 0, 0)),
            ],
            out_specs=[full] * 4,
            scratch_shapes=[pltpu.VMEM((4 * TOK, 256), F32), pltpu.VMEM((4 * TOK, 64), F32)],
        ),
        compiler_params=params(),
        name="project",
    )(where, states, *near, far, weights)


def attend_kernel(
    q0, q1, q2, q3, kv, visible, weighted, cos_q, sin_q, cos_k, sin_k, attn_out, dq_out
):
    scaling = 1.0 / math.sqrt(HEAD)
    k_lin = jnp.concatenate([kv[s, :32, :] for s in range(4)], axis=0)
    values = jnp.concatenate([kv[s, 32:, :] for s in range(4)], axis=0).astype(BF16)
    k1, k2 = k_lin[:64], k_lin[64:]
    ck, sk = cos_k[...], sin_k[...]
    keys = jnp.concatenate([k1 * ck - k2 * sk, k2 * ck + k1 * sk], axis=0).astype(BF16)
    seen = visible[...] > 0
    cq, sq = cos_q[...], sin_q[...]
    for head in range(2):
        cols = pl.ds(head * HEAD, HEAD)
        q_lin = q0[:256, cols]
        for part in (q1, q2, q3):
            q_lin = q_lin + part[:256, cols].astype(F32)
        queries = ((q_lin * cq + pltpu.roll(q_lin, 64, 1) * sq) * scaling).astype(BF16)
        scores = jnp.dot(queries, keys, preferred_element_type=F32)
        raised = jnp.where(seen, jnp.exp(scores), 0.0)
        attend = raised / jnp.sum(raised, axis=1, keepdims=True)
        mixed = lax.dot_general(
            attend.astype(BF16), values, (((1,), (1,)), ((), ())), preferred_element_type=F32
        )
        attn_out[:, cols] = mixed.astype(BF16)
        pressure = jnp.dot(weighted[:, cols], values, preferred_element_type=F32)
        centre = jnp.sum(attend * pressure, axis=1, keepdims=True)
        slope = (attend * (pressure - centre)).astype(BF16)
        dq_rot = (
            lax.dot_general(slope, keys, (((1,), (1,)), ((), ())), preferred_element_type=F32)
            * scaling
        )
        dq = dq_rot * cq - pltpu.roll(dq_rot, 64, 1) * sq
        dq_out[cols, :] = dq.T.astype(BF16)


def attend(parts, kv, visible, weighted, tables):
    return pl.pallas_call(
        attend_kernel,
        out_shape=(
            jax.ShapeDtypeStruct((TOK, 256), BF16),
            jax.ShapeDtypeStruct((256, TOK), BF16),
        ),
        compiler_params=params(),
        name="attend",
    )(*parts, kv, visible, weighted, *tables)


def gradient_kernel(where_ref, own, n1, n2, n3, far, d0, d1, d2, d3, out):
    step = pl.program_id(0)

    def term(tokens):
        total = None
        for x, d in zip(tokens, (d0, d1, d2, d3)):
            product = jnp.dot(d[...], x, preferred_element_type=F32)
            total = product if total is None else total + product
        out[0] = total.astype(BF16)

    @pl.when(step < 4)
    def _():
        term((own[...], n1[...], n2[...], n3[...]))

    @pl.when(step >= 4)
    def _():
        term((own[...], far[0], far[1], far[2]))


def gradient(where, states, near, far, slopes):
    whole = pl.BlockSpec((256, TOK), lambda i, w: (0, 0))
    return pl.pallas_call(
        gradient_kernel,
        out_shape=jax.ShapeDtypeStruct((8, 256, 256), BF16),
        grid_spec=pltpu.PrefetchScalarGridSpec(
            num_scalar_prefetch=1,
            grid=(8,),
            in_specs=[*token_specs(), *[whole] * 4],
            out_specs=pl.BlockSpec((1, 256, 256), lambda i, w: (z_block(i, w), 0, 0)),
        ),
        compiler_params=params(),
        name="gradient",
    )(where, states, *near, far, *slopes)


def total_kernel(terms, out):
    total = terms[0].astype(F32)
    for z in range(1, 8):
        total = total + terms[z].astype(F32)
    out[...] = total.T


def add_up(terms):
    return pl.pallas_call(
        total_kernel,
        out_shape=jax.ShapeDtypeStruct((256, 256), F32),
        compiler_params=params(),
        name="add_up",
    )(terms)


def shards(states, query_weight, key_matrix, value_matrix, block_mask, risk_weight, upstream):
    core = lax.axis_index("c")
    lane = lax.axis_index("yl")
    where = jnp.stack([core, lane]).astype(jnp.int32)

    key_t, value_t = key_matrix.T, value_matrix.T
    halves = []
    for half in range(2):
        a, b, e = 256 * half, 256 * half + 128, 256 * half + 256
        halves.append(
            jnp.concatenate(
                [
                    query_weight[a:e],
                    key_t[:, a:b],
                    value_t[:, a:b],
                    key_t[:, b:e],
                    value_t[:, b:e],
                ],
                axis=0,
            )
        )
    even = lane % 2 == 0
    first = jnp.where(even, halves[0], halves[1])
    second = jnp.where(even, halves[1], halves[0])
    first = lax.ppermute(first, AXES, home_pairs(0))
    second = lax.ppermute(second, AXES, home_pairs(1))

    outgoing = cut(where, states)
    near = [swap(outgoing[j - 1], "yl", 4, j) for j in (1, 2, 3)]

    piece = jnp.stack([jnp.where(even, first, second), jnp.where(even, second, first)])
    weights = lax.all_to_all(
        jnp.broadcast_to(piece[None], (8,) + piece.shape), "z", split_axis=0, concat_axis=0
    )
    far = swap(jnp.stack(near), "c", 2, 1)

    parts = project(where, states, near, far, weights)
    parts = (parts[0], *[swap(parts[j], "yl", 4, j) for j in (1, 2, 3)])
    kv = parts[0][256:]
    for part in parts[1:]:
        kv = kv + part[256:].astype(F32)
    kv = lax.all_gather(kv, ("xb", "c"), axis=0, tiled=False)

    depths = jnp.sum(block_mask, axis=1) - 1
    places = (depths[:, None] * BS + jnp.arange(BS, dtype=jnp.int32)[None, :]).reshape(TOK)
    frequency = jnp.exp(
        -math.log(1000000.0) * jnp.arange(HEAD // 2, dtype=F32) * 2.0 / HEAD
    )
    angles = places.astype(F32)[:, None] * frequency[None, :]
    cosine, sine = jnp.cos(angles), jnp.sin(angles)
    tables = (
        jnp.concatenate([cosine, cosine], axis=1),
        jnp.concatenate([-sine, sine], axis=1),
        cosine.T,
        sine.T,
    )
    position = jnp.arange(TOK, dtype=jnp.int32)
    blocks = position // BS
    wide_mask = jnp.repeat(jnp.repeat(block_mask, BS, axis=0), BS, axis=1) > 0
    visible = wide_mask & (
        (blocks[:, None] != blocks[None, :]) | (position[:, None] >= position[None, :])
    )
    visible = visible.astype(F32)
    weighted = (upstream.astype(F32) * jnp.repeat(risk_weight, BS)[:, None]).astype(BF16)

    attn_out, dq = attend(parts, kv, visible, weighted, tables)
    slopes = (dq, *[swap(dq, "yl", 4, j) for j in (1, 2, 3)])
    terms = gradient(where, states, near, far, slopes)
    terms = lax.all_to_all(terms, "z", split_axis=0, concat_axis=0)
    return attn_out, add_up(terms)


def solution(mesh):
    fine = Mesh(mesh.devices.reshape(SIZES), AXES)
    dp, tensor = ("z", "yl"), ("yh", "xh", "xb", "c")
    in_specs = (
        P(dp, None),
        P(tensor, dp),
        P(tensor, dp),
        P(tensor, dp),
        P(dp, None),
        P(dp),
        P(dp, tensor),
    )
    out_specs = (P(dp, tensor), P(dp, tensor))
    return jax.shard_map(shards, mesh=fine, in_specs=in_specs, out_specs=out_specs, check_vma=False)
```

time: 775 us -> 209 us (0.27)
  waiting for transfers between devices: 637 us -> 60.2 us
  starting transfers between devices: 27 us -> 67.4 us
  local copies, waits for them, and re-layouts: 45.6 us -> 12.2 us
  matrix products: 18.7 us -> 0 us
  Pallas kernels: 0 us -> 17.1 us
  between operations: 14 us -> 0.93 us
  blocking collectives: 29.6 us -> 40.7 us
    all_gather x3 -> x0, waiting for transfers between devices: 452 us -> none  [the longest x1 189 us: shards(): lax.all_gather(value_part, 'dp', axis=0, tiled=True)]
    reduce_scatter x1 -> x0, waiting for transfers between devices: 176 us -> none  [shards(): lax.psum_scatter(lax.dot_general(columns, dq_rows, (((0,), (0,)), ((), ()...]
    ppermute x0 -> x12, waiting for transfers between devices: none -> 60.2 us  [the longest x10 52 us: swap(): return lax.ppermute(value, axis, [(i, i ^ offset) for i in range(size)])]
    ppermute x0 -> x12, starting transfers between devices: none -> 52 us  [the longest x10 41.2 us: swap(): return lax.ppermute(value, axis, [(i, i ^ offset) for i in range(size)])]
    dot_general x8 -> x0, matrix products: 18.7 us -> none  [the longest x1 5.4 us: shards(): lax.dot_general(columns, dq_rows, (((0,), (0,)), ((), ())), preferred_ele...]
    pallas_call x0 -> x5, Pallas kernels: none -> 17.1 us  [the longest x1 6.97 us: project(): pl.pallas_call(project_kernel, out_shape=(jax.ShapeDtypeStruct((320, 256)...]
    gather x4 -> x0, local copies, waits for them, and re-layouts: 13.4 us -> none  [pair_buffer(): picked = row_block[:, column_table]]
    reshape x2 -> x0, local copies, waits for them, and re-layouts: 12.8 us -> none  [the longest x1 6.42 us: shards(): query_cols.reshape(query_cols.shape[0], tensor_size, per_dev * HEAD_DIMEN...]
  transfers between devices with their start and end apart: 7 -> 13, of which waited for: 5 -> 5; matrix products, arithmetic and copies ran while one was open for 6% -> 4% of each run, Pallas kernels for 0% -> 1%
where the time goes in v1:
time: 209 us; the launch traced here: 205 us
  starting transfers between devices  67.4 us (32%)
  waiting for transfers between devices  60.2 us (29%)
  blocking collectives  40.7 us (19%)
  Pallas kernels  17.1 us (8%)
  local copies, waits for them, and re-layouts  12.2 us (6%)
  other arithmetic  6.1 us (3%)
    ppermute x10, waiting for transfers between devices, swap(): return lax.ppermute(value, axis, [(i, i ^ offset) for i in range(size)])  52 us
    ppermute x10, starting transfers between devices, swap(): return lax.ppermute(value, axis, [(i, i ^ offset) for i in range(size)])  41.2 us
    all_to_all x1, blocking collectives, shards(): terms = lax.all_to_all(terms, 'z', split_axis=0, concat_axis=0)  34.9 us
    all_to_all x1, starting transfers between devices, shards(): lax.all_to_all(jnp.broadcast_to(piece[None], (8,) + piece.shape), 'z', sp...  15.4 us
    unnamed x30, local copies, waits for them, and re-layouts  8.88 us
    ppermute x1, waiting for transfers between devices, shards(): second = lax.ppermute(second, AXES, home_pairs(1))  8.17 us
    ppermute x1, starting transfers between devices, shards(): first = lax.ppermute(first, AXES, home_pairs(0))  7.81 us
    pallas_call x1, Pallas kernels, project(): pl.pallas_call(project_kernel, out_shape=(jax.ShapeDtypeStruct((320, 256)...  6.97 us
  transfers between devices with their start and end apart: 13, of which 5 were waited for; matrix products, arithmetic and copies ran while one was open for 4% of the time, Pallas kernels for 1%

profile of v1, /device:TPU:6, one launch (start us, length us, event | category | flops | bytes accessed | tf_op | source)
XLA Modules:
  0.0 204.5 jit_solution(6159662009725563808)
XLA Ops:
  0.6 0.9 slice_dynamic-update-slice_fusion.1
  1.5 0.7 constant_dynamic-update-slice_fusion.3
  2.3 0.7 constant_dynamic-update-slice_fusion.2
  3.0 0.7 constant_dynamic-update-slice_fusion.1
  3.7 0.7 constant_dynamic-update-slice_fusion
  4.4 7.8 %collective-permute-start.4 = (bf16[320,128]{1,0:T(8,128)(2,1)S(1)}, bf16[320,128]{1,0:T(8,128)(2,1)S(1)}, u32[]{:S(2)}, u32[]{:S(2)}) collective-permute-start(bf16[320,128]{1,0:T(8,128)(2,1)S(1)} %get-tuple-element.22), channel_id=1, source_target_pairs={{0,0},{1,32},{2,64},{3,96},{4,128},{5,160},{6,192},{7,224},{8,256}... | collective-permute-start | bytes 245768 | tf_op jit(solution)/shard_map/ppermute | solution.py:281
  12.2 3.0 %collective-permute-start.5 = (bf16[320,128]{1,0:T(8,128)(2,1)S(1)}, bf16[320,128]{1,0:T(8,128)(2,1)S(1)}, u32[]{:S(2)}, u32[]{:S(2)}) collective-permute-start(bf16[320,128]{1,0:T(8,128)(2,1)S(1)} %get-tuple-element.23), channel_id=1, source_target_pairs={{0,16},{1,48},{2,80},{3,112},{4,144},{5,176},{6,208},{7,240},{8,27... | collective-permute-start | bytes 245768 | tf_op jit(solution)/shard_map/ppermute | solution.py:282
  15.2 8.2 %collective-permute-done.5 = bf16[320,128]{1,0:T(8,128)(2,1)S(1)} collective-permute-done((bf16[320,128]{1,0:T(8,128)(2,1)S(1)}, bf16[320,128]{1,0:T(8,128)(2,1)S(1)}, u32[]{:S(2)}, u32[]{:S(2)}) %collective-permute-start.5) | collective-permute-done | bytes 81952 | tf_op jit(solution)/shard_map/ppermute | solution.py:282
  23.4 1.3 broadcast_in_dim.8
  24.7 15.4 %all-to-all-start = ((bf16[8,2,320,128]{3,2,1,0:T(8,128)(2,1)}), bf16[8,2,320,128]{3,2,1,0:T(8,128)(2,1)S(1)}, u32[]{:S(2)}, u32[]{:S(2)}) async-start(bf16[8,2,320,128]{3,2,1,0:T(8,128)(2,1)} %broadcast_in_dim.8), calls=%async_computation | async-start | bytes 2621440 | tf_op jit(solution)/shard_map/all_to_all | solution.py:288
  40.2 2.2 %copy-done = bf16[256,8192]{1,0:T(8,128)(2,1)S(1)} copy-done((bf16[256,8192]{1,0:T(8,128)(2,1)S(1)}, bf16[256,8192]{1,0:T(8,128)(2,1)}, u32[]{:S(2)}) %copy-start) | copy-done | bytes 4194328
  42.4 1.7 cut_states.1
  44.0 4.3 %collective-permute-start = (bf16[256,1024]{1,0:T(8,128)(2,1)}, bf16[256,1024]{1,0:T(8,128)(2,1)S(1)}, u32[]{:S(2)}, u32[]{:S(2)}) collective-permute-start(bf16[256,1024]{1,0:T(8,128)(2,1)} %get-tuple-element.11), channel_id=1, source_target_pairs={{0,16},{16,0},{32,48},{48,32},{1,17},{17,1},{33,49},{49,33},{2,18}... | collective-permute-start | bytes 1572872 | tf_op jit(solution)/shard_map/ppermute | solution.py:38
  48.3 2.4 %collective-permute-start.1 = (bf16[256,1024]{1,0:T(8,128)(2,1)}, bf16[256,1024]{1,0:T(8,128)(2,1)S(1)}, u32[]{:S(2)}, u32[]{:S(2)}) collective-permute-start(bf16[256,1024]{1,0:T(8,128)(2,1)} %get-tuple-element.12), channel_id=1, source_target_pairs={{0,32},{16,48},{32,0},{48,16},{1,33},{17,49},{33,1},{49,17},{2,34}... | collective-permute-start | bytes 1572872 | tf_op jit(solution)/shard_map/ppermute | solution.py:38
  50.7 3.8 %collective-permute-start.2 = (bf16[256,1024]{1,0:T(8,128)(2,1)S(1)}, bf16[256,1024]{1,0:T(8,128)(2,1)S(1)}, u32[]{:S(2)}, u32[]{:S(2)}) collective-permute-start(bf16[256,1024]{1,0:T(8,128)(2,1)S(1)} %get-tuple-element.13), channel_id=1, source_target_pairs={{0,48},{16,32},{32,16},{48,0},{1,49},{17,33},{33,17},{49,1},{2,50}... | collective-permute-start | bytes 1572872 | tf_op jit(solution)/shard_map/ppermute | solution.py:38
  54.5 0.1 reduce_sum.9
  54.6 13.3 %collective-permute-done.n1 = bf16[256,1024]{1,0:T(8,128)(2,1)S(1)} collective-permute-done((bf16[256,1024]{1,0:T(8,128)(2,1)}, bf16[256,1024]{1,0:T(8,128)(2,1)S(1)}, u32[]{:S(2)}, u32[]{:S(2)}) %collective-permute-start) | collective-permute-done | bytes 524320 | tf_op jit(solution)/shard_map/ppermute | solution.py:38
  67.9 20.7 %collective-permute-done.1.n2 = bf16[256,1024]{1,0:T(8,128)(2,1)S(1)} collective-permute-done((bf16[256,1024]{1,0:T(8,128)(2,1)}, bf16[256,1024]{1,0:T(8,128)(2,1)S(1)}, u32[]{:S(2)}, u32[]{:S(2)}) %collective-permute-start.1) | collective-permute-done | bytes 524320 | tf_op jit(solution)/shard_map/ppermute | solution.py:38
  88.6 1.4 pad_maximum_fusion
  90.0 0.8 copy-done.1
  90.8 0.8 copy-done.4
  91.6 1.9 collective-permute-start.3
  93.5 0.1 copy.9
  93.7 0.1 gt.16
  93.8 0.8 copy.10
  94.6 0.1 mul.44
  94.8 0.1 convert_element_type.35
  94.9 1.0 multiply_convert_fusion.weighted
  95.9 1.7 fusion.2.visible
  97.6 1.3 fusion.3
  98.9 1.0 copy-done.2
  99.9 1.0 copy-done.5
  101.0 7.0 %project.1 = (f32[320,256]{1,0:T(8,128)S(1)}, bf16[320,256]{1,0:T(8,128)(2,1)S(1)}, bf16[320,256]{1,0:T(8,128)(2,1)S(1)}, bf16[320,256]{1,0:T(8,128)(2,1)S(1)}) custom-call(s32[2]{0:T(128)S(1)} %pad_add_fusion.where_ref, bf16[256,8192]{1,0:T(8,128)(2,1)} %own.3, bf16[256,1024]{1,0:T(8,128)(2,1)S(1)} %collective-permute-done.n1, ...), custom_call_target="tpu_custom_call" | custom-call | tf_op jit(solution)/shard_map/project/pallas_call | solution.py:136
  107.9 11.1 %collective-permute-start.6 = (bf16[320,256]{1,0:T(8,128)(2,1)S(1)}, bf16[320,256]{1,0:T(8,128)(2,1)S(1)}, u32[]{:S(2)}, u32[]{:S(2)}) collective-permute-start(bf16[320,256]{1,0:T(8,128)(2,1)S(1)} %get-tuple-element.15), channel_id=1, source_target_pairs={{0,16},{16,0},{32,48},{48,32},{1,17},{17,1},{33,49},{49,33},{2,18}... | collective-permute-start | bytes 491528 | tf_op jit(solution)/shard_map/ppermute | solution.py:38
  119.1 2.4 %collective-permute-start.7 = (bf16[320,256]{1,0:T(8,128)(2,1)S(1)}, bf16[320,256]{1,0:T(8,128)(2,1)S(1)}, u32[]{:S(2)}, u32[]{:S(2)}) collective-permute-start(bf16[320,256]{1,0:T(8,128)(2,1)S(1)} %get-tuple-element.16), channel_id=1, source_target_pairs={{0,32},{16,48},{32,0},{48,16},{1,33},{17,49},{33,1},{49,17},{2,34}... | collective-permute-start | bytes 491528 | tf_op jit(solution)/shard_map/ppermute | solution.py:38
  121.5 3.7 %collective-permute-start.8 = (bf16[320,256]{1,0:T(8,128)(2,1)S(1)}, bf16[320,256]{1,0:T(8,128)(2,1)S(1)}, u32[]{:S(2)}, u32[]{:S(2)}) collective-permute-start(bf16[320,256]{1,0:T(8,128)(2,1)S(1)} %get-tuple-element.17), channel_id=1, source_target_pairs={{0,48},{16,32},{32,16},{48,0},{1,49},{17,33},{33,17},{49,1},{2,50}... | collective-permute-start | bytes 491528 | tf_op jit(solution)/shard_map/ppermute | solution.py:38
  125.3 0.3 multiply_sine_fusion.1
  125.6 0.1 pad_maximum_fusion.2
  125.8 10.0 %collective-permute-done.7.q2 = bf16[320,256]{1,0:T(8,128)(2,1)S(1)} collective-permute-done((bf16[320,256]{1,0:T(8,128)(2,1)S(1)}, bf16[320,256]{1,0:T(8,128)(2,1)S(1)}, u32[]{:S(2)}, u32[]{:S(2)}) %collective-permute-start.7) | collective-permute-done | bytes 163872 | tf_op jit(solution)/shard_map/ppermute | solution.py:38
  135.8 5.8 %all-gather = f32[256,256]{1,0:T(8,128)S(1)} all-gather(f32[64,256]{1,0:T(8,128)S(1)} %convert_add_fusion), channel_id=2, replica_groups=mesh['z'=8,'yl'=4,'yh'=2,'xh'=2,'xb'=2,'c'=2] {'xb','c'}, dimensions={0}, use_global_device_ids=true | all-gather | bytes 327680 | tf_op jit(solution)/shard_map/all_gather | solution.py:298
  141.6 1.5 attend.1
  143.1 5.4 %collective-permute-start.9 = (bf16[256,256]{1,0:T(8,128)(2,1)S(1)}, bf16[256,256]{1,0:T(8,128)(2,1)S(1)}, u32[]{:S(2)}, u32[]{:S(2)}) collective-permute-start(bf16[256,256]{1,0:T(8,128)(2,1)S(1)} %get-tuple-element.19.d0), channel_id=1, source_target_pairs={{0,16},{16,0},{32,48},{48,32},{1,17},{17,1},{33,49},{49,33},{2,18}... | collective-permute-start | bytes 393224 | tf_op jit(solution)/shard_map/ppermute | solution.py:38
  148.5 2.4 %collective-permute-start.10 = (bf16[256,256]{1,0:T(8,128)(2,1)S(1)}, bf16[256,256]{1,0:T(8,128)(2,1)S(1)}, u32[]{:S(2)}, u32[]{:S(2)}) collective-permute-start(bf16[256,256]{1,0:T(8,128)(2,1)S(1)} %get-tuple-element.19.d0), channel_id=1, source_target_pairs={{0,32},{16,48},{32,0},{48,16},{1,33},{17,49},{33,1},{49,17},{2,34}... | collective-permute-start | bytes 393224 | tf_op jit(solution)/shard_map/ppermute | solution.py:38
  150.9 3.7 %collective-permute-start.11 = (bf16[256,256]{1,0:T(8,128)(2,1)S(1)}, bf16[256,256]{1,0:T(8,128)(2,1)S(1)}, u32[]{:S(2)}, u32[]{:S(2)}) collective-permute-start(bf16[256,256]{1,0:T(8,128)(2,1)S(1)} %get-tuple-element.19.d0), channel_id=1, source_target_pairs={{0,48},{16,32},{32,16},{48,0},{1,49},{17,33},{33,17},{49,1},{2,50}... | collective-permute-start | bytes 393224 | tf_op jit(solution)/shard_map/ppermute | solution.py:38
  154.7 8.0 %collective-permute-done.10.d2 = bf16[256,256]{1,0:T(8,128)(2,1)S(1)} collective-permute-done((bf16[256,256]{1,0:T(8,128)(2,1)S(1)}, bf16[256,256]{1,0:T(8,128)(2,1)S(1)}, u32[]{:S(2)}, u32[]{:S(2)}) %collective-permute-start.10) | collective-permute-done | bytes 131104 | tf_op jit(solution)/shard_map/ppermute | solution.py:38
  162.7 6.1 %gradient.1 = bf16[8,256,256]{2,1,0:T(8,128)(2,1)S(1)} custom-call(s32[2]{0:T(128)S(1)} %pad_add_fusion.where_ref, bf16[256,8192]{1,0:T(8,128)(2,1)} %own.3, bf16[256,1024]{1,0:T(8,128)(2,1)S(1)} %collective-permute-done.n1, bf16[256,1024]{1,0:T(8,128)(2,1)S(1)} %copy-done.3, bf16[256,1024]{1,0:T(8,128)(2,1)S(1)} %copy-done.6, ...), custom_call_target="tpu_custom_call" | custom-call | tf_op jit(solution)/shard_map/gradient/pallas_call | solution.py:227
  168.7 34.9 %all_to_all.10.terms = bf16[8,256,256]{2,1,0:T(8,128)(2,1)S(1)} all-to-all(bf16[8,256,256]{2,1,0:T(8,128)(2,1)S(1)} %gradient.1), channel_id=1, replica_groups=mesh['z'=8,'yl'=4,'yh'=2,'xh'=2,'xb'=2,'c'=2] {'z'}, dimensions={0} | all-to-all | bytes 2097152 | tf_op jit(solution)/shard_map/all_to_all | solution.py:325
  203.6 0.9 add_up.1
  (42 shorter events, 0.5 us)
Async XLA Ops:
  4.4 10.8 %collective-permute-start.4 = (bf16[320,128]{1,0:T(8,128)(2,1)S(1)}, bf16[320,128]{1,0:T(8,128)(2,1)S(1)}, u32[]{:S(2)}, u32[]{:S(2)}) collective-permute-start(bf16[320,128]{1,0:T(8,128)(2,1)S(1)} %get-tuple-element.22), channel_id=1, source_target_pairs={{0,0},{1,32},{2,64},{3,96},{4,128},{5,160},{6,192},{7,224},{8,256}... | collective-permute-start | bytes 245768 | tf_op jit(solution)/shard_map/ppermute | solution.py:281
  12.2 11.1 %collective-permute-start.5 = (bf16[320,128]{1,0:T(8,128)(2,1)S(1)}, bf16[320,128]{1,0:T(8,128)(2,1)S(1)}, u32[]{:S(2)}, u32[]{:S(2)}) collective-permute-start(bf16[320,128]{1,0:T(8,128)(2,1)S(1)} %get-tuple-element.23), channel_id=1, source_target_pairs={{0,16},{1,48},{2,80},{3,112},{4,144},{5,176},{6,208},{7,240},{8,27... | collective-permute-start | bytes 245768 | tf_op jit(solution)/shard_map/ppermute | solution.py:282
  24.7 74.2 %all-to-all-start = ((bf16[8,2,320,128]{3,2,1,0:T(8,128)(2,1)}), bf16[8,2,320,128]{3,2,1,0:T(8,128)(2,1)S(1)}, u32[]{:S(2)}, u32[]{:S(2)}) async-start(bf16[8,2,320,128]{3,2,1,0:T(8,128)(2,1)} %broadcast_in_dim.8), calls=%async_computation | async-start | bytes 2621440 | tf_op jit(solution)/shard_map/all_to_all | solution.py:288
  40.2 2.2 %copy-start = (bf16[256,8192]{1,0:T(8,128)(2,1)S(1)}, bf16[256,8192]{1,0:T(8,128)(2,1)}, u32[]{:S(2)}) copy-start(bf16[256,8192]{1,0:T(8,128)(2,1)} %own.3) | copy-start | bytes 12582916
  42.4 12.1 %copy-start.11 = (s32[4,4]{1,0:T(4,128)S(1)}, s32[4,4]{1,0:T(4,128)}, u32[]{:S(2)}) copy-start(s32[4,4]{1,0:T(4,128)} %param.11) | copy-start | bytes 196
  44.0 23.9 %collective-permute-start = (bf16[256,1024]{1,0:T(8,128)(2,1)}, bf16[256,1024]{1,0:T(8,128)(2,1)S(1)}, u32[]{:S(2)}, u32[]{:S(2)}) collective-permute-start(bf16[256,1024]{1,0:T(8,128)(2,1)} %get-tuple-element.11), channel_id=1, source_target_pairs={{0,16},{16,0},{32,48},{48,32},{1,17},{17,1},{33,49},{49,33},{2,18}... | collective-permute-start | bytes 1572872 | tf_op jit(solution)/shard_map/ppermute | solution.py:38
  48.3 40.3 %collective-permute-start.1 = (bf16[256,1024]{1,0:T(8,128)(2,1)}, bf16[256,1024]{1,0:T(8,128)(2,1)S(1)}, u32[]{:S(2)}, u32[]{:S(2)}) collective-permute-start(bf16[256,1024]{1,0:T(8,128)(2,1)} %get-tuple-element.12), channel_id=1, source_target_pairs={{0,32},{16,48},{32,0},{48,16},{1,33},{17,49},{33,1},{49,17},{2,34}... | collective-permute-start | bytes 1572872 | tf_op jit(solution)/shard_map/ppermute | solution.py:38
  50.7 37.9 %collective-permute-start.2 = (bf16[256,1024]{1,0:T(8,128)(2,1)S(1)}, bf16[256,1024]{1,0:T(8,128)(2,1)S(1)}, u32[]{:S(2)}, u32[]{:S(2)}) collective-permute-start(bf16[256,1024]{1,0:T(8,128)(2,1)S(1)} %get-tuple-element.13), channel_id=1, source_target_pairs={{0,48},{16,32},{32,16},{48,0},{1,49},{17,33},{33,17},{49,1},{2,50}... | collective-permute-start | bytes 1572872 | tf_op jit(solution)/shard_map/ppermute | solution.py:38
  88.6 5.9 %copy-start.12 = (f32[4]{0:T(128)S(1)}, f32[4]{0:T(128)}, u32[]{:S(2)}) copy-start(f32[4]{0:T(128)} %param.12) | copy-start | bytes 52
  90.0 0.8 copy-start.1
  90.8 0.8 copy-start.4
  91.6 7.3 %collective-permute-start.3 = (bf16[3,256,1024]{2,1,0:T(8,128)(2,1)}, bf16[3,256,1024]{2,1,0:T(8,128)(2,1)S(1)}, u32[]{:S(2)}, u32[]{:S(2)}) collective-permute-start(bf16[3,256,1024]{2,1,0:T(8,128)(2,1)} %pad_maximum_fusion), channel_id=1, source_target_pairs={{0,1},{1,0},{2,3},{3,2},{4,5},{5,4},{6,7},{7,6},{8,9},{9,8},{10,11... | collective-permute-start | bytes 4718600 | tf_op jit(solution)/shard_map/ppermute | solution.py:38
  98.9 1.0 copy-start.2
  99.9 1.0 copy-start.5
  101.0 24.6 %copy-start.8 = (f32[256,64]{1,0:T(8,128)S(1)}, f32[256,64]{1,0:T(8,128)}, u32[]{:S(2)}) copy-start(f32[256,64]{1,0:T(8,128)} %get-tuple-element.36) | copy-start | bytes 196612
  101.0 24.7 %copy-start.9 = (f32[256,64]{1,0:T(8,128)S(1)}, f32[256,64]{1,0:T(8,128)}, u32[]{:S(2)}) copy-start(f32[256,64]{1,0:T(8,128)} %get-tuple-element.37) | copy-start | bytes 196612
  101.0 24.7 %copy-start.10 = (f32[256,64]{1,0:T(8,128)S(1)}, f32[256,64]{1,0:T(8,128)}, u32[]{:S(2)}) copy-start(f32[256,64]{1,0:T(8,128)} %get-tuple-element.38) | copy-start | bytes 196612
  101.0 40.6 %copy-start.7 = (f32[256,256]{1,0:T(8,128)S(1)}, f32[256,256]{1,0:T(8,128)}, u32[]{:S(2)}) copy-start(f32[256,256]{1,0:T(8,128)} %fusion.2.visible) | copy-start | bytes 786436
  107.9 17.8 %collective-permute-start.6 = (bf16[320,256]{1,0:T(8,128)(2,1)S(1)}, bf16[320,256]{1,0:T(8,128)(2,1)S(1)}, u32[]{:S(2)}, u32[]{:S(2)}) collective-permute-start(bf16[320,256]{1,0:T(8,128)(2,1)S(1)} %get-tuple-element.15), channel_id=1, source_target_pairs={{0,16},{16,0},{32,48},{48,32},{1,17},{17,1},{33,49},{49,33},{2,18}... | collective-permute-start | bytes 491528 | tf_op jit(solution)/shard_map/ppermute | solution.py:38
  119.1 16.7 %collective-permute-start.7 = (bf16[320,256]{1,0:T(8,128)(2,1)S(1)}, bf16[320,256]{1,0:T(8,128)(2,1)S(1)}, u32[]{:S(2)}, u32[]{:S(2)}) collective-permute-start(bf16[320,256]{1,0:T(8,128)(2,1)S(1)} %get-tuple-element.16), channel_id=1, source_target_pairs={{0,32},{16,48},{32,0},{48,16},{1,33},{17,49},{33,1},{49,17},{2,34}... | collective-permute-start | bytes 491528 | tf_op jit(solution)/shard_map/ppermute | solution.py:38
  121.5 14.3 %collective-permute-start.8 = (bf16[320,256]{1,0:T(8,128)(2,1)S(1)}, bf16[320,256]{1,0:T(8,128)(2,1)S(1)}, u32[]{:S(2)}, u32[]{:S(2)}) collective-permute-start(bf16[320,256]{1,0:T(8,128)(2,1)S(1)} %get-tuple-element.17), channel_id=1, source_target_pairs={{0,48},{16,32},{32,16},{48,0},{1,49},{17,33},{33,17},{49,1},{2,50}... | collective-permute-start | bytes 491528 | tf_op jit(solution)/shard_map/ppermute | solution.py:38
  125.6 37.1 %copy-start.3 = (bf16[256,1024]{1,0:T(8,128)(2,1)S(1)}, bf16[256,1024]{1,0:T(8,128)(2,1)}, u32[]{:S(2)}) copy-start(bf16[256,1024]{1,0:T(8,128)(2,1)} %copy-done.1) | copy-start | bytes 1572868
  125.6 37.1 %copy-start.6 = (bf16[256,1024]{1,0:T(8,128)(2,1)S(1)}, bf16[256,1024]{1,0:T(8,128)(2,1)}, u32[]{:S(2)}) copy-start(bf16[256,1024]{1,0:T(8,128)(2,1)} %copy-done.4) | copy-start | bytes 1572868
  143.1 11.6 %collective-permute-start.9 = (bf16[256,256]{1,0:T(8,128)(2,1)S(1)}, bf16[256,256]{1,0:T(8,128)(2,1)S(1)}, u32[]{:S(2)}, u32[]{:S(2)}) collective-permute-start(bf16[256,256]{1,0:T(8,128)(2,1)S(1)} %get-tuple-element.19.d0), channel_id=1, source_target_pairs={{0,16},{16,0},{32,48},{48,32},{1,17},{17,1},{33,49},{49,33},{2,18}... | collective-permute-start | bytes 393224 | tf_op jit(solution)/shard_map/ppermute | solution.py:38
  148.5 14.2 %collective-permute-start.10 = (bf16[256,256]{1,0:T(8,128)(2,1)S(1)}, bf16[256,256]{1,0:T(8,128)(2,1)S(1)}, u32[]{:S(2)}, u32[]{:S(2)}) collective-permute-start(bf16[256,256]{1,0:T(8,128)(2,1)S(1)} %get-tuple-element.19.d0), channel_id=1, source_target_pairs={{0,32},{16,48},{32,0},{48,16},{1,33},{17,49},{33,1},{49,17},{2,34}... | collective-permute-start | bytes 393224 | tf_op jit(solution)/shard_map/ppermute | solution.py:38
  150.9 11.7 %collective-permute-start.11 = (bf16[256,256]{1,0:T(8,128)(2,1)S(1)}, bf16[256,256]{1,0:T(8,128)(2,1)S(1)}, u32[]{:S(2)}, u32[]{:S(2)}) collective-permute-start(bf16[256,256]{1,0:T(8,128)(2,1)S(1)} %get-tuple-element.19.d0), channel_id=1, source_target_pairs={{0,48},{16,32},{32,16},{48,0},{1,49},{17,33},{33,17},{49,1},{2,50}... | collective-permute-start | bytes 393224 | tf_op jit(solution)/shard_map/ppermute | solution.py:38

commit v2 on v1

v2 whole, which is shorter than its diff:
```python
import math

import jax
import jax.numpy as jnp
from jax import lax
from jax.experimental import pallas as pl
from jax.experimental.pallas import tpu as pltpu
from jax.sharding import Mesh
from jax.sharding import PartitionSpec as P

HEAD = 128
BS = 64
TOK = 256
AXES = ("zh", "zb", "yu", "yb", "yh", "xh", "xb", "c")
SIZES = (4, 2, 2, 2, 2, 2, 2, 2)
GROUP = ("zb", "yb")
OTHERS = ("zh", "yu")
F32 = jnp.float32
BF16 = jnp.bfloat16
VMEM_LIMIT = 48 * 1024 * 1024


def params():
    return pltpu.CompilerParams(vmem_limit_bytes=VMEM_LIMIT)


def home_pairs(turn):
    pairs = []
    for d in range(32):
        for t in range(16):
            half = (d % 2) ^ turn
            pairs.append((d * 16 + t, (2 * t + half) * 16 + d // 2))
    return pairs


def swap(value, offset):
    return lax.ppermute(value, GROUP, [(i, i ^ offset) for i in range(4)])


def swap_core(value):
    return lax.ppermute(value, "c", [(0, 1), (1, 0)])


def block_of(part, core):
    return 4 * (core ^ (part // 4)) + part % 4


def cut_kernel(where_ref, states_ref, own_ref, one_ref, two_ref, three_ref, sems):
    core, place = where_ref[0], where_ref[1]
    copies = []
    for number, out in enumerate((own_ref, one_ref, two_ref, three_ref)):
        other = place ^ number
        for part in range(8 if number == 0 else 4):
            block = block_of(part, core)
            start = (block // 2) * 2048 + (block % 2) * 512 + (other // 2) * 1024 + (other % 2) * 256
            copies.append(
                pltpu.make_async_copy(
                    states_ref.at[:, pl.ds(pl.multiple_of(start, 256), 256)],
                    out.at[:, pl.ds(256 * part, 256)],
                    sems.at[len(copies)],
                )
            )
    for copy in copies:
        copy.start()
    for copy in copies:
        copy.wait()


def cut(where, states):
    part = jax.ShapeDtypeStruct((TOK, 1024), BF16)
    return pl.pallas_call(
        cut_kernel,
        out_shape=(jax.ShapeDtypeStruct((TOK, 2048), BF16), part, part, part),
        in_specs=[pl.BlockSpec(memory_space=pltpu.SMEM), pl.BlockSpec(memory_space=pl.ANY)],
        out_specs=(pl.BlockSpec(memory_space=pl.ANY),) * 4,
        scratch_shapes=[pltpu.SemaphoreType.DMA((20,))],
        compiler_params=params(),
        name="cut_states",
    )(where, states)


def pack_kernel(where_ref, query, key_t, value_t, first, second):
    odd = where_ref[1] % 2
    for turn, out in enumerate((first, second)):
        half = odd ^ turn
        out[:256, :] = query[pl.ds(pl.multiple_of(256 * half, 256), 256), :]
        for chunk in range(2):
            lanes = pl.ds(pl.multiple_of(256 * half + 128 * chunk, 128), 128)
            base = 256 + 32 * chunk
            out[base : base + 16, :] = key_t[:, lanes]
            out[base + 16 : base + 32, :] = value_t[:, lanes]


def pack(where, query, key_t, value_t):
    part = jax.ShapeDtypeStruct((320, 128), BF16)
    vmem = pl.BlockSpec(memory_space=pltpu.VMEM)
    return pl.pallas_call(
        pack_kernel,
        out_shape=(part, part),
        in_specs=[pl.BlockSpec(memory_space=pltpu.SMEM), vmem, vmem, vmem],
        compiler_params=params(),
        name="pack_weights",
    )(where, query, key_t, value_t)


def copies_kernel(where_ref, first, second, out):
    odd = where_ref[1] % 2
    for device in range(8):
        out[device, odd] = first[...]
        out[device, 1 - odd] = second[...]


def copies(where, first, second):
    vmem = pl.BlockSpec(memory_space=pltpu.VMEM)
    return pl.pallas_call(
        copies_kernel,
        out_shape=jax.ShapeDtypeStruct((8, 2, 320, 128), BF16),
        in_specs=[pl.BlockSpec(memory_space=pltpu.SMEM), vmem, vmem],
        compiler_params=params(),
        name="weight_copies",
    )(where, first, second)


def project_kernel(
    where_ref, own, n1, n2, n3, f1, f2, f3, weights, own_out, o1, o2, o3, w_q, w_kv
):
    core = where_ref[0]
    for part in range(8):
        block = block_of(part, core)
        for head in range(2):
            rows, cols = pl.ds(256 * part, 256), pl.ds(HEAD * head, HEAD)
            w_q[rows, cols] = weights[block, head, :256, :]
            for chunk in range(2):
                lanes = pl.ds(256 * part + 128 * chunk, 128)
                base = 256 + 32 * chunk
                w_kv[16 * head : 16 * head + 16, lanes] = weights[block, head, base : base + 16, :]
                w_kv[32 + 16 * head : 48 + 16 * head, lanes] = weights[
                    block, head, base + 16 : base + 32, :
                ]

    def product(x, rows):
        q = jnp.dot(x, w_q[rows, :], preferred_element_type=F32)
        kv = lax.dot_general(
            x, w_kv[:, rows], (((1,), (1,)), ((), ())), preferred_element_type=F32
        )
        return q, kv

    low, high = pl.ds(0, 1024), pl.ds(1024, 1024)
    pieces = (
        (own[:, low], own[:, high]),
        (n1[...], f1[...]),
        (n2[...], f2[...]),
        (n3[...], f3[...]),
    )
    for (near, far), out in zip(pieces, (own_out, o1, o2, o3)):
        q_near, kv_near = product(near, low)
        q_far, kv_far = product(far, high)
        out[:256, :] = (q_near + q_far).astype(out.dtype)
        out[256:, :] = (kv_near + kv_far).T.astype(out.dtype)


def project(where, own, near, far, weights):
    part = jax.ShapeDtypeStruct((320, 256), BF16)
    return pl.pallas_call(
        project_kernel,
        out_shape=(jax.ShapeDtypeStruct((320, 256), F32), part, part, part),
        in_specs=[pl.BlockSpec(memory_space=pltpu.SMEM)]
        + [pl.BlockSpec(memory_space=pltpu.VMEM)] * 8,
        scratch_shapes=[pltpu.VMEM((2048, 256), BF16), pltpu.VMEM((64, 2048), BF16)],
        compiler_params=params(),
        name="project",
    )(where, own, *near, *far, weights)


def attend_kernel(
    q0, q1, q2, q3, kv, visible, weighted, cos_q, sin_q, cos_k, sin_k, attn_out, dq_out
):
    scaling = 1.0 / math.sqrt(HEAD)
    k_lin = jnp.concatenate([kv[s, :32, :] for s in range(4)], axis=0)
    values = jnp.concatenate([kv[s, 32:, :] for s in range(4)], axis=0).astype(BF16)
    k1, k2 = k_lin[:64], k_lin[64:]
    ck, sk = cos_k[...], sin_k[...]
    keys = jnp.concatenate([k1 * ck - k2 * sk, k2 * ck + k1 * sk], axis=0).astype(BF16)
    seen = visible[...] > 0
    cq, sq = cos_q[...], sin_q[...]
    for head in range(2):
        cols = pl.ds(head * HEAD, HEAD)
        q_lin = q0[:256, cols]
        for part in (q1, q2, q3):
            q_lin = q_lin + part[:256, cols].astype(F32)
        queries = ((q_lin * cq + pltpu.roll(q_lin, 64, 1) * sq) * scaling).astype(BF16)
        scores = jnp.dot(queries, keys, preferred_element_type=F32)
        raised = jnp.where(seen, jnp.exp(scores), 0.0)
        attend = raised / jnp.sum(raised, axis=1, keepdims=True)
        mixed = lax.dot_general(
            attend.astype(BF16), values, (((1,), (1,)), ((), ())), preferred_element_type=F32
        )
        attn_out[:, cols] = mixed.astype(BF16)
        pressure = jnp.dot(weighted[:, cols], values, preferred_element_type=F32)
        centre = jnp.sum(attend * pressure, axis=1, keepdims=True)
        slope = (attend * (pressure - centre)).astype(BF16)
        dq_rot = (
            lax.dot_general(slope, keys, (((1,), (1,)), ((), ())), preferred_element_type=F32)
            * scaling
        )
        dq = dq_rot * cq - pltpu.roll(dq_rot, 64, 1) * sq
        dq_out[cols, :] = dq.T.astype(BF16)


def attend(parts, kv, visible, weighted, tables):
    return pl.pallas_call(
        attend_kernel,
        out_shape=(
            jax.ShapeDtypeStruct((TOK, 256), BF16),
            jax.ShapeDtypeStruct((256, TOK), BF16),
        ),
        compiler_params=params(),
        name="attend",
    )(*parts, kv, visible, weighted, *tables)


def gradient_kernel(where_ref, own, n1, n2, n3, f1, f2, f3, d0, d1, d2, d3, out):
    core = where_ref[0]
    for part in range(8):
        near = part < 4
        cols = pl.ds(256 * (part % 4), 256)
        tokens = (own[:, pl.ds(256 * part, 256)],) + tuple(
            x[:, cols] for x in ((n1, n2, n3) if near else (f1, f2, f3))
        )
        total = None
        for x, d in zip(tokens, (d0, d1, d2, d3)):
            term = jnp.dot(d[...], x, preferred_element_type=F32)
            total = term if total is None else total + term
        out[block_of(part, core)] = total.astype(BF16)


def gradient(where, own, near, far, slopes):
    return pl.pallas_call(
        gradient_kernel,
        out_shape=jax.ShapeDtypeStruct((8, 256, 256), BF16),
        in_specs=[pl.BlockSpec(memory_space=pltpu.SMEM)]
        + [pl.BlockSpec(memory_space=pltpu.VMEM)] * 11,
        compiler_params=params(),
        name="gradient",
    )(where, own, *near, *far, *slopes)


def total_kernel(terms, out):
    total = terms[0].astype(F32)
    for block in range(1, 8):
        total = total + terms[block].astype(F32)
    out[...] = total.T


def add_up(terms):
    return pl.pallas_call(
        total_kernel,
        out_shape=jax.ShapeDtypeStruct((256, 256), F32),
        compiler_params=params(),
        name="add_up",
    )(terms)


def shards(states, query_weight, key_matrix, value_matrix, block_mask, risk_weight, upstream):
    core = lax.axis_index("c")
    place = 2 * lax.axis_index("zb") + lax.axis_index("yb")
    where = jnp.stack([core, place]).astype(jnp.int32)

    own, *outgoing = cut(where, states)
    near = [swap(outgoing[j - 1], j) for j in (1, 2, 3)]
    far = [swap_core(x) for x in near]

    query_weight, _ = lax.optimization_barrier((query_weight, outgoing))
    first, second = pack(where, query_weight, key_matrix.T, value_matrix.T)
    first = lax.ppermute(first, AXES, home_pairs(0))
    second = lax.ppermute(second, AXES, home_pairs(1))
    weights = lax.all_to_all(
        copies(where, first, second), OTHERS, split_axis=0, concat_axis=0
    )

    parts = project(where, own, near, far, weights)
    parts = (parts[0], *[swap(parts[j], j) for j in (1, 2, 3)])
    kv = parts[0][256:]
    for part in parts[1:]:
        kv = kv + part[256:].astype(F32)
    kv = lax.all_gather(kv, ("xb", "c"), axis=0, tiled=False)

    depths = jnp.sum(block_mask, axis=1) - 1
    places = (depths[:, None] * BS + jnp.arange(BS, dtype=jnp.int32)[None, :]).reshape(TOK)
    frequency = jnp.exp(
        -math.log(1000000.0) * jnp.arange(HEAD // 2, dtype=F32) * 2.0 / HEAD
    )
    angles = places.astype(F32)[:, None] * frequency[None, :]
    cosine, sine = jnp.cos(angles), jnp.sin(angles)
    tables = (
        jnp.concatenate([cosine, cosine], axis=1),
        jnp.concatenate([-sine, sine], axis=1),
        cosine.T,
        sine.T,
    )
    position = jnp.arange(TOK, dtype=jnp.int32)
    blocks = position // BS
    wide_mask = jnp.repeat(jnp.repeat(block_mask, BS, axis=0), BS, axis=1) > 0
    visible = wide_mask & (
        (blocks[:, None] != blocks[None, :]) | (position[:, None] >= position[None, :])
    )
    visible = visible.astype(F32)
    weighted = (upstream.astype(F32) * jnp.repeat(risk_weight, BS)[:, None]).astype(BF16)

    attn_out, dq = attend(parts, kv, visible, weighted, tables)
    slopes = (dq, *[swap(dq, j) for j in (1, 2, 3)])
    terms = gradient(where, own, near, far, slopes)
    terms = lax.all_to_all(terms, OTHERS, split_axis=0, concat_axis=0)
    return attn_out, add_up(terms)


def solution(mesh):
    fine = Mesh(mesh.devices.reshape(SIZES), AXES)
    dp, tensor = AXES[:4], AXES[4:]
    in_specs = (
        P(dp, None),
        P(tensor, dp),
        P(tensor, dp),
        P(tensor, dp),
        P(dp, None),
        P(dp),
        P(dp, tensor),
    )
    out_specs = (P(dp, tensor), P(dp, tensor))
    return jax.shard_map(shards, mesh=fine, in_specs=in_specs, out_specs=out_specs, check_vma=False)
```

time: 209 us -> 215 us (1.029); the launches traced: 205 us -> 213 us
  Pallas kernels: 17.1 us -> 44.1 us
  local copies, waits for them, and re-layouts: 12.2 us -> 5.01 us
  starting transfers between devices: 67.4 us -> 61.4 us
  other arithmetic: 6.1 us -> 3.08 us
  waiting for transfers between devices: 60.2 us -> 57.3 us
    pallas_call x1 -> x3, Pallas kernels: 1.65 us -> 36.1 us  [the longest x1 33.7 us: cut(): pl.pallas_call(cut_kernel, out_shape=(jax.ShapeDtypeStruct((TOK, 2048), B...]
    unnamed x30, local copies, waits for them, and re-layouts: 8.88 us -> 3.7 us
    ppermute x10 -> x12, starting transfers between devices: 41.2 us -> 36.2 us  [the longest x9 30 us: swap(): return lax.ppermute(value, GROUP, [(i, i ^ offset) for i in range(4)])]
    pallas_call x1, Pallas kernels: 6.06 us -> 1.81 us  [gradient(): pl.pallas_call(gradient_kernel, out_shape=jax.ShapeDtypeStruct((8, 256, 2...]
    pallas_call x1, Pallas kernels: 6.97 us -> 3.83 us  [project(): pl.pallas_call(project_kernel, out_shape=(jax.ShapeDtypeStruct((320, 256)...]
    ppermute x10 -> x12, waiting for transfers between devices: 52 us -> 49.1 us  [the longest x9 49.1 us: swap(): return lax.ppermute(value, GROUP, [(i, i ^ offset) for i in range(4)])]
  transfers between devices with their start and end apart: 13 -> 15, of which waited for: 5 -> 7; matrix products, arithmetic and copies ran while one was open for 4% -> 2% of each run, Pallas kernels for 1% -> 0%
where the time goes in v2:
time: 215 us; the launch traced here: 213 us
  starting transfers between devices  61.4 us (29%)
  waiting for transfers between devices  57.3 us (27%)
  Pallas kernels  44.1 us (21%)
  blocking collectives  41.3 us (19%)
  local copies, waits for them, and re-layouts  5.01 us (2%)
  other arithmetic  3.08 us (1%)
    ppermute x9, waiting for transfers between devices, swap(): return lax.ppermute(value, GROUP, [(i, i ^ offset) for i in range(4)])  49.1 us
    all_to_all x1, blocking collectives, shards(): terms = lax.all_to_all(terms, OTHERS, split_axis=0, concat_axis=0)  35.5 us
    pallas_call x1, Pallas kernels, cut(): pl.pallas_call(cut_kernel, out_shape=(jax.ShapeDtypeStruct((TOK, 2048), B...  33.7 us
    ppermute x9, starting transfers between devices, swap(): return lax.ppermute(value, GROUP, [(i, i ^ offset) for i in range(4)])  30 us
    all_to_all x1, starting transfers between devices, shards(): lax.all_to_all(copies(where, first, second), OTHERS, split_axis=0, concat...  14.4 us
    ppermute x1, waiting for transfers between devices, shards(): second = lax.ppermute(second, AXES, home_pairs(1))  8.17 us
    ppermute x1, starting transfers between devices, shards(): first = lax.ppermute(first, AXES, home_pairs(0))  7.81 us
    ppermute x3, starting transfers between devices, swap_core(): return lax.ppermute(value, 'c', [(0, 1), (1, 0)])  6.22 us
  transfers between devices with their start and end apart: 15, of which 7 were waited for; matrix products, arithmetic and copies ran while one was open for 2% of the time, Pallas kernels for 0%

profile of v2, /device:TPU:6, one launch (start us, length us, event | category | flops | bytes accessed | tf_op | source)
XLA Modules:
  0.0 213.1 jit_solution(3281941567021930406)
XLA Ops:
  0.6 0.1 pad_add_fusion.where_ref
  0.7 33.7 %cut_states.1 = (bf16[256,2048]{1,0:T(8,128)(2,1)S(1)}, bf16[256,1024]{1,0:T(8,128)(2,1)S(1)}, bf16[256,1024]{1,0:T(8,128)(2,1)}, bf16[256,1024]{1,0:T(8,128)(2,1)}) custom-call(s32[2]{0:T(128)S(1)} %pad_add_fusion.where_ref, bf16[256,8192]{1,0:T(8,128)(2,1)} %states_ref.1), custom_call_target="tpu_custom_call" | custom-call | tf_op jit(solution)/shard_map/cut_states/pallas_call | solution.py:71
  34.5 0.6 pack_weights.1
  35.0 7.8 %collective-permute-start.6 = (bf16[320,128]{1,0:T(8,128)(2,1)S(1)}, bf16[320,128]{1,0:T(8,128)(2,1)S(1)}, u32[]{:S(2)}, u32[]{:S(2)}) collective-permute-start(bf16[320,128]{1,0:T(8,128)(2,1)S(1)} %get-tuple-element.20), channel_id=1, source_target_pairs={{0,0},{1,32},{2,64},{3,96},{4,128},{5,160},{6,192},{7,224},{8,256}... | collective-permute-start | bytes 245768 | tf_op jit(solution)/shard_map/ppermute | solution.py:275
  42.9 3.0 %collective-permute-start.7 = (bf16[320,128]{1,0:T(8,128)(2,1)S(1)}, bf16[320,128]{1,0:T(8,128)(2,1)S(1)}, u32[]{:S(2)}, u32[]{:S(2)}) collective-permute-start(bf16[320,128]{1,0:T(8,128)(2,1)S(1)} %get-tuple-element.21), channel_id=1, source_target_pairs={{0,16},{1,48},{2,80},{3,112},{4,144},{5,176},{6,208},{7,240},{8,27... | collective-permute-start | bytes 245768 | tf_op jit(solution)/shard_map/ppermute | solution.py:276
  45.8 8.2 %collective-permute-done.7.second = bf16[320,128]{1,0:T(8,128)(2,1)S(1)} collective-permute-done((bf16[320,128]{1,0:T(8,128)(2,1)S(1)}, bf16[320,128]{1,0:T(8,128)(2,1)S(1)}, u32[]{:S(2)}, u32[]{:S(2)}) %collective-permute-start.7) | collective-permute-done | bytes 81952 | tf_op jit(solution)/shard_map/ppermute | solution.py:276
  54.0 1.8 weight_copies.1
  55.8 14.4 %all-to-all-start = ((bf16[8,2,320,128]{3,2,1,0:T(8,128)(2,1)}), bf16[8,2,320,128]{3,2,1,0:T(8,128)(2,1)}, u32[]{:S(2)}, u32[]{:S(2)}) async-start(bf16[8,2,320,128]{3,2,1,0:T(8,128)(2,1)} %weight_copies.1), calls=%async_computation | async-start | bytes 2621440 | tf_op jit(solution)/shard_map/all_to_all | solution.py:277
  70.2 3.3 %collective-permute-start = (bf16[256,1024]{1,0:T(8,128)(2,1)S(1)}, bf16[256,1024]{1,0:T(8,128)(2,1)S(1)}, u32[]{:S(2)}, u32[]{:S(2)}) collective-permute-start(bf16[256,1024]{1,0:T(8,128)(2,1)S(1)} %get-tuple-element.16), channel_id=1, source_target_pairs={{0,16},{16,0},{64,80},{80,64},{1,17},{17,1},{65,81},{81,65},{2,18}... | collective-permute-start | bytes 1572872 | tf_op jit(solution)/shard_map/ppermute | solution.py:37
  73.6 5.4 %collective-permute-start.1 = (bf16[256,1024]{1,0:T(8,128)(2,1)}, bf16[256,1024]{1,0:T(8,128)(2,1)S(1)}, u32[]{:S(2)}, u32[]{:S(2)}) collective-permute-start(bf16[256,1024]{1,0:T(8,128)(2,1)} %get-tuple-element.17), channel_id=1, source_target_pairs={{0,64},{16,80},{64,0},{80,16},{1,65},{17,81},{65,1},{81,17},{2,66}... | collective-permute-start | bytes 1572872 | tf_op jit(solution)/shard_map/ppermute | solution.py:37
  79.0 2.3 %collective-permute-start.2 = (bf16[256,1024]{1,0:T(8,128)(2,1)}, bf16[256,1024]{1,0:T(8,128)(2,1)S(1)}, u32[]{:S(2)}, u32[]{:S(2)}) collective-permute-start(bf16[256,1024]{1,0:T(8,128)(2,1)} %get-tuple-element.18), channel_id=1, source_target_pairs={{0,80},{16,64},{64,16},{80,0},{1,81},{17,65},{65,17},{81,1},{2,82}... | collective-permute-start | bytes 1572872 | tf_op jit(solution)/shard_map/ppermute | solution.py:37
  81.3 0.1 reduce_sum.9
  81.5 0.1 convert_element_type.35
  81.6 0.1 copy.9
  81.7 0.1 broadcast_in_dim.6
  81.8 0.1 gt.16
  81.9 0.8 copy.10
  82.8 0.1 mul.44
  82.8 0.1 multiply_convert_fusion.weighted
  83.0 18.1 %collective-permute-done.n1 = bf16[256,1024]{1,0:T(8,128)(2,1)S(1)} collective-permute-done((bf16[256,1024]{1,0:T(8,128)(2,1)S(1)}, bf16[256,1024]{1,0:T(8,128)(2,1)S(1)}, u32[]{:S(2)}, u32[]{:S(2)}) %collective-permute-start) | collective-permute-done | bytes 524320 | tf_op jit(solution)/shard_map/ppermute | solution.py:37
  101.0 1.9 collective-permute-start.3
  102.9 21.3 %collective-permute-done.1.n2 = bf16[256,1024]{1,0:T(8,128)(2,1)S(1)} collective-permute-done((bf16[256,1024]{1,0:T(8,128)(2,1)}, bf16[256,1024]{1,0:T(8,128)(2,1)S(1)}, u32[]{:S(2)}, u32[]{:S(2)}) %collective-permute-start.1) | collective-permute-done | bytes 524320 | tf_op jit(solution)/shard_map/ppermute | solution.py:37
  124.3 1.9 collective-permute-start.4
  126.2 2.4 %collective-permute-start.5 = (bf16[256,1024]{1,0:T(8,128)(2,1)S(1)}, bf16[256,1024]{1,0:T(8,128)(2,1)S(1)}, u32[]{:S(2)}, u32[]{:S(2)}) collective-permute-start(bf16[256,1024]{1,0:T(8,128)(2,1)S(1)} %collective-permute-done.2.n3), channel_id=1, source_target_pairs={{0,1},{1,0},{2,3},{3,2},{4,5},{5,4},{6,7},{7,6},{8,9},{9,8},{10,11... | collective-permute-start | bytes 1572872 | tf_op jit(solution)/shard_map/ppermute | solution.py:41
  128.6 1.0 fusion.2.visible
  129.6 1.3 fusion.3
  130.9 0.8 copy-done
  131.7 0.8 copy-done.3
  132.5 1.0 copy-done.1
  133.5 1.0 copy-done.4
  134.5 3.8 %project.1 = (f32[320,256]{1,0:T(8,128)S(1)}, bf16[320,256]{1,0:T(8,128)(2,1)S(1)}, bf16[320,256]{1,0:T(8,128)(2,1)S(1)}, bf16[320,256]{1,0:T(8,128)(2,1)S(1)}) custom-call(s32[2]{0:T(128)S(1)} %pad_add_fusion.where_ref, bf16[256,2048]{1,0:T(8,128)(2,1)S(1)} %get-tuple-element.15.own, bf16[256,1024]{1,0:T(8,128)(2,1)S(1)} %collective-permute-done.n1, ...), custom_call_target="tpu_custom_call" | custom-call | tf_op jit(solution)/shard_map/project/pallas_call | solution.py:164
  138.4 3.5 %collective-permute-start.10 = (bf16[320,256]{1,0:T(8,128)(2,1)S(1)}, bf16[320,256]{1,0:T(8,128)(2,1)S(1)}, u32[]{:S(2)}, u32[]{:S(2)}) collective-permute-start(bf16[320,256]{1,0:T(8,128)(2,1)S(1)} %get-tuple-element.25), channel_id=1, source_target_pairs={{0,80},{16,64},{64,16},{80,0},{1,81},{17,65},{65,17},{81,1},{2,82}... | collective-permute-start | bytes 491528 | tf_op jit(solution)/shard_map/ppermute | solution.py:37
  141.9 2.8 %collective-permute-start.8 = (bf16[320,256]{1,0:T(8,128)(2,1)S(1)}, bf16[320,256]{1,0:T(8,128)(2,1)S(1)}, u32[]{:S(2)}, u32[]{:S(2)}) collective-permute-start(bf16[320,256]{1,0:T(8,128)(2,1)S(1)} %get-tuple-element.23), channel_id=1, source_target_pairs={{0,16},{16,0},{64,80},{80,64},{1,17},{17,1},{65,81},{81,65},{2,18}... | collective-permute-start | bytes 491528 | tf_op jit(solution)/shard_map/ppermute | solution.py:37
  144.8 3.4 %collective-permute-start.9 = (bf16[320,256]{1,0:T(8,128)(2,1)S(1)}, bf16[320,256]{1,0:T(8,128)(2,1)S(1)}, u32[]{:S(2)}, u32[]{:S(2)}) collective-permute-start(bf16[320,256]{1,0:T(8,128)(2,1)S(1)} %get-tuple-element.24), channel_id=1, source_target_pairs={{0,64},{16,80},{64,0},{80,16},{1,65},{17,81},{65,1},{81,17},{2,66}... | collective-permute-start | bytes 491528 | tf_op jit(solution)/shard_map/ppermute | solution.py:37
  148.1 0.3 multiply_sine_fusion.1
  148.5 0.1 pad_maximum_fusion
  148.7 2.1 collective-permute-done.8.q1
  150.8 1.8 collective-permute-done.9.q2
  152.6 5.8 %all-gather = f32[256,256]{1,0:T(8,128)S(1)} all-gather(f32[64,256]{1,0:T(8,128)S(1)} %convert_add_fusion), channel_id=2, replica_groups=mesh['zh'=4,'zb'=2,'yu'=2,'yb'=2,'yh'=2,'xh'=2,'xb'=2,'c'=2] {'xb','c'}, dimensions={0}, use_global_device_ids=true | all-gather | bytes 327680 | tf_op jit(solution)/shard_map/all_gather | solution.py:286
  158.4 1.5 attend.1
  159.9 3.5 %collective-permute-start.11 = (bf16[256,256]{1,0:T(8,128)(2,1)S(1)}, bf16[256,256]{1,0:T(8,128)(2,1)S(1)}, u32[]{:S(2)}, u32[]{:S(2)}) collective-permute-start(bf16[256,256]{1,0:T(8,128)(2,1)S(1)} %get-tuple-element.27.d0), channel_id=1, source_target_pairs={{0,16},{16,0},{64,80},{80,64},{1,17},{17,1},{65,81},{81,65},{2,18}... | collective-permute-start | bytes 393224 | tf_op jit(solution)/shard_map/ppermute | solution.py:37
  163.3 3.5 %collective-permute-start.12 = (bf16[256,256]{1,0:T(8,128)(2,1)S(1)}, bf16[256,256]{1,0:T(8,128)(2,1)S(1)}, u32[]{:S(2)}, u32[]{:S(2)}) collective-permute-start(bf16[256,256]{1,0:T(8,128)(2,1)S(1)} %get-tuple-element.27.d0), channel_id=1, source_target_pairs={{0,64},{16,80},{64,0},{80,16},{1,65},{17,81},{65,1},{81,17},{2,66}... | collective-permute-start | bytes 393224 | tf_op jit(solution)/shard_map/ppermute | solution.py:37
  166.9 2.2 %collective-permute-start.13 = (bf16[256,256]{1,0:T(8,128)(2,1)S(1)}, bf16[256,256]{1,0:T(8,128)(2,1)S(1)}, u32[]{:S(2)}, u32[]{:S(2)}) collective-permute-start(bf16[256,256]{1,0:T(8,128)(2,1)S(1)} %get-tuple-element.27.d0), channel_id=1, source_target_pairs={{0,80},{16,64},{64,16},{80,0},{1,81},{17,65},{65,17},{81,1},{2,82}... | collective-permute-start | bytes 393224 | tf_op jit(solution)/shard_map/ppermute | solution.py:37
  169.1 1.6 collective-permute-done.12.d2
  170.7 4.1 %collective-permute-done.13.d3 = bf16[256,256]{1,0:T(8,128)(2,1)S(1)} collective-permute-done((bf16[256,256]{1,0:T(8,128)(2,1)S(1)}, bf16[256,256]{1,0:T(8,128)(2,1)S(1)}, u32[]{:S(2)}, u32[]{:S(2)}) %collective-permute-start.13) | collective-permute-done | bytes 131104 | tf_op jit(solution)/shard_map/ppermute | solution.py:37
  174.9 1.8 gradient.1
  176.7 35.5 %all_to_all.10.terms = bf16[8,256,256]{2,1,0:T(8,128)(2,1)S(1)} all-to-all(bf16[8,256,256]{2,1,0:T(8,128)(2,1)S(1)} %gradient.1), channel_id=1, replica_groups=mesh['zh'=4,'zb'=2,'yu'=2,'yb'=2,'yh'=2,'xh'=2,'xb'=2,'c'=2] {'zh','yu'}, dimensions={0} | all-to-all | bytes 2097152 | tf_op jit(solution)/shard_map/all_to_all | solution.py:313
  212.2 0.9 add_up.1
  (42 shorter events, 0.3 us)
Async XLA Ops:
  0.7 33.7 %copy-start.6 = (bf16[512,128]{1,0:T(8,128)(2,1)S(1)}, bf16[512,128]{1,0:T(8,128)(2,1)}, u32[]{:S(2)}) copy-start(bf16[512,128]{1,0:T(8,128)(2,1)} %query) | copy-start | bytes 393220
  0.7 33.7 %copy-start.7 = (bf16[512,16]{0,1:T(8,128)(2,1)S(1)}, bf16[512,16]{0,1:T(8,128)(2,1)}, u32[]{:S(2)}) copy-start(bf16[512,16]{0,1:T(8,128)(2,1)} %param.9) | copy-start | bytes 49156
  0.7 33.7 %copy-start.8 = (bf16[512,16]{0,1:T(8,128)(2,1)S(1)}, bf16[512,16]{0,1:T(8,128)(2,1)}, u32[]{:S(2)}) copy-start(bf16[512,16]{0,1:T(8,128)(2,1)} %param.10) | copy-start | bytes 49156
  35.0 10.8 %collective-permute-start.6 = (bf16[320,128]{1,0:T(8,128)(2,1)S(1)}, bf16[320,128]{1,0:T(8,128)(2,1)S(1)}, u32[]{:S(2)}, u32[]{:S(2)}) collective-permute-start(bf16[320,128]{1,0:T(8,128)(2,1)S(1)} %get-tuple-element.20), channel_id=1, source_target_pairs={{0,0},{1,32},{2,64},{3,96},{4,128},{5,160},{6,192},{7,224},{8,256}... | collective-permute-start | bytes 245768 | tf_op jit(solution)/shard_map/ppermute | solution.py:275
  42.9 11.1 %collective-permute-start.7 = (bf16[320,128]{1,0:T(8,128)(2,1)S(1)}, bf16[320,128]{1,0:T(8,128)(2,1)S(1)}, u32[]{:S(2)}, u32[]{:S(2)}) collective-permute-start(bf16[320,128]{1,0:T(8,128)(2,1)S(1)} %get-tuple-element.21), channel_id=1, source_target_pairs={{0,16},{1,48},{2,80},{3,112},{4,144},{5,176},{6,208},{7,240},{8,27... | collective-permute-start | bytes 245768 | tf_op jit(solution)/shard_map/ppermute | solution.py:276
  55.8 25.5 %copy-start.13 = (s32[4,4]{1,0:T(4,128)S(1)}, s32[4,4]{1,0:T(4,128)}, u32[]{:S(2)}) copy-start(s32[4,4]{1,0:T(4,128)} %param.11) | copy-start | bytes 196
  55.8 26.9 %copy-start.14 = (f32[4]{0:T(128)S(1)}, f32[4]{0:T(128)}, u32[]{:S(2)}) copy-start(f32[4]{0:T(128)} %param.12) | copy-start | bytes 52
  55.8 27.0 %copy-start.12 = (bf16[256,256]{1,0:T(8,128)(2,1)S(1)}, bf16[256,256]{1,0:T(8,128)(2,1)}, u32[]{:S(2)}) copy-start(bf16[256,256]{1,0:T(8,128)(2,1)} %param.13) | copy-start | bytes 393220
  55.8 76.6 %all-to-all-start = ((bf16[8,2,320,128]{3,2,1,0:T(8,128)(2,1)}), bf16[8,2,320,128]{3,2,1,0:T(8,128)(2,1)}, u32[]{:S(2)}, u32[]{:S(2)}) async-start(bf16[8,2,320,128]{3,2,1,0:T(8,128)(2,1)} %weight_copies.1), calls=%async_computation | async-start | bytes 2621440 | tf_op jit(solution)/shard_map/all_to_all | solution.py:277
  70.2 30.8 %collective-permute-start = (bf16[256,1024]{1,0:T(8,128)(2,1)S(1)}, bf16[256,1024]{1,0:T(8,128)(2,1)S(1)}, u32[]{:S(2)}, u32[]{:S(2)}) collective-permute-start(bf16[256,1024]{1,0:T(8,128)(2,1)S(1)} %get-tuple-element.16), channel_id=1, source_target_pairs={{0,16},{16,0},{64,80},{80,64},{1,17},{17,1},{65,81},{81,65},{2,18}... | collective-permute-start | bytes 1572872 | tf_op jit(solution)/shard_map/ppermute | solution.py:37
  73.6 50.7 %collective-permute-start.1 = (bf16[256,1024]{1,0:T(8,128)(2,1)}, bf16[256,1024]{1,0:T(8,128)(2,1)S(1)}, u32[]{:S(2)}, u32[]{:S(2)}) collective-permute-start(bf16[256,1024]{1,0:T(8,128)(2,1)} %get-tuple-element.17), channel_id=1, source_target_pairs={{0,64},{16,80},{64,0},{80,16},{1,65},{17,81},{65,1},{81,17},{2,66}... | collective-permute-start | bytes 1572872 | tf_op jit(solution)/shard_map/ppermute | solution.py:37
  79.0 47.2 %collective-permute-start.2 = (bf16[256,1024]{1,0:T(8,128)(2,1)}, bf16[256,1024]{1,0:T(8,128)(2,1)S(1)}, u32[]{:S(2)}, u32[]{:S(2)}) collective-permute-start(bf16[256,1024]{1,0:T(8,128)(2,1)} %get-tuple-element.18), channel_id=1, source_target_pairs={{0,80},{16,64},{64,16},{80,0},{1,81},{17,65},{65,17},{81,1},{2,82}... | collective-permute-start | bytes 1572872 | tf_op jit(solution)/shard_map/ppermute | solution.py:37
  101.0 29.8 %collective-permute-start.3 = (bf16[256,1024]{1,0:T(8,128)(2,1)S(1)}, bf16[256,1024]{1,0:T(8,128)(2,1)S(1)}, u32[]{:S(2)}, u32[]{:S(2)}) collective-permute-start(bf16[256,1024]{1,0:T(8,128)(2,1)S(1)} %collective-permute-done.n1), channel_id=1, source_target_pairs={{0,1},{1,0},{2,3},{3,2},{4,5},{5,4},{6,7},{7,6},{8,9},{9,8},{10,11... | collective-permute-start | bytes 1572872 | tf_op jit(solution)/shard_map/ppermute | solution.py:41
  124.3 6.6 %collective-permute-start.4 = (bf16[256,1024]{1,0:T(8,128)(2,1)S(1)}, bf16[256,1024]{1,0:T(8,128)(2,1)S(1)}, u32[]{:S(2)}, u32[]{:S(2)}) collective-permute-start(bf16[256,1024]{1,0:T(8,128)(2,1)S(1)} %collective-permute-done.1.n2), channel_id=1, source_target_pairs={{0,1},{1,0},{2,3},{3,2},{4,5},{5,4},{6,7},{7,6},{8,9},{9,8},{10,11... | collective-permute-start | bytes 1572872 | tf_op jit(solution)/shard_map/ppermute | solution.py:41
  126.2 5.5 %collective-permute-start.5 = (bf16[256,1024]{1,0:T(8,128)(2,1)S(1)}, bf16[256,1024]{1,0:T(8,128)(2,1)S(1)}, u32[]{:S(2)}, u32[]{:S(2)}) collective-permute-start(bf16[256,1024]{1,0:T(8,128)(2,1)S(1)} %collective-permute-done.2.n3), channel_id=1, source_target_pairs={{0,1},{1,0},{2,3},{3,2},{4,5},{5,4},{6,7},{7,6},{8,9},{9,8},{10,11... | collective-permute-start | bytes 1572872 | tf_op jit(solution)/shard_map/ppermute | solution.py:41
  130.9 0.8 copy-start
  131.7 0.8 copy-start.3
  132.5 1.0 copy-start.1
  133.5 1.0 copy-start.4
  134.5 13.9 %copy-start.9 = (f32[256,64]{1,0:T(8,128)S(1)}, f32[256,64]{1,0:T(8,128)}, u32[]{:S(2)}) copy-start(f32[256,64]{1,0:T(8,128)} %get-tuple-element.30) | copy-start | bytes 196612
  134.5 13.9 %copy-start.10 = (f32[256,64]{1,0:T(8,128)S(1)}, f32[256,64]{1,0:T(8,128)}, u32[]{:S(2)}) copy-start(f32[256,64]{1,0:T(8,128)} %get-tuple-element.31) | copy-start | bytes 196612
  134.5 13.9 %copy-start.11 = (f32[256,64]{1,0:T(8,128)S(1)}, f32[256,64]{1,0:T(8,128)}, u32[]{:S(2)}) copy-start(f32[256,64]{1,0:T(8,128)} %get-tuple-element.32) | copy-start | bytes 196612
  138.4 10.3 %collective-permute-start.10 = (bf16[320,256]{1,0:T(8,128)(2,1)S(1)}, bf16[320,256]{1,0:T(8,128)(2,1)S(1)}, u32[]{:S(2)}, u32[]{:S(2)}) collective-permute-start(bf16[320,256]{1,0:T(8,128)(2,1)S(1)} %get-tuple-element.25), channel_id=1, source_target_pairs={{0,80},{16,64},{64,16},{80,0},{1,81},{17,65},{65,17},{81,1},{2,82}... | collective-permute-start | bytes 491528 | tf_op jit(solution)/shard_map/ppermute | solution.py:37
  141.9 8.9 %collective-permute-start.8 = (bf16[320,256]{1,0:T(8,128)(2,1)S(1)}, bf16[320,256]{1,0:T(8,128)(2,1)S(1)}, u32[]{:S(2)}, u32[]{:S(2)}) collective-permute-start(bf16[320,256]{1,0:T(8,128)(2,1)S(1)} %get-tuple-element.23), channel_id=1, source_target_pairs={{0,16},{16,0},{64,80},{80,64},{1,17},{17,1},{65,81},{81,65},{2,18}... | collective-permute-start | bytes 491528 | tf_op jit(solution)/shard_map/ppermute | solution.py:37
  144.8 7.8 %collective-permute-start.9 = (bf16[320,256]{1,0:T(8,128)(2,1)S(1)}, bf16[320,256]{1,0:T(8,128)(2,1)S(1)}, u32[]{:S(2)}, u32[]{:S(2)}) collective-permute-start(bf16[320,256]{1,0:T(8,128)(2,1)S(1)} %get-tuple-element.24), channel_id=1, source_target_pairs={{0,64},{16,80},{64,0},{80,16},{1,65},{17,81},{65,1},{81,17},{2,66}... | collective-permute-start | bytes 491528 | tf_op jit(solution)/shard_map/ppermute | solution.py:37
  148.6 26.2 %copy-start.2 = (bf16[256,1024]{1,0:T(8,128)(2,1)S(1)}, bf16[256,1024]{1,0:T(8,128)(2,1)}, u32[]{:S(2)}) copy-start(bf16[256,1024]{1,0:T(8,128)(2,1)} %copy-done) | copy-start | bytes 1572868
  148.6 26.2 %copy-start.5 = (bf16[256,1024]{1,0:T(8,128)(2,1)S(1)}, bf16[256,1024]{1,0:T(8,128)(2,1)}, u32[]{:S(2)}) copy-start(bf16[256,1024]{1,0:T(8,128)(2,1)} %copy-done.3) | copy-start | bytes 1572868
  159.9 9.2 %collective-permute-start.11 = (bf16[256,256]{1,0:T(8,128)(2,1)S(1)}, bf16[256,256]{1,0:T(8,128)(2,1)S(1)}, u32[]{:S(2)}, u32[]{:S(2)}) collective-permute-start(bf16[256,256]{1,0:T(8,128)(2,1)S(1)} %get-tuple-element.27.d0), channel_id=1, source_target_pairs={{0,16},{16,0},{64,80},{80,64},{1,17},{17,1},{65,81},{81,65},{2,18}... | collective-permute-start | bytes 393224 | tf_op jit(solution)/shard_map/ppermute | solution.py:37
  163.3 7.4 %collective-permute-start.12 = (bf16[256,256]{1,0:T(8,128)(2,1)S(1)}, bf16[256,256]{1,0:T(8,128)(2,1)S(1)}, u32[]{:S(2)}, u32[]{:S(2)}) collective-permute-start(bf16[256,256]{1,0:T(8,128)(2,1)S(1)} %get-tuple-element.27.d0), channel_id=1, source_target_pairs={{0,64},{16,80},{64,0},{80,16},{1,65},{17,81},{65,1},{81,17},{2,66}... | collective-permute-start | bytes 393224 | tf_op jit(solution)/shard_map/ppermute | solution.py:37
  166.9 8.0 %collective-permute-start.13 = (bf16[256,256]{1,0:T(8,128)(2,1)S(1)}, bf16[256,256]{1,0:T(8,128)(2,1)S(1)}, u32[]{:S(2)}, u32[]{:S(2)}) collective-permute-start(bf16[256,256]{1,0:T(8,128)(2,1)S(1)} %get-tuple-element.27.d0), channel_id=1, source_target_pairs={{0,80},{16,64},{64,16},{80,0},{1,81},{17,65},{65,17},{81,1},{2,82}... | collective-permute-start | bytes 393224 | tf_op jit(solution)/shard_map/ppermute | solution.py:37

commit v3 on v2

--- a/solution.py
+++ b/solution.py
@@ -17,7 +17,7 @@
 OTHERS = ("zh", "yu")
 F32 = jnp.float32
 BF16 = jnp.bfloat16
-VMEM_LIMIT = 48 * 1024 * 1024
+VMEM_LIMIT = 16 * 1024 * 1024
 
 
 def params():
@@ -72,14 +72,14 @@
         cut_kernel,
         out_shape=(jax.ShapeDtypeStruct((TOK, 2048), BF16), part, part, part),
         in_specs=[pl.BlockSpec(memory_space=pltpu.SMEM), pl.BlockSpec(memory_space=pl.ANY)],
-        out_specs=(pl.BlockSpec(memory_space=pl.ANY),) * 4,
+        out_specs=(pl.BlockSpec(memory_space=pltpu.VMEM),) * 4,
         scratch_shapes=[pltpu.SemaphoreType.DMA((20,))],
         compiler_params=params(),
         name="cut_states",
     )(where, states)
 
 
-def pack_kernel(where_ref, query, key_t, value_t, first, second):
+def pack_kernel(where_ref, query, key_t, value_t, after, first, second):
     odd = where_ref[1] % 2
     for turn, out in enumerate((first, second)):
         half = odd ^ turn
@@ -91,38 +91,46 @@
             out[base + 16 : base + 32, :] = value_t[:, lanes]
 
 
-def pack(where, query, key_t, value_t):
+def pack(where, query, key_t, value_t, after):
     part = jax.ShapeDtypeStruct((320, 128), BF16)
     vmem = pl.BlockSpec(memory_space=pltpu.VMEM)
     return pl.pallas_call(
         pack_kernel,
         out_shape=(part, part),
-        in_specs=[pl.BlockSpec(memory_space=pltpu.SMEM), vmem, vmem, vmem],
+        in_specs=[
+            pl.BlockSpec(memory_space=pltpu.SMEM),
+            *[vmem] * 3,
+            pl.BlockSpec(memory_space=pl.ANY),
+        ],
         compiler_params=params(),
         name="pack_weights",
-    )(where, query, key_t, value_t)
-
-
-def copies_kernel(where_ref, first, second, out):
+    )(where, query, key_t, value_t, after)
+
+
+def copies_kernel(where_ref, first, second, n1, n2, n3, out):
     odd = where_ref[1] % 2
     for device in range(8):
         out[device, odd] = first[...]
         out[device, 1 - odd] = second[...]
 
 
-def copies(where, first, second):
+def copies(where, first, second, near):
     vmem = pl.BlockSpec(memory_space=pltpu.VMEM)
     return pl.pallas_call(
         copies_kernel,
         out_shape=jax.ShapeDtypeStruct((8, 2, 320, 128), BF16),
-        in_specs=[pl.BlockSpec(memory_space=pltpu.SMEM), vmem, vmem],
+        in_specs=[
+            pl.BlockSpec(memory_space=pltpu.SMEM),
+            *[vmem] * 2,
+            *[pl.BlockSpec(memory_space=pl.ANY)] * 3,
+        ],
         compiler_params=params(),
         name="weight_copies",
-    )(where, first, second)
+    )(where, first, second, *near)
 
 
 def project_kernel(
-    where_ref, own, n1, n2, n3, f1, f2, f3, weights, own_out, o1, o2, o3, w_q, w_kv
+    where_ref, own, n1, n2, n3, f1, f2, f3, weights, out, w_q, w_kv
 ):
     core = where_ref[0]
     for part in range(8):
@@ -152,18 +160,18 @@
         (n2[...], f2[...]),
         (n3[...], f3[...]),
     )
-    for (near, far), out in zip(pieces, (own_out, o1, o2, o3)):
+    for number, (near, far) in enumerate(pieces):
+        other = where_ref[1] ^ number
         q_near, kv_near = product(near, low)
         q_far, kv_far = product(far, high)
-        out[:256, :] = (q_near + q_far).astype(out.dtype)
-        out[256:, :] = (kv_near + kv_far).T.astype(out.dtype)
+        out[other, :256, :] = (q_near + q_far).astype(BF16)
+        out[other, 256:, :] = (kv_near + kv_far).T.astype(BF16)
 
 
 def project(where, own, near, far, weights):
-    part = jax.ShapeDtypeStruct((320, 256), BF16)
     return pl.pallas_call(
         project_kernel,
-        out_shape=(jax.ShapeDtypeStruct((320, 256), F32), part, part, part),
+        out_shape=jax.ShapeDtypeStruct((4, 320, 256), BF16),
         in_specs=[pl.BlockSpec(memory_space=pltpu.SMEM)]
         + [pl.BlockSpec(memory_space=pltpu.VMEM)] * 8,
         scratch_shapes=[pltpu.VMEM((2048, 256), BF16), pltpu.VMEM((64, 2048), BF16)],
@@ -173,7 +181,7 @@
 
 
 def attend_kernel(
-    q0, q1, q2, q3, kv, visible, weighted, cos_q, sin_q, cos_k, sin_k, attn_out, dq_out
+    parts, kv, visible, weighted, cos_q, sin_q, cos_k, sin_k, attn_out, dq_out
 ):
     scaling = 1.0 / math.sqrt(HEAD)
     k_lin = jnp.concatenate([kv[s, :32, :] for s in range(4)], axis=0)
@@ -185,9 +193,9 @@
     cq, sq = cos_q[...], sin_q[...]
     for head in range(2):
         cols = pl.ds(head * HEAD, HEAD)
-        q_lin = q0[:256, cols]
-        for part in (q1, q2, q3):
-            q_lin = q_lin + part[:256, cols].astype(F32)
+        q_lin = parts[0, :256, cols].astype(F32)
+        for part in range(1, 4):
+            q_lin = q_lin + parts[part, :256, cols].astype(F32)
         queries = ((q_lin * cq + pltpu.roll(q_lin, 64, 1) * sq) * scaling).astype(BF16)
         scores = jnp.dot(queries, keys, preferred_element_type=F32)
         raised = jnp.where(seen, jnp.exp(scores), 0.0)
@@ -204,7 +212,9 @@
             * scaling
         )
         dq = dq_rot * cq - pltpu.roll(dq_rot, 64, 1) * sq
-        dq_out[cols, :] = dq.T.astype(BF16)
+        dq_t = dq.T.astype(BF16)
+        for part in range(4):
+            dq_out[part, cols, :] = dq_t
 
 
 def attend(parts, kv, visible, weighted, tables):
@@ -212,14 +222,14 @@
         attend_kernel,
         out_shape=(
             jax.ShapeDtypeStruct((TOK, 256), BF16),
-            jax.ShapeDtypeStruct((256, TOK), BF16),
+            jax.ShapeDtypeStruct((4, 256, TOK), BF16),
         ),
         compiler_params=params(),
         name="attend",
-    )(*parts, kv, visible, weighted, *tables)
-
-
-def gradient_kernel(where_ref, own, n1, n2, n3, f1, f2, f3, d0, d1, d2, d3, out):
+    )(parts, kv, visible, weighted, *tables)
+
+
+def gradient_kernel(where_ref, own, n1, n2, n3, f1, f2, f3, slopes, out):
     core = where_ref[0]
     for part in range(8):
         near = part < 4
@@ -228,8 +238,8 @@
             x[:, cols] for x in ((n1, n2, n3) if near else (f1, f2, f3))
         )
         total = None
-        for x, d in zip(tokens, (d0, d1, d2, d3)):
-            term = jnp.dot(d[...], x, preferred_element_type=F32)
+        for number, x in enumerate(tokens):
+            term = jnp.dot(slopes[where_ref[1] ^ number], x, preferred_element_type=F32)
             total = term if total is None else total + term
         out[block_of(part, core)] = total.astype(BF16)
 
@@ -239,10 +249,10 @@
         gradient_kernel,
         out_shape=jax.ShapeDtypeStruct((8, 256, 256), BF16),
         in_specs=[pl.BlockSpec(memory_space=pltpu.SMEM)]
-        + [pl.BlockSpec(memory_space=pltpu.VMEM)] * 11,
+        + [pl.BlockSpec(memory_space=pltpu.VMEM)] * 8,
         compiler_params=params(),
         name="gradient",
-    )(where, own, *near, *far, *slopes)
+    )(where, own, *near, *far, slopes)
 
 
 def total_kernel(terms, out):
@@ -270,19 +280,16 @@
     near = [swap(outgoing[j - 1], j) for j in (1, 2, 3)]
     far = [swap_core(x) for x in near]
 
-    query_weight, _ = lax.optimization_barrier((query_weight, outgoing))
-    first, second = pack(where, query_weight, key_matrix.T, value_matrix.T)
+    first, second = pack(where, query_weight, key_matrix.T, value_matrix.T, outgoing[0])
     first = lax.ppermute(first, AXES, home_pairs(0))
     second = lax.ppermute(second, AXES, home_pairs(1))
     weights = lax.all_to_all(
-        copies(where, first, second), OTHERS, split_axis=0, concat_axis=0
+        copies(where, first, second, near), OTHERS, split_axis=0, concat_axis=0
     )
 
     parts = project(where, own, near, far, weights)
-    parts = (parts[0], *[swap(parts[j], j) for j in (1, 2, 3)])
-    kv = parts[0][256:]
-    for part in parts[1:]:
-        kv = kv + part[256:].astype(F32)
+    parts = lax.all_to_all(parts, GROUP, split_axis=0, concat_axis=0)
+    kv = jnp.sum(parts[:, 256:].astype(F32), axis=0)
     kv = lax.all_gather(kv, ("xb", "c"), axis=0, tiled=False)
 
     depths = jnp.sum(block_mask, axis=1) - 1
@@ -308,7 +315,7 @@
     weighted = (upstream.astype(F32) * jnp.repeat(risk_weight, BS)[:, None]).astype(BF16)
 
     attn_out, dq = attend(parts, kv, visible, weighted, tables)
-    slopes = (dq, *[swap(dq, j) for j in (1, 2, 3)])
+    slopes = lax.all_to_all(dq, GROUP, split_axis=0, concat_axis=0)
     terms = gradient(where, own, near, far, slopes)
     terms = lax.all_to_all(terms, OTHERS, split_axis=0, concat_axis=0)
     return attn_out, add_up(terms)

time: 215 us -> 178 us (0.83)
  Pallas kernels: 44.1 us -> 12.9 us
  starting transfers between devices: 61.4 us -> 41 us
  blocking collectives: 41.3 us -> 53.2 us
  local copies, waits for them, and re-layouts: 5.01 us -> 8.31 us
    ppermute x9 -> x3, waiting for transfers between devices: 49.1 us -> 0.01 us  [swap(): return lax.ppermute(value, GROUP, [(i, i ^ offset) for i in range(4)])]
    all_to_all x1 -> x2, waiting for transfers between devices: 0.01 us -> 39.1 us  [the longest x1 32 us: shards(): lax.all_to_all(copies(where, first, second, near), OTHERS, split_axis=0,...]
    pallas_call x1, Pallas kernels: 33.7 us -> 1.27 us  [cut(): pl.pallas_call(cut_kernel, out_shape=(jax.ShapeDtypeStruct((TOK, 2048), B...]
    ppermute x9 -> x3, starting transfers between devices: 30 us -> 9.67 us  [swap(): return lax.ppermute(value, GROUP, [(i, i ^ offset) for i in range(4)])]
    ppermute x1, waiting for transfers between devices: 0.01 us -> 16.3 us  [shards(): first = lax.ppermute(first, AXES, home_pairs(0))]
    all_to_all x0 -> x1, blocking collectives: none -> 11.7 us  [shards(): slopes = lax.all_to_all(dq, GROUP, split_axis=0, concat_axis=0)]
    ppermute x1, waiting for transfers between devices: 8.17 us -> 0.01 us  [shards(): second = lax.ppermute(second, AXES, home_pairs(1))]
    unnamed x30 -> x28, local copies, waits for them, and re-layouts: 3.7 us -> 7 us
  transfers between devices with their start and end apart: 15 -> 10, of which waited for: 7 -> 4; matrix products, arithmetic and copies ran while one was open for 2% -> 2% of each run, Pallas kernels for 0% -> 0%
where the time goes in v3:
time: 178 us; the launch traced here: 175 us
  waiting for transfers between devices  55.9 us (31%)
  blocking collectives  53.2 us (30%)
  starting transfers between devices  41 us (23%)
  Pallas kernels  12.9 us (7%)
  local copies, waits for them, and re-layouts  8.31 us (5%)
  other arithmetic  2.81 us (2%)
    all_to_all x1, blocking collectives, shards(): terms = lax.all_to_all(terms, OTHERS, split_axis=0, concat_axis=0)  35.7 us
    all_to_all x1, waiting for transfers between devices, shards(): lax.all_to_all(copies(where, first, second, near), OTHERS, split_axis=0,...  32 us
    ppermute x1, waiting for transfers between devices, shards(): first = lax.ppermute(first, AXES, home_pairs(0))  16.3 us
    all_to_all x1, blocking collectives, shards(): slopes = lax.all_to_all(dq, GROUP, split_axis=0, concat_axis=0)  11.7 us
    all_to_all x1, starting transfers between devices, shards(): lax.all_to_all(copies(where, first, second, near), OTHERS, split_axis=0,...  10.8 us
    ppermute x3, starting transfers between devices, swap(): return lax.ppermute(value, GROUP, [(i, i ^ offset) for i in range(4)])  9.67 us
    ppermute x1, starting transfers between devices, shards(): first = lax.ppermute(first, AXES, home_pairs(0))  7.35 us
    all_to_all x1, waiting for transfers between devices, shards(): parts = lax.all_to_all(parts, GROUP, split_axis=0, concat_axis=0)  7.02 us
  transfers between devices with their start and end apart: 10, of which 4 were waited for; matrix products, arithmetic and copies ran while one was open for 2% of the time, Pallas kernels for 0%

profile of v3, /device:TPU:6, one launch (start us, length us, event | category | flops | bytes accessed | tf_op | source)
XLA Modules:
  0.0 175.0 jit_solution(9537768604396631217)
XLA Ops:
  0.6 0.1 pad_add_fusion.where_ref
  0.7 2.2 %copy-done = bf16[256,8192]{1,0:T(8,128)(2,1)S(1)} copy-done((bf16[256,8192]{1,0:T(8,128)(2,1)S(1)}, bf16[256,8192]{1,0:T(8,128)(2,1)}, u32[]{:S(2)}) %copy-start) | copy-done | bytes 4194328
  2.9 1.3 cut_states.1
  4.2 1.0 copy-done.1
  5.2 3.5 %collective-permute-start = (bf16[256,1024]{1,0:T(8,128)(2,1)S(1)}, bf16[256,1024]{1,0:T(8,128)(2,1)S(1)}, u32[]{:S(2)}, u32[]{:S(2)}) collective-permute-start(bf16[256,1024]{1,0:T(8,128)(2,1)S(1)} %get-tuple-element.11.after), channel_id=1, source_target_pairs={{0,16},{16,0},{64,80},{80,64},{1,17},{17,1},{65,81},{81,65},{2,18}... | collective-permute-start | bytes 1572872 | tf_op jit(solution)/shard_map/ppermute | solution.py:37
  8.6 4.3 %collective-permute-start.1 = (bf16[256,1024]{1,0:T(8,128)(2,1)S(1)}, bf16[256,1024]{1,0:T(8,128)(2,1)S(1)}, u32[]{:S(2)}, u32[]{:S(2)}) collective-permute-start(bf16[256,1024]{1,0:T(8,128)(2,1)S(1)} %get-tuple-element.12), channel_id=1, source_target_pairs={{0,64},{16,80},{64,0},{80,16},{1,65},{17,81},{65,1},{81,17},{2,66}... | collective-permute-start | bytes 1572872 | tf_op jit(solution)/shard_map/ppermute | solution.py:37
  12.9 1.9 %collective-permute-start.2 = (bf16[256,1024]{1,0:T(8,128)(2,1)S(1)}, bf16[256,1024]{1,0:T(8,128)(2,1)S(1)}, u32[]{:S(2)}, u32[]{:S(2)}) collective-permute-start(bf16[256,1024]{1,0:T(8,128)(2,1)S(1)} %get-tuple-element.13), channel_id=1, source_target_pairs={{0,80},{16,64},{64,16},{80,0},{1,81},{17,65},{65,17},{81,1},{2,82}... | collective-permute-start | bytes 1572872 | tf_op jit(solution)/shard_map/ppermute | solution.py:37
  14.9 0.6 pack_weights.1
  15.5 7.3 %collective-permute-start.6 = (bf16[320,128]{1,0:T(8,128)(2,1)S(1)}, bf16[320,128]{1,0:T(8,128)(2,1)S(1)}, u32[]{:S(2)}, u32[]{:S(2)}) collective-permute-start(bf16[320,128]{1,0:T(8,128)(2,1)S(1)} %get-tuple-element.14), channel_id=1, source_target_pairs={{0,0},{1,32},{2,64},{3,96},{4,128},{5,160},{6,192},{7,224},{8,256}... | collective-permute-start | bytes 245768 | tf_op jit(solution)/shard_map/ppermute | solution.py:284
  22.8 3.3 %collective-permute-start.7 = (bf16[320,128]{1,0:T(8,128)(2,1)S(1)}, bf16[320,128]{1,0:T(8,128)(2,1)S(1)}, u32[]{:S(2)}, u32[]{:S(2)}) collective-permute-start(bf16[320,128]{1,0:T(8,128)(2,1)S(1)} %get-tuple-element.15), channel_id=1, source_target_pairs={{0,16},{1,48},{2,80},{3,112},{4,144},{5,176},{6,208},{7,240},{8,27... | collective-permute-start | bytes 245768 | tf_op jit(solution)/shard_map/ppermute | solution.py:285
  26.1 16.3 %collective-permute-done.6.first = bf16[320,128]{1,0:T(8,128)(2,1)S(1)} collective-permute-done((bf16[320,128]{1,0:T(8,128)(2,1)S(1)}, bf16[320,128]{1,0:T(8,128)(2,1)S(1)}, u32[]{:S(2)}, u32[]{:S(2)}) %collective-permute-start.6) | collective-permute-done | bytes 81952 | tf_op jit(solution)/shard_map/ppermute | solution.py:284
  42.4 0.0 collective-permute-done.7.second
  42.4 0.0 collective-permute-done.n1
  42.4 0.0 collective-permute-done.1.n2
  42.4 1.8 %weight_copies.1 = bf16[8,2,320,128]{3,2,1,0:T(8,128)(2,1)} custom-call(s32[2]{0:T(128)S(1)} %pad_add_fusion.where_ref, bf16[320,128]{1,0:T(8,128)(2,1)S(1)} %collective-permute-done.6.first, bf16[320,128]{1,0:T(8,128)(2,1)S(1)} %collective-permute-done.7.second, bf16[256,1024]{1,0:T(8,128)(2,1)S(1)} %collective-permute-done.n1, ...), custom_call_target="tpu_custom_call" | custom-call | tf_op jit(solution)/shard_map/weight_copies/pallas_call | solution.py:119
  44.2 10.8 %all-to-all-start = ((bf16[8,2,320,128]{3,2,1,0:T(8,128)(2,1)}), bf16[8,2,320,128]{3,2,1,0:T(8,128)(2,1)S(1)}, u32[]{:S(2)}, u32[]{:S(2)}) async-start(bf16[8,2,320,128]{3,2,1,0:T(8,128)(2,1)} %weight_copies.1), calls=%async_computation | async-start | bytes 2621440 | tf_op jit(solution)/shard_map/all_to_all | solution.py:286
  55.0 0.1 reduce_sum.19
  55.2 1.9 %collective-permute-start.3 = (bf16[256,1024]{1,0:T(8,128)(2,1)S(1)}, bf16[256,1024]{1,0:T(8,128)(2,1)S(1)}, u32[]{:S(2)}, u32[]{:S(2)}) collective-permute-start(bf16[256,1024]{1,0:T(8,128)(2,1)S(1)} %collective-permute-done.n1), channel_id=1, source_target_pairs={{0,1},{1,0},{2,3},{3,2},{4,5},{5,4},{6,7},{7,6},{8,9},{9,8},{10,11... | collective-permute-start | bytes 1572872 | tf_op jit(solution)/shard_map/ppermute | solution.py:41
  57.1 2.4 %collective-permute-start.4 = (bf16[256,1024]{1,0:T(8,128)(2,1)S(1)}, bf16[256,1024]{1,0:T(8,128)(2,1)}, u32[]{:S(2)}, u32[]{:S(2)}) collective-permute-start(bf16[256,1024]{1,0:T(8,128)(2,1)S(1)} %collective-permute-done.1.n2), channel_id=1, source_target_pairs={{0,1},{1,0},{2,3},{3,2},{4,5},{5,4},{6,7},{7,6},{8,9},{9,8},{10,11... | collective-permute-start | bytes 1572872 | tf_op jit(solution)/shard_map/ppermute | solution.py:41
  59.5 1.9 %collective-permute-start.5 = (bf16[256,1024]{1,0:T(8,128)(2,1)S(1)}, bf16[256,1024]{1,0:T(8,128)(2,1)}, u32[]{:S(2)}, u32[]{:S(2)}) collective-permute-start(bf16[256,1024]{1,0:T(8,128)(2,1)S(1)} %collective-permute-done.2.n3), channel_id=1, source_target_pairs={{0,1},{1,0},{2,3},{3,2},{4,5},{5,4},{6,7},{7,6},{8,9},{9,8},{10,11... | collective-permute-start | bytes 1572872 | tf_op jit(solution)/shard_map/ppermute | solution.py:41
  61.4 0.1 add_convert_fusion
  61.5 0.1 convert_element_type.27
  61.6 0.1 copy.9
  61.7 0.1 broadcast_in_dim.6
  61.8 0.1 gt.16
  61.9 0.8 copy.10
  62.7 0.1 broadcast_in_dim.8
  62.7 0.1 mul.44
  62.9 0.6 collective-permute-done.5.f3
  63.4 32.0 %all-to-all-done.weights = bf16[8,2,320,128]{3,2,1,0:T(8,128)(2,1)S(1)} async-done(((bf16[8,2,320,128]{3,2,1,0:T(8,128)(2,1)}), bf16[8,2,320,128]{3,2,1,0:T(8,128)(2,1)S(1)}, u32[]{:S(2)}, u32[]{:S(2)}) %all-to-all-start) | async-done | bytes 1310752 | tf_op jit(solution)/shard_map/all_to_all | solution.py:286
  95.5 1.2 copy-done.2
  96.7 4.5 %project.1 = bf16[4,320,256]{2,1,0:T(8,128)(2,1)} custom-call(s32[2]{0:T(128)S(1)} %pad_add_fusion.where_ref, bf16[256,2048]{1,0:T(8,128)(2,1)S(1)} %copy-done.2, bf16[256,1024]{1,0:T(8,128)(2,1)S(1)} %collective-permute-done.n1, bf16[256,1024]{1,0:T(8,128)(2,1)S(1)} %collective-permute-done.1.n2, bf16[256,1024]{1,0:T(8,128)(2,1)S(1)} %collective-permute-done.2.n3, ...), custom_call_target="tpu_custom_call" | custom-call | tf_op jit(solution)/shard_map/project/pallas_call | solution.py:172
  101.2 3.6 %all-to-all-start.1 = ((bf16[4,320,256]{2,1,0:T(8,128)(2,1)}), bf16[4,320,256]{2,1,0:T(8,128)(2,1)S(1)}, u32[]{:S(2)}, u32[]{:S(2)}) async-start(bf16[4,320,256]{2,1,0:T(8,128)(2,1)} %project.1), calls=%async_computation.1 | async-start | bytes 1310720 | tf_op jit(solution)/shard_map/all_to_all | solution.py:291
  104.8 0.5 fusion.3
  105.4 0.1 pad_maximum_fusion
  105.5 1.0 multiply_sine_fusion.1
  106.5 0.8 multiply_convert_fusion.weighted
  107.2 0.1 fusion.2.visible
  107.4 7.0 %all-to-all-done.1.parts = bf16[4,320,256]{2,1,0:T(8,128)(2,1)S(1)} async-done(((bf16[4,320,256]{2,1,0:T(8,128)(2,1)}), bf16[4,320,256]{2,1,0:T(8,128)(2,1)S(1)}, u32[]{:S(2)}, u32[]{:S(2)}) %all-to-all-start.1) | async-done | bytes 655392 | tf_op jit(solution)/shard_map/all_to_all | solution.py:291
  114.4 5.8 %all-gather = f32[256,256]{1,0:T(8,128)S(1)} all-gather(f32[64,256]{1,0:T(8,128)S(1)} %convert_reduce_fusion), channel_id=2, replica_groups=mesh['zh'=4,'zb'=2,'yu'=2,'yb'=2,'yh'=2,'xh'=2,'xb'=2,'c'=2] {'xb','c'}, dimensions={0}, use_global_device_ids=true | all-gather | bytes 327680 | tf_op jit(solution)/shard_map/all_gather | solution.py:293
  120.2 0.9 copy-done.4
  121.1 0.8 copy-done.5
  121.9 0.8 copy-done.6
  122.8 1.4 attend.1
  124.2 11.7 %all_to_all.20.slopes = bf16[4,256,256]{2,1,0:T(8,128)(2,1)S(1)} all-to-all(bf16[4,256,256]{2,1,0:T(8,128)(2,1)S(1)} %get-tuple-element.17), channel_id=1, replica_groups=mesh['zh'=4,'zb'=2,'yu'=2,'yb'=2,'yh'=2,'xh'=2,'xb'=2,'c'=2] {'zb','yb'}, dimensions={0} | all-to-all | bytes 1048576 | tf_op jit(solution)/shard_map/all_to_all | solution.py:318
  135.9 2.5 %gradient.1 = bf16[8,256,256]{2,1,0:T(8,128)(2,1)S(1)} custom-call(s32[2]{0:T(128)S(1)} %pad_add_fusion.where_ref, bf16[256,2048]{1,0:T(8,128)(2,1)S(1)} %copy-done.3, bf16[256,1024]{1,0:T(8,128)(2,1)S(1)} %collective-permute-done.n1, bf16[256,1024]{1,0:T(8,128)(2,1)S(1)} %collective-permute-done.1.n2, bf16[256,1024]{1,0:T(8,128)(2,1)S(1)} %collective-permute-done.2.n3, ...), custom_call_target="tpu_custom_call" | custom-call | tf_op jit(solution)/shard_map/gradient/pallas_call | solution.py:248
  138.4 35.7 %all_to_all.21.terms = bf16[8,256,256]{2,1,0:T(8,128)(2,1)S(1)} all-to-all(bf16[8,256,256]{2,1,0:T(8,128)(2,1)S(1)} %gradient.1), channel_id=1, replica_groups=mesh['zh'=4,'zb'=2,'yu'=2,'yb'=2,'yh'=2,'xh'=2,'xb'=2,'c'=2] {'zh','yu'}, dimensions={0} | all-to-all | bytes 2097152 | tf_op jit(solution)/shard_map/all_to_all | solution.py:320
  174.1 0.9 add_up.1
  (31 shorter events, 0.1 us)
Async XLA Ops:
  0.7 2.2 %copy-start = (bf16[256,8192]{1,0:T(8,128)(2,1)S(1)}, bf16[256,8192]{1,0:T(8,128)(2,1)}, u32[]{:S(2)}) copy-start(bf16[256,8192]{1,0:T(8,128)(2,1)} %states_ref.1) | copy-start | bytes 12582916
  2.9 12.0 %copy-start.7 = (bf16[512,128]{1,0:T(8,128)(2,1)S(1)}, bf16[512,128]{1,0:T(8,128)(2,1)}, u32[]{:S(2)}) copy-start(bf16[512,128]{1,0:T(8,128)(2,1)} %query.1) | copy-start | bytes 393220
  2.9 12.0 %copy-start.8 = (bf16[512,16]{0,1:T(8,128)(2,1)S(1)}, bf16[512,16]{0,1:T(8,128)(2,1)}, u32[]{:S(2)}) copy-start(bf16[512,16]{0,1:T(8,128)(2,1)} %param.9) | copy-start | bytes 49156
  2.9 12.0 %copy-start.9 = (bf16[512,16]{0,1:T(8,128)(2,1)S(1)}, bf16[512,16]{0,1:T(8,128)(2,1)}, u32[]{:S(2)}) copy-start(bf16[512,16]{0,1:T(8,128)(2,1)} %param.10) | copy-start | bytes 49156
  4.2 1.0 copy-start.1
  5.2 37.2 %collective-permute-start = (bf16[256,1024]{1,0:T(8,128)(2,1)S(1)}, bf16[256,1024]{1,0:T(8,128)(2,1)S(1)}, u32[]{:S(2)}, u32[]{:S(2)}) collective-permute-start(bf16[256,1024]{1,0:T(8,128)(2,1)S(1)} %get-tuple-element.11.after), channel_id=1, source_target_pairs={{0,16},{16,0},{64,80},{80,64},{1,17},{17,1},{65,81},{81,65},{2,18}... | collective-permute-start | bytes 1572872 | tf_op jit(solution)/shard_map/ppermute | solution.py:37
  8.6 33.8 %collective-permute-start.1 = (bf16[256,1024]{1,0:T(8,128)(2,1)S(1)}, bf16[256,1024]{1,0:T(8,128)(2,1)S(1)}, u32[]{:S(2)}, u32[]{:S(2)}) collective-permute-start(bf16[256,1024]{1,0:T(8,128)(2,1)S(1)} %get-tuple-element.12), channel_id=1, source_target_pairs={{0,64},{16,80},{64,0},{80,16},{1,65},{17,81},{65,1},{81,17},{2,66}... | collective-permute-start | bytes 1572872 | tf_op jit(solution)/shard_map/ppermute | solution.py:37
  12.9 29.5 %collective-permute-start.2 = (bf16[256,1024]{1,0:T(8,128)(2,1)S(1)}, bf16[256,1024]{1,0:T(8,128)(2,1)S(1)}, u32[]{:S(2)}, u32[]{:S(2)}) collective-permute-start(bf16[256,1024]{1,0:T(8,128)(2,1)S(1)} %get-tuple-element.13), channel_id=1, source_target_pairs={{0,80},{16,64},{64,16},{80,0},{1,81},{17,65},{65,17},{81,1},{2,82}... | collective-permute-start | bytes 1572872 | tf_op jit(solution)/shard_map/ppermute | solution.py:37
  15.5 26.9 %collective-permute-start.6 = (bf16[320,128]{1,0:T(8,128)(2,1)S(1)}, bf16[320,128]{1,0:T(8,128)(2,1)S(1)}, u32[]{:S(2)}, u32[]{:S(2)}) collective-permute-start(bf16[320,128]{1,0:T(8,128)(2,1)S(1)} %get-tuple-element.14), channel_id=1, source_target_pairs={{0,0},{1,32},{2,64},{3,96},{4,128},{5,160},{6,192},{7,224},{8,256}... | collective-permute-start | bytes 245768 | tf_op jit(solution)/shard_map/ppermute | solution.py:284
  22.8 19.6 %collective-permute-start.7 = (bf16[320,128]{1,0:T(8,128)(2,1)S(1)}, bf16[320,128]{1,0:T(8,128)(2,1)S(1)}, u32[]{:S(2)}, u32[]{:S(2)}) collective-permute-start(bf16[320,128]{1,0:T(8,128)(2,1)S(1)} %get-tuple-element.15), channel_id=1, source_target_pairs={{0,16},{1,48},{2,80},{3,112},{4,144},{5,176},{6,208},{7,240},{8,27... | collective-permute-start | bytes 245768 | tf_op jit(solution)/shard_map/ppermute | solution.py:285
  44.2 10.8 %copy-start.12 = (s32[4,4]{1,0:T(4,128)S(1)}, s32[4,4]{1,0:T(4,128)}, u32[]{:S(2)}) copy-start(s32[4,4]{1,0:T(4,128)} %param.11) | copy-start | bytes 196
  44.2 18.4 %copy-start.13 = (f32[4]{0:T(128)S(1)}, f32[4]{0:T(128)}, u32[]{:S(2)}) copy-start(f32[4]{0:T(128)} %param.12) | copy-start | bytes 52
  44.2 51.2 %all-to-all-start = ((bf16[8,2,320,128]{3,2,1,0:T(8,128)(2,1)}), bf16[8,2,320,128]{3,2,1,0:T(8,128)(2,1)S(1)}, u32[]{:S(2)}, u32[]{:S(2)}) async-start(bf16[8,2,320,128]{3,2,1,0:T(8,128)(2,1)} %weight_copies.1), calls=%async_computation | async-start | bytes 2621440 | tf_op jit(solution)/shard_map/all_to_all | solution.py:286
  55.2 7.7 %collective-permute-start.3 = (bf16[256,1024]{1,0:T(8,128)(2,1)S(1)}, bf16[256,1024]{1,0:T(8,128)(2,1)S(1)}, u32[]{:S(2)}, u32[]{:S(2)}) collective-permute-start(bf16[256,1024]{1,0:T(8,128)(2,1)S(1)} %collective-permute-done.n1), channel_id=1, source_target_pairs={{0,1},{1,0},{2,3},{3,2},{4,5},{5,4},{6,7},{7,6},{8,9},{9,8},{10,11... | collective-permute-start | bytes 1572872 | tf_op jit(solution)/shard_map/ppermute | solution.py:41
  57.1 5.8 %collective-permute-start.4 = (bf16[256,1024]{1,0:T(8,128)(2,1)S(1)}, bf16[256,1024]{1,0:T(8,128)(2,1)}, u32[]{:S(2)}, u32[]{:S(2)}) collective-permute-start(bf16[256,1024]{1,0:T(8,128)(2,1)S(1)} %collective-permute-done.1.n2), channel_id=1, source_target_pairs={{0,1},{1,0},{2,3},{3,2},{4,5},{5,4},{6,7},{7,6},{8,9},{9,8},{10,11... | collective-permute-start | bytes 1572872 | tf_op jit(solution)/shard_map/ppermute | solution.py:41
  59.5 3.9 %collective-permute-start.5 = (bf16[256,1024]{1,0:T(8,128)(2,1)S(1)}, bf16[256,1024]{1,0:T(8,128)(2,1)}, u32[]{:S(2)}, u32[]{:S(2)}) collective-permute-start(bf16[256,1024]{1,0:T(8,128)(2,1)S(1)} %collective-permute-done.2.n3), channel_id=1, source_target_pairs={{0,1},{1,0},{2,3},{3,2},{4,5},{5,4},{6,7},{7,6},{8,9},{9,8},{10,11... | collective-permute-start | bytes 1572872 | tf_op jit(solution)/shard_map/ppermute | solution.py:41
  95.5 1.2 copy-start.2
  101.2 5.3 %copy-start.11 = (bf16[256,256]{1,0:T(8,128)(2,1)S(1)}, bf16[256,256]{1,0:T(8,128)(2,1)}, u32[]{:S(2)}) copy-start(bf16[256,256]{1,0:T(8,128)(2,1)} %param.13) | copy-start | bytes 393220
  101.2 6.0 %copy-start.10 = (pred[256,256]{1,0:T(8,128)(4,1)S(1)}, pred[256,256]{1,0:T(8,128)(4,1)}, u32[]{:S(2)}) copy-start(pred[256,256]{1,0:T(8,128)(4,1)} %copy.10) | copy-start | bytes 196612
  101.2 13.2 %all-to-all-start.1 = ((bf16[4,320,256]{2,1,0:T(8,128)(2,1)}), bf16[4,320,256]{2,1,0:T(8,128)(2,1)S(1)}, u32[]{:S(2)}, u32[]{:S(2)}) async-start(bf16[4,320,256]{2,1,0:T(8,128)(2,1)} %project.1), calls=%async_computation.1 | async-start | bytes 1310720 | tf_op jit(solution)/shard_map/all_to_all | solution.py:291
  120.2 0.9 copy-start.4
  121.1 0.8 copy-start.5
  121.9 0.8 copy-start.6
  122.8 13.1 %copy-start.3 = (bf16[256,2048]{1,0:T(8,128)(2,1)S(1)}, bf16[256,2048]{1,0:T(8,128)(2,1)}, u32[]{:S(2)}) copy-start(bf16[256,2048]{1,0:T(8,128)(2,1)} %copy-done.1) | copy-start | bytes 3145732

commit v4 on v3

v4 whole, which is shorter than its diff:
```python
import math

import jax
import jax.numpy as jnp
from jax import lax
from jax.experimental import pallas as pl
from jax.experimental.pallas import tpu as pltpu
from jax.sharding import Mesh
from jax.sharding import PartitionSpec as P

HEAD = 128
BS = 64
TOK = 256
AXES = ("zh", "zb", "yu", "yb", "yh", "xh", "xb", "c")
SIZES = (4, 2, 2, 2, 2, 2, 2, 2)
GROUP = ("zb", "yb")
OTHERS = ("zh", "yu")
F32 = jnp.float32
BF16 = jnp.bfloat16
VMEM_LIMIT = 16 * 1024 * 1024


def params():
    return pltpu.CompilerParams(vmem_limit_bytes=VMEM_LIMIT)


def home_pairs(turn, far):
    pairs = []
    for d in range(32):
        for t in range(16):
            half = (d % 2) ^ turn
            block = (2 * t + half) ^ (2 * far)
            pairs.append((d * 16 + t, block * 16 + d // 2))
    return pairs


def along_z(value, step):
    return lax.ppermute(value, "zh", [(i, (i + step) % 4) for i in range(4)])


def swap(value, offset):
    return lax.ppermute(value, GROUP, [(i, i ^ offset) for i in range(4)])


def swap_core(value):
    return lax.ppermute(value, "c", [(0, 1), (1, 0)])


def block_of(part, core):
    return 4 * (core ^ (part // 4)) + part % 4


def column_of(block, place):
    return pl.multiple_of(
        (block // 2) * 2048 + (block % 2) * 512 + (place // 2) * 1024 + (place % 2) * 256, 256
    )


def in_smem():
    return pl.BlockSpec(memory_space=pltpu.SMEM)


def in_vmem(count):
    return [pl.BlockSpec(memory_space=pltpu.VMEM)] * count


def in_hbm():
    return pl.BlockSpec(memory_space=pltpu.HBM)


def anywhere():
    return pl.BlockSpec(memory_space=pl.ANY)


def pack_kernel(where_ref, query, key_t, value_t, first, second):
    odd = where_ref[1] % 2
    for turn, out in enumerate((first, second)):
        half = odd ^ turn
        out[:256, :] = query[pl.ds(pl.multiple_of(256 * half, 256), 256), :]
        for chunk in range(2):
            lanes = pl.ds(pl.multiple_of(256 * half + 128 * chunk, 128), 128)
            base = 256 + 32 * chunk
            out[base : base + 16, :] = key_t[:, lanes]
            out[base + 16 : base + 32, :] = value_t[:, lanes]


def pack(where, query, key_t, value_t):
    part = jax.ShapeDtypeStruct((320, 128), BF16)
    return pl.pallas_call(
        pack_kernel,
        out_shape=(part, part),
        in_specs=[in_smem(), *in_vmem(3)],
        compiler_params=params(),
        name="pack_weights",
    )(where, query, key_t, value_t)


def cut_kernel(where_ref, states_ref, after, one_ref, two_ref, three_ref, sems):
    core, place = where_ref[0], where_ref[1]
    copies = []
    for number, out in enumerate((one_ref, two_ref, three_ref)):
        for part in range(4):
            start = column_of(block_of(part, core), place ^ (number + 1))
            copies.append(
                pltpu.make_async_copy(
                    states_ref.at[:, pl.ds(start, 256)],
                    out.at[:, pl.ds(256 * part, 256)],
                    sems.at[len(copies)],
                )
            )
    for copy in copies:
        copy.start()
    for copy in copies:
        copy.wait()


def cut(where, states, after):
    part = jax.ShapeDtypeStruct((TOK, 1024), BF16)
    return pl.pallas_call(
        cut_kernel,
        out_shape=(part, part, part),
        in_specs=[in_smem(), in_hbm(), anywhere()],
        out_specs=tuple(in_vmem(3)),
        scratch_shapes=[pltpu.SemaphoreType.DMA((12,))],
        compiler_params=params(),
        name="cut_states",
    )(where, states, after)


def own_columns(where_ref, states_ref, own, sems):
    copies = []
    for part in range(8):
        start = column_of(block_of(part, where_ref[0]), where_ref[1])
        copies.append(
            pltpu.make_async_copy(
                states_ref.at[:, pl.ds(start, 256)],
                own.at[:, pl.ds(256 * part, 256)],
                sems.at[part],
            )
        )
    return copies


def collect_kernel(where_ref, near_one, near_two, far_one, far_two, out):
    odd, upper = where_ref[1] % 2, where_ref[3]
    out[upper, odd] = near_one[...]
    out[upper, 1 - odd] = near_two[...]
    out[1 - upper, odd] = far_one[...]
    out[1 - upper, 1 - odd] = far_two[...]


def collect(where, pieces):
    return pl.pallas_call(
        collect_kernel,
        out_shape=jax.ShapeDtypeStruct((2, 2, 320, 128), BF16),
        in_specs=[in_smem(), *in_vmem(4)],
        compiler_params=params(),
        name="collect_weights",
    )(where, *pieces)


def project_kernel(
    where_ref, states_ref, n1, n2, n3, f1, f2, f3, w0, w1, w2_low, w2_high, w3, out, own, w_q, w_kv, sems
):
    core = where_ref[0]
    copies = own_columns(where_ref, states_ref, own, sems)
    for copy in copies:
        copy.start()
    for step in range(4):
        for upper in range(2):
            block = 2 * ((where_ref[2] + step) % 4) + upper
            start = pl.multiple_of(256 * block_of(block, core), 256)
            rows = pl.ds(start, 256)
            for head in range(2):
                if step == 2:
                    piece = (w2_low, w2_high)[upper].at[head]
                else:
                    piece = {0: w0, 1: w1, 3: w3}[step].at[upper, head]
                w_q[rows, pl.ds(HEAD * head, HEAD)] = piece[:256, :]
                for chunk in range(2):
                    lanes = pl.ds(start + 128 * chunk, 128)
                    base = 256 + 32 * chunk
                    w_kv[16 * head : 16 * head + 16, lanes] = piece[base : base + 16, :]
                    w_kv[32 + 16 * head : 48 + 16 * head, lanes] = piece[base + 16 : base + 32, :]

    def product(x, rows):
        q = jnp.dot(x, w_q[rows, :], preferred_element_type=F32)
        kv = lax.dot_general(
            x, w_kv[:, rows], (((1,), (1,)), ((), ())), preferred_element_type=F32
        )
        return q, kv

    low, high = pl.ds(0, 1024), pl.ds(1024, 1024)
    pieces = (
        (n1.at[:, :], f1.at[:, :]),
        (n2.at[:, :], f2.at[:, :]),
        (n3.at[:, :], f3.at[:, :]),
        (own.at[:, low], own.at[:, high]),
    )
    for number, (near_ref, far_ref) in enumerate(pieces):
        if number == 3:
            for copy in copies:
                copy.wait()
        near, far = near_ref[...], far_ref[...]
        other = where_ref[1] ^ ((number + 1) % 4)
        q_near, kv_near = product(near, low)
        q_far, kv_far = product(far, high)
        out[other, :256, :] = (q_near + q_far).astype(BF16)
        out[other, 256:, :] = (kv_near + kv_far).T.astype(BF16)


def project(where, states, near, far, weights):
    return pl.pallas_call(
        project_kernel,
        out_shape=jax.ShapeDtypeStruct((4, 320, 256), BF16),
        in_specs=[in_smem(), in_hbm(), *in_vmem(11)],
        scratch_shapes=[
            pltpu.VMEM((TOK, 2048), BF16),
            pltpu.VMEM((2048, 256), BF16),
            pltpu.VMEM((64, 2048), BF16),
            pltpu.SemaphoreType.DMA((8,)),
        ],
        compiler_params=params(),
        name="project",
    )(where, states, *near, *far, *weights)


def attend_kernel(
    mask_ref, risk_ref, parts, kv, upstream_ref, tables_ref, attn_out, dq_out, upstream, tables, sems
):
    copies = [
        pltpu.make_async_copy(tables_ref, tables, sems.at[0]),
        pltpu.make_async_copy(upstream_ref, upstream, sems.at[1]),
    ]
    for copy in copies:
        copy.start()
    scaling = 1.0 / math.sqrt(HEAD)
    k_lin = jnp.concatenate([kv[s, :32, :] for s in range(4)], axis=0)
    values = jnp.concatenate([kv[s, 32:, :] for s in range(4)], axis=0).astype(BF16)

    row = lax.broadcasted_iota(jnp.int32, (BS, TOK), 0)
    column = lax.broadcasted_iota(jnp.int32, (BS, TOK), 1)
    seen, risk = [], []
    for b in range(4):
        on_path = jnp.zeros((BS, TOK), jnp.int32)
        for c in range(4):
            on_path = jnp.where(column // BS == c, mask_ref[b, c], on_path)
        seen.append((on_path > 0) & ((column // BS != b) | (column - BS * b <= row)))
        risk.append(jnp.full((BS, 1), risk_ref[b], F32))
    seen = jnp.concatenate(seen, axis=0)
    risk = jnp.concatenate(risk, axis=0)

    copies[0].wait()
    cq, sq = tables[:, :HEAD], tables[:, HEAD:]
    ck, sk = cq[:, :64].T, sq[:, 64:].T
    k1, k2 = k_lin[:64], k_lin[64:]
    keys = jnp.concatenate([k1 * ck - k2 * sk, k2 * ck + k1 * sk], axis=0).astype(BF16)
    copies[1].wait()
    weighted = (upstream[...].astype(F32) * risk).astype(BF16)
    for head in range(2):
        cols = pl.ds(head * HEAD, HEAD)
        q_lin = parts[0, :256, cols].astype(F32)
        for part in range(1, 4):
            q_lin = q_lin + parts[part, :256, cols].astype(F32)
        queries = ((q_lin * cq + pltpu.roll(q_lin, 64, 1) * sq) * scaling).astype(BF16)
        scores = jnp.dot(queries, keys, preferred_element_type=F32)
        raised = jnp.where(seen, jnp.exp(scores), 0.0)
        attend = raised / jnp.sum(raised, axis=1, keepdims=True)
        mixed = lax.dot_general(
            attend.astype(BF16), values, (((1,), (1,)), ((), ())), preferred_element_type=F32
        )
        attn_out[:, cols] = mixed.astype(BF16)
        pressure = jnp.dot(weighted[:, HEAD * head : HEAD * head + HEAD], values, preferred_element_type=F32)
        centre = jnp.sum(attend * pressure, axis=1, keepdims=True)
        slope = (attend * (pressure - centre)).astype(BF16)
        dq_rot = (
            lax.dot_general(slope, keys, (((1,), (1,)), ((), ())), preferred_element_type=F32)
            * scaling
        )
        dq = dq_rot * cq - pltpu.roll(dq_rot, 64, 1) * sq
        dq_t = dq.T.astype(BF16)
        for part in range(4):
            dq_out[part, cols, :] = dq_t


def attend(block_mask, risk_weight, parts, kv, upstream, tables):
    return pl.pallas_call(
        attend_kernel,
        out_shape=(
            jax.ShapeDtypeStruct((TOK, 256), BF16),
            jax.ShapeDtypeStruct((4, 256, TOK), BF16),
        ),
        in_specs=[in_smem(), in_smem(), *in_vmem(2), in_hbm(), in_hbm()],
        scratch_shapes=[
            pltpu.VMEM((TOK, 256), BF16),
            pltpu.VMEM((TOK, 2 * HEAD), F32),
            pltpu.SemaphoreType.DMA((2,)),
        ],
        compiler_params=params(),
        name="attend",
    )(block_mask, risk_weight, parts, kv, upstream, tables)


def gradient_kernel(where_ref, states_ref, n1, n2, n3, f1, f2, f3, slopes, out, own, sems):
    core = where_ref[0]
    copies = own_columns(where_ref, states_ref, own, sems)
    for copy in copies:
        copy.start()
    for part in range(8):
        cols = pl.ds(256 * (part % 4), 256)
        total = None
        for number in (1, 2, 3, 0):
            if number == 0:
                copies[part].wait()
                x = own[:, pl.ds(256 * part, 256)]
            else:
                x = ((n1, n2, n3) if part < 4 else (f1, f2, f3))[number - 1][:, cols]
            term = jnp.dot(slopes[where_ref[1] ^ number], x, preferred_element_type=F32)
            total = term if total is None else total + term
        out[block_of(part, core)] = total.astype(BF16)


def gradient(where, states, near, far, slopes):
    return pl.pallas_call(
        gradient_kernel,
        out_shape=jax.ShapeDtypeStruct((8, 256, 256), BF16),
        in_specs=[in_smem(), in_hbm(), *in_vmem(7)],
        scratch_shapes=[pltpu.VMEM((TOK, 2048), BF16), pltpu.SemaphoreType.DMA((8,))],
        compiler_params=params(),
        name="gradient",
    )(where, states, *near, *far, slopes)


def total_kernel(terms, out):
    total = terms[0].astype(F32)
    for block in range(1, 8):
        total = total + terms[block].astype(F32)
    out[...] = total.T


def add_up(terms):
    return pl.pallas_call(
        total_kernel,
        out_shape=jax.ShapeDtypeStruct((256, 256), F32),
        compiler_params=params(),
        name="add_up",
    )(terms)


def shards(states, query_weight, key_matrix, value_matrix, block_mask, risk_weight, upstream):
    place = 2 * lax.axis_index("zb") + lax.axis_index("yb")
    where = jnp.stack([lax.axis_index("c"), place, lax.axis_index("zh"), lax.axis_index("yu")])
    where = where.astype(jnp.int32)

    halves = pack(where, query_weight, key_matrix.T, value_matrix.T)
    pieces = [
        lax.ppermute(halves[turn], AXES, home_pairs(turn, far))
        for far in range(2)
        for turn in range(2)
    ]

    outgoing = cut(where, states, halves[0])
    near = [swap(outgoing[j - 1], j) for j in (1, 2, 3)]
    far = [swap_core(x) for x in near]

    w0 = collect(where, pieces)
    w3 = along_z(w0, 1)
    w1 = along_z(w0, -1)
    w2_low = along_z(w3[0], 1)
    w2_high = along_z(w1[1], -1)

    parts = project(where, states, near, far, (w0, w1, w2_low, w2_high, w3))
    parts = lax.all_to_all(parts, GROUP, split_axis=0, concat_axis=0)
    kv = jnp.sum(parts[:, 256:].astype(F32), axis=0)
    kv = lax.all_gather(kv, ("xb", "c"), axis=0, tiled=False)

    depths = jnp.sum(block_mask, axis=1) - 1
    places = (depths[:, None] * BS + jnp.arange(BS, dtype=jnp.int32)[None, :]).reshape(TOK)
    frequency = jnp.exp(
        -math.log(1000000.0) * jnp.arange(HEAD // 2, dtype=F32) * 2.0 / HEAD
    )
    angles = places.astype(F32)[:, None] * frequency[None, :]
    cosine, sine = jnp.cos(angles), jnp.sin(angles)
    tables = jnp.concatenate([cosine, cosine, -sine, sine], axis=1)

    attn_out, dq = attend(block_mask, risk_weight, parts, kv, upstream, tables)
    slopes = lax.all_to_all(dq, GROUP, split_axis=0, concat_axis=0)
    terms = gradient(where, states, near, far, slopes)
    terms = lax.all_to_all(terms, OTHERS, split_axis=0, concat_axis=0)
    return attn_out, add_up(terms)


def solution(mesh):
    fine = Mesh(mesh.devices.reshape(SIZES), AXES)
    dp, tensor = AXES[:4], AXES[4:]
    in_specs = (
        P(dp, None),
        P(tensor, dp),
        P(tensor, dp),
        P(tensor, dp),
        P(dp, None),
        P(dp),
        P(dp, tensor),
    )
    out_specs = (P(dp, tensor), P(dp, tensor))
    return jax.shard_map(shards, mesh=fine, in_specs=in_specs, out_specs=out_specs, check_vma=False)
```

time: 178 us -> 190 us (1.067)
  the two profiles are of different devices: /device:TPU:6 before, /device:TPU:1 now
where the time goes in v4:
time: 190 us; the launch traced here: 189 us
  starting transfers between devices  82.7 us (44%)
  blocking collectives  57.5 us (30%)
  waiting for transfers between devices  23.8 us (13%)
  Pallas kernels  13.2 us (7%)
  local copies, waits for them, and re-layouts  9.58 us (5%)
    all_to_all x1, blocking collectives, shards(): terms = lax.all_to_all(terms, OTHERS, split_axis=0, concat_axis=0)  35.6 us
    ppermute x4, starting transfers between devices, along_z(): return lax.ppermute(value, 'zh', [(i, (i + step) % 4) for i in range(4)])  32.3 us
    ppermute x4, starting transfers between devices, shards(): lax.ppermute(halves[turn], AXES, home_pairs(turn, far))  22.7 us
    ppermute x3, starting transfers between devices, swap_core(): return lax.ppermute(value, 'c', [(0, 1), (1, 0)])  14.2 us
    all_gather x1, blocking collectives, shards(): kv = lax.all_gather(kv, ('xb', 'c'), axis=0, tiled=False)  11.5 us
    all_to_all x1, blocking collectives, shards(): slopes = lax.all_to_all(dq, GROUP, split_axis=0, concat_axis=0)  10.4 us
    ppermute x4, waiting for transfers between devices, shards(): lax.ppermute(halves[turn], AXES, home_pairs(turn, far))  10.1 us
    ppermute x3, starting transfers between devices, swap(): return lax.ppermute(value, GROUP, [(i, i ^ offset) for i in range(4)])  10.1 us
  transfers between devices with their start and end apart: 15, of which 6 were waited for; matrix products, arithmetic and copies ran while one was open for 1% of the time, Pallas kernels for 0%

profile of v4, /device:TPU:1, one launch (start us, length us, event | category | flops | bytes accessed | tf_op | source)
XLA Modules:
  0.0 188.9 jit_solution(7712223093768945861)
XLA Ops:
  0.6 0.1 pad_add_fusion.where_ref
  0.7 0.9 copy-done.6
  1.6 0.7 copy-done.7
  2.3 0.7 copy-done.8
  3.1 0.6 pack_weights.1
  3.6 0.0 copy-start
  3.6 2.2 %copy-done = bf16[256,8192]{1,0:T(8,128)(2,1)S(1)} copy-done((bf16[256,8192]{1,0:T(8,128)(2,1)S(1)}, bf16[256,8192]{1,0:T(8,128)(2,1)}, u32[]{:S(2)}) %copy-start) | copy-done | bytes 4194328
  5.8 1.0 cut_states.1
  6.8 4.2 %collective-permute-start = (bf16[256,1024]{1,0:T(8,128)(2,1)S(1)}, bf16[256,1024]{1,0:T(8,128)(2,1)S(1)}, u32[]{:S(2)}, u32[]{:S(2)}) collective-permute-start(bf16[256,1024]{1,0:T(8,128)(2,1)S(1)} %get-tuple-element.10), channel_id=1, source_target_pairs={{0,16},{16,0},{64,80},{80,64},{1,17},{17,1},{65,81},{81,65},{2,18}... | collective-permute-start | bytes 1572872 | tf_op jit(solution)/shard_map/ppermute | solution.py:42
  11.0 4.0 %collective-permute-start.1 = (bf16[256,1024]{1,0:T(8,128)(2,1)S(1)}, bf16[256,1024]{1,0:T(8,128)(2,1)S(1)}, u32[]{:S(2)}, u32[]{:S(2)}) collective-permute-start(bf16[256,1024]{1,0:T(8,128)(2,1)S(1)} %get-tuple-element.11), channel_id=1, source_target_pairs={{0,64},{16,80},{64,0},{80,16},{1,65},{17,81},{65,1},{81,17},{2,66}... | collective-permute-start | bytes 1572872 | tf_op jit(solution)/shard_map/ppermute | solution.py:42
  15.0 1.9 %collective-permute-start.2 = (bf16[256,1024]{1,0:T(8,128)(2,1)S(1)}, bf16[256,1024]{1,0:T(8,128)(2,1)S(1)}, u32[]{:S(2)}, u32[]{:S(2)}) collective-permute-start(bf16[256,1024]{1,0:T(8,128)(2,1)S(1)} %get-tuple-element.12), channel_id=1, source_target_pairs={{0,80},{16,64},{64,16},{80,0},{1,81},{17,65},{65,17},{81,1},{2,82}... | collective-permute-start | bytes 1572872 | tf_op jit(solution)/shard_map/ppermute | solution.py:42
  16.9 5.3 %collective-permute-start.6 = (bf16[320,128]{1,0:T(8,128)(2,1)S(1)}, bf16[320,128]{1,0:T(8,128)(2,1)S(1)}, u32[]{:S(2)}, u32[]{:S(2)}) collective-permute-start(bf16[320,128]{1,0:T(8,128)(2,1)S(1)} %get-tuple-element.9.after), channel_id=1, source_target_pairs={{0,0},{1,32},{2,64},{3,96},{4,128},{5,160},{6,192},{7,224},{8,256}... | collective-permute-start | bytes 245768 | tf_op jit(solution)/shard_map/ppermute | solution.py:357
  22.2 3.4 %collective-permute-start.8 = (bf16[320,128]{1,0:T(8,128)(2,1)S(1)}, bf16[320,128]{1,0:T(8,128)(2,1)S(1)}, u32[]{:S(2)}, u32[]{:S(2)}) collective-permute-start(bf16[320,128]{1,0:T(8,128)(2,1)S(1)} %get-tuple-element.9.after), channel_id=1, source_target_pairs={{0,32},{1,0},{2,96},{3,64},{4,160},{5,128},{6,224},{7,192},{8,288}... | collective-permute-start | bytes 245768 | tf_op jit(solution)/shard_map/ppermute | solution.py:357
  25.6 5.1 %collective-permute-done.6.near_one = bf16[320,128]{1,0:T(8,128)(2,1)S(1)} collective-permute-done((bf16[320,128]{1,0:T(8,128)(2,1)S(1)}, bf16[320,128]{1,0:T(8,128)(2,1)S(1)}, u32[]{:S(2)}, u32[]{:S(2)}) %collective-permute-start.6) | collective-permute-done | bytes 81952 | tf_op jit(solution)/shard_map/ppermute | solution.py:357
  30.7 12.0 %collective-permute-start.7 = (bf16[320,128]{1,0:T(8,128)(2,1)S(1)}, bf16[320,128]{1,0:T(8,128)(2,1)S(1)}, u32[]{:S(2)}, u32[]{:S(2)}) collective-permute-start(bf16[320,128]{1,0:T(8,128)(2,1)S(1)} %get-tuple-element.13), channel_id=1, source_target_pairs={{0,16},{1,48},{2,80},{3,112},{4,144},{5,176},{6,208},{7,240},{8,27... | collective-permute-start | bytes 245768 | tf_op jit(solution)/shard_map/ppermute | solution.py:357
  42.8 1.9 %collective-permute-start.9 = (bf16[320,128]{1,0:T(8,128)(2,1)S(1)}, bf16[320,128]{1,0:T(8,128)(2,1)S(1)}, u32[]{:S(2)}, u32[]{:S(2)}) collective-permute-start(bf16[320,128]{1,0:T(8,128)(2,1)S(1)} %get-tuple-element.13), channel_id=1, source_target_pairs={{0,48},{1,16},{2,112},{3,80},{4,176},{5,144},{6,240},{7,208},{8,30... | collective-permute-start | bytes 245768 | tf_op jit(solution)/shard_map/ppermute | solution.py:357
  44.7 0.4 collective-permute-done.7.near_two
  45.1 4.6 %collective-permute-done.9.far_two = bf16[320,128]{1,0:T(8,128)(2,1)S(1)} collective-permute-done((bf16[320,128]{1,0:T(8,128)(2,1)S(1)}, bf16[320,128]{1,0:T(8,128)(2,1)S(1)}, u32[]{:S(2)}, u32[]{:S(2)}) %collective-permute-start.9) | collective-permute-done | bytes 81952 | tf_op jit(solution)/shard_map/ppermute | solution.py:357
  49.7 0.6 collect_weights.1.w0
  50.3 12.1 %collective-permute-start.11 = (bf16[2,2,320,128]{3,2,1,0:T(8,128)(2,1)S(1)}, bf16[2,2,320,128]{3,2,1,0:T(8,128)(2,1)S(1)}, u32[]{:S(2)}, u32[]{:S(2)}) collective-permute-start(bf16[2,2,320,128]{3,2,1,0:T(8,128)(2,1)S(1)} %collect_weights.1.w0), channel_id=1, source_target_pairs={{0,128},{128,256},{256,384},{384,0},{1,129},{129,257},{257,385},{3... | collective-permute-start | bytes 983048 | tf_op jit(solution)/shard_map/ppermute | solution.py:38
  62.4 11.8 %collective-permute-start.10 = (bf16[2,2,320,128]{3,2,1,0:T(8,128)(2,1)S(1)}, bf16[2,2,320,128]{3,2,1,0:T(8,128)(2,1)S(1)}, u32[]{:S(2)}, u32[]{:S(2)}) collective-permute-start(bf16[2,2,320,128]{3,2,1,0:T(8,128)(2,1)S(1)} %collect_weights.1.w0), channel_id=1, source_target_pairs={{0,384},{128,0},{256,128},{384,256},{1,385},{129,1},{257,129},{385... | collective-permute-start | bytes 983048 | tf_op jit(solution)/shard_map/ppermute | solution.py:38
  74.2 9.9 %collective-permute-start.3 = (bf16[256,1024]{1,0:T(8,128)(2,1)S(1)}, bf16[256,1024]{1,0:T(8,128)(2,1)S(1)}, u32[]{:S(2)}, u32[]{:S(2)}) collective-permute-start(bf16[256,1024]{1,0:T(8,128)(2,1)S(1)} %collective-permute-done.n1), channel_id=1, source_target_pairs={{0,1},{1,0},{2,3},{3,2},{4,5},{5,4},{6,7},{7,6},{8,9},{9,8},{10,11... | collective-permute-start | bytes 1572872 | tf_op jit(solution)/shard_map/ppermute | solution.py:46
  84.1 1.9 %collective-permute-start.4 = (bf16[256,1024]{1,0:T(8,128)(2,1)S(1)}, bf16[256,1024]{1,0:T(8,128)(2,1)S(1)}, u32[]{:S(2)}, u32[]{:S(2)}) collective-permute-start(bf16[256,1024]{1,0:T(8,128)(2,1)S(1)} %collective-permute-done.1.n2), channel_id=1, source_target_pairs={{0,1},{1,0},{2,3},{3,2},{4,5},{5,4},{6,7},{7,6},{8,9},{9,8},{10,11... | collective-permute-start | bytes 1572872 | tf_op jit(solution)/shard_map/ppermute | solution.py:46
  86.1 2.4 %collective-permute-start.5 = (bf16[256,1024]{1,0:T(8,128)(2,1)S(1)}, bf16[256,1024]{1,0:T(8,128)(2,1)S(1)}, u32[]{:S(2)}, u32[]{:S(2)}) collective-permute-start(bf16[256,1024]{1,0:T(8,128)(2,1)S(1)} %collective-permute-done.2.n3), channel_id=1, source_target_pairs={{0,1},{1,0},{2,3},{3,2},{4,5},{5,4},{6,7},{7,6},{8,9},{9,8},{10,11... | collective-permute-start | bytes 1572872 | tf_op jit(solution)/shard_map/ppermute | solution.py:46
  88.5 6.5 %collective-permute-start.12 = (bf16[2,320,128]{2,1,0:T(8,128)(2,1)S(1)}, bf16[2,320,128]{2,1,0:T(8,128)(2,1)S(1)}, u32[]{:S(2)}, u32[]{:S(2)}) collective-permute-start(bf16[2,320,128]{2,1,0:T(8,128)(2,1)S(1)} %slice_bitcast_fusion.1), channel_id=1, source_target_pairs={{0,128},{128,256},{256,384},{384,0},{1,129},{129,257},{257,385},{3... | collective-permute-start | bytes 491528 | tf_op jit(solution)/shard_map/ppermute | solution.py:38
  95.1 0.0 copy-start.9
  95.1 0.0 copy-start.10
  95.1 1.9 %collective-permute-start.13 = (bf16[2,320,128]{2,1,0:T(8,128)(2,1)S(1)}, bf16[2,320,128]{2,1,0:T(8,128)(2,1)S(1)}, u32[]{:S(2)}, u32[]{:S(2)}) collective-permute-start(bf16[2,320,128]{2,1,0:T(8,128)(2,1)S(1)} %slice_bitcast_fusion), channel_id=1, source_target_pairs={{0,384},{128,0},{256,128},{384,256},{1,385},{129,1},{257,129},{385... | collective-permute-start | bytes 491528 | tf_op jit(solution)/shard_map/ppermute | solution.py:38
  97.0 4.1 %collective-permute-done.12.w2_low = bf16[2,320,128]{2,1,0:T(8,128)(2,1)S(1)} collective-permute-done((bf16[2,320,128]{2,1,0:T(8,128)(2,1)S(1)}, bf16[2,320,128]{2,1,0:T(8,128)(2,1)S(1)}, u32[]{:S(2)}, u32[]{:S(2)}) %collective-permute-start.12) | collective-permute-done | bytes 163872 | tf_op jit(solution)/shard_map/ppermute | solution.py:38
  101.1 4.5 %collective-permute-done.13.w2_high = bf16[2,320,128]{2,1,0:T(8,128)(2,1)S(1)} collective-permute-done((bf16[2,320,128]{2,1,0:T(8,128)(2,1)S(1)}, bf16[2,320,128]{2,1,0:T(8,128)(2,1)S(1)}, u32[]{:S(2)}, u32[]{:S(2)}) %collective-permute-start.13) | collective-permute-done | bytes 163872 | tf_op jit(solution)/shard_map/ppermute | solution.py:38
  105.6 4.6 %project.1 = bf16[4,320,256]{2,1,0:T(8,128)(2,1)} custom-call(s32[4]{0:T(128)S(1)} %pad_add_fusion.where_ref, bf16[256,8192]{1,0:T(8,128)(2,1)S(1)} %copy-done.1, bf16[256,1024]{1,0:T(8,128)(2,1)S(1)} %collective-permute-done.n1, bf16[256,1024]{1,0:T(8,128)(2,1)S(1)} %collective-permute-done.1.n2, bf16[256,1024]{1,0:T(8,128)(2,1)S(1)} %collective-permute-done.2.n3, ...), custom_call_target="tpu_custom_call" | custom-call | tf_op jit(solution)/shard_map/project/pallas_call | solution.py:213
  110.2 0.8 copy-done.3
  111.0 3.5 %all-to-all-start = ((bf16[4,320,256]{2,1,0:T(8,128)(2,1)}), bf16[4,320,256]{2,1,0:T(8,128)(2,1)S(1)}, u32[]{:S(2)}, u32[]{:S(2)}) async-start(bf16[4,320,256]{2,1,0:T(8,128)(2,1)} %project.1), calls=%async_computation | async-start | bytes 1310720 | tf_op jit(solution)/shard_map/all_to_all | solution.py:373
  114.5 0.1 reduce_sum.19
  114.6 0.1 add_convert_fusion
  114.7 0.1 convert_element_type.15
  114.8 0.5 multiply_cosine_fusion
  115.3 0.2 pad_maximum_fusion.tables_ref
  115.5 5.1 %all-to-all-done.parts = bf16[4,320,256]{2,1,0:T(8,128)(2,1)S(1)} async-done(((bf16[4,320,256]{2,1,0:T(8,128)(2,1)}), bf16[4,320,256]{2,1,0:T(8,128)(2,1)S(1)}, u32[]{:S(2)}, u32[]{:S(2)}) %all-to-all-start) | async-done | bytes 655392 | tf_op jit(solution)/shard_map/all_to_all | solution.py:373
  120.6 11.5 %all-gather = f32[256,256]{1,0:T(8,128)S(1)} all-gather(f32[64,256]{1,0:T(8,128)S(1)} %convert_reduce_fusion), channel_id=2, replica_groups=mesh['zh'=4,'zb'=2,'yu'=2,'yb'=2,'yh'=2,'xh'=2,'xb'=2,'c'=2] {'xb','c'}, dimensions={0}, use_global_device_ids=true | all-gather | bytes 327680 | tf_op jit(solution)/shard_map/all_gather | solution.py:375
  132.2 0.9 copy-done.5
  133.1 2.5 %attend.1 = (bf16[256,256]{1,0:T(8,128)(2,1)}, bf16[4,256,256]{2,1,0:T(8,128)(2,1)S(1)}) custom-call(s32[4,4]{1,0:T(4,128)S(1)} %copy-done.9, f32[4]{0:T(128)S(1)} %copy-done.10, bf16[4,320,256]{2,1,0:T(8,128)(2,1)S(1)} %all-to-all-done.parts, f32[4,64,256]{2,1,0:T(8,128)S(1)} %bitcast.11, bf16[256,256]{1,0:T(8,128)(2,1)S(1)} %copy-done.5, ...), custom_call_target="tpu_custom_call" | custom-call | tf_op jit(solution)/shard_map/attend/pallas_call | solution.py:287
  135.6 10.4 %all_to_all.15.slopes = bf16[4,256,256]{2,1,0:T(8,128)(2,1)S(1)} all-to-all(bf16[4,256,256]{2,1,0:T(8,128)(2,1)S(1)} %get-tuple-element.15), channel_id=1, replica_groups=mesh['zh'=4,'zb'=2,'yu'=2,'yb'=2,'yh'=2,'xh'=2,'xb'=2,'c'=2] {'zb','yb'}, dimensions={0} | all-to-all | bytes 1048576 | tf_op jit(solution)/shard_map/all_to_all | solution.py:387
  146.0 2.2 %copy-done.2 = bf16[256,8192]{1,0:T(8,128)(2,1)S(1)} copy-done((bf16[256,8192]{1,0:T(8,128)(2,1)S(1)}, bf16[256,8192]{1,0:T(8,128)(2,1)}, u32[]{:S(2)}) %copy-start.2) | copy-done | bytes 4194328
  148.2 1.0 copy-done.4
  149.2 3.1 %gradient.1 = bf16[8,256,256]{2,1,0:T(8,128)(2,1)S(1)} custom-call(s32[4]{0:T(128)S(1)} %pad_add_fusion.where_ref, bf16[256,8192]{1,0:T(8,128)(2,1)S(1)} %copy-done.2, bf16[256,1024]{1,0:T(8,128)(2,1)S(1)} %collective-permute-done.n1, bf16[256,1024]{1,0:T(8,128)(2,1)S(1)} %collective-permute-done.1.n2, bf16[256,1024]{1,0:T(8,128)(2,1)S(1)} %collective-permute-done.2.n3, ...), custom_call_target="tpu_custom_call" | custom-call | tf_op jit(solution)/shard_map/gradient/pallas_call | solution.py:324
  152.4 35.6 %all_to_all.16.terms = bf16[8,256,256]{2,1,0:T(8,128)(2,1)S(1)} all-to-all(bf16[8,256,256]{2,1,0:T(8,128)(2,1)S(1)} %gradient.1), channel_id=1, replica_groups=mesh['zh'=4,'zb'=2,'yu'=2,'yb'=2,'yh'=2,'xh'=2,'xb'=2,'c'=2] {'zh','yu'}, dimensions={0} | all-to-all | bytes 2097152 | tf_op jit(solution)/shard_map/all_to_all | solution.py:389
  188.0 0.9 add_up.1
  (25 shorter events, 0.1 us)
Async XLA Ops:
  0.7 0.9 copy-start.6
  1.6 0.7 copy-start.7
  2.3 0.7 copy-start.8
  3.6 2.2 %copy-start = (bf16[256,8192]{1,0:T(8,128)(2,1)S(1)}, bf16[256,8192]{1,0:T(8,128)(2,1)}, u32[]{:S(2)}) copy-start(bf16[256,8192]{1,0:T(8,128)(2,1)} %states_ref.5) | copy-start | bytes 12582916
  5.8 99.8 %copy-start.1 = (bf16[256,8192]{1,0:T(8,128)(2,1)S(1)}, bf16[256,8192]{1,0:T(8,128)(2,1)}, u32[]{:S(2)}) copy-start(bf16[256,8192]{1,0:T(8,128)(2,1)} %states_ref.5) | copy-start | bytes 12582916
  6.8 67.4 %collective-permute-start = (bf16[256,1024]{1,0:T(8,128)(2,1)S(1)}, bf16[256,1024]{1,0:T(8,128)(2,1)S(1)}, u32[]{:S(2)}, u32[]{:S(2)}) collective-permute-start(bf16[256,1024]{1,0:T(8,128)(2,1)S(1)} %get-tuple-element.10), channel_id=1, source_target_pairs={{0,16},{16,0},{64,80},{80,64},{1,17},{17,1},{65,81},{81,65},{2,18}... | collective-permute-start | bytes 1572872 | tf_op jit(solution)/shard_map/ppermute | solution.py:42
  11.0 73.1 %collective-permute-start.1 = (bf16[256,1024]{1,0:T(8,128)(2,1)S(1)}, bf16[256,1024]{1,0:T(8,128)(2,1)S(1)}, u32[]{:S(2)}, u32[]{:S(2)}) collective-permute-start(bf16[256,1024]{1,0:T(8,128)(2,1)S(1)} %get-tuple-element.11), channel_id=1, source_target_pairs={{0,64},{16,80},{64,0},{80,16},{1,65},{17,81},{65,1},{81,17},{2,66}... | collective-permute-start | bytes 1572872 | tf_op jit(solution)/shard_map/ppermute | solution.py:42
  15.0 71.1 %collective-permute-start.2 = (bf16[256,1024]{1,0:T(8,128)(2,1)S(1)}, bf16[256,1024]{1,0:T(8,128)(2,1)S(1)}, u32[]{:S(2)}, u32[]{:S(2)}) collective-permute-start(bf16[256,1024]{1,0:T(8,128)(2,1)S(1)} %get-tuple-element.12), channel_id=1, source_target_pairs={{0,80},{16,64},{64,16},{80,0},{1,81},{17,65},{65,17},{81,1},{2,82}... | collective-permute-start | bytes 1572872 | tf_op jit(solution)/shard_map/ppermute | solution.py:42
  16.9 13.8 %collective-permute-start.6 = (bf16[320,128]{1,0:T(8,128)(2,1)S(1)}, bf16[320,128]{1,0:T(8,128)(2,1)S(1)}, u32[]{:S(2)}, u32[]{:S(2)}) collective-permute-start(bf16[320,128]{1,0:T(8,128)(2,1)S(1)} %get-tuple-element.9.after), channel_id=1, source_target_pairs={{0,0},{1,32},{2,64},{3,96},{4,128},{5,160},{6,192},{7,224},{8,256}... | collective-permute-start | bytes 245768 | tf_op jit(solution)/shard_map/ppermute | solution.py:357
  22.2 20.5 %collective-permute-start.8 = (bf16[320,128]{1,0:T(8,128)(2,1)S(1)}, bf16[320,128]{1,0:T(8,128)(2,1)S(1)}, u32[]{:S(2)}, u32[]{:S(2)}) collective-permute-start(bf16[320,128]{1,0:T(8,128)(2,1)S(1)} %get-tuple-element.9.after), channel_id=1, source_target_pairs={{0,32},{1,0},{2,96},{3,64},{4,160},{5,128},{6,224},{7,192},{8,288}... | collective-permute-start | bytes 245768 | tf_op jit(solution)/shard_map/ppermute | solution.py:357
  30.7 14.4 %collective-permute-start.7 = (bf16[320,128]{1,0:T(8,128)(2,1)S(1)}, bf16[320,128]{1,0:T(8,128)(2,1)S(1)}, u32[]{:S(2)}, u32[]{:S(2)}) collective-permute-start(bf16[320,128]{1,0:T(8,128)(2,1)S(1)} %get-tuple-element.13), channel_id=1, source_target_pairs={{0,16},{1,48},{2,80},{3,112},{4,144},{5,176},{6,208},{7,240},{8,27... | collective-permute-start | bytes 245768 | tf_op jit(solution)/shard_map/ppermute | solution.py:357
  42.8 7.0 %collective-permute-start.9 = (bf16[320,128]{1,0:T(8,128)(2,1)S(1)}, bf16[320,128]{1,0:T(8,128)(2,1)S(1)}, u32[]{:S(2)}, u32[]{:S(2)}) collective-permute-start(bf16[320,128]{1,0:T(8,128)(2,1)S(1)} %get-tuple-element.13), channel_id=1, source_target_pairs={{0,48},{1,16},{2,112},{3,80},{4,176},{5,144},{6,240},{7,208},{8,30... | collective-permute-start | bytes 245768 | tf_op jit(solution)/shard_map/ppermute | solution.py:357
  50.3 38.2 %collective-permute-start.11 = (bf16[2,2,320,128]{3,2,1,0:T(8,128)(2,1)S(1)}, bf16[2,2,320,128]{3,2,1,0:T(8,128)(2,1)S(1)}, u32[]{:S(2)}, u32[]{:S(2)}) collective-permute-start(bf16[2,2,320,128]{3,2,1,0:T(8,128)(2,1)S(1)} %collect_weights.1.w0), channel_id=1, source_target_pairs={{0,128},{128,256},{256,384},{384,0},{1,129},{129,257},{257,385},{3... | collective-permute-start | bytes 983048 | tf_op jit(solution)/shard_map/ppermute | solution.py:38
  62.4 32.6 %collective-permute-start.10 = (bf16[2,2,320,128]{3,2,1,0:T(8,128)(2,1)S(1)}, bf16[2,2,320,128]{3,2,1,0:T(8,128)(2,1)S(1)}, u32[]{:S(2)}, u32[]{:S(2)}) collective-permute-start(bf16[2,2,320,128]{3,2,1,0:T(8,128)(2,1)S(1)} %collect_weights.1.w0), channel_id=1, source_target_pairs={{0,384},{128,0},{256,128},{384,256},{1,385},{129,1},{257,129},{385... | collective-permute-start | bytes 983048 | tf_op jit(solution)/shard_map/ppermute | solution.py:38
  74.2 31.4 %collective-permute-start.3 = (bf16[256,1024]{1,0:T(8,128)(2,1)S(1)}, bf16[256,1024]{1,0:T(8,128)(2,1)S(1)}, u32[]{:S(2)}, u32[]{:S(2)}) collective-permute-start(bf16[256,1024]{1,0:T(8,128)(2,1)S(1)} %collective-permute-done.n1), channel_id=1, source_target_pairs={{0,1},{1,0},{2,3},{3,2},{4,5},{5,4},{6,7},{7,6},{8,9},{9,8},{10,11... | collective-permute-start | bytes 1572872 | tf_op jit(solution)/shard_map/ppermute | solution.py:46
  84.1 21.5 %collective-permute-start.4 = (bf16[256,1024]{1,0:T(8,128)(2,1)S(1)}, bf16[256,1024]{1,0:T(8,128)(2,1)S(1)}, u32[]{:S(2)}, u32[]{:S(2)}) collective-permute-start(bf16[256,1024]{1,0:T(8,128)(2,1)S(1)} %collective-permute-done.1.n2), channel_id=1, source_target_pairs={{0,1},{1,0},{2,3},{3,2},{4,5},{5,4},{6,7},{7,6},{8,9},{9,8},{10,11... | collective-permute-start | bytes 1572872 | tf_op jit(solution)/shard_map/ppermute | solution.py:46
  86.1 19.5 %collective-permute-start.5 = (bf16[256,1024]{1,0:T(8,128)(2,1)S(1)}, bf16[256,1024]{1,0:T(8,128)(2,1)S(1)}, u32[]{:S(2)}, u32[]{:S(2)}) collective-permute-start(bf16[256,1024]{1,0:T(8,128)(2,1)S(1)} %collective-permute-done.2.n3), channel_id=1, source_target_pairs={{0,1},{1,0},{2,3},{3,2},{4,5},{5,4},{6,7},{7,6},{8,9},{9,8},{10,11... | collective-permute-start | bytes 1572872 | tf_op jit(solution)/shard_map/ppermute | solution.py:46
  88.5 12.6 %collective-permute-start.12 = (bf16[2,320,128]{2,1,0:T(8,128)(2,1)S(1)}, bf16[2,320,128]{2,1,0:T(8,128)(2,1)S(1)}, u32[]{:S(2)}, u32[]{:S(2)}) collective-permute-start(bf16[2,320,128]{2,1,0:T(8,128)(2,1)S(1)} %slice_bitcast_fusion.1), channel_id=1, source_target_pairs={{0,128},{128,256},{256,384},{384,0},{1,129},{129,257},{257,385},{3... | collective-permute-start | bytes 491528 | tf_op jit(solution)/shard_map/ppermute | solution.py:38
  95.1 19.4 %copy-start.9 = (s32[4,4]{1,0:T(4,128)S(1)}, s32[4,4]{1,0:T(4,128)}, u32[]{:S(2)}) copy-start(s32[4,4]{1,0:T(4,128)} %mask_ref.1) | copy-start | bytes 196
  95.1 37.1 %copy-start.10 = (f32[4]{0:T(128)S(1)}, f32[4]{0:T(128)}, u32[]{:S(2)}) copy-start(f32[4]{0:T(128)} %risk_ref.1) | copy-start | bytes 52
  95.1 10.5 %collective-permute-start.13 = (bf16[2,320,128]{2,1,0:T(8,128)(2,1)S(1)}, bf16[2,320,128]{2,1,0:T(8,128)(2,1)S(1)}, u32[]{:S(2)}, u32[]{:S(2)}) collective-permute-start(bf16[2,320,128]{2,1,0:T(8,128)(2,1)S(1)} %slice_bitcast_fusion), channel_id=1, source_target_pairs={{0,384},{128,0},{256,128},{384,256},{1,385},{129,1},{257,129},{385... | collective-permute-start | bytes 491528 | tf_op jit(solution)/shard_map/ppermute | solution.py:38
  110.2 0.8 copy-start.3
  111.0 9.6 %all-to-all-start = ((bf16[4,320,256]{2,1,0:T(8,128)(2,1)}), bf16[4,320,256]{2,1,0:T(8,128)(2,1)S(1)}, u32[]{:S(2)}, u32[]{:S(2)}) async-start(bf16[4,320,256]{2,1,0:T(8,128)(2,1)} %project.1), calls=%async_computation | async-start | bytes 1310720 | tf_op jit(solution)/shard_map/all_to_all | solution.py:373
  132.2 0.9 copy-start.5
  146.0 2.2 %copy-start.2 = (bf16[256,8192]{1,0:T(8,128)(2,1)S(1)}, bf16[256,8192]{1,0:T(8,128)(2,1)}, u32[]{:S(2)}) copy-start(bf16[256,8192]{1,0:T(8,128)(2,1)} %states_ref.5) | copy-start | bytes 12582916
  148.2 1.0 copy-start.4

commit v5 on v4

--- a/solution.py
+++ b/solution.py
@@ -13,29 +13,25 @@
 TOK = 256
 AXES = ("zh", "zb", "yu", "yb", "yh", "xh", "xb", "c")
 SIZES = (4, 2, 2, 2, 2, 2, 2, 2)
-GROUP = ("zb", "yb")
-OTHERS = ("zh", "yu")
+GROUP = ("yu", "yb")
+OTHERS = ("zh", "zb")
 F32 = jnp.float32
 BF16 = jnp.bfloat16
 VMEM_LIMIT = 16 * 1024 * 1024
-
-
-def params():
-    return pltpu.CompilerParams(vmem_limit_bytes=VMEM_LIMIT)
-
-
-def home_pairs(turn, far):
+VMEM_MOST = 56 * 1024 * 1024
+
+
+def params(limit=VMEM_LIMIT):
+    return pltpu.CompilerParams(vmem_limit_bytes=limit)
+
+
+def home_pairs(turn):
     pairs = []
     for d in range(32):
         for t in range(16):
             half = (d % 2) ^ turn
-            block = (2 * t + half) ^ (2 * far)
-            pairs.append((d * 16 + t, block * 16 + d // 2))
+            pairs.append((d * 16 + t, (2 * t + half) * 16 + d // 2))
     return pairs
-
-
-def along_z(value, step):
-    return lax.ppermute(value, "zh", [(i, (i + step) % 4) for i in range(4)])
 
 
 def swap(value, offset):
@@ -51,9 +47,7 @@
 
 
 def column_of(block, place):
-    return pl.multiple_of(
-        (block // 2) * 2048 + (block % 2) * 512 + (place // 2) * 1024 + (place % 2) * 256, 256
-    )
+    return pl.multiple_of(1024 * block + 256 * place, 256)
 
 
 def in_smem():
@@ -122,7 +116,7 @@
         in_specs=[in_smem(), in_hbm(), anywhere()],
         out_specs=tuple(in_vmem(3)),
         scratch_shapes=[pltpu.SemaphoreType.DMA((12,))],
-        compiler_params=params(),
+        compiler_params=params(VMEM_MOST),
         name="cut_states",
     )(where, states, after)
 
@@ -141,47 +135,41 @@
     return copies
 
 
-def collect_kernel(where_ref, near_one, near_two, far_one, far_two, out):
-    odd, upper = where_ref[1] % 2, where_ref[3]
-    out[upper, odd] = near_one[...]
-    out[upper, 1 - odd] = near_two[...]
-    out[1 - upper, odd] = far_one[...]
-    out[1 - upper, 1 - odd] = far_two[...]
-
-
-def collect(where, pieces):
+def collect_kernel(where_ref, first, second, out):
+    odd = where_ref[1] % 2
+    out[odd] = first[...]
+    out[1 - odd] = second[...]
+
+
+def collect(where, first, second):
     return pl.pallas_call(
         collect_kernel,
-        out_shape=jax.ShapeDtypeStruct((2, 2, 320, 128), BF16),
-        in_specs=[in_smem(), *in_vmem(4)],
+        out_shape=jax.ShapeDtypeStruct((2, 320, 128), BF16),
+        in_specs=[in_smem(), *in_vmem(2)],
         compiler_params=params(),
         name="collect_weights",
-    )(where, *pieces)
+    )(where, first, second)
 
 
 def project_kernel(
-    where_ref, states_ref, n1, n2, n3, f1, f2, f3, w0, w1, w2_low, w2_high, w3, out, own, w_q, w_kv, sems
+    where_ref, states_ref, n1, n2, n3, f1, f2, f3, weights, out, own, w_q, w_kv, sems
 ):
     core = where_ref[0]
     copies = own_columns(where_ref, states_ref, own, sems)
     for copy in copies:
         copy.start()
-    for step in range(4):
-        for upper in range(2):
-            block = 2 * ((where_ref[2] + step) % 4) + upper
-            start = pl.multiple_of(256 * block_of(block, core), 256)
-            rows = pl.ds(start, 256)
-            for head in range(2):
-                if step == 2:
-                    piece = (w2_low, w2_high)[upper].at[head]
-                else:
-                    piece = {0: w0, 1: w1, 3: w3}[step].at[upper, head]
-                w_q[rows, pl.ds(HEAD * head, HEAD)] = piece[:256, :]
-                for chunk in range(2):
-                    lanes = pl.ds(start + 128 * chunk, 128)
-                    base = 256 + 32 * chunk
-                    w_kv[16 * head : 16 * head + 16, lanes] = piece[base : base + 16, :]
-                    w_kv[32 + 16 * head : 48 + 16 * head, lanes] = piece[base + 16 : base + 32, :]
+    for part in range(8):
+        block = block_of(part, core)
+        for head in range(2):
+            rows, cols = pl.ds(256 * part, 256), pl.ds(HEAD * head, HEAD)
+            w_q[rows, cols] = weights[block, head, :256, :]
+            for chunk in range(2):
+                lanes = pl.ds(256 * part + 128 * chunk, 128)
+                base = 256 + 32 * chunk
+                w_kv[16 * head : 16 * head + 16, lanes] = weights[block, head, base : base + 16, :]
+                w_kv[32 + 16 * head : 48 + 16 * head, lanes] = weights[
+                    block, head, base + 16 : base + 32, :
+                ]
 
     def product(x, rows):
         q = jnp.dot(x, w_q[rows, :], preferred_element_type=F32)
@@ -213,16 +201,16 @@
     return pl.pallas_call(
         project_kernel,
         out_shape=jax.ShapeDtypeStruct((4, 320, 256), BF16),
-        in_specs=[in_smem(), in_hbm(), *in_vmem(11)],
+        in_specs=[in_smem(), in_hbm(), *in_vmem(7)],
         scratch_shapes=[
             pltpu.VMEM((TOK, 2048), BF16),
             pltpu.VMEM((2048, 256), BF16),
             pltpu.VMEM((64, 2048), BF16),
             pltpu.SemaphoreType.DMA((8,)),
         ],
-        compiler_params=params(),
+        compiler_params=params(VMEM_MOST),
         name="project",
-    )(where, states, *near, *far, *weights)
+    )(where, states, *near, *far, weights)
 
 
 def attend_kernel(
@@ -326,7 +314,7 @@
         out_shape=jax.ShapeDtypeStruct((8, 256, 256), BF16),
         in_specs=[in_smem(), in_hbm(), *in_vmem(7)],
         scratch_shapes=[pltpu.VMEM((TOK, 2048), BF16), pltpu.SemaphoreType.DMA((8,))],
-        compiler_params=params(),
+        compiler_params=params(VMEM_MOST),
         name="gradient",
     )(where, states, *near, *far, slopes)
 
@@ -348,28 +336,20 @@
 
 
 def shards(states, query_weight, key_matrix, value_matrix, block_mask, risk_weight, upstream):
-    place = 2 * lax.axis_index("zb") + lax.axis_index("yb")
-    where = jnp.stack([lax.axis_index("c"), place, lax.axis_index("zh"), lax.axis_index("yu")])
-    where = where.astype(jnp.int32)
-
-    halves = pack(where, query_weight, key_matrix.T, value_matrix.T)
-    pieces = [
-        lax.ppermute(halves[turn], AXES, home_pairs(turn, far))
-        for far in range(2)
-        for turn in range(2)
-    ]
-
-    outgoing = cut(where, states, halves[0])
+    place = lax.axis_index(GROUP)
+    where = jnp.stack([lax.axis_index("c"), place]).astype(jnp.int32)
+
+    first, second = pack(where, query_weight, key_matrix.T, value_matrix.T)
+    first = lax.ppermute(first, AXES, home_pairs(0))
+    second = lax.ppermute(second, AXES, home_pairs(1))
+    piece = collect(where, first, second)
+    weights = lax.all_gather(piece, OTHERS, axis=0, tiled=False)
+
+    outgoing = cut(where, states, piece)
     near = [swap(outgoing[j - 1], j) for j in (1, 2, 3)]
     far = [swap_core(x) for x in near]
 
-    w0 = collect(where, pieces)
-    w3 = along_z(w0, 1)
-    w1 = along_z(w0, -1)
-    w2_low = along_z(w3[0], 1)
-    w2_high = along_z(w1[1], -1)
-
-    parts = project(where, states, near, far, (w0, w1, w2_low, w2_high, w3))
+    parts = project(where, states, near, far, weights)
     parts = lax.all_to_all(parts, GROUP, split_axis=0, concat_axis=0)
     kv = jnp.sum(parts[:, 256:].astype(F32), axis=0)
     kv = lax.all_gather(kv, ("xb", "c"), axis=0, tiled=False)

time: 190 us -> 204 us (1.074)
  the two profiles are of different devices: /device:TPU:1 before, /device:TPU:6 now
where the time goes in v5:
time: 204 us; the launch traced here: 202 us
  blocking collectives  64.6 us (32%)
  waiting for transfers between devices  57.3 us (28%)
  starting transfers between devices  41 us (20%)
  Pallas kernels  21.5 us (11%)
  between operations  14.3 us (7%)
  local copies, waits for them, and re-layouts  2.47 us (1%)
    all_to_all x1, blocking collectives, shards(): terms = lax.all_to_all(terms, OTHERS, split_axis=0, concat_axis=0)  40.5 us
    ppermute x3, waiting for transfers between devices, swap(): return lax.ppermute(value, GROUP, [(i, i ^ offset) for i in range(4)])  30.9 us
    all_to_all x1, blocking collectives, shards(): slopes = lax.all_to_all(dq, GROUP, split_axis=0, concat_axis=0)  18.4 us
    all_to_all x1, waiting for transfers between devices, shards(): parts = lax.all_to_all(parts, GROUP, split_axis=0, concat_axis=0)  16.6 us
    ppermute x3, starting transfers between devices, swap(): return lax.ppermute(value, GROUP, [(i, i ^ offset) for i in range(4)])  12.3 us
    all_to_all x1, starting transfers between devices, shards(): parts = lax.all_to_all(parts, GROUP, split_axis=0, concat_axis=0)  10.8 us
    ppermute x1, waiting for transfers between devices, shards(): second = lax.ppermute(second, AXES, home_pairs(1))  8.17 us
    ppermute x1, starting transfers between devices, shards(): first = lax.ppermute(first, AXES, home_pairs(0))  7.81 us
  transfers between devices with their start and end apart: 10, of which 5 were waited for; matrix products, arithmetic and copies ran while one was open for 0% of the time, Pallas kernels for 2%

profile of v5, /device:TPU:6, one launch (start us, length us, event | category | flops | bytes accessed | tf_op | source)
XLA Modules:
  0.0 202.2 jit_solution(10379369465055249253)
XLA Ops:
  7.2 0.0 all-gather.4.cloned.1.call-start
  7.2 0.1 pad_add_fusion.where_ref
  7.3 0.9 copy-done.1
  8.2 0.7 copy-done.2
  8.9 0.7 copy-done.3
  9.6 0.6 pack_weights.1
  10.2 7.8 %collective-permute-start = (bf16[320,128]{1,0:T(8,128)(2,1)S(1)}, bf16[320,128]{1,0:T(8,128)(2,1)S(1)}, u32[]{:S(2)}, u32[]{:S(2)}) collective-permute-start(bf16[320,128]{1,0:T(8,128)(2,1)S(1)} %get-tuple-element.9), channel_id=1, source_target_pairs={{0,0},{1,32},{2,64},{3,96},{4,128},{5,160},{6,192},{7,224},{8,256}... | collective-permute-start | bytes 245768 | tf_op jit(solution)/shard_map/ppermute | solution.py:343
  18.0 3.0 %collective-permute-start.1 = (bf16[320,128]{1,0:T(8,128)(2,1)S(1)}, bf16[320,128]{1,0:T(8,128)(2,1)S(1)}, u32[]{:S(2)}, u32[]{:S(2)}) collective-permute-start(bf16[320,128]{1,0:T(8,128)(2,1)S(1)} %get-tuple-element.10), channel_id=1, source_target_pairs={{0,16},{1,48},{2,80},{3,112},{4,144},{5,176},{6,208},{7,240},{8,27... | collective-permute-start | bytes 245768 | tf_op jit(solution)/shard_map/ppermute | solution.py:344
  21.0 0.0 collective-permute-done.first
  21.0 8.2 %collective-permute-done.1.second = bf16[320,128]{1,0:T(8,128)(2,1)S(1)} collective-permute-done((bf16[320,128]{1,0:T(8,128)(2,1)S(1)}, bf16[320,128]{1,0:T(8,128)(2,1)S(1)}, u32[]{:S(2)}, u32[]{:S(2)}) %collective-permute-start.1) | collective-permute-done | bytes 81952 | tf_op jit(solution)/shard_map/ppermute | solution.py:344
  29.2 1.2 collect_weights.1.after
  30.4 0.0 all-gather.4.cloned.1.call-update
  30.4 0.0 copy-done.4
  30.4 3.4 %cut_states.1 = (bf16[256,1024]{1,0:T(8,128)(2,1)}, bf16[256,1024]{1,0:T(8,128)(2,1)}, bf16[256,1024]{1,0:T(8,128)(2,1)}) custom-call(s32[2]{0:T(128)} %copy-done.4, bf16[256,8192]{1,0:T(8,128)(2,1)} %states_ref.5, bf16[2,320,128]{2,1,0:T(8,128)(2,1)} %collect_weights.1.after), custom_call_target="tpu_custom_call" | custom-call | tf_op jit(solution)/shard_map/cut_states/pallas_call | solution.py:113
  33.8 5.7 %collective-permute-start.2 = (bf16[256,1024]{1,0:T(8,128)(2,1)}, bf16[256,1024]{1,0:T(8,128)(2,1)S(1)}, u32[]{:S(2)}, u32[]{:S(2)}) collective-permute-start(bf16[256,1024]{1,0:T(8,128)(2,1)} %get-tuple-element.11), channel_id=1, source_target_pairs={{0,16},{16,0},{32,48},{48,32},{1,17},{17,1},{33,49},{49,33},{2,18}... | collective-permute-start | bytes 1572872 | tf_op jit(solution)/shard_map/ppermute | solution.py:38
  39.5 4.6 %collective-permute-start.3 = (bf16[256,1024]{1,0:T(8,128)(2,1)}, bf16[256,1024]{1,0:T(8,128)(2,1)S(1)}, u32[]{:S(2)}, u32[]{:S(2)}) collective-permute-start(bf16[256,1024]{1,0:T(8,128)(2,1)} %get-tuple-element.12), channel_id=1, source_target_pairs={{0,32},{16,48},{32,0},{48,16},{1,33},{17,49},{33,1},{49,17},{2,34}... | collective-permute-start | bytes 1572872 | tf_op jit(solution)/shard_map/ppermute | solution.py:38
  44.2 1.9 collective-permute-start.4
  46.1 10.8 %collective-permute-done.2.n1 = bf16[256,1024]{1,0:T(8,128)(2,1)S(1)} collective-permute-done((bf16[256,1024]{1,0:T(8,128)(2,1)}, bf16[256,1024]{1,0:T(8,128)(2,1)S(1)}, u32[]{:S(2)}, u32[]{:S(2)}) %collective-permute-start.2) | collective-permute-done | bytes 524320 | tf_op jit(solution)/shard_map/ppermute | solution.py:38
  56.9 2.8 %collective-permute-start.5 = (bf16[256,1024]{1,0:T(8,128)(2,1)S(1)}, bf16[256,1024]{1,0:T(8,128)(2,1)S(1)}, u32[]{:S(2)}, u32[]{:S(2)}) collective-permute-start(bf16[256,1024]{1,0:T(8,128)(2,1)S(1)} %collective-permute-done.2.n1), channel_id=1, source_target_pairs={{0,1},{1,0},{2,3},{3,2},{4,5},{5,4},{6,7},{7,6},{8,9},{9,8},{10,11... | collective-permute-start | bytes 1572872 | tf_op jit(solution)/shard_map/ppermute | solution.py:42
  59.8 20.1 %collective-permute-done.3.n2 = bf16[256,1024]{1,0:T(8,128)(2,1)S(1)} collective-permute-done((bf16[256,1024]{1,0:T(8,128)(2,1)}, bf16[256,1024]{1,0:T(8,128)(2,1)S(1)}, u32[]{:S(2)}, u32[]{:S(2)}) %collective-permute-start.3) | collective-permute-done | bytes 524320 | tf_op jit(solution)/shard_map/ppermute | solution.py:38
  79.9 1.9 collective-permute-start.6
  81.8 0.0 collective-permute-done.4.n3
  81.8 0.0 copy-start.9
  81.8 2.4 %collective-permute-start.7 = (bf16[256,1024]{1,0:T(8,128)(2,1)S(1)}, bf16[256,1024]{1,0:T(8,128)(2,1)}, u32[]{:S(2)}, u32[]{:S(2)}) collective-permute-start(bf16[256,1024]{1,0:T(8,128)(2,1)S(1)} %collective-permute-done.4.n3), channel_id=1, source_target_pairs={{0,1},{1,0},{2,3},{3,2},{4,5},{5,4},{6,7},{7,6},{8,9},{9,8},{10,11... | collective-permute-start | bytes 1572872 | tf_op jit(solution)/shard_map/ppermute | solution.py:42
  84.2 0.0 collective-permute-done.5.f1
  84.2 0.0 copy-start.10
  84.2 0.0 collective-permute-done.6.f2
  84.2 0.0 copy-start.11
  84.2 1.6 collective-permute-done.7.f3
  85.9 0.0 copy-done.7
  85.9 0.0 copy-done.8
  85.9 0.0 copy-start.5
  85.9 0.0 copy-start
  85.9 0.0 copy-start.6
  85.9 6.9 %project.1 = bf16[4,320,256]{2,1,0:T(8,128)(2,1)} custom-call(s32[2]{0:T(128)} %copy-done.4, bf16[256,8192]{1,0:T(8,128)(2,1)} %states_ref.5, bf16[256,1024]{1,0:T(8,128)(2,1)} %copy-done.7, bf16[256,1024]{1,0:T(8,128)(2,1)} %copy-done.8, bf16[256,1024]{1,0:T(8,128)(2,1)} %copy-done.9, bf16[256,1024]{1,0:T(8,128)(2,1)} %copy-done.10, ...), custom_call_target="tpu_custom_call" | custom-call | tf_op jit(solution)/shard_map/project/pallas_call | solution.py:201
  92.9 10.8 %all-to-all-start = ((bf16[4,320,256]{2,1,0:T(8,128)(2,1)}), bf16[4,320,256]{2,1,0:T(8,128)(2,1)S(1)}, u32[]{:S(2)}, u32[]{:S(2)}) async-start(bf16[4,320,256]{2,1,0:T(8,128)(2,1)} %project.1), calls=%async_computation | async-start | bytes 1310720 | tf_op jit(solution)/shard_map/all_to_all | solution.py:353
  103.7 0.1 reduce_sum.19
  103.8 0.1 add_convert_fusion
  103.9 0.1 convert_element_type.15
  104.0 0.5 multiply_cosine_fusion
  104.5 0.2 pad_maximum_fusion.tables_ref
  104.7 16.6 %all-to-all-done.parts = bf16[4,320,256]{2,1,0:T(8,128)(2,1)S(1)} async-done(((bf16[4,320,256]{2,1,0:T(8,128)(2,1)}), bf16[4,320,256]{2,1,0:T(8,128)(2,1)S(1)}, u32[]{:S(2)}, u32[]{:S(2)}) %all-to-all-start) | async-done | bytes 655392 | tf_op jit(solution)/shard_map/all_to_all | solution.py:353
  121.3 5.8 %all-gather.1 = f32[256,256]{1,0:T(8,128)S(1)} all-gather(f32[64,256]{1,0:T(8,128)S(1)} %convert_reduce_fusion), channel_id=3, replica_groups=mesh['zh'=4,'zb'=2,'yu'=2,'yb'=2,'yh'=2,'xh'=2,'xb'=2,'c'=2] {'xb','c'}, dimensions={0}, use_global_device_ids=true | all-gather | bytes 327680 | tf_op jit(solution)/shard_map/all_gather | solution.py:355
  127.1 2.5 %attend.1 = (bf16[256,256]{1,0:T(8,128)(2,1)}, bf16[4,256,256]{2,1,0:T(8,128)(2,1)S(1)}) custom-call(s32[4,4]{1,0:T(4,128)S(1)} %copy-done.5, f32[4]{0:T(128)S(1)} %copy-done.6, bf16[4,320,256]{2,1,0:T(8,128)(2,1)S(1)} %all-to-all-done.parts, f32[4,64,256]{2,1,0:T(8,128)S(1)} %bitcast.6, bf16[256,256]{1,0:T(8,128)(2,1)S(1)} %copy-done, ...), custom_call_target="tpu_custom_call" | custom-call | tf_op jit(solution)/shard_map/attend/pallas_call | solution.py:275
  129.6 18.4 %all_to_all.15.slopes = bf16[4,256,256]{2,1,0:T(8,128)(2,1)} all-to-all(bf16[4,256,256]{2,1,0:T(8,128)(2,1)S(1)} %get-tuple-element.15), channel_id=1, replica_groups=mesh['zh'=4,'zb'=2,'yu'=2,'yb'=2,'yh'=2,'xh'=2,'xb'=2,'c'=2] {'yu','yb'}, dimensions={0} | all-to-all | bytes 1048576 | tf_op jit(solution)/shard_map/all_to_all | solution.py:367
  148.0 6.0 %gradient.1 = bf16[8,256,256]{2,1,0:T(8,128)(2,1)} custom-call(s32[2]{0:T(128)} %copy-done.4, bf16[256,8192]{1,0:T(8,128)(2,1)} %states_ref.5, bf16[256,1024]{1,0:T(8,128)(2,1)} %copy-done.7, bf16[256,1024]{1,0:T(8,128)(2,1)} %copy-done.8, bf16[256,1024]{1,0:T(8,128)(2,1)} %copy-done.9, bf16[256,1024]{1,0:T(8,128)(2,1)} %copy-done.10, ...), custom_call_target="tpu_custom_call" | custom-call | tf_op jit(solution)/shard_map/gradient/pallas_call | solution.py:312
  154.0 40.5 %all_to_all.16.terms = bf16[8,256,256]{2,1,0:T(8,128)(2,1)S(1)} all-to-all(bf16[8,256,256]{2,1,0:T(8,128)(2,1)} %gradient.1), channel_id=1, replica_groups=mesh['zh'=4,'zb'=2,'yu'=2,'yb'=2,'yh'=2,'xh'=2,'xb'=2,'c'=2] {'zh','zb'}, dimensions={0} | all-to-all | bytes 2097152 | tf_op jit(solution)/shard_map/all_to_all | solution.py:369
  194.5 0.9 add_up.1
  (16 shorter events, 0.1 us)
Async XLA Ops:
  7.2 78.7 %all-gather.4.cloned.1.call-start = ((), (), s32[]{:S(2)}) async-start(), calls=%async_computation.3 | async-start | bytes 1474560 | tf_op jit(solution)/shard_map/all_gather | solution.py:346
  7.3 23.1 %copy-start.4 = (s32[2]{0:T(128)}, s32[2]{0:T(128)S(1)}, u32[]{:S(2)}) copy-start(s32[2]{0:T(128)S(1)} %pad_add_fusion.where_ref) | copy-start | bytes 28
  7.3 0.9 copy-start.1
  8.2 0.7 copy-start.2
  8.9 0.7 copy-start.3
  10.2 10.8 %collective-permute-start = (bf16[320,128]{1,0:T(8,128)(2,1)S(1)}, bf16[320,128]{1,0:T(8,128)(2,1)S(1)}, u32[]{:S(2)}, u32[]{:S(2)}) collective-permute-start(bf16[320,128]{1,0:T(8,128)(2,1)S(1)} %get-tuple-element.9), channel_id=1, source_target_pairs={{0,0},{1,32},{2,64},{3,96},{4,128},{5,160},{6,192},{7,224},{8,256}... | collective-permute-start | bytes 245768 | tf_op jit(solution)/shard_map/ppermute | solution.py:343
  18.0 11.1 %collective-permute-start.1 = (bf16[320,128]{1,0:T(8,128)(2,1)S(1)}, bf16[320,128]{1,0:T(8,128)(2,1)S(1)}, u32[]{:S(2)}, u32[]{:S(2)}) collective-permute-start(bf16[320,128]{1,0:T(8,128)(2,1)S(1)} %get-tuple-element.10), channel_id=1, source_target_pairs={{0,16},{1,48},{2,80},{3,112},{4,144},{5,176},{6,208},{7,240},{8,27... | collective-permute-start | bytes 245768 | tf_op jit(solution)/shard_map/ppermute | solution.py:344
  33.8 23.1 %collective-permute-start.2 = (bf16[256,1024]{1,0:T(8,128)(2,1)}, bf16[256,1024]{1,0:T(8,128)(2,1)S(1)}, u32[]{:S(2)}, u32[]{:S(2)}) collective-permute-start(bf16[256,1024]{1,0:T(8,128)(2,1)} %get-tuple-element.11), channel_id=1, source_target_pairs={{0,16},{16,0},{32,48},{48,32},{1,17},{17,1},{33,49},{49,33},{2,18}... | collective-permute-start | bytes 1572872 | tf_op jit(solution)/shard_map/ppermute | solution.py:38
  39.5 40.3 %collective-permute-start.3 = (bf16[256,1024]{1,0:T(8,128)(2,1)}, bf16[256,1024]{1,0:T(8,128)(2,1)S(1)}, u32[]{:S(2)}, u32[]{:S(2)}) collective-permute-start(bf16[256,1024]{1,0:T(8,128)(2,1)} %get-tuple-element.12), channel_id=1, source_target_pairs={{0,32},{16,48},{32,0},{48,16},{1,33},{17,49},{33,1},{49,17},{2,34}... | collective-permute-start | bytes 1572872 | tf_op jit(solution)/shard_map/ppermute | solution.py:38
  44.2 37.6 %collective-permute-start.4 = (bf16[256,1024]{1,0:T(8,128)(2,1)}, bf16[256,1024]{1,0:T(8,128)(2,1)S(1)}, u32[]{:S(2)}, u32[]{:S(2)}) collective-permute-start(bf16[256,1024]{1,0:T(8,128)(2,1)} %get-tuple-element.13), channel_id=1, source_target_pairs={{0,48},{16,32},{32,16},{48,0},{1,49},{17,33},{33,17},{49,1},{2,50}... | collective-permute-start | bytes 1572872 | tf_op jit(solution)/shard_map/ppermute | solution.py:38
  56.9 28.9 %copy-start.7 = (bf16[256,1024]{1,0:T(8,128)(2,1)}, bf16[256,1024]{1,0:T(8,128)(2,1)S(1)}, u32[]{:S(2)}) copy-start(bf16[256,1024]{1,0:T(8,128)(2,1)S(1)} %collective-permute-done.2.n1) | copy-start | bytes 1572868
  56.9 27.3 %collective-permute-start.5 = (bf16[256,1024]{1,0:T(8,128)(2,1)S(1)}, bf16[256,1024]{1,0:T(8,128)(2,1)S(1)}, u32[]{:S(2)}, u32[]{:S(2)}) collective-permute-start(bf16[256,1024]{1,0:T(8,128)(2,1)S(1)} %collective-permute-done.2.n1), channel_id=1, source_target_pairs={{0,1},{1,0},{2,3},{3,2},{4,5},{5,4},{6,7},{7,6},{8,9},{9,8},{10,11... | collective-permute-start | bytes 1572872 | tf_op jit(solution)/shard_map/ppermute | solution.py:42
  79.9 6.0 %copy-start.8 = (bf16[256,1024]{1,0:T(8,128)(2,1)}, bf16[256,1024]{1,0:T(8,128)(2,1)S(1)}, u32[]{:S(2)}) copy-start(bf16[256,1024]{1,0:T(8,128)(2,1)S(1)} %collective-permute-done.3.n2) | copy-start | bytes 1572868
  79.9 4.4 %collective-permute-start.6 = (bf16[256,1024]{1,0:T(8,128)(2,1)S(1)}, bf16[256,1024]{1,0:T(8,128)(2,1)S(1)}, u32[]{:S(2)}, u32[]{:S(2)}) collective-permute-start(bf16[256,1024]{1,0:T(8,128)(2,1)S(1)} %collective-permute-done.3.n2), channel_id=1, source_target_pairs={{0,1},{1,0},{2,3},{3,2},{4,5},{5,4},{6,7},{7,6},{8,9},{9,8},{10,11... | collective-permute-start | bytes 1572872 | tf_op jit(solution)/shard_map/ppermute | solution.py:42
  81.8 4.1 %copy-start.9 = (bf16[256,1024]{1,0:T(8,128)(2,1)}, bf16[256,1024]{1,0:T(8,128)(2,1)S(1)}, u32[]{:S(2)}) copy-start(bf16[256,1024]{1,0:T(8,128)(2,1)S(1)} %collective-permute-done.4.n3) | copy-start | bytes 1572868
  81.8 4.1 %collective-permute-start.7 = (bf16[256,1024]{1,0:T(8,128)(2,1)S(1)}, bf16[256,1024]{1,0:T(8,128)(2,1)}, u32[]{:S(2)}, u32[]{:S(2)}) collective-permute-start(bf16[256,1024]{1,0:T(8,128)(2,1)S(1)} %collective-permute-done.4.n3), channel_id=1, source_target_pairs={{0,1},{1,0},{2,3},{3,2},{4,5},{5,4},{6,7},{7,6},{8,9},{9,8},{10,11... | collective-permute-start | bytes 1572872 | tf_op jit(solution)/shard_map/ppermute | solution.py:42
  84.2 1.7 copy-start.10
  84.2 1.6 copy-start.11
  85.9 17.8 %copy-start.5 = (s32[4,4]{1,0:T(4,128)S(1)}, s32[4,4]{1,0:T(4,128)}, u32[]{:S(2)}) copy-start(s32[4,4]{1,0:T(4,128)} %mask_ref.1) | copy-start | bytes 196
  85.9 41.2 %copy-start = (bf16[256,256]{1,0:T(8,128)(2,1)S(1)}, bf16[256,256]{1,0:T(8,128)(2,1)}, u32[]{:S(2)}) copy-start(bf16[256,256]{1,0:T(8,128)(2,1)} %upstream_ref.1) | copy-start | bytes 393220
  85.9 41.2 %copy-start.6 = (f32[4]{0:T(128)S(1)}, f32[4]{0:T(128)}, u32[]{:S(2)}) copy-start(f32[4]{0:T(128)} %risk_ref.1) | copy-start | bytes 52
  92.9 28.4 %all-to-all-start = ((bf16[4,320,256]{2,1,0:T(8,128)(2,1)}), bf16[4,320,256]{2,1,0:T(8,128)(2,1)S(1)}, u32[]{:S(2)}, u32[]{:S(2)}) async-start(bf16[4,320,256]{2,1,0:T(8,128)(2,1)} %project.1), calls=%async_computation | async-start | bytes 1310720 | tf_op jit(solution)/shard_map/all_to_all | solution.py:353
Sparse Core Ops, SparseCore 0:
  30.5 50.2 all-gather.3

commit v6 on v5

--- a/solution.py
+++ b/solution.py
@@ -18,11 +18,10 @@
 F32 = jnp.float32
 BF16 = jnp.bfloat16
 VMEM_LIMIT = 16 * 1024 * 1024
-VMEM_MOST = 56 * 1024 * 1024
-
-
-def params(limit=VMEM_LIMIT):
-    return pltpu.CompilerParams(vmem_limit_bytes=limit)
+
+
+def params():
+    return pltpu.CompilerParams(vmem_limit_bytes=VMEM_LIMIT)
 
 
 def home_pairs(turn):
@@ -34,8 +33,19 @@
     return pairs
 
 
-def swap(value, offset):
-    return lax.ppermute(value, GROUP, [(i, i ^ offset) for i in range(4)])
+def ring_pairs(first, second):
+    pairs = []
+    for z in range(8):
+        for y in range(8):
+            for x in range(4):
+                for c in range(2):
+                    to = (y + (second if c else first)) % 8
+
+                    def index(y):
+                        return (4 * z + y % 4) * 16 + (y // 4) * 8 + 2 * x + c
+
+                    pairs.append((index(y), index(to)))
+    return pairs
 
 
 def swap_core(value):
@@ -89,12 +99,12 @@
     )(where, query, key_t, value_t)
 
 
-def cut_kernel(where_ref, states_ref, after, one_ref, two_ref, three_ref, sems):
+def cut_kernel(where_ref, states_ref, after, up_ref, two_ref, down_ref, sems):
     core, place = where_ref[0], where_ref[1]
     copies = []
-    for number, out in enumerate((one_ref, two_ref, three_ref)):
+    for number, out in enumerate((up_ref, two_ref, down_ref)):
         for part in range(4):
-            start = column_of(block_of(part, core), place ^ (number + 1))
+            start = column_of(block_of(part, core), (place + number + 1) % 4)
             copies.append(
                 pltpu.make_async_copy(
                     states_ref.at[:, pl.ds(start, 256)],
@@ -116,7 +126,7 @@
         in_specs=[in_smem(), in_hbm(), anywhere()],
         out_specs=tuple(in_vmem(3)),
         scratch_shapes=[pltpu.SemaphoreType.DMA((12,))],
-        compiler_params=params(VMEM_MOST),
+        compiler_params=params(),
         name="cut_states",
     )(where, states, after)
 
@@ -135,19 +145,20 @@
     return copies
 
 
-def collect_kernel(where_ref, first, second, out):
+def copies_kernel(where_ref, first, second, out):
     odd = where_ref[1] % 2
-    out[odd] = first[...]
-    out[1 - odd] = second[...]
-
-
-def collect(where, first, second):
-    return pl.pallas_call(
-        collect_kernel,
-        out_shape=jax.ShapeDtypeStruct((2, 320, 128), BF16),
+    for device in range(8):
+        out[device, odd] = first[...]
+        out[device, 1 - odd] = second[...]
+
+
+def copies(where, first, second):
+    return pl.pallas_call(
+        copies_kernel,
+        out_shape=jax.ShapeDtypeStruct((8, 2, 320, 128), BF16),
         in_specs=[in_smem(), *in_vmem(2)],
         compiler_params=params(),
-        name="collect_weights",
+        name="weight_copies",
     )(where, first, second)
 
 
@@ -190,7 +201,7 @@
             for copy in copies:
                 copy.wait()
         near, far = near_ref[...], far_ref[...]
-        other = where_ref[1] ^ ((number + 1) % 4)
+        other = (where_ref[1] + number + 1) % 4
         q_near, kv_near = product(near, low)
         q_far, kv_far = product(far, high)
         out[other, :256, :] = (q_near + q_far).astype(BF16)
@@ -200,15 +211,17 @@
 def project(where, states, near, far, weights):
     return pl.pallas_call(
         project_kernel,
-        out_shape=jax.ShapeDtypeStruct((4, 320, 256), BF16),
+        out_shape=(
+            jax.ShapeDtypeStruct((4, 320, 256), BF16),
+            jax.ShapeDtypeStruct((TOK, 2048), BF16),
+        ),
         in_specs=[in_smem(), in_hbm(), *in_vmem(7)],
         scratch_shapes=[
-            pltpu.VMEM((TOK, 2048), BF16),
             pltpu.VMEM((2048, 256), BF16),
             pltpu.VMEM((64, 2048), BF16),
             pltpu.SemaphoreType.DMA((8,)),
         ],
-        compiler_params=params(VMEM_MOST),
+        compiler_params=params(),
         name="project",
     )(where, states, *near, *far, weights)
 
@@ -289,34 +302,29 @@
     )(block_mask, risk_weight, parts, kv, upstream, tables)
 
 
-def gradient_kernel(where_ref, states_ref, n1, n2, n3, f1, f2, f3, slopes, out, own, sems):
+def gradient_kernel(where_ref, own, n1, n2, n3, f1, f2, f3, slopes, out):
     core = where_ref[0]
-    copies = own_columns(where_ref, states_ref, own, sems)
-    for copy in copies:
-        copy.start()
     for part in range(8):
         cols = pl.ds(256 * (part % 4), 256)
         total = None
-        for number in (1, 2, 3, 0):
+        for number in range(4):
             if number == 0:
-                copies[part].wait()
                 x = own[:, pl.ds(256 * part, 256)]
             else:
                 x = ((n1, n2, n3) if part < 4 else (f1, f2, f3))[number - 1][:, cols]
-            term = jnp.dot(slopes[where_ref[1] ^ number], x, preferred_element_type=F32)
+            term = jnp.dot(slopes[(where_ref[1] + number) % 4], x, preferred_element_type=F32)
             total = term if total is None else total + term
         out[block_of(part, core)] = total.astype(BF16)
 
 
-def gradient(where, states, near, far, slopes):
+def gradient(where, own, near, far, slopes):
     return pl.pallas_call(
         gradient_kernel,
         out_shape=jax.ShapeDtypeStruct((8, 256, 256), BF16),
-        in_specs=[in_smem(), in_hbm(), *in_vmem(7)],
-        scratch_shapes=[pltpu.VMEM((TOK, 2048), BF16), pltpu.SemaphoreType.DMA((8,))],
-        compiler_params=params(VMEM_MOST),
+        in_specs=[in_smem(), *in_vmem(8)],
+        compiler_params=params(),
         name="gradient",
-    )(where, states, *near, *far, slopes)
+    )(where, own, *near, *far, slopes)
 
 
 def total_kernel(terms, out):
@@ -342,14 +350,18 @@
     first, second = pack(where, query_weight, key_matrix.T, value_matrix.T)
     first = lax.ppermute(first, AXES, home_pairs(0))
     second = lax.ppermute(second, AXES, home_pairs(1))
-    piece = collect(where, first, second)
-    weights = lax.all_gather(piece, OTHERS, axis=0, tiled=False)
-
-    outgoing = cut(where, states, piece)
-    near = [swap(outgoing[j - 1], j) for j in (1, 2, 3)]
+    weights = copies(where, first, second)
+
+    up, two, down = cut(where, states, weights)
+    near = (
+        lax.ppermute(down, AXES, ring_pairs(-1, -1)),
+        lax.ppermute(two, AXES, ring_pairs(2, -2)),
+        lax.ppermute(up, AXES, ring_pairs(1, 1)),
+    )
     far = [swap_core(x) for x in near]
-
-    parts = project(where, states, near, far, weights)
+    weights = lax.all_to_all(weights, OTHERS, split_axis=0, concat_axis=0)
+
+    parts, own = project(where, states, near, far, weights)
     parts = lax.all_to_all(parts, GROUP, split_axis=0, concat_axis=0)
     kv = jnp.sum(parts[:, 256:].astype(F32), axis=0)
     kv = lax.all_gather(kv, ("xb", "c"), axis=0, tiled=False)
@@ -365,7 +377,7 @@
 
     attn_out, dq = attend(block_mask, risk_weight, parts, kv, upstream, tables)
     slopes = lax.all_to_all(dq, GROUP, split_axis=0, concat_axis=0)
-    terms = gradient(where, states, near, far, slopes)
+    terms = gradient(where, own, near, far, slopes)
     terms = lax.all_to_all(terms, OTHERS, split_axis=0, concat_axis=0)
     return attn_out, add_up(terms)
 

time: 204 us -> 178 us (0.87)
  waiting for transfers between devices: 57.3 us -> 43.3 us
  between operations: 14.3 us -> 0.85 us
  local copies, waits for them, and re-layouts: 2.47 us -> 13.3 us
  Pallas kernels: 21.5 us -> 12 us
  blocking collectives: 64.6 us -> 58.9 us
  starting transfers between devices: 41 us -> 46.5 us
    all_to_all x0 -> x1, starting transfers between devices: none -> 15.4 us  [shards(): weights = lax.all_to_all(weights, OTHERS, split_axis=0, concat_axis=0)]
    ppermute x3, waiting for transfers between devices: 30.9 us -> 17.9 us  [the longest x1 8.98 us: shards(): lax.ppermute(down, AXES, ring_pairs(-1, -1))]
    unnamed x24 -> x36, local copies, waits for them, and re-layouts: 2.38 us -> 13.2 us
    all_to_all x1, starting transfers between devices: 10.8 us -> 3.61 us  [shards(): parts = lax.all_to_all(parts, GROUP, split_axis=0, concat_axis=0)]
    all_to_all x1, blocking collectives: 40.5 us -> 35.3 us  [shards(): terms = lax.all_to_all(terms, OTHERS, split_axis=0, concat_axis=0)]
    pallas_call x1, Pallas kernels: 5.98 us -> 1.79 us  [gradient(): pl.pallas_call(gradient_kernel, out_shape=jax.ShapeDtypeStruct((8, 256, 2...]
    pallas_call x2, Pallas kernels: 8.15 us -> 5.29 us  [the longest x1 3.46 us: project(): pl.pallas_call(project_kernel, out_shape=(jax.ShapeDtypeStruct((4, 320, 2...]
    ppermute x3, starting transfers between devices: 12.3 us -> 9.59 us  [the longest x1 5.7 us: shards(): lax.ppermute(two, AXES, ring_pairs(2, -2))]
  transfers between devices with their start and end apart: 10 -> 10, of which waited for: 5 -> 6; matrix products, arithmetic and copies ran while one was open for 0% -> 1% of each run, Pallas kernels for 2% -> 1%
where the time goes in v6:
time: 178 us; the launch traced here: 176 us
  blocking collectives  58.9 us (33%)
  starting transfers between devices  46.5 us (26%)
  waiting for transfers between devices  43.3 us (24%)
  local copies, waits for them, and re-layouts  13.3 us (7%)
  Pallas kernels  12 us (7%)
    all_to_all x1, blocking collectives, shards(): terms = lax.all_to_all(terms, OTHERS, split_axis=0, concat_axis=0)  35.3 us
    all_to_all x1, blocking collectives, shards(): slopes = lax.all_to_all(dq, GROUP, split_axis=0, concat_axis=0)  17.7 us
    all_to_all x1, waiting for transfers between devices, shards(): parts = lax.all_to_all(parts, GROUP, split_axis=0, concat_axis=0)  16.1 us
    all_to_all x1, starting transfers between devices, shards(): weights = lax.all_to_all(weights, OTHERS, split_axis=0, concat_axis=0)  15.4 us
    unnamed x36, local copies, waits for them, and re-layouts  13.2 us
    ppermute x1, waiting for transfers between devices, shards(): lax.ppermute(down, AXES, ring_pairs(-1, -1))  8.98 us
    ppermute x1, waiting for transfers between devices, shards(): second = lax.ppermute(second, AXES, home_pairs(1))  8.17 us
    ppermute x1, starting transfers between devices, shards(): first = lax.ppermute(first, AXES, home_pairs(0))  7.81 us
  transfers between devices with their start and end apart: 10, of which 6 were waited for; matrix products, arithmetic and copies ran while one was open for 1% of the time, Pallas kernels for 1%

profile of v6, /device:TPU:6, one launch (start us, length us, event | category | flops | bytes accessed | tf_op | source)
XLA Modules:
  0.0 176.5 jit_solution(16217120852795461376)
XLA Ops:
  0.6 0.1 pad_add_fusion.where_ref
  0.7 0.9 copy-done.13
  1.6 0.7 copy-done.14
  2.3 0.7 copy-done.15
  3.1 0.6 pack_weights.1
  3.6 7.8 %collective-permute-start = (bf16[320,128]{1,0:T(8,128)(2,1)S(1)}, bf16[320,128]{1,0:T(8,128)(2,1)S(1)}, u32[]{:S(2)}, u32[]{:S(2)}) collective-permute-start(bf16[320,128]{1,0:T(8,128)(2,1)S(1)} %get-tuple-element.11), channel_id=1, source_target_pairs={{0,0},{1,32},{2,64},{3,96},{4,128},{5,160},{6,192},{7,224},{8,256}... | collective-permute-start | bytes 245768 | tf_op jit(solution)/shard_map/ppermute | solution.py:351
  11.4 3.0 %collective-permute-start.1 = (bf16[320,128]{1,0:T(8,128)(2,1)S(1)}, bf16[320,128]{1,0:T(8,128)(2,1)S(1)}, u32[]{:S(2)}, u32[]{:S(2)}) collective-permute-start(bf16[320,128]{1,0:T(8,128)(2,1)S(1)} %get-tuple-element.12), channel_id=1, source_target_pairs={{0,16},{1,48},{2,80},{3,112},{4,144},{5,176},{6,208},{7,240},{8,27... | collective-permute-start | bytes 245768 | tf_op jit(solution)/shard_map/ppermute | solution.py:352
  14.4 0.0 collective-permute-done.first
  14.4 8.2 %collective-permute-done.1.second = bf16[320,128]{1,0:T(8,128)(2,1)S(1)} collective-permute-done((bf16[320,128]{1,0:T(8,128)(2,1)S(1)}, bf16[320,128]{1,0:T(8,128)(2,1)S(1)}, u32[]{:S(2)}, u32[]{:S(2)}) %collective-permute-start.1) | collective-permute-done | bytes 81952 | tf_op jit(solution)/shard_map/ppermute | solution.py:352
  22.6 1.8 %weight_copies.1.after = bf16[8,2,320,128]{3,2,1,0:T(8,128)(2,1)} custom-call(s32[2]{0:T(128)S(1)} %pad_add_fusion.where_ref, bf16[320,128]{1,0:T(8,128)(2,1)S(1)} %collective-permute-done.first, bf16[320,128]{1,0:T(8,128)(2,1)S(1)} %collective-permute-done.1.second), custom_call_target="tpu_custom_call" | custom-call | tf_op jit(solution)/shard_map/weight_copies/pallas_call | solution.py:156
  24.4 15.4 %all-to-all-start = ((bf16[8,2,320,128]{3,2,1,0:T(8,128)(2,1)}), bf16[8,2,320,128]{3,2,1,0:T(8,128)(2,1)S(1)}, u32[]{:S(2)}, u32[]{:S(2)}) async-start(bf16[8,2,320,128]{3,2,1,0:T(8,128)(2,1)} %weight_copies.1.after), calls=%async_computation | async-start | bytes 2621440 | tf_op jit(solution)/shard_map/all_to_all | solution.py:362
  39.8 2.2 %copy-done = bf16[256,8192]{1,0:T(8,128)(2,1)S(1)} copy-done((bf16[256,8192]{1,0:T(8,128)(2,1)S(1)}, bf16[256,8192]{1,0:T(8,128)(2,1)}, u32[]{:S(2)}) %copy-start) | copy-done | bytes 4194328
  42.0 0.9 cut_states.1
  42.9 1.9 %collective-permute-start.2 = (bf16[256,1024]{1,0:T(8,128)(2,1)S(1)}, bf16[256,1024]{1,0:T(8,128)(2,1)S(1)}, u32[]{:S(2)}, u32[]{:S(2)}) collective-permute-start(bf16[256,1024]{1,0:T(8,128)(2,1)S(1)} %get-tuple-element.13), channel_id=1, source_target_pairs={{0,56},{1,57},{2,58},{3,59},{4,60},{5,61},{6,62},{7,63},{16,0},{17... | collective-permute-start | bytes 1572872 | tf_op jit(solution)/shard_map/ppermute | solution.py:357
  44.9 5.7 %collective-permute-start.3 = (bf16[256,1024]{1,0:T(8,128)(2,1)S(1)}, bf16[256,1024]{1,0:T(8,128)(2,1)S(1)}, u32[]{:S(2)}, u32[]{:S(2)}) collective-permute-start(bf16[256,1024]{1,0:T(8,128)(2,1)S(1)} %get-tuple-element.14), channel_id=1, source_target_pairs={{0,32},{1,41},{2,34},{3,43},{4,36},{5,45},{6,38},{7,47},{16,48},{1... | collective-permute-start | bytes 1572872 | tf_op jit(solution)/shard_map/ppermute | solution.py:358
  50.6 2.0 %collective-permute-start.4 = (bf16[256,1024]{1,0:T(8,128)(2,1)S(1)}, bf16[256,1024]{1,0:T(8,128)(2,1)S(1)}, u32[]{:S(2)}, u32[]{:S(2)}) collective-permute-start(bf16[256,1024]{1,0:T(8,128)(2,1)S(1)} %get-tuple-element.15), channel_id=1, source_target_pairs={{0,16},{1,17},{2,18},{3,19},{4,20},{5,21},{6,22},{7,23},{16,32},{1... | collective-permute-start | bytes 1572872 | tf_op jit(solution)/shard_map/ppermute | solution.py:359
  52.5 9.0 %collective-permute-done.2.n1 = bf16[256,1024]{1,0:T(8,128)(2,1)S(1)} collective-permute-done((bf16[256,1024]{1,0:T(8,128)(2,1)S(1)}, bf16[256,1024]{1,0:T(8,128)(2,1)S(1)}, u32[]{:S(2)}, u32[]{:S(2)}) %collective-permute-start.2) | collective-permute-done | bytes 524320 | tf_op jit(solution)/shard_map/ppermute | solution.py:357
  61.5 1.9 %collective-permute-start.5 = (bf16[256,1024]{1,0:T(8,128)(2,1)S(1)}, bf16[256,1024]{1,0:T(8,128)(2,1)S(1)}, u32[]{:S(2)}, u32[]{:S(2)}) collective-permute-start(bf16[256,1024]{1,0:T(8,128)(2,1)S(1)} %collective-permute-done.2.n1), channel_id=1, source_target_pairs={{0,1},{1,0},{2,3},{3,2},{4,5},{5,4},{6,7},{7,6},{8,9},{9,8},{10,11... | collective-permute-start | bytes 1572872 | tf_op jit(solution)/shard_map/ppermute | solution.py:52
  63.4 5.6 %collective-permute-done.3.n2 = bf16[256,1024]{1,0:T(8,128)(2,1)S(1)} collective-permute-done((bf16[256,1024]{1,0:T(8,128)(2,1)S(1)}, bf16[256,1024]{1,0:T(8,128)(2,1)S(1)}, u32[]{:S(2)}, u32[]{:S(2)}) %collective-permute-start.3) | collective-permute-done | bytes 524320 | tf_op jit(solution)/shard_map/ppermute | solution.py:358
  69.0 3.3 %collective-permute-start.6 = (bf16[256,1024]{1,0:T(8,128)(2,1)S(1)}, bf16[256,1024]{1,0:T(8,128)(2,1)S(1)}, u32[]{:S(2)}, u32[]{:S(2)}) collective-permute-start(bf16[256,1024]{1,0:T(8,128)(2,1)S(1)} %collective-permute-done.3.n2), channel_id=1, source_target_pairs={{0,1},{1,0},{2,3},{3,2},{4,5},{5,4},{6,7},{7,6},{8,9},{9,8},{10,11... | collective-permute-start | bytes 1572872 | tf_op jit(solution)/shard_map/ppermute | solution.py:52
  72.4 3.4 %collective-permute-done.4.n3 = bf16[256,1024]{1,0:T(8,128)(2,1)S(1)} collective-permute-done((bf16[256,1024]{1,0:T(8,128)(2,1)S(1)}, bf16[256,1024]{1,0:T(8,128)(2,1)S(1)}, u32[]{:S(2)}, u32[]{:S(2)}) %collective-permute-start.4) | collective-permute-done | bytes 524320 | tf_op jit(solution)/shard_map/ppermute | solution.py:359
  75.7 1.9 %collective-permute-start.7 = (bf16[256,1024]{1,0:T(8,128)(2,1)S(1)}, bf16[256,1024]{1,0:T(8,128)(2,1)S(1)}, u32[]{:S(2)}, u32[]{:S(2)}) collective-permute-start(bf16[256,1024]{1,0:T(8,128)(2,1)S(1)} %collective-permute-done.4.n3), channel_id=1, source_target_pairs={{0,1},{1,0},{2,3},{3,2},{4,5},{5,4},{6,7},{7,6},{8,9},{9,8},{10,11... | collective-permute-start | bytes 1572872 | tf_op jit(solution)/shard_map/ppermute | solution.py:52
  77.6 0.0 collective-permute-done.5.f1
  77.7 0.0 collective-permute-done.6.f2
  77.7 0.8 copy-done.2
  78.5 1.1 collective-permute-done.7.f3
  79.5 0.8 copy-done.5
  80.3 0.0 all-to-all-done.weights
  80.3 2.2 %copy-done.1 = bf16[256,8192]{1,0:T(8,128)(2,1)S(1)} copy-done((bf16[256,8192]{1,0:T(8,128)(2,1)S(1)}, bf16[256,8192]{1,0:T(8,128)(2,1)}, u32[]{:S(2)}) %copy-start.1) | copy-done | bytes 4194328
  82.5 1.0 copy-done.3
  83.6 1.0 copy-done.6
  84.6 3.5 %project.1 = (bf16[4,320,256]{2,1,0:T(8,128)(2,1)S(1)}, bf16[256,2048]{1,0:T(8,128)(2,1)S(1)}) custom-call(s32[2]{0:T(128)S(1)} %pad_add_fusion.where_ref, bf16[256,8192]{1,0:T(8,128)(2,1)S(1)} %copy-done.1, bf16[256,1024]{1,0:T(8,128)(2,1)S(1)} %collective-permute-done.2.n1, bf16[256,1024]{1,0:T(8,128)(2,1)S(1)} %collective-permute-done.3.n2, ...), custom_call_target="tpu_custom_call" | custom-call | tf_op jit(solution)/shard_map/project/pallas_call | solution.py:212
  88.1 1.0 copy-done.9
  89.1 0.8 copy-done.11
  89.9 3.6 %all-to-all-start.1 = ((bf16[4,320,256]{2,1,0:T(8,128)(2,1)}), bf16[4,320,256]{2,1,0:T(8,128)(2,1)S(1)}, u32[]{:S(2)}, u32[]{:S(2)}) async-start(bf16[4,320,256]{2,1,0:T(8,128)(2,1)} %copy-done.11), calls=%async_computation.1 | async-start | bytes 1310720 | tf_op jit(solution)/shard_map/all_to_all | solution.py:365
  93.5 0.1 reduce_sum.19
  93.7 0.1 add_convert_fusion
  93.7 0.1 convert_element_type.15
  93.8 0.5 multiply_cosine_fusion
  94.4 0.9 pad_maximum_fusion.tables_ref
  95.3 16.1 %all-to-all-done.1.parts = bf16[4,320,256]{2,1,0:T(8,128)(2,1)S(1)} async-done(((bf16[4,320,256]{2,1,0:T(8,128)(2,1)}), bf16[4,320,256]{2,1,0:T(8,128)(2,1)S(1)}, u32[]{:S(2)}, u32[]{:S(2)}) %all-to-all-start.1) | async-done | bytes 655392 | tf_op jit(solution)/shard_map/all_to_all | solution.py:365
  111.4 5.9 %all-gather = f32[256,256]{1,0:T(8,128)S(1)} all-gather(f32[64,256]{1,0:T(8,128)S(1)} %convert_reduce_fusion), channel_id=2, replica_groups=mesh['zh'=4,'zb'=2,'yu'=2,'yb'=2,'yh'=2,'xh'=2,'xb'=2,'c'=2] {'xb','c'}, dimensions={0}, use_global_device_ids=true | all-gather | bytes 327680 | tf_op jit(solution)/shard_map/all_gather | solution.py:367
  117.3 0.9 copy-done.8
  118.3 2.5 %attend.1 = (bf16[256,256]{1,0:T(8,128)(2,1)}, bf16[4,256,256]{2,1,0:T(8,128)(2,1)S(1)}) custom-call(s32[4,4]{1,0:T(4,128)S(1)} %copy-done.16, f32[4]{0:T(128)S(1)} %copy-done.17, bf16[4,320,256]{2,1,0:T(8,128)(2,1)S(1)} %all-to-all-done.1.parts, f32[4,64,256]{2,1,0:T(8,128)S(1)} %bitcast.5, bf16[256,256]{1,0:T(8,128)(2,1)S(1)} %copy-done.12, ...), custom_call_target="tpu_custom_call" | custom-call | tf_op jit(solution)/shard_map/attend/pallas_call | solution.py:288
  120.8 17.7 %all_to_all.20.slopes = bf16[4,256,256]{2,1,0:T(8,128)(2,1)S(1)} all-to-all(bf16[4,256,256]{2,1,0:T(8,128)(2,1)S(1)} %get-tuple-element.19), channel_id=1, replica_groups=mesh['zh'=4,'zb'=2,'yu'=2,'yb'=2,'yh'=2,'xh'=2,'xb'=2,'c'=2] {'yu','yb'}, dimensions={0} | all-to-all | bytes 1048576 | tf_op jit(solution)/shard_map/all_to_all | solution.py:379
  138.5 1.8 %gradient.1 = bf16[8,256,256]{2,1,0:T(8,128)(2,1)S(1)} custom-call(s32[2]{0:T(128)S(1)} %pad_add_fusion.where_ref, bf16[256,2048]{1,0:T(8,128)(2,1)S(1)} %copy-done.10, bf16[256,1024]{1,0:T(8,128)(2,1)S(1)} %collective-permute-done.2.n1, bf16[256,1024]{1,0:T(8,128)(2,1)S(1)} %collective-permute-done.3.n2, bf16[256,1024]{1,0:T(8,128)(2,1)S(1)} %collective-permute-done.4.n3, ...), custom_call_target="tpu_custom_call" | custom-call | tf_op jit(solution)/shard_map/gradient/pallas_call | solution.py:321
  140.3 35.3 %all_to_all.21.terms = bf16[8,256,256]{2,1,0:T(8,128)(2,1)S(1)} all-to-all(bf16[8,256,256]{2,1,0:T(8,128)(2,1)S(1)} %gradient.1), channel_id=1, replica_groups=mesh['zh'=4,'zb'=2,'yu'=2,'yb'=2,'yh'=2,'xh'=2,'xb'=2,'c'=2] {'zh','zb'}, dimensions={0} | all-to-all | bytes 2097152 | tf_op jit(solution)/shard_map/all_to_all | solution.py:381
  175.6 0.9 add_up.1
  (27 shorter events, 0.1 us)
Async XLA Ops:
  0.7 0.9 copy-start.13
  1.6 0.7 copy-start.14
  2.3 0.7 copy-start.15
  3.6 10.8 %collective-permute-start = (bf16[320,128]{1,0:T(8,128)(2,1)S(1)}, bf16[320,128]{1,0:T(8,128)(2,1)S(1)}, u32[]{:S(2)}, u32[]{:S(2)}) collective-permute-start(bf16[320,128]{1,0:T(8,128)(2,1)S(1)} %get-tuple-element.11), channel_id=1, source_target_pairs={{0,0},{1,32},{2,64},{3,96},{4,128},{5,160},{6,192},{7,224},{8,256}... | collective-permute-start | bytes 245768 | tf_op jit(solution)/shard_map/ppermute | solution.py:351
  11.4 11.1 %collective-permute-start.1 = (bf16[320,128]{1,0:T(8,128)(2,1)S(1)}, bf16[320,128]{1,0:T(8,128)(2,1)S(1)}, u32[]{:S(2)}, u32[]{:S(2)}) collective-permute-start(bf16[320,128]{1,0:T(8,128)(2,1)S(1)} %get-tuple-element.12), channel_id=1, source_target_pairs={{0,16},{1,48},{2,80},{3,112},{4,144},{5,176},{6,208},{7,240},{8,27... | collective-permute-start | bytes 245768 | tf_op jit(solution)/shard_map/ppermute | solution.py:352
  24.4 55.9 %all-to-all-start = ((bf16[8,2,320,128]{3,2,1,0:T(8,128)(2,1)}), bf16[8,2,320,128]{3,2,1,0:T(8,128)(2,1)S(1)}, u32[]{:S(2)}, u32[]{:S(2)}) async-start(bf16[8,2,320,128]{3,2,1,0:T(8,128)(2,1)} %weight_copies.1.after), calls=%async_computation | async-start | bytes 2621440 | tf_op jit(solution)/shard_map/all_to_all | solution.py:362
  39.8 2.2 %copy-start = (bf16[256,8192]{1,0:T(8,128)(2,1)S(1)}, bf16[256,8192]{1,0:T(8,128)(2,1)}, u32[]{:S(2)}) copy-start(bf16[256,8192]{1,0:T(8,128)(2,1)} %states_ref.3) | copy-start | bytes 12582916
  42.9 18.6 %collective-permute-start.2 = (bf16[256,1024]{1,0:T(8,128)(2,1)S(1)}, bf16[256,1024]{1,0:T(8,128)(2,1)S(1)}, u32[]{:S(2)}, u32[]{:S(2)}) collective-permute-start(bf16[256,1024]{1,0:T(8,128)(2,1)S(1)} %get-tuple-element.13), channel_id=1, source_target_pairs={{0,56},{1,57},{2,58},{3,59},{4,60},{5,61},{6,62},{7,63},{16,0},{17... | collective-permute-start | bytes 1572872 | tf_op jit(solution)/shard_map/ppermute | solution.py:357
  44.9 24.1 %collective-permute-start.3 = (bf16[256,1024]{1,0:T(8,128)(2,1)S(1)}, bf16[256,1024]{1,0:T(8,128)(2,1)S(1)}, u32[]{:S(2)}, u32[]{:S(2)}) collective-permute-start(bf16[256,1024]{1,0:T(8,128)(2,1)S(1)} %get-tuple-element.14), channel_id=1, source_target_pairs={{0,32},{1,41},{2,34},{3,43},{4,36},{5,45},{6,38},{7,47},{16,48},{1... | collective-permute-start | bytes 1572872 | tf_op jit(solution)/shard_map/ppermute | solution.py:358
  50.6 25.2 %collective-permute-start.4 = (bf16[256,1024]{1,0:T(8,128)(2,1)S(1)}, bf16[256,1024]{1,0:T(8,128)(2,1)S(1)}, u32[]{:S(2)}, u32[]{:S(2)}) collective-permute-start(bf16[256,1024]{1,0:T(8,128)(2,1)S(1)} %get-tuple-element.15), channel_id=1, source_target_pairs={{0,16},{1,17},{2,18},{3,19},{4,20},{5,21},{6,22},{7,23},{16,32},{1... | collective-permute-start | bytes 1572872 | tf_op jit(solution)/shard_map/ppermute | solution.py:359
  61.5 16.1 %collective-permute-start.5 = (bf16[256,1024]{1,0:T(8,128)(2,1)S(1)}, bf16[256,1024]{1,0:T(8,128)(2,1)S(1)}, u32[]{:S(2)}, u32[]{:S(2)}) collective-permute-start(bf16[256,1024]{1,0:T(8,128)(2,1)S(1)} %collective-permute-done.2.n1), channel_id=1, source_target_pairs={{0,1},{1,0},{2,3},{3,2},{4,5},{5,4},{6,7},{7,6},{8,9},{9,8},{10,11... | collective-permute-start | bytes 1572872 | tf_op jit(solution)/shard_map/ppermute | solution.py:52
  69.0 8.7 %collective-permute-start.6 = (bf16[256,1024]{1,0:T(8,128)(2,1)S(1)}, bf16[256,1024]{1,0:T(8,128)(2,1)S(1)}, u32[]{:S(2)}, u32[]{:S(2)}) collective-permute-start(bf16[256,1024]{1,0:T(8,128)(2,1)S(1)} %collective-permute-done.3.n2), channel_id=1, source_target_pairs={{0,1},{1,0},{2,3},{3,2},{4,5},{5,4},{6,7},{7,6},{8,9},{9,8},{10,11... | collective-permute-start | bytes 1572872 | tf_op jit(solution)/shard_map/ppermute | solution.py:52
  75.7 3.8 %collective-permute-start.7 = (bf16[256,1024]{1,0:T(8,128)(2,1)S(1)}, bf16[256,1024]{1,0:T(8,128)(2,1)S(1)}, u32[]{:S(2)}, u32[]{:S(2)}) collective-permute-start(bf16[256,1024]{1,0:T(8,128)(2,1)S(1)} %collective-permute-done.4.n3), channel_id=1, source_target_pairs={{0,1},{1,0},{2,3},{3,2},{4,5},{5,4},{6,7},{7,6},{8,9},{9,8},{10,11... | collective-permute-start | bytes 1572872 | tf_op jit(solution)/shard_map/ppermute | solution.py:52
  77.7 0.8 copy-start.2
  79.5 0.8 copy-start.5
  80.3 2.2 %copy-start.1 = (bf16[256,8192]{1,0:T(8,128)(2,1)S(1)}, bf16[256,8192]{1,0:T(8,128)(2,1)}, u32[]{:S(2)}) copy-start(bf16[256,8192]{1,0:T(8,128)(2,1)} %states_ref.3) | copy-start | bytes 12582916
  82.5 1.0 copy-start.3
  83.6 1.0 copy-start.6
  88.1 1.0 copy-start.9
  89.1 0.8 copy-start.11
  89.9 3.6 %copy-start.16 = (s32[4,4]{1,0:T(4,128)S(1)}, s32[4,4]{1,0:T(4,128)}, u32[]{:S(2)}) copy-start(s32[4,4]{1,0:T(4,128)} %mask_ref.1) | copy-start | bytes 196
  89.9 27.4 %copy-start.12 = (bf16[256,256]{1,0:T(8,128)(2,1)S(1)}, bf16[256,256]{1,0:T(8,128)(2,1)}, u32[]{:S(2)}) copy-start(bf16[256,256]{1,0:T(8,128)(2,1)} %upstream_ref.1) | copy-start | bytes 393220
  89.9 27.4 %copy-start.17 = (f32[4]{0:T(128)S(1)}, f32[4]{0:T(128)}, u32[]{:S(2)}) copy-start(f32[4]{0:T(128)} %risk_ref.1) | copy-start | bytes 52
  89.9 21.5 %all-to-all-start.1 = ((bf16[4,320,256]{2,1,0:T(8,128)(2,1)}), bf16[4,320,256]{2,1,0:T(8,128)(2,1)S(1)}, u32[]{:S(2)}, u32[]{:S(2)}) async-start(bf16[4,320,256]{2,1,0:T(8,128)(2,1)} %copy-done.11), calls=%async_computation.1 | async-start | bytes 1310720 | tf_op jit(solution)/shard_map/all_to_all | solution.py:365
  111.4 27.1 %copy-start.4 = (bf16[256,1024]{1,0:T(8,128)(2,1)S(1)}, bf16[256,1024]{1,0:T(8,128)(2,1)}, u32[]{:S(2)}) copy-start(bf16[256,1024]{1,0:T(8,128)(2,1)} %copy-done.2) | copy-start | bytes 1572868
  111.4 27.1 %copy-start.7 = (bf16[256,1024]{1,0:T(8,128)(2,1)S(1)}, bf16[256,1024]{1,0:T(8,128)(2,1)}, u32[]{:S(2)}) copy-start(bf16[256,1024]{1,0:T(8,128)(2,1)} %copy-done.5) | copy-start | bytes 1572868
  117.3 1.0 copy-start.8
  118.3 20.2 %copy-start.10 = (bf16[256,2048]{1,0:T(8,128)(2,1)S(1)}, bf16[256,2048]{1,0:T(8,128)(2,1)}, u32[]{:S(2)}) copy-start(bf16[256,2048]{1,0:T(8,128)(2,1)} %copy-done.9) | copy-start | bytes 3145732

commit v7 on v6

--- a/solution.py
+++ b/solution.py
@@ -29,7 +29,8 @@
     for d in range(32):
         for t in range(16):
             half = (d % 2) ^ turn
-            pairs.append((d * 16 + t, (2 * t + half) * 16 + d // 2))
+            block = 4 * ((t // 2) ^ (d // 4)) + 2 * (t % 2) + half
+            pairs.append((d * 16 + t, block * 16 + d // 2))
     return pairs
 
 
@@ -72,20 +73,33 @@
     return pl.BlockSpec(memory_space=pltpu.HBM)
 
 
+def held(value):
+    return pltpu.with_memory_space_constraint(value, pltpu.HBM)
+
+
 def anywhere():
     return pl.BlockSpec(memory_space=pl.ANY)
 
 
-def pack_kernel(where_ref, query, key_t, value_t, first, second):
+def pack_kernel(where_ref, query, key_t, value_t, first, second, sems):
     odd = where_ref[1] % 2
+    copies = []
+
+    def copy(source, target):
+        copies.append(pltpu.make_async_copy(source, target, sems.at[len(copies)]))
+        copies[-1].start()
+
     for turn, out in enumerate((first, second)):
         half = odd ^ turn
-        out[:256, :] = query[pl.ds(pl.multiple_of(256 * half, 256), 256), :]
+        rows = pl.ds(pl.multiple_of(256 * half, 256), 256)
+        copy(query.at[rows, :], out.at[pl.ds(0, 256), :])
         for chunk in range(2):
             lanes = pl.ds(pl.multiple_of(256 * half + 128 * chunk, 128), 128)
             base = 256 + 32 * chunk
-            out[base : base + 16, :] = key_t[:, lanes]
-            out[base + 16 : base + 32, :] = value_t[:, lanes]
+            copy(key_t.at[:, lanes], out.at[pl.ds(base, 16), :])
+            copy(value_t.at[:, lanes], out.at[pl.ds(base + 16, 16), :])
+    for each in copies:
+        each.wait()
 
 
 def pack(where, query, key_t, value_t):
@@ -93,13 +107,15 @@
     return pl.pallas_call(
         pack_kernel,
         out_shape=(part, part),
-        in_specs=[in_smem(), *in_vmem(3)],
+        in_specs=[in_smem(), in_hbm(), in_hbm(), in_hbm()],
+        out_specs=tuple(in_vmem(2)),
+        scratch_shapes=[pltpu.SemaphoreType.DMA((10,))],
         compiler_params=params(),
         name="pack_weights",
-    )(where, query, key_t, value_t)
-
-
-def cut_kernel(where_ref, states_ref, after, up_ref, two_ref, down_ref, sems):
+    )(where, held(query), held(key_t), held(value_t))
+
+
+def cut_kernel(where_ref, states_ref, up_ref, two_ref, down_ref, sems):
     core, place = where_ref[0], where_ref[1]
     copies = []
     for number, out in enumerate((up_ref, two_ref, down_ref)):
@@ -118,17 +134,34 @@
         copy.wait()
 
 
-def cut(where, states, after):
+def cut(where, states):
     part = jax.ShapeDtypeStruct((TOK, 1024), BF16)
     return pl.pallas_call(
         cut_kernel,
         out_shape=(part, part, part),
-        in_specs=[in_smem(), in_hbm(), anywhere()],
+        in_specs=[in_smem(), in_hbm()],
         out_specs=tuple(in_vmem(3)),
         scratch_shapes=[pltpu.SemaphoreType.DMA((12,))],
         compiler_params=params(),
         name="cut_states",
-    )(where, states, after)
+    )(where, held(states))
+
+
+def gate_kernel(*refs):
+    del refs
+
+
+def gate(parts, after):
+    count = len(parts)
+    return pl.pallas_call(
+        gate_kernel,
+        out_shape=tuple(jax.ShapeDtypeStruct(x.shape, x.dtype) for x in parts),
+        in_specs=[anywhere()] * (count + 1),
+        out_specs=tuple([anywhere()] * count),
+        input_output_aliases={i: i for i in range(count)},
+        compiler_params=params(),
+        name="gate",
+    )(*parts, after)
 
 
 def own_columns(where_ref, states_ref, own, sems):
@@ -163,14 +196,24 @@
 
 
 def project_kernel(
-    where_ref, states_ref, n1, n2, n3, f1, f2, f3, weights, out, own, w_q, w_kv, sems
+    where_ref, states_ref, n1, n2, n3, f1, f2, f3, weights, out, tokens, w_q, w_kv, result, sems, out_sems
 ):
     core = where_ref[0]
-    copies = own_columns(where_ref, states_ref, own, sems)
-    for copy in copies:
-        copy.start()
+    arrivals = []
+    for number, (near, far) in enumerate(((n1, f1), (n2, f2), (n3, f3))):
+        place = tokens.at[number]
+        arrivals.append(
+            [
+                pltpu.make_async_copy(near, place.at[:, pl.ds(0, 1024)], sems.at[8 + 2 * number]),
+                pltpu.make_async_copy(far, place.at[:, pl.ds(1024, 1024)], sems.at[9 + 2 * number]),
+            ]
+        )
+    arrivals.append(own_columns(where_ref, states_ref, tokens.at[3], sems))
+    for copies in arrivals:
+        for copy in copies:
+            copy.start()
     for part in range(8):
-        block = block_of(part, core)
+        block = block_of(part, core) ^ where_ref[2]
         for head in range(2):
             rows, cols = pl.ds(256 * part, 256), pl.ds(HEAD * head, HEAD)
             w_q[rows, cols] = weights[block, head, :256, :]
@@ -181,49 +224,41 @@
                 w_kv[32 + 16 * head : 48 + 16 * head, lanes] = weights[
                     block, head, base + 16 : base + 32, :
                 ]
-
-    def product(x, rows):
-        q = jnp.dot(x, w_q[rows, :], preferred_element_type=F32)
-        kv = lax.dot_general(
-            x, w_kv[:, rows], (((1,), (1,)), ((), ())), preferred_element_type=F32
+    departures = []
+    for number in range(4):
+        for copy in arrivals[number]:
+            copy.wait()
+        x = tokens[number]
+        q = jnp.dot(x, w_q[...], preferred_element_type=F32)
+        kv = lax.dot_general(x, w_kv[...], (((1,), (1,)), ((), ())), preferred_element_type=F32)
+        result[number, :256, :] = q.astype(BF16)
+        result[number, 256:, :] = kv.T.astype(BF16)
+        other = (where_ref[1] + number + 1) % 4
+        departures.append(
+            pltpu.make_async_copy(result.at[number], out.at[other], out_sems.at[number])
         )
-        return q, kv
-
-    low, high = pl.ds(0, 1024), pl.ds(1024, 1024)
-    pieces = (
-        (n1.at[:, :], f1.at[:, :]),
-        (n2.at[:, :], f2.at[:, :]),
-        (n3.at[:, :], f3.at[:, :]),
-        (own.at[:, low], own.at[:, high]),
-    )
-    for number, (near_ref, far_ref) in enumerate(pieces):
-        if number == 3:
-            for copy in copies:
-                copy.wait()
-        near, far = near_ref[...], far_ref[...]
-        other = (where_ref[1] + number + 1) % 4
-        q_near, kv_near = product(near, low)
-        q_far, kv_far = product(far, high)
-        out[other, :256, :] = (q_near + q_far).astype(BF16)
-        out[other, 256:, :] = (kv_near + kv_far).T.astype(BF16)
+        departures[-1].start()
+    for copy in departures:
+        copy.wait()
 
 
 def project(where, states, near, far, weights):
     return pl.pallas_call(
         project_kernel,
-        out_shape=(
-            jax.ShapeDtypeStruct((4, 320, 256), BF16),
-            jax.ShapeDtypeStruct((TOK, 2048), BF16),
-        ),
-        in_specs=[in_smem(), in_hbm(), *in_vmem(7)],
+        out_shape=pltpu.HBM((4, 320, 256), BF16),
+        in_specs=[in_smem(), in_hbm(), *[anywhere()] * 6, *in_vmem(1)],
+        out_specs=in_hbm(),
         scratch_shapes=[
+            pltpu.VMEM((4, TOK, 2048), BF16),
             pltpu.VMEM((2048, 256), BF16),
             pltpu.VMEM((64, 2048), BF16),
-            pltpu.SemaphoreType.DMA((8,)),
+            pltpu.VMEM((4, 320, 256), BF16),
+            pltpu.SemaphoreType.DMA((14,)),
+            pltpu.SemaphoreType.DMA((4,)),
         ],
         compiler_params=params(),
         name="project",
-    )(where, states, *near, *far, weights)
+    )(where, held(states), *near, *far, weights)
 
 
 def attend_kernel(
@@ -279,9 +314,7 @@
             * scaling
         )
         dq = dq_rot * cq - pltpu.roll(dq_rot, 64, 1) * sq
-        dq_t = dq.T.astype(BF16)
-        for part in range(4):
-            dq_out[part, cols, :] = dq_t
+        dq_out[cols, :] = dq.T.astype(BF16)
 
 
 def attend(block_mask, risk_weight, parts, kv, upstream, tables):
@@ -289,7 +322,7 @@
         attend_kernel,
         out_shape=(
             jax.ShapeDtypeStruct((TOK, 256), BF16),
-            jax.ShapeDtypeStruct((4, 256, TOK), BF16),
+            jax.ShapeDtypeStruct((256, TOK), BF16),
         ),
         in_specs=[in_smem(), in_smem(), *in_vmem(2), in_hbm(), in_hbm()],
         scratch_shapes=[
@@ -299,16 +332,20 @@
         ],
         compiler_params=params(),
         name="attend",
-    )(block_mask, risk_weight, parts, kv, upstream, tables)
-
-
-def gradient_kernel(where_ref, own, n1, n2, n3, f1, f2, f3, slopes, out):
+    )(block_mask, risk_weight, parts, kv, held(upstream), held(tables))
+
+
+def gradient_kernel(where_ref, states_ref, n1, n2, n3, f1, f2, f3, slopes, out, own, sems):
     core = where_ref[0]
+    copies = own_columns(where_ref, states_ref, own, sems)
+    for copy in copies:
+        copy.start()
     for part in range(8):
         cols = pl.ds(256 * (part % 4), 256)
         total = None
-        for number in range(4):
+        for number in (1, 2, 3, 0):
             if number == 0:
+                copies[part].wait()
                 x = own[:, pl.ds(256 * part, 256)]
             else:
                 x = ((n1, n2, n3) if part < 4 else (f1, f2, f3))[number - 1][:, cols]
@@ -317,14 +354,15 @@
         out[block_of(part, core)] = total.astype(BF16)
 
 
-def gradient(where, own, near, far, slopes):
+def gradient(where, states, near, far, slopes):
     return pl.pallas_call(
         gradient_kernel,
         out_shape=jax.ShapeDtypeStruct((8, 256, 256), BF16),
-        in_specs=[in_smem(), *in_vmem(8)],
+        in_specs=[in_smem(), in_hbm(), *in_vmem(7)],
+        scratch_shapes=[pltpu.VMEM((TOK, 2048), BF16), pltpu.SemaphoreType.DMA((8,))],
         compiler_params=params(),
         name="gradient",
-    )(where, own, *near, *far, slopes)
+    )(where, held(states), *near, *far, slopes)
 
 
 def total_kernel(terms, out):
@@ -345,14 +383,15 @@
 
 def shards(states, query_weight, key_matrix, value_matrix, block_mask, risk_weight, upstream):
     place = lax.axis_index(GROUP)
-    where = jnp.stack([lax.axis_index("c"), place]).astype(jnp.int32)
+    plane = lax.axis_index(("yh", "xh", "xb"))
+    where = jnp.stack([lax.axis_index("c"), place, plane]).astype(jnp.int32)
 
     first, second = pack(where, query_weight, key_matrix.T, value_matrix.T)
     first = lax.ppermute(first, AXES, home_pairs(0))
     second = lax.ppermute(second, AXES, home_pairs(1))
     weights = copies(where, first, second)
 
-    up, two, down = cut(where, states, weights)
+    up, two, down = gate(cut(where, states), weights)
     near = (
         lax.ppermute(down, AXES, ring_pairs(-1, -1)),
         lax.ppermute(two, AXES, ring_pairs(2, -2)),
@@ -361,7 +400,7 @@
     far = [swap_core(x) for x in near]
     weights = lax.all_to_all(weights, OTHERS, split_axis=0, concat_axis=0)
 
-    parts, own = project(where, states, near, far, weights)
+    parts = project(where, states, near, far, weights)
     parts = lax.all_to_all(parts, GROUP, split_axis=0, concat_axis=0)
     kv = jnp.sum(parts[:, 256:].astype(F32), axis=0)
     kv = lax.all_gather(kv, ("xb", "c"), axis=0, tiled=False)
@@ -376,8 +415,8 @@
     tables = jnp.concatenate([cosine, cosine, -sine, sine], axis=1)
 
     attn_out, dq = attend(block_mask, risk_weight, parts, kv, upstream, tables)
-    slopes = lax.all_to_all(dq, GROUP, split_axis=0, concat_axis=0)
-    terms = gradient(where, own, near, far, slopes)
+    slopes = lax.all_gather(dq, GROUP, axis=0, tiled=False)
+    terms = gradient(where, states, near, far, slopes)
     terms = lax.all_to_all(terms, OTHERS, split_axis=0, concat_axis=0)
     return attn_out, add_up(terms)
 

time: 178 us -> 170 us (0.955)
  local copies, waits for them, and re-layouts: 13.3 us -> 3.76 us
  Pallas kernels: 12 us -> 18.1 us
  waiting for transfers between devices: 43.3 us -> 37.2 us
  starting transfers between devices: 46.5 us -> 50.6 us
  blocking collectives: 58.9 us -> 55 us
    all_to_all x1 -> x0, blocking collectives: 17.7 us -> none  [shards(): slopes = lax.all_to_all(dq, GROUP, split_axis=0, concat_axis=0)]
    all_gather x0 -> x1, blocking collectives: none -> 16.1 us  [shards(): slopes = lax.all_gather(dq, GROUP, axis=0, tiled=False)]
    unnamed x36 -> x16, local copies, waits for them, and re-layouts: 13.2 us -> 3.68 us
    ppermute x1, waiting for transfers between devices: 8.17 us -> 3.59 us  [shards(): second = lax.ppermute(second, AXES, home_pairs(1))]
    ppermute x1, waiting for transfers between devices: 5.57 us -> 1.42 us  [shards(): lax.ppermute(two, AXES, ring_pairs(2, -2))]
    ppermute x1, starting transfers between devices: 2.95 us -> 5.68 us  [shards(): second = lax.ppermute(second, AXES, home_pairs(1))]
    all_to_all x1, blocking collectives: 35.3 us -> 33 us  [shards(): terms = lax.all_to_all(terms, OTHERS, split_axis=0, concat_axis=0)]
    ppermute x1, waiting for transfers between devices: 8.98 us -> 11 us  [shards(): lax.ppermute(down, AXES, ring_pairs(-1, -1))]
where the time goes in v7:
time: 170 us; the launch traced here: 167 us
  blocking collectives  55 us (32%)
  starting transfers between devices  50.6 us (30%)
  waiting for transfers between devices  37.2 us (22%)
  Pallas kernels  18.1 us (11%)
  local copies, waits for them, and re-layouts  3.76 us (2%)
  other arithmetic  1.73 us (1%)
    all_to_all x1, blocking collectives, shards(): terms = lax.all_to_all(terms, OTHERS, split_axis=0, concat_axis=0)  33 us
    all_to_all x1, starting transfers between devices, shards(): weights = lax.all_to_all(weights, OTHERS, split_axis=0, concat_axis=0)  17.2 us
    all_gather x1, blocking collectives, shards(): slopes = lax.all_gather(dq, GROUP, axis=0, tiled=False)  16.1 us
    all_to_all x1, waiting for transfers between devices, shards(): parts = lax.all_to_all(parts, GROUP, split_axis=0, concat_axis=0)  16.1 us
    ppermute x1, waiting for transfers between devices, shards(): lax.ppermute(down, AXES, ring_pairs(-1, -1))  11 us
    ppermute x1, starting transfers between devices, shards(): first = lax.ppermute(first, AXES, home_pairs(0))  7.81 us
    ppermute x3, starting transfers between devices, swap_core(): return lax.ppermute(value, 'c', [(0, 1), (1, 0)])  7.55 us
    all_gather x1, blocking collectives, shards(): kv = lax.all_gather(kv, ('xb', 'c'), axis=0, tiled=False)  5.92 us
  transfers between devices with their start and end apart: 10, of which 6 were waited for; matrix products, arithmetic and copies ran while one was open for 1% of the time, Pallas kernels for 1%

profile of v7, /device:TPU:6, one launch (start us, length us, event | category | flops | bytes accessed | tf_op | source)
XLA Modules:
  0.0 167.2 jit_solution(14905823306126982323)
XLA Ops:
  0.6 0.1 pad_add_fusion.where_ref
  0.7 1.6 pack_weights.1
  2.3 7.8 %collective-permute-start = (bf16[320,128]{1,0:T(8,128)(2,1)S(1)}, bf16[320,128]{1,0:T(8,128)(2,1)S(1)}, u32[]{:S(2)}, u32[]{:S(2)}) collective-permute-start(bf16[320,128]{1,0:T(8,128)(2,1)S(1)} %get-tuple-element.15), channel_id=1, source_target_pairs={{0,0},{1,32},{2,64},{3,96},{4,128},{5,160},{6,192},{7,224},{8,256}... | collective-permute-start | bytes 245768 | tf_op jit(solution)/shard_map/ppermute | solution.py:390
  10.1 5.7 %collective-permute-start.1 = (bf16[320,128]{1,0:T(8,128)(2,1)S(1)}, bf16[320,128]{1,0:T(8,128)(2,1)S(1)}, u32[]{:S(2)}, u32[]{:S(2)}) collective-permute-start(bf16[320,128]{1,0:T(8,128)(2,1)S(1)} %get-tuple-element.16), channel_id=1, source_target_pairs={{0,16},{1,48},{2,80},{3,112},{4,144},{5,176},{6,208},{7,240},{8,27... | collective-permute-start | bytes 245768 | tf_op jit(solution)/shard_map/ppermute | solution.py:391
  15.8 0.0 collective-permute-done.first
  15.8 3.6 %collective-permute-done.1.second = bf16[320,128]{1,0:T(8,128)(2,1)S(1)} collective-permute-done((bf16[320,128]{1,0:T(8,128)(2,1)S(1)}, bf16[320,128]{1,0:T(8,128)(2,1)S(1)}, u32[]{:S(2)}, u32[]{:S(2)}) %collective-permute-start.1) | collective-permute-done | bytes 81952 | tf_op jit(solution)/shard_map/ppermute | solution.py:391
  19.4 1.8 %weight_copies.1.refs_3_ = bf16[8,2,320,128]{3,2,1,0:T(8,128)(2,1)} custom-call(s32[3]{0:T(128)S(1)} %pad_add_fusion.where_ref, bf16[320,128]{1,0:T(8,128)(2,1)S(1)} %collective-permute-done.first, bf16[320,128]{1,0:T(8,128)(2,1)S(1)} %collective-permute-done.1.second), custom_call_target="tpu_custom_call" | custom-call | tf_op jit(solution)/shard_map/weight_copies/pallas_call | solution.py:189
  21.3 17.2 %all-to-all-start = ((bf16[8,2,320,128]{3,2,1,0:T(8,128)(2,1)}), bf16[8,2,320,128]{3,2,1,0:T(8,128)(2,1)S(1)}, u32[]{:S(2)}, u32[]{:S(2)}) async-start(bf16[8,2,320,128]{3,2,1,0:T(8,128)(2,1)} %weight_copies.1.refs_3_), calls=%async_computation | async-start | bytes 2621440 | tf_op jit(solution)/shard_map/all_to_all | solution.py:401
  38.4 2.1 %cut_states.1 = (bf16[256,1024]{1,0:T(8,128)(2,1)S(1)}, bf16[256,1024]{1,0:T(8,128)(2,1)S(1)}, bf16[256,1024]{1,0:T(8,128)(2,1)S(1)}) custom-call(s32[3]{0:T(128)S(1)} %pad_add_fusion.where_ref, bf16[256,8192]{1,0:T(8,128)(2,1)} %states_ref.5), custom_call_target="tpu_custom_call" | custom-call | tf_op jit(solution)/shard_map/cut_states/pallas_call | solution.py:139
  40.6 1.9 %collective-permute-start.2 = (bf16[256,1024]{1,0:T(8,128)(2,1)S(1)}, bf16[256,1024]{1,0:T(8,128)(2,1)S(1)}, u32[]{:S(2)}, u32[]{:S(2)}) collective-permute-start(bf16[256,1024]{1,0:T(8,128)(2,1)S(1)} %get-tuple-element.17), channel_id=1, source_target_pairs={{0,56},{1,57},{2,58},{3,59},{4,60},{5,61},{6,62},{7,63},{16,0},{17... | collective-permute-start | bytes 1572872 | tf_op jit(solution)/shard_map/ppermute | solution.py:396
  42.5 4.5 %collective-permute-start.3 = (bf16[256,1024]{1,0:T(8,128)(2,1)S(1)}, bf16[256,1024]{1,0:T(8,128)(2,1)S(1)}, u32[]{:S(2)}, u32[]{:S(2)}) collective-permute-start(bf16[256,1024]{1,0:T(8,128)(2,1)S(1)} %get-tuple-element.18), channel_id=1, source_target_pairs={{0,32},{1,41},{2,34},{3,43},{4,36},{5,45},{6,38},{7,47},{16,48},{1... | collective-permute-start | bytes 1572872 | tf_op jit(solution)/shard_map/ppermute | solution.py:397
  47.0 2.4 %collective-permute-start.4 = (bf16[256,1024]{1,0:T(8,128)(2,1)S(1)}, bf16[256,1024]{1,0:T(8,128)(2,1)S(1)}, u32[]{:S(2)}, u32[]{:S(2)}) collective-permute-start(bf16[256,1024]{1,0:T(8,128)(2,1)S(1)} %get-tuple-element.19), channel_id=1, source_target_pairs={{0,16},{1,17},{2,18},{3,19},{4,20},{5,21},{6,22},{7,23},{16,32},{1... | collective-permute-start | bytes 1572872 | tf_op jit(solution)/shard_map/ppermute | solution.py:398
  49.5 11.0 %collective-permute-done.2.n1 = bf16[256,1024]{1,0:T(8,128)(2,1)S(1)} collective-permute-done((bf16[256,1024]{1,0:T(8,128)(2,1)S(1)}, bf16[256,1024]{1,0:T(8,128)(2,1)S(1)}, u32[]{:S(2)}, u32[]{:S(2)}) %collective-permute-start.2) | collective-permute-done | bytes 524320 | tf_op jit(solution)/shard_map/ppermute | solution.py:396
  60.5 1.9 %collective-permute-start.5 = (bf16[256,1024]{1,0:T(8,128)(2,1)S(1)}, bf16[256,1024]{1,0:T(8,128)(2,1)S(1)}, u32[]{:S(2)}, u32[]{:S(2)}) collective-permute-start(bf16[256,1024]{1,0:T(8,128)(2,1)S(1)} %collective-permute-done.2.n1), channel_id=1, source_target_pairs={{0,1},{1,0},{2,3},{3,2},{4,5},{5,4},{6,7},{7,6},{8,9},{9,8},{10,11... | collective-permute-start | bytes 1572872 | tf_op jit(solution)/shard_map/ppermute | solution.py:53
  62.4 1.4 collective-permute-done.3.n2
  63.8 3.7 %collective-permute-start.6 = (bf16[256,1024]{1,0:T(8,128)(2,1)S(1)}, bf16[256,1024]{1,0:T(8,128)(2,1)S(1)}, u32[]{:S(2)}, u32[]{:S(2)}) collective-permute-start(bf16[256,1024]{1,0:T(8,128)(2,1)S(1)} %collective-permute-done.3.n2), channel_id=1, source_target_pairs={{0,1},{1,0},{2,3},{3,2},{4,5},{5,4},{6,7},{7,6},{8,9},{9,8},{10,11... | collective-permute-start | bytes 1572872 | tf_op jit(solution)/shard_map/ppermute | solution.py:53
  67.6 4.0 %collective-permute-done.4.n3 = bf16[256,1024]{1,0:T(8,128)(2,1)S(1)} collective-permute-done((bf16[256,1024]{1,0:T(8,128)(2,1)S(1)}, bf16[256,1024]{1,0:T(8,128)(2,1)S(1)}, u32[]{:S(2)}, u32[]{:S(2)}) %collective-permute-start.4) | collective-permute-done | bytes 524320 | tf_op jit(solution)/shard_map/ppermute | solution.py:398
  71.5 1.9 %collective-permute-start.7 = (bf16[256,1024]{1,0:T(8,128)(2,1)S(1)}, bf16[256,1024]{1,0:T(8,128)(2,1)S(1)}, u32[]{:S(2)}, u32[]{:S(2)}) collective-permute-start(bf16[256,1024]{1,0:T(8,128)(2,1)S(1)} %collective-permute-done.4.n3), channel_id=1, source_target_pairs={{0,1},{1,0},{2,3},{3,2},{4,5},{5,4},{6,7},{7,6},{8,9},{9,8},{10,11... | collective-permute-start | bytes 1572872 | tf_op jit(solution)/shard_map/ppermute | solution.py:53
  73.5 0.0 collective-permute-done.5.f1
  73.5 0.0 collective-permute-done.6.f2
  73.5 0.0 copy-start
  73.5 0.8 copy-done
  74.3 1.1 collective-permute-done.7.f3
  75.3 0.0 copy-start.3
  75.3 0.8 copy-done.3
  76.1 0.0 all-to-all-done.weights
  76.1 1.0 copy-done.1
  77.2 1.0 copy-done.4
  78.2 4.9 %project.1 = bf16[4,320,256]{2,1,0:T(8,128)(2,1)} custom-call(s32[3]{0:T(128)S(1)} %pad_add_fusion.where_ref, bf16[256,8192]{1,0:T(8,128)(2,1)} %states_ref.5, bf16[256,1024]{1,0:T(8,128)(2,1)S(1)} %collective-permute-done.2.n1, bf16[256,1024]{1,0:T(8,128)(2,1)S(1)} %collective-permute-done.3.n2, bf16[256,1024]{1,0:T(8,128)(2,1)S(1)} %collective-permute-done.4.n3, ...), custom_call_target="tpu_custom_call" | custom-call | tf_op jit(solution)/shard_map/project/pallas_call | solution.py:246
  83.1 0.0 copy-start.6
  83.1 0.0 copy-start.7
  83.1 3.5 %all-to-all-start.1 = ((bf16[4,320,256]{2,1,0:T(8,128)(2,1)}), bf16[4,320,256]{2,1,0:T(8,128)(2,1)S(1)}, u32[]{:S(2)}, u32[]{:S(2)}) async-start(bf16[4,320,256]{2,1,0:T(8,128)(2,1)} %project.1), calls=%async_computation.1 | async-start | bytes 1310720 | tf_op jit(solution)/shard_map/all_to_all | solution.py:404
  86.6 0.0 copy-done.6
  86.6 0.1 reduce_sum.19
  86.7 0.1 add_convert_fusion
  86.8 0.1 convert_element_type.15
  86.9 0.5 multiply_cosine_fusion
  87.5 0.9 pad_maximum_fusion.tables_ref
  88.3 16.1 %all-to-all-done.1.parts = bf16[4,320,256]{2,1,0:T(8,128)(2,1)S(1)} async-done(((bf16[4,320,256]{2,1,0:T(8,128)(2,1)}), bf16[4,320,256]{2,1,0:T(8,128)(2,1)S(1)}, u32[]{:S(2)}, u32[]{:S(2)}) %all-to-all-start.1) | async-done | bytes 655392 | tf_op jit(solution)/shard_map/all_to_all | solution.py:404
  104.5 5.9 %all-gather = f32[256,256]{1,0:T(8,128)S(1)} all-gather(f32[64,256]{1,0:T(8,128)S(1)} %convert_reduce_fusion), channel_id=2, replica_groups=mesh['zh'=4,'zb'=2,'yu'=2,'yb'=2,'yh'=2,'xh'=2,'xb'=2,'c'=2] {'xb','c'}, dimensions={0}, use_global_device_ids=true | all-gather | bytes 327680 | tf_op jit(solution)/shard_map/all_gather | solution.py:406
  110.4 0.0 copy-done.7
  110.4 3.2 %attend.1 = (bf16[256,256]{1,0:T(8,128)(2,1)}, bf16[256,256]{1,0:T(8,128)(2,1)S(1)}) custom-call(s32[4,4]{1,0:T(4,128)S(1)} %copy-done.6, f32[4]{0:T(128)S(1)} %copy-done.7, bf16[4,320,256]{2,1,0:T(8,128)(2,1)S(1)} %all-to-all-done.1.parts, f32[4,64,256]{2,1,0:T(8,128)S(1)} %bitcast.8, bf16[256,256]{1,0:T(8,128)(2,1)} %upstream_ref.1, ...), custom_call_target="tpu_custom_call" | custom-call | tf_op jit(solution)/shard_map/attend/pallas_call | solution.py:321
  113.6 16.1 %all-gather.1 = bf16[1024,256]{1,0:T(8,128)(2,1)S(1)} all-gather(bf16[256,256]{1,0:T(8,128)(2,1)S(1)} %get-tuple-element.21), channel_id=3, replica_groups=mesh['zh'=4,'zb'=2,'yu'=2,'yb'=2,'yh'=2,'xh'=2,'xb'=2,'c'=2] {'yu','yb'}, dimensions={0}, use_global_device_ids=true | all-gather | bytes 655360 | tf_op jit(solution)/shard_map/all_gather | solution.py:418
  129.7 0.0 copy-done.2
  129.7 0.0 copy-done.5
  129.8 3.6 %gradient.1 = bf16[8,256,256]{2,1,0:T(8,128)(2,1)S(1)} custom-call(s32[3]{0:T(128)S(1)} %pad_add_fusion.where_ref, bf16[256,8192]{1,0:T(8,128)(2,1)} %states_ref.5, bf16[256,1024]{1,0:T(8,128)(2,1)S(1)} %collective-permute-done.2.n1, bf16[256,1024]{1,0:T(8,128)(2,1)S(1)} %collective-permute-done.3.n2, bf16[256,1024]{1,0:T(8,128)(2,1)S(1)} %collective-permute-done.4.n3, ...), custom_call_target="tpu_custom_call" | custom-call | tf_op jit(solution)/shard_map/gradient/pallas_call | solution.py:358
  133.3 33.0 %all_to_all.15.terms = bf16[8,256,256]{2,1,0:T(8,128)(2,1)S(1)} all-to-all(bf16[8,256,256]{2,1,0:T(8,128)(2,1)S(1)} %gradient.1), channel_id=1, replica_groups=mesh['zh'=4,'zb'=2,'yu'=2,'yb'=2,'yh'=2,'xh'=2,'xb'=2,'c'=2] {'zh','zb'}, dimensions={0} | all-to-all | bytes 2097152 | tf_op jit(solution)/shard_map/all_to_all | solution.py:420
  166.3 0.9 add_up.1
  (8 shorter events, 0.0 us)
Async XLA Ops:
  2.3 13.5 %collective-permute-start = (bf16[320,128]{1,0:T(8,128)(2,1)S(1)}, bf16[320,128]{1,0:T(8,128)(2,1)S(1)}, u32[]{:S(2)}, u32[]{:S(2)}) collective-permute-start(bf16[320,128]{1,0:T(8,128)(2,1)S(1)} %get-tuple-element.15), channel_id=1, source_target_pairs={{0,0},{1,32},{2,64},{3,96},{4,128},{5,160},{6,192},{7,224},{8,256}... | collective-permute-start | bytes 245768 | tf_op jit(solution)/shard_map/ppermute | solution.py:390
  10.1 9.3 %collective-permute-start.1 = (bf16[320,128]{1,0:T(8,128)(2,1)S(1)}, bf16[320,128]{1,0:T(8,128)(2,1)S(1)}, u32[]{:S(2)}, u32[]{:S(2)}) collective-permute-start(bf16[320,128]{1,0:T(8,128)(2,1)S(1)} %get-tuple-element.16), channel_id=1, source_target_pairs={{0,16},{1,48},{2,80},{3,112},{4,144},{5,176},{6,208},{7,240},{8,27... | collective-permute-start | bytes 245768 | tf_op jit(solution)/shard_map/ppermute | solution.py:391
  21.3 54.9 %all-to-all-start = ((bf16[8,2,320,128]{3,2,1,0:T(8,128)(2,1)}), bf16[8,2,320,128]{3,2,1,0:T(8,128)(2,1)S(1)}, u32[]{:S(2)}, u32[]{:S(2)}) async-start(bf16[8,2,320,128]{3,2,1,0:T(8,128)(2,1)} %weight_copies.1.refs_3_), calls=%async_computation | async-start | bytes 2621440 | tf_op jit(solution)/shard_map/all_to_all | solution.py:401
  40.6 19.9 %collective-permute-start.2 = (bf16[256,1024]{1,0:T(8,128)(2,1)S(1)}, bf16[256,1024]{1,0:T(8,128)(2,1)S(1)}, u32[]{:S(2)}, u32[]{:S(2)}) collective-permute-start(bf16[256,1024]{1,0:T(8,128)(2,1)S(1)} %get-tuple-element.17), channel_id=1, source_target_pairs={{0,56},{1,57},{2,58},{3,59},{4,60},{5,61},{6,62},{7,63},{16,0},{17... | collective-permute-start | bytes 1572872 | tf_op jit(solution)/shard_map/ppermute | solution.py:396
  42.5 21.3 %collective-permute-start.3 = (bf16[256,1024]{1,0:T(8,128)(2,1)S(1)}, bf16[256,1024]{1,0:T(8,128)(2,1)S(1)}, u32[]{:S(2)}, u32[]{:S(2)}) collective-permute-start(bf16[256,1024]{1,0:T(8,128)(2,1)S(1)} %get-tuple-element.18), channel_id=1, source_target_pairs={{0,32},{1,41},{2,34},{3,43},{4,36},{5,45},{6,38},{7,47},{16,48},{1... | collective-permute-start | bytes 1572872 | tf_op jit(solution)/shard_map/ppermute | solution.py:397
  47.0 24.5 %collective-permute-start.4 = (bf16[256,1024]{1,0:T(8,128)(2,1)S(1)}, bf16[256,1024]{1,0:T(8,128)(2,1)S(1)}, u32[]{:S(2)}, u32[]{:S(2)}) collective-permute-start(bf16[256,1024]{1,0:T(8,128)(2,1)S(1)} %get-tuple-element.19), channel_id=1, source_target_pairs={{0,16},{1,17},{2,18},{3,19},{4,20},{5,21},{6,22},{7,23},{16,32},{1... | collective-permute-start | bytes 1572872 | tf_op jit(solution)/shard_map/ppermute | solution.py:398
  60.5 13.0 %collective-permute-start.5 = (bf16[256,1024]{1,0:T(8,128)(2,1)S(1)}, bf16[256,1024]{1,0:T(8,128)(2,1)S(1)}, u32[]{:S(2)}, u32[]{:S(2)}) collective-permute-start(bf16[256,1024]{1,0:T(8,128)(2,1)S(1)} %collective-permute-done.2.n1), channel_id=1, source_target_pairs={{0,1},{1,0},{2,3},{3,2},{4,5},{5,4},{6,7},{7,6},{8,9},{9,8},{10,11... | collective-permute-start | bytes 1572872 | tf_op jit(solution)/shard_map/ppermute | solution.py:53
  63.8 9.6 %collective-permute-start.6 = (bf16[256,1024]{1,0:T(8,128)(2,1)S(1)}, bf16[256,1024]{1,0:T(8,128)(2,1)S(1)}, u32[]{:S(2)}, u32[]{:S(2)}) collective-permute-start(bf16[256,1024]{1,0:T(8,128)(2,1)S(1)} %collective-permute-done.3.n2), channel_id=1, source_target_pairs={{0,1},{1,0},{2,3},{3,2},{4,5},{5,4},{6,7},{7,6},{8,9},{9,8},{10,11... | collective-permute-start | bytes 1572872 | tf_op jit(solution)/shard_map/ppermute | solution.py:53
  71.5 3.8 %collective-permute-start.7 = (bf16[256,1024]{1,0:T(8,128)(2,1)S(1)}, bf16[256,1024]{1,0:T(8,128)(2,1)S(1)}, u32[]{:S(2)}, u32[]{:S(2)}) collective-permute-start(bf16[256,1024]{1,0:T(8,128)(2,1)S(1)} %collective-permute-done.4.n3), channel_id=1, source_target_pairs={{0,1},{1,0},{2,3},{3,2},{4,5},{5,4},{6,7},{7,6},{8,9},{9,8},{10,11... | collective-permute-start | bytes 1572872 | tf_op jit(solution)/shard_map/ppermute | solution.py:53
  73.5 0.8 copy-start
  75.3 0.8 copy-start.3
  76.1 1.0 copy-start.1
  77.2 1.0 copy-start.4
  83.1 3.5 %copy-start.6 = (s32[4,4]{1,0:T(4,128)S(1)}, s32[4,4]{1,0:T(4,128)}, u32[]{:S(2)}) copy-start(s32[4,4]{1,0:T(4,128)} %mask_ref.1) | copy-start | bytes 196
  83.1 27.3 %copy-start.7 = (f32[4]{0:T(128)S(1)}, f32[4]{0:T(128)}, u32[]{:S(2)}) copy-start(f32[4]{0:T(128)} %risk_ref.1) | copy-start | bytes 52
  83.1 21.3 %all-to-all-start.1 = ((bf16[4,320,256]{2,1,0:T(8,128)(2,1)}), bf16[4,320,256]{2,1,0:T(8,128)(2,1)S(1)}, u32[]{:S(2)}, u32[]{:S(2)}) async-start(bf16[4,320,256]{2,1,0:T(8,128)(2,1)} %project.1), calls=%async_computation.1 | async-start | bytes 1310720 | tf_op jit(solution)/shard_map/all_to_all | solution.py:404
  88.3 41.4 %copy-start.2 = (bf16[256,1024]{1,0:T(8,128)(2,1)S(1)}, bf16[256,1024]{1,0:T(8,128)(2,1)}, u32[]{:S(2)}) copy-start(bf16[256,1024]{1,0:T(8,128)(2,1)} %copy-done) | copy-start | bytes 1572868
  104.5 25.3 %copy-start.5 = (bf16[256,1024]{1,0:T(8,128)(2,1)S(1)}, bf16[256,1024]{1,0:T(8,128)(2,1)}, u32[]{:S(2)}) copy-start(bf16[256,1024]{1,0:T(8,128)(2,1)} %copy-done.3) | copy-start | bytes 1572868

commit v8 on v7

--- a/solution.py
+++ b/solution.py
@@ -178,21 +178,22 @@
     return copies
 
 
-def copies_kernel(where_ref, first, second, out):
+def copies_kernel(where_ref, first, second, after, out):
+    del after
     odd = where_ref[1] % 2
     for device in range(8):
         out[device, odd] = first[...]
         out[device, 1 - odd] = second[...]
 
 
-def copies(where, first, second):
+def copies(where, first, second, after):
     return pl.pallas_call(
         copies_kernel,
         out_shape=jax.ShapeDtypeStruct((8, 2, 320, 128), BF16),
-        in_specs=[in_smem(), *in_vmem(2)],
+        in_specs=[in_smem(), *in_vmem(2), anywhere()],
         compiler_params=params(),
         name="weight_copies",
-    )(where, first, second)
+    )(where, first, second, after)
 
 
 def project_kernel(
@@ -200,14 +201,9 @@
 ):
     core = where_ref[0]
     arrivals = []
-    for number, (near, far) in enumerate(((n1, f1), (n2, f2), (n3, f3))):
-        place = tokens.at[number]
-        arrivals.append(
-            [
-                pltpu.make_async_copy(near, place.at[:, pl.ds(0, 1024)], sems.at[8 + 2 * number]),
-                pltpu.make_async_copy(far, place.at[:, pl.ds(1024, 1024)], sems.at[9 + 2 * number]),
-            ]
-        )
+    for number, far in enumerate((f1, f2, f3)):
+        place = tokens.at[number, :, pl.ds(0, 1024)]
+        arrivals.append([pltpu.make_async_copy(far, place, sems.at[8 + number])])
     arrivals.append(own_columns(where_ref, states_ref, tokens.at[3], sems))
     for copies in arrivals:
         for copy in copies:
@@ -224,13 +220,25 @@
                 w_kv[32 + 16 * head : 48 + 16 * head, lanes] = weights[
                     block, head, base + 16 : base + 32, :
                 ]
+    def product(x, rows):
+        q = jnp.dot(x, w_q[rows, :], preferred_element_type=F32)
+        kv = lax.dot_general(
+            x, w_kv[:, rows], (((1,), (1,)), ((), ())), preferred_element_type=F32
+        )
+        return q, kv
+
+    low, high = pl.ds(0, 1024), pl.ds(1024, 1024)
     departures = []
-    for number in range(4):
-        for copy in arrivals[number]:
-            copy.wait()
-        x = tokens[number]
-        q = jnp.dot(x, w_q[...], preferred_element_type=F32)
-        kv = lax.dot_general(x, w_kv[...], (((1,), (1,)), ((), ())), preferred_element_type=F32)
+    for number, near in enumerate((n1, n2, n3, None)):
+        if near is None:
+            for copy in arrivals[number]:
+                copy.wait()
+            q, kv = product(tokens[number], pl.ds(0, 2048))
+        else:
+            q_near, kv_near = product(near[...], low)
+            arrivals[number][0].wait()
+            q_far, kv_far = product(tokens[number, :, :1024], high)
+            q, kv = q_near + q_far, kv_near + kv_far
         result[number, :256, :] = q.astype(BF16)
         result[number, 256:, :] = kv.T.astype(BF16)
         other = (where_ref[1] + number + 1) % 4
@@ -246,27 +254,50 @@
     return pl.pallas_call(
         project_kernel,
         out_shape=pltpu.HBM((4, 320, 256), BF16),
-        in_specs=[in_smem(), in_hbm(), *[anywhere()] * 6, *in_vmem(1)],
+        in_specs=[in_smem(), in_hbm(), *in_vmem(3), *[in_hbm()] * 3, *in_vmem(1)],
         out_specs=in_hbm(),
         scratch_shapes=[
             pltpu.VMEM((4, TOK, 2048), BF16),
             pltpu.VMEM((2048, 256), BF16),
             pltpu.VMEM((64, 2048), BF16),
             pltpu.VMEM((4, 320, 256), BF16),
-            pltpu.SemaphoreType.DMA((14,)),
+            pltpu.SemaphoreType.DMA((11,)),
             pltpu.SemaphoreType.DMA((4,)),
         ],
         compiler_params=params(),
         name="project",
-    )(where, held(states), *near, *far, weights)
+    )(where, held(states), *near, *[held(x) for x in far], weights)
 
 
 def attend_kernel(
-    mask_ref, risk_ref, parts, kv, upstream_ref, tables_ref, attn_out, dq_out, upstream, tables, sems
+    where_ref,
+    mask_ref,
+    risk_ref,
+    parts,
+    kv,
+    upstream_ref,
+    tables_ref,
+    states_ref,
+    f1_ref,
+    f2_ref,
+    f3_ref,
+    attn_out,
+    dq_out,
+    own,
+    f1,
+    f2,
+    f3,
+    upstream,
+    tables,
+    sems,
 ):
     copies = [
-        pltpu.make_async_copy(tables_ref, tables, sems.at[0]),
-        pltpu.make_async_copy(upstream_ref, upstream, sems.at[1]),
+        pltpu.make_async_copy(tables_ref, tables, sems.at[8]),
+        pltpu.make_async_copy(upstream_ref, upstream, sems.at[9]),
+        pltpu.make_async_copy(f1_ref, f1, sems.at[10]),
+        pltpu.make_async_copy(f2_ref, f2, sems.at[11]),
+        pltpu.make_async_copy(f3_ref, f3, sems.at[12]),
+        *own_columns(where_ref, states_ref, own, sems),
     ]
     for copy in copies:
         copy.start()
@@ -281,9 +312,9 @@
         on_path = jnp.zeros((BS, TOK), jnp.int32)
         for c in range(4):
             on_path = jnp.where(column // BS == c, mask_ref[b, c], on_path)
-        seen.append((on_path > 0) & ((column // BS != b) | (column - BS * b <= row)))
+        seen.append(jnp.where((column // BS != b) | (column - BS * b <= row), on_path, 0))
         risk.append(jnp.full((BS, 1), risk_ref[b], F32))
-    seen = jnp.concatenate(seen, axis=0)
+    seen = jnp.concatenate(seen, axis=0) > 0
     risk = jnp.concatenate(risk, axis=0)
 
     copies[0].wait()
@@ -314,38 +345,47 @@
             * scaling
         )
         dq = dq_rot * cq - pltpu.roll(dq_rot, 64, 1) * sq
-        dq_out[cols, :] = dq.T.astype(BF16)
-
-
-def attend(block_mask, risk_weight, parts, kv, upstream, tables):
+        dq_out[cols, :] = dq.astype(BF16).T
+    for copy in copies[2:]:
+        copy.wait()
+
+
+def attend(where, block_mask, risk_weight, parts, kv, upstream, tables, states, far):
+    own = jax.ShapeDtypeStruct((TOK, 2048), BF16)
+    part = jax.ShapeDtypeStruct((TOK, 1024), BF16)
+    square = jax.ShapeDtypeStruct((TOK, 256), BF16)
     return pl.pallas_call(
         attend_kernel,
-        out_shape=(
-            jax.ShapeDtypeStruct((TOK, 256), BF16),
-            jax.ShapeDtypeStruct((256, TOK), BF16),
-        ),
-        in_specs=[in_smem(), in_smem(), *in_vmem(2), in_hbm(), in_hbm()],
+        out_shape=(square, square, own, part, part, part),
+        in_specs=[*[in_smem()] * 3, *in_vmem(2), *[in_hbm()] * 6],
+        out_specs=tuple(in_vmem(6)),
         scratch_shapes=[
             pltpu.VMEM((TOK, 256), BF16),
             pltpu.VMEM((TOK, 2 * HEAD), F32),
-            pltpu.SemaphoreType.DMA((2,)),
+            pltpu.SemaphoreType.DMA((13,)),
         ],
         compiler_params=params(),
         name="attend",
-    )(block_mask, risk_weight, parts, kv, held(upstream), held(tables))
-
-
-def gradient_kernel(where_ref, states_ref, n1, n2, n3, f1, f2, f3, slopes, out, own, sems):
+    )(
+        where,
+        block_mask,
+        risk_weight,
+        parts,
+        kv,
+        held(upstream),
+        held(tables),
+        held(states),
+        *[held(x) for x in far],
+    )
+
+
+def gradient_kernel(where_ref, own, n1, n2, n3, f1, f2, f3, slopes, out):
     core = where_ref[0]
-    copies = own_columns(where_ref, states_ref, own, sems)
-    for copy in copies:
-        copy.start()
     for part in range(8):
         cols = pl.ds(256 * (part % 4), 256)
         total = None
-        for number in (1, 2, 3, 0):
+        for number in range(4):
             if number == 0:
-                copies[part].wait()
                 x = own[:, pl.ds(256 * part, 256)]
             else:
                 x = ((n1, n2, n3) if part < 4 else (f1, f2, f3))[number - 1][:, cols]
@@ -354,15 +394,14 @@
         out[block_of(part, core)] = total.astype(BF16)
 
 
-def gradient(where, states, near, far, slopes):
+def gradient(where, own, near, far, slopes):
     return pl.pallas_call(
         gradient_kernel,
         out_shape=jax.ShapeDtypeStruct((8, 256, 256), BF16),
-        in_specs=[in_smem(), in_hbm(), *in_vmem(7)],
-        scratch_shapes=[pltpu.VMEM((TOK, 2048), BF16), pltpu.SemaphoreType.DMA((8,))],
+        in_specs=[in_smem(), *in_vmem(8)],
         compiler_params=params(),
         name="gradient",
-    )(where, held(states), *near, *far, slopes)
+    )(where, own, *near, *far, slopes)
 
 
 def total_kernel(terms, out):
@@ -389,9 +428,10 @@
     first, second = pack(where, query_weight, key_matrix.T, value_matrix.T)
     first = lax.ppermute(first, AXES, home_pairs(0))
     second = lax.ppermute(second, AXES, home_pairs(1))
-    weights = copies(where, first, second)
-
-    up, two, down = gate(cut(where, states), weights)
+    outgoing = cut(where, states)
+    weights = copies(where, first, second, outgoing[0])
+
+    up, two, down = gate(outgoing, weights)
     near = (
         lax.ppermute(down, AXES, ring_pairs(-1, -1)),
         lax.ppermute(two, AXES, ring_pairs(2, -2)),
@@ -414,9 +454,11 @@
     cosine, sine = jnp.cos(angles), jnp.sin(angles)
     tables = jnp.concatenate([cosine, cosine, -sine, sine], axis=1)
 
-    attn_out, dq = attend(block_mask, risk_weight, parts, kv, upstream, tables)
+    attn_out, dq, own, *far = attend(
+        where, block_mask, risk_weight, parts, kv, upstream, tables, states, far
+    )
     slopes = lax.all_gather(dq, GROUP, axis=0, tiled=False)
-    terms = gradient(where, states, near, far, slopes)
+    terms = gradient(where, own, near, far, slopes)
     terms = lax.all_to_all(terms, OTHERS, split_axis=0, concat_axis=0)
     return attn_out, add_up(terms)
 

time: 170 us -> 165 us (0.971)
  waiting for transfers between devices: 37.2 us -> 33.5 us
    ppermute x1, waiting for transfers between devices: 3.59 us -> 0.49 us  [shards(): second = lax.ppermute(second, AXES, home_pairs(1))]
    pallas_call x1, Pallas kernels: 3.58 us -> 1.79 us  [gradient(): pl.pallas_call(gradient_kernel, out_shape=jax.ShapeDtypeStruct((8, 256, 2...]
    unnamed x16 -> x10, local copies, waits for them, and re-layouts: 3.68 us -> 2.4 us
  transfers between devices with their start and end apart: 10 -> 10, of which waited for: 6 -> 6; matrix products, arithmetic and copies ran while one was open for 1% -> 1% of each run, Pallas kernels for 1% -> 2%
where the time goes in v8:
time: 165 us; the launch traced here: 162 us
  blocking collectives  54.9 us (33%)
  starting transfers between devices  50.5 us (31%)
  waiting for transfers between devices  33.5 us (20%)
  Pallas kernels  18.2 us (11%)
  local copies, waits for them, and re-layouts  2.49 us (2%)
  other arithmetic  1.73 us (1%)
    all_to_all x1, blocking collectives, shards(): terms = lax.all_to_all(terms, OTHERS, split_axis=0, concat_axis=0)  33 us
    all_to_all x1, starting transfers between devices, shards(): weights = lax.all_to_all(weights, OTHERS, split_axis=0, concat_axis=0)  17.2 us
    all_to_all x1, waiting for transfers between devices, shards(): parts = lax.all_to_all(parts, GROUP, split_axis=0, concat_axis=0)  16.2 us
    all_gather x1, blocking collectives, shards(): slopes = lax.all_gather(dq, GROUP, axis=0, tiled=False)  16.1 us
    ppermute x1, waiting for transfers between devices, shards(): lax.ppermute(down, AXES, ring_pairs(-1, -1))  11.2 us
    ppermute x1, starting transfers between devices, shards(): first = lax.ppermute(first, AXES, home_pairs(0))  7.81 us
    ppermute x3, starting transfers between devices, swap_core(): return lax.ppermute(value, 'c', [(0, 1), (1, 0)])  7.47 us
    all_gather x1, blocking collectives, shards(): kv = lax.all_gather(kv, ('xb', 'c'), axis=0, tiled=False)  5.79 us
  transfers between devices with their start and end apart: 10, of which 6 were waited for; matrix products, arithmetic and copies ran while one was open for 1% of the time, Pallas kernels for 2%

profile of v8, /device:TPU:6, one launch (start us, length us, event | category | flops | bytes accessed | tf_op | source)
XLA Modules:
  0.0 162.1 jit_solution(14081246840767835271)
XLA Ops:
  0.6 0.1 pad_add_fusion.where_ref
  0.7 1.6 pack_weights.1
  2.3 7.8 %collective-permute-start = (bf16[320,128]{1,0:T(8,128)(2,1)S(1)}, bf16[320,128]{1,0:T(8,128)(2,1)S(1)}, u32[]{:S(2)}, u32[]{:S(2)}) collective-permute-start(bf16[320,128]{1,0:T(8,128)(2,1)S(1)} %get-tuple-element.19), channel_id=1, source_target_pairs={{0,0},{1,32},{2,64},{3,96},{4,128},{5,160},{6,192},{7,224},{8,256}... | collective-permute-start | bytes 245768 | tf_op jit(solution)/shard_map/ppermute | solution.py:429
  10.1 5.7 %collective-permute-start.1 = (bf16[320,128]{1,0:T(8,128)(2,1)S(1)}, bf16[320,128]{1,0:T(8,128)(2,1)S(1)}, u32[]{:S(2)}, u32[]{:S(2)}) collective-permute-start(bf16[320,128]{1,0:T(8,128)(2,1)S(1)} %get-tuple-element.20), channel_id=1, source_target_pairs={{0,16},{1,48},{2,80},{3,112},{4,144},{5,176},{6,208},{7,240},{8,27... | collective-permute-start | bytes 245768 | tf_op jit(solution)/shard_map/ppermute | solution.py:430
  15.8 3.1 %cut_states.1 = (bf16[256,1024]{1,0:T(8,128)(2,1)S(1)}, bf16[256,1024]{1,0:T(8,128)(2,1)}, bf16[256,1024]{1,0:T(8,128)(2,1)}) custom-call(s32[3]{0:T(128)S(1)} %pad_add_fusion.where_ref, bf16[256,8192]{1,0:T(8,128)(2,1)} %states_ref.5), custom_call_target="tpu_custom_call" | custom-call | tf_op jit(solution)/shard_map/cut_states/pallas_call | solution.py:139
  18.9 0.0 collective-permute-done.first
  18.9 0.5 collective-permute-done.1.second
  19.4 1.8 %weight_copies.1.refs_3_ = bf16[8,2,320,128]{3,2,1,0:T(8,128)(2,1)} custom-call(s32[3]{0:T(128)S(1)} %pad_add_fusion.where_ref, bf16[320,128]{1,0:T(8,128)(2,1)S(1)} %collective-permute-done.first, bf16[320,128]{1,0:T(8,128)(2,1)S(1)} %collective-permute-done.1.second, bf16[256,1024]{1,0:T(8,128)(2,1)S(1)} %get-tuple-element.16.after.refs_0_), custom_call_target="tpu_custom_call" | custom-call | tf_op jit(solution)/shard_map/weight_copies/pallas_call | solution.py:190
  21.2 17.2 %all-to-all-start = ((bf16[8,2,320,128]{3,2,1,0:T(8,128)(2,1)}), bf16[8,2,320,128]{3,2,1,0:T(8,128)(2,1)S(1)}, u32[]{:S(2)}, u32[]{:S(2)}) async-start(bf16[8,2,320,128]{3,2,1,0:T(8,128)(2,1)} %weight_copies.1.refs_3_), calls=%async_computation | async-start | bytes 2621440 | tf_op jit(solution)/shard_map/all_to_all | solution.py:441
  38.4 1.9 %collective-permute-start.2 = (bf16[256,1024]{1,0:T(8,128)(2,1)}, bf16[256,1024]{1,0:T(8,128)(2,1)S(1)}, u32[]{:S(2)}, u32[]{:S(2)}) collective-permute-start(bf16[256,1024]{1,0:T(8,128)(2,1)} %get-tuple-element.21), channel_id=1, source_target_pairs={{0,56},{1,57},{2,58},{3,59},{4,60},{5,61},{6,62},{7,63},{16,0},{17... | collective-permute-start | bytes 1572872 | tf_op jit(solution)/shard_map/ppermute | solution.py:436
  40.3 4.5 %collective-permute-start.3 = (bf16[256,1024]{1,0:T(8,128)(2,1)}, bf16[256,1024]{1,0:T(8,128)(2,1)S(1)}, u32[]{:S(2)}, u32[]{:S(2)}) collective-permute-start(bf16[256,1024]{1,0:T(8,128)(2,1)} %get-tuple-element.22), channel_id=1, source_target_pairs={{0,32},{1,41},{2,34},{3,43},{4,36},{5,45},{6,38},{7,47},{16,48},{1... | collective-permute-start | bytes 1572872 | tf_op jit(solution)/shard_map/ppermute | solution.py:437
  44.9 2.4 %collective-permute-start.4 = (bf16[256,1024]{1,0:T(8,128)(2,1)S(1)}, bf16[256,1024]{1,0:T(8,128)(2,1)S(1)}, u32[]{:S(2)}, u32[]{:S(2)}) collective-permute-start(bf16[256,1024]{1,0:T(8,128)(2,1)S(1)} %get-tuple-element.23), channel_id=1, source_target_pairs={{0,16},{1,17},{2,18},{3,19},{4,20},{5,21},{6,22},{7,23},{16,32},{1... | collective-permute-start | bytes 1572872 | tf_op jit(solution)/shard_map/ppermute | solution.py:438
  47.3 11.2 %collective-permute-done.2.n1 = bf16[256,1024]{1,0:T(8,128)(2,1)S(1)} collective-permute-done((bf16[256,1024]{1,0:T(8,128)(2,1)}, bf16[256,1024]{1,0:T(8,128)(2,1)S(1)}, u32[]{:S(2)}, u32[]{:S(2)}) %collective-permute-start.2) | collective-permute-done | bytes 524320 | tf_op jit(solution)/shard_map/ppermute | solution.py:436
  58.5 1.9 %collective-permute-start.5 = (bf16[256,1024]{1,0:T(8,128)(2,1)S(1)}, bf16[256,1024]{1,0:T(8,128)(2,1)S(1)}, u32[]{:S(2)}, u32[]{:S(2)}) collective-permute-start(bf16[256,1024]{1,0:T(8,128)(2,1)S(1)} %collective-permute-done.2.n1), channel_id=1, source_target_pairs={{0,1},{1,0},{2,3},{3,2},{4,5},{5,4},{6,7},{7,6},{8,9},{9,8},{10,11... | collective-permute-start | bytes 1572872 | tf_op jit(solution)/shard_map/ppermute | solution.py:53
  60.5 1.2 collective-permute-done.3.n2
  61.7 3.6 %collective-permute-start.6 = (bf16[256,1024]{1,0:T(8,128)(2,1)S(1)}, bf16[256,1024]{1,0:T(8,128)(2,1)S(1)}, u32[]{:S(2)}, u32[]{:S(2)}) collective-permute-start(bf16[256,1024]{1,0:T(8,128)(2,1)S(1)} %collective-permute-done.3.n2), channel_id=1, source_target_pairs={{0,1},{1,0},{2,3},{3,2},{4,5},{5,4},{6,7},{7,6},{8,9},{9,8},{10,11... | collective-permute-start | bytes 1572872 | tf_op jit(solution)/shard_map/ppermute | solution.py:53
  65.3 4.0 %collective-permute-done.4.n3 = bf16[256,1024]{1,0:T(8,128)(2,1)S(1)} collective-permute-done((bf16[256,1024]{1,0:T(8,128)(2,1)S(1)}, bf16[256,1024]{1,0:T(8,128)(2,1)S(1)}, u32[]{:S(2)}, u32[]{:S(2)}) %collective-permute-start.4) | collective-permute-done | bytes 524320 | tf_op jit(solution)/shard_map/ppermute | solution.py:438
  69.4 1.9 %collective-permute-start.7 = (bf16[256,1024]{1,0:T(8,128)(2,1)S(1)}, bf16[256,1024]{1,0:T(8,128)(2,1)S(1)}, u32[]{:S(2)}, u32[]{:S(2)}) collective-permute-start(bf16[256,1024]{1,0:T(8,128)(2,1)S(1)} %collective-permute-done.4.n3), channel_id=1, source_target_pairs={{0,1},{1,0},{2,3},{3,2},{4,5},{5,4},{6,7},{7,6},{8,9},{9,8},{10,11... | collective-permute-start | bytes 1572872 | tf_op jit(solution)/shard_map/ppermute | solution.py:53
  71.3 0.0 collective-permute-done.5.f1.f1_ref
  71.3 0.0 copy-start.2
  71.3 0.0 collective-permute-done.6.f2.f2_ref
  71.3 0.8 copy-done.2
  72.1 0.0 copy-start.3
  72.1 0.8 copy-done.3
  72.9 0.3 collective-permute-done.7.f3.f3_ref
  73.2 0.0 copy-start.4
  73.2 0.0 all-to-all-done.weights
  73.2 0.8 copy-done.4
  74.0 5.5 %project.1 = bf16[4,320,256]{2,1,0:T(8,128)(2,1)} custom-call(s32[3]{0:T(128)S(1)} %pad_add_fusion.where_ref, bf16[256,8192]{1,0:T(8,128)(2,1)} %states_ref.5, bf16[256,1024]{1,0:T(8,128)(2,1)S(1)} %collective-permute-done.2.n1, bf16[256,1024]{1,0:T(8,128)(2,1)S(1)} %collective-permute-done.3.n2, bf16[256,1024]{1,0:T(8,128)(2,1)S(1)} %collective-permute-done.4.n3, ...), custom_call_target="tpu_custom_call" | custom-call | tf_op jit(solution)/shard_map/project/pallas_call | solution.py:254
  79.5 0.0 copy-start
  79.5 0.0 copy-start.1
  79.6 3.5 %all-to-all-start.1 = ((bf16[4,320,256]{2,1,0:T(8,128)(2,1)}), bf16[4,320,256]{2,1,0:T(8,128)(2,1)S(1)}, u32[]{:S(2)}, u32[]{:S(2)}) async-start(bf16[4,320,256]{2,1,0:T(8,128)(2,1)} %project.1), calls=%async_computation.1 | async-start | bytes 1310720 | tf_op jit(solution)/shard_map/all_to_all | solution.py:444
  83.1 0.0 copy-done
  83.1 0.1 reduce_sum.19
  83.2 0.1 add_convert_fusion
  83.3 0.1 convert_element_type.15
  83.4 0.5 multiply_cosine_fusion
  83.9 0.9 pad_maximum_fusion.tables_ref
  84.8 16.2 %all-to-all-done.1.parts = bf16[4,320,256]{2,1,0:T(8,128)(2,1)S(1)} async-done(((bf16[4,320,256]{2,1,0:T(8,128)(2,1)}), bf16[4,320,256]{2,1,0:T(8,128)(2,1)S(1)}, u32[]{:S(2)}, u32[]{:S(2)}) %all-to-all-start.1) | async-done | bytes 655392 | tf_op jit(solution)/shard_map/all_to_all | solution.py:444
  101.0 5.8 %all-gather = f32[256,256]{1,0:T(8,128)S(1)} all-gather(f32[64,256]{1,0:T(8,128)S(1)} %convert_reduce_fusion), channel_id=2, replica_groups=mesh['zh'=4,'zb'=2,'yu'=2,'yb'=2,'yh'=2,'xh'=2,'xb'=2,'c'=2] {'xb','c'}, dimensions={0}, use_global_device_ids=true | all-gather | bytes 327680 | tf_op jit(solution)/shard_map/all_gather | solution.py:446
  106.8 0.0 copy-done.1
  106.8 3.4 %attend.1 = (bf16[256,256]{1,0:T(8,128)(2,1)}, bf16[256,256]{1,0:T(8,128)(2,1)S(1)}, bf16[256,2048]{1,0:T(8,128)(2,1)S(1)}, bf16[256,1024]{1,0:T(8,128)(2,1)S(1)...) custom-call(s32[3]{0:T(128)S(1)} %pad_add_fusion.where_ref, s32[4,4]{1,0:T(4,128)S(1)} %copy-done, ...), custom_call_target="tpu_custom_call" | custom-call | tf_op jit(solution)/shard_map/attend/pallas_call | solution.py:357
  110.3 16.1 %all-gather.1 = bf16[1024,256]{1,0:T(8,128)(2,1)S(1)} all-gather(bf16[256,256]{1,0:T(8,128)(2,1)S(1)} %get-tuple-element.29), channel_id=3, replica_groups=mesh['zh'=4,'zb'=2,'yu'=2,'yb'=2,'yh'=2,'xh'=2,'xb'=2,'c'=2] {'yu','yb'}, dimensions={0}, use_global_device_ids=true | all-gather | bytes 655360 | tf_op jit(solution)/shard_map/all_gather | solution.py:460
  126.4 1.8 %gradient.1 = bf16[8,256,256]{2,1,0:T(8,128)(2,1)S(1)} custom-call(s32[3]{0:T(128)S(1)} %pad_add_fusion.where_ref, bf16[256,2048]{1,0:T(8,128)(2,1)S(1)} %get-tuple-element.25.own, bf16[256,1024]{1,0:T(8,128)(2,1)S(1)} %collective-permute-done.2.n1, bf16[256,1024]{1,0:T(8,128)(2,1)S(1)} %collective-permute-done.3.n2, ...), custom_call_target="tpu_custom_call" | custom-call | tf_op jit(solution)/shard_map/gradient/pallas_call | solution.py:398
  128.2 33.0 %all_to_all.15.terms = bf16[8,256,256]{2,1,0:T(8,128)(2,1)S(1)} all-to-all(bf16[8,256,256]{2,1,0:T(8,128)(2,1)S(1)} %gradient.1), channel_id=1, replica_groups=mesh['zh'=4,'zb'=2,'yu'=2,'yb'=2,'yh'=2,'xh'=2,'xb'=2,'c'=2] {'zh','zb'}, dimensions={0} | all-to-all | bytes 2097152 | tf_op jit(solution)/shard_map/all_to_all | solution.py:462
  161.2 0.9 add_up.1
  (4 shorter events, 0.0 us)
Async XLA Ops:
  2.3 16.6 %collective-permute-start = (bf16[320,128]{1,0:T(8,128)(2,1)S(1)}, bf16[320,128]{1,0:T(8,128)(2,1)S(1)}, u32[]{:S(2)}, u32[]{:S(2)}) collective-permute-start(bf16[320,128]{1,0:T(8,128)(2,1)S(1)} %get-tuple-element.19), channel_id=1, source_target_pairs={{0,0},{1,32},{2,64},{3,96},{4,128},{5,160},{6,192},{7,224},{8,256}... | collective-permute-start | bytes 245768 | tf_op jit(solution)/shard_map/ppermute | solution.py:429
  10.1 9.3 %collective-permute-start.1 = (bf16[320,128]{1,0:T(8,128)(2,1)S(1)}, bf16[320,128]{1,0:T(8,128)(2,1)S(1)}, u32[]{:S(2)}, u32[]{:S(2)}) collective-permute-start(bf16[320,128]{1,0:T(8,128)(2,1)S(1)} %get-tuple-element.20), channel_id=1, source_target_pairs={{0,16},{1,48},{2,80},{3,112},{4,144},{5,176},{6,208},{7,240},{8,27... | collective-permute-start | bytes 245768 | tf_op jit(solution)/shard_map/ppermute | solution.py:430
  21.2 51.9 %all-to-all-start = ((bf16[8,2,320,128]{3,2,1,0:T(8,128)(2,1)}), bf16[8,2,320,128]{3,2,1,0:T(8,128)(2,1)S(1)}, u32[]{:S(2)}, u32[]{:S(2)}) async-start(bf16[8,2,320,128]{3,2,1,0:T(8,128)(2,1)} %weight_copies.1.refs_3_), calls=%async_computation | async-start | bytes 2621440 | tf_op jit(solution)/shard_map/all_to_all | solution.py:441
  38.4 20.1 %collective-permute-start.2 = (bf16[256,1024]{1,0:T(8,128)(2,1)}, bf16[256,1024]{1,0:T(8,128)(2,1)S(1)}, u32[]{:S(2)}, u32[]{:S(2)}) collective-permute-start(bf16[256,1024]{1,0:T(8,128)(2,1)} %get-tuple-element.21), channel_id=1, source_target_pairs={{0,56},{1,57},{2,58},{3,59},{4,60},{5,61},{6,62},{7,63},{16,0},{17... | collective-permute-start | bytes 1572872 | tf_op jit(solution)/shard_map/ppermute | solution.py:436
  40.3 21.3 %collective-permute-start.3 = (bf16[256,1024]{1,0:T(8,128)(2,1)}, bf16[256,1024]{1,0:T(8,128)(2,1)S(1)}, u32[]{:S(2)}, u32[]{:S(2)}) collective-permute-start(bf16[256,1024]{1,0:T(8,128)(2,1)} %get-tuple-element.22), channel_id=1, source_target_pairs={{0,32},{1,41},{2,34},{3,43},{4,36},{5,45},{6,38},{7,47},{16,48},{1... | collective-permute-start | bytes 1572872 | tf_op jit(solution)/shard_map/ppermute | solution.py:437
  44.9 24.5 %collective-permute-start.4 = (bf16[256,1024]{1,0:T(8,128)(2,1)S(1)}, bf16[256,1024]{1,0:T(8,128)(2,1)S(1)}, u32[]{:S(2)}, u32[]{:S(2)}) collective-permute-start(bf16[256,1024]{1,0:T(8,128)(2,1)S(1)} %get-tuple-element.23), channel_id=1, source_target_pairs={{0,16},{1,17},{2,18},{3,19},{4,20},{5,21},{6,22},{7,23},{16,32},{1... | collective-permute-start | bytes 1572872 | tf_op jit(solution)/shard_map/ppermute | solution.py:438
  58.5 12.8 %collective-permute-start.5 = (bf16[256,1024]{1,0:T(8,128)(2,1)S(1)}, bf16[256,1024]{1,0:T(8,128)(2,1)S(1)}, u32[]{:S(2)}, u32[]{:S(2)}) collective-permute-start(bf16[256,1024]{1,0:T(8,128)(2,1)S(1)} %collective-permute-done.2.n1), channel_id=1, source_target_pairs={{0,1},{1,0},{2,3},{3,2},{4,5},{5,4},{6,7},{7,6},{8,9},{9,8},{10,11... | collective-permute-start | bytes 1572872 | tf_op jit(solution)/shard_map/ppermute | solution.py:53
  61.7 9.6 %collective-permute-start.6 = (bf16[256,1024]{1,0:T(8,128)(2,1)S(1)}, bf16[256,1024]{1,0:T(8,128)(2,1)S(1)}, u32[]{:S(2)}, u32[]{:S(2)}) collective-permute-start(bf16[256,1024]{1,0:T(8,128)(2,1)S(1)} %collective-permute-done.3.n2), channel_id=1, source_target_pairs={{0,1},{1,0},{2,3},{3,2},{4,5},{5,4},{6,7},{7,6},{8,9},{9,8},{10,11... | collective-permute-start | bytes 1572872 | tf_op jit(solution)/shard_map/ppermute | solution.py:53
  69.4 3.8 %collective-permute-start.7 = (bf16[256,1024]{1,0:T(8,128)(2,1)S(1)}, bf16[256,1024]{1,0:T(8,128)(2,1)S(1)}, u32[]{:S(2)}, u32[]{:S(2)}) collective-permute-start(bf16[256,1024]{1,0:T(8,128)(2,1)S(1)} %collective-permute-done.4.n3), channel_id=1, source_target_pairs={{0,1},{1,0},{2,3},{3,2},{4,5},{5,4},{6,7},{7,6},{8,9},{9,8},{10,11... | collective-permute-start | bytes 1572872 | tf_op jit(solution)/shard_map/ppermute | solution.py:53
  71.3 0.8 copy-start.2
  72.1 0.8 copy-start.3
  73.2 0.8 copy-start.4
  79.5 3.5 %copy-start = (s32[4,4]{1,0:T(4,128)S(1)}, s32[4,4]{1,0:T(4,128)}, u32[]{:S(2)}) copy-start(s32[4,4]{1,0:T(4,128)} %mask_ref.1) | copy-start | bytes 196
  79.5 27.3 %copy-start.1 = (f32[4]{0:T(128)S(1)}, f32[4]{0:T(128)}, u32[]{:S(2)}) copy-start(f32[4]{0:T(128)} %risk_ref.1) | copy-start | bytes 52
  79.6 21.5 %all-to-all-start.1 = ((bf16[4,320,256]{2,1,0:T(8,128)(2,1)}), bf16[4,320,256]{2,1,0:T(8,128)(2,1)S(1)}, u32[]{:S(2)}, u32[]{:S(2)}) async-start(bf16[4,320,256]{2,1,0:T(8,128)(2,1)} %project.1), calls=%async_computation.1 | async-start | bytes 1310720 | tf_op jit(solution)/shard_map/all_to_all | solution.py:444

commit v9 on v8

--- a/solution.py
+++ b/solution.py
@@ -15,6 +15,7 @@
 SIZES = (4, 2, 2, 2, 2, 2, 2, 2)
 GROUP = ("yu", "yb")
 OTHERS = ("zh", "zb")
+SENDERS = ("zh", "zb", "yb")
 F32 = jnp.float32
 BF16 = jnp.bfloat16
 VMEM_LIMIT = 16 * 1024 * 1024
@@ -24,12 +25,11 @@
     return pltpu.CompilerParams(vmem_limit_bytes=VMEM_LIMIT)
 
 
-def home_pairs(turn):
+def home_pairs():
     pairs = []
     for d in range(32):
         for t in range(16):
-            half = (d % 2) ^ turn
-            block = 4 * ((t // 2) ^ (d // 4)) + 2 * (t % 2) + half
+            block = 4 * ((t // 2) ^ (d // 4)) + 2 * (t % 2) + d % 2
             pairs.append((d * 16 + t, block * 16 + d // 2))
     return pairs
 
@@ -81,67 +81,71 @@
     return pl.BlockSpec(memory_space=pl.ANY)
 
 
-def pack_kernel(where_ref, query, key_t, value_t, first, second, sems):
-    odd = where_ref[1] % 2
+def pack_kernel(query, key_t, value_t, out, sems):
     copies = []
 
     def copy(source, target):
         copies.append(pltpu.make_async_copy(source, target, sems.at[len(copies)]))
         copies[-1].start()
 
-    for turn, out in enumerate((first, second)):
-        half = odd ^ turn
-        rows = pl.ds(pl.multiple_of(256 * half, 256), 256)
-        copy(query.at[rows, :], out.at[pl.ds(0, 256), :])
+    for half in range(2):
+        copy(query.at[pl.ds(256 * half, 256), :], out.at[half, pl.ds(0, 256), :])
         for chunk in range(2):
-            lanes = pl.ds(pl.multiple_of(256 * half + 128 * chunk, 128), 128)
+            lanes = pl.ds(256 * half + 128 * chunk, 128)
             base = 256 + 32 * chunk
-            copy(key_t.at[:, lanes], out.at[pl.ds(base, 16), :])
-            copy(value_t.at[:, lanes], out.at[pl.ds(base + 16, 16), :])
+            copy(key_t.at[:, lanes], out.at[half, pl.ds(base, 16), :])
+            copy(value_t.at[:, lanes], out.at[half, pl.ds(base + 16, 16), :])
     for each in copies:
         each.wait()
 
 
-def pack(where, query, key_t, value_t):
-    part = jax.ShapeDtypeStruct((320, 128), BF16)
+def pack(query, key_t, value_t):
     return pl.pallas_call(
         pack_kernel,
-        out_shape=(part, part),
-        in_specs=[in_smem(), in_hbm(), in_hbm(), in_hbm()],
-        out_specs=tuple(in_vmem(2)),
+        out_shape=jax.ShapeDtypeStruct((2, 320, 128), BF16),
+        in_specs=[in_hbm(), in_hbm(), in_hbm()],
+        out_specs=in_vmem(1)[0],
         scratch_shapes=[pltpu.SemaphoreType.DMA((10,))],
         compiler_params=params(),
         name="pack_weights",
-    )(where, held(query), held(key_t), held(value_t))
-
-
-def cut_kernel(where_ref, states_ref, up_ref, two_ref, down_ref, sems):
+    )(held(query), held(key_t), held(value_t))
+
+
+def cut_kernel(where_ref, states_ref, up_ref, two_ref, down_ref, columns, sems, out_sems):
     core, place = where_ref[0], where_ref[1]
     copies = []
-    for number, out in enumerate((up_ref, two_ref, down_ref)):
+    for number in range(3):
         for part in range(4):
             start = column_of(block_of(part, core), (place + number + 1) % 4)
             copies.append(
                 pltpu.make_async_copy(
                     states_ref.at[:, pl.ds(start, 256)],
-                    out.at[:, pl.ds(256 * part, 256)],
+                    columns.at[number, :, pl.ds(256 * part, 256)],
                     sems.at[len(copies)],
                 )
             )
-    for copy in copies:
-        copy.start()
-    for copy in copies:
+            copies[-1].start()
+    departures = []
+    for number, out in enumerate((up_ref, two_ref, down_ref)):
+        for copy in copies[4 * number : 4 * number + 4]:
+            copy.wait()
+        departures.append(pltpu.make_async_copy(columns.at[number], out, out_sems.at[number]))
+        departures[-1].start()
+    for copy in departures:
         copy.wait()
 
 
 def cut(where, states):
-    part = jax.ShapeDtypeStruct((TOK, 1024), BF16)
     return pl.pallas_call(
         cut_kernel,
-        out_shape=(part, part, part),
+        out_shape=(pltpu.HBM((TOK, 1024), BF16),) * 3,
         in_specs=[in_smem(), in_hbm()],
-        out_specs=tuple(in_vmem(3)),
-        scratch_shapes=[pltpu.SemaphoreType.DMA((12,))],
+        out_specs=(in_hbm(),) * 3,
+        scratch_shapes=[
+            pltpu.VMEM((3, TOK, 1024), BF16),
+            pltpu.SemaphoreType.DMA((12,)),
+            pltpu.SemaphoreType.DMA((3,)),
+        ],
         compiler_params=params(),
         name="cut_states",
     )(where, held(states))
@@ -155,13 +159,13 @@
     count = len(parts)
     return pl.pallas_call(
         gate_kernel,
-        out_shape=tuple(jax.ShapeDtypeStruct(x.shape, x.dtype) for x in parts),
-        in_specs=[anywhere()] * (count + 1),
-        out_specs=tuple([anywhere()] * count),
+        out_shape=tuple(pltpu.HBM(x.shape, x.dtype) for x in parts),
+        in_specs=[*[in_hbm()] * count, anywhere()],
+        out_specs=tuple([in_hbm()] * count),
         input_output_aliases={i: i for i in range(count)},
         compiler_params=params(),
         name="gate",
-    )(*parts, after)
+    )(*[held(x) for x in parts], after)
 
 
 def own_columns(where_ref, states_ref, own, sems):
@@ -178,36 +182,29 @@
     return copies
 
 
-def copies_kernel(where_ref, first, second, after, out):
+def copies_kernel(piece, after, out):
     del after
-    odd = where_ref[1] % 2
     for device in range(8):
-        out[device, odd] = first[...]
-        out[device, 1 - odd] = second[...]
-
-
-def copies(where, first, second, after):
+        out[device] = piece[...]
+
+
+def copies(piece, after):
     return pl.pallas_call(
         copies_kernel,
         out_shape=jax.ShapeDtypeStruct((8, 2, 320, 128), BF16),
-        in_specs=[in_smem(), *in_vmem(2), anywhere()],
+        in_specs=[*in_vmem(1), anywhere()],
         compiler_params=params(),
         name="weight_copies",
-    )(where, first, second, after)
+    )(piece, after)
 
 
 def project_kernel(
-    where_ref, states_ref, n1, n2, n3, f1, f2, f3, weights, out, tokens, w_q, w_kv, result, sems, out_sems
+    where_ref, states_ref, n1, n2, n3, f1, f2, f3, weights, out, own, w_q, w_kv, result, sems, out_sems
 ):
     core = where_ref[0]
-    arrivals = []
-    for number, far in enumerate((f1, f2, f3)):
-        place = tokens.at[number, :, pl.ds(0, 1024)]
-        arrivals.append([pltpu.make_async_copy(far, place, sems.at[8 + number])])
-    arrivals.append(own_columns(where_ref, states_ref, tokens.at[3], sems))
-    for copies in arrivals:
-        for copy in copies:
-            copy.start()
+    copies = own_columns(where_ref, states_ref, own, sems)
+    for copy in copies:
+        copy.start()
     for part in range(8):
         block = block_of(part, core) ^ where_ref[2]
         for head in range(2):
@@ -229,15 +226,14 @@
 
     low, high = pl.ds(0, 1024), pl.ds(1024, 1024)
     departures = []
-    for number, near in enumerate((n1, n2, n3, None)):
+    for number, (near, far) in enumerate(((n1, f1), (n2, f2), (n3, f3), (None, None))):
         if near is None:
-            for copy in arrivals[number]:
+            for copy in copies:
                 copy.wait()
-            q, kv = product(tokens[number], pl.ds(0, 2048))
+            q, kv = product(own[...], pl.ds(0, 2048))
         else:
             q_near, kv_near = product(near[...], low)
-            arrivals[number][0].wait()
-            q_far, kv_far = product(tokens[number, :, :1024], high)
+            q_far, kv_far = product(far[...], high)
             q, kv = q_near + q_far, kv_near + kv_far
         result[number, :256, :] = q.astype(BF16)
         result[number, 256:, :] = kv.T.astype(BF16)
@@ -254,19 +250,19 @@
     return pl.pallas_call(
         project_kernel,
         out_shape=pltpu.HBM((4, 320, 256), BF16),
-        in_specs=[in_smem(), in_hbm(), *in_vmem(3), *[in_hbm()] * 3, *in_vmem(1)],
+        in_specs=[in_smem(), in_hbm(), *in_vmem(7)],
         out_specs=in_hbm(),
         scratch_shapes=[
-            pltpu.VMEM((4, TOK, 2048), BF16),
+            pltpu.VMEM((TOK, 2048), BF16),
             pltpu.VMEM((2048, 256), BF16),
             pltpu.VMEM((64, 2048), BF16),
             pltpu.VMEM((4, 320, 256), BF16),
-            pltpu.SemaphoreType.DMA((11,)),
+            pltpu.SemaphoreType.DMA((8,)),
             pltpu.SemaphoreType.DMA((4,)),
         ],
         compiler_params=params(),
         name="project",
-    )(where, held(states), *near, *[held(x) for x in far], weights)
+    )(where, held(states), *near, *far, weights)
 
 
 def attend_kernel(
@@ -278,15 +274,9 @@
     upstream_ref,
     tables_ref,
     states_ref,
-    f1_ref,
-    f2_ref,
-    f3_ref,
     attn_out,
     dq_out,
     own,
-    f1,
-    f2,
-    f3,
     upstream,
     tables,
     sems,
@@ -294,9 +284,6 @@
     copies = [
         pltpu.make_async_copy(tables_ref, tables, sems.at[8]),
         pltpu.make_async_copy(upstream_ref, upstream, sems.at[9]),
-        pltpu.make_async_copy(f1_ref, f1, sems.at[10]),
-        pltpu.make_async_copy(f2_ref, f2, sems.at[11]),
-        pltpu.make_async_copy(f3_ref, f3, sems.at[12]),
         *own_columns(where_ref, states_ref, own, sems),
     ]
     for copy in copies:
@@ -350,19 +337,18 @@
         copy.wait()
 
 
-def attend(where, block_mask, risk_weight, parts, kv, upstream, tables, states, far):
+def attend(where, block_mask, risk_weight, parts, kv, upstream, tables, states):
     own = jax.ShapeDtypeStruct((TOK, 2048), BF16)
-    part = jax.ShapeDtypeStruct((TOK, 1024), BF16)
     square = jax.ShapeDtypeStruct((TOK, 256), BF16)
     return pl.pallas_call(
         attend_kernel,
-        out_shape=(square, square, own, part, part, part),
-        in_specs=[*[in_smem()] * 3, *in_vmem(2), *[in_hbm()] * 6],
-        out_specs=tuple(in_vmem(6)),
+        out_shape=(square, square, own),
+        in_specs=[*[in_smem()] * 3, *in_vmem(2), *[in_hbm()] * 3],
+        out_specs=tuple(in_vmem(3)),
         scratch_shapes=[
             pltpu.VMEM((TOK, 256), BF16),
             pltpu.VMEM((TOK, 2 * HEAD), F32),
-            pltpu.SemaphoreType.DMA((13,)),
+            pltpu.SemaphoreType.DMA((10,)),
         ],
         compiler_params=params(),
         name="attend",
@@ -375,7 +361,6 @@
         held(upstream),
         held(tables),
         held(states),
-        *[held(x) for x in far],
     )
 
 
@@ -425,11 +410,10 @@
     plane = lax.axis_index(("yh", "xh", "xb"))
     where = jnp.stack([lax.axis_index("c"), place, plane]).astype(jnp.int32)
 
-    first, second = pack(where, query_weight, key_matrix.T, value_matrix.T)
-    first = lax.ppermute(first, AXES, home_pairs(0))
-    second = lax.ppermute(second, AXES, home_pairs(1))
+    piece = pack(query_weight, key_matrix.T, value_matrix.T)
+    piece = lax.ppermute(piece, AXES, home_pairs())
     outgoing = cut(where, states)
-    weights = copies(where, first, second, outgoing[0])
+    weights = copies(piece, outgoing[0])
 
     up, two, down = gate(outgoing, weights)
     near = (
@@ -438,7 +422,9 @@
         lax.ppermute(up, AXES, ring_pairs(1, 1)),
     )
     far = [swap_core(x) for x in near]
-    weights = lax.all_to_all(weights, OTHERS, split_axis=0, concat_axis=0)
+    weights = lax.all_to_all(
+        weights.reshape(16, 320, 128), SENDERS, split_axis=0, concat_axis=0
+    ).reshape(8, 2, 320, 128)
 
     parts = project(where, states, near, far, weights)
     parts = lax.all_to_all(parts, GROUP, split_axis=0, concat_axis=0)
@@ -454,8 +440,8 @@
     cosine, sine = jnp.cos(angles), jnp.sin(angles)
     tables = jnp.concatenate([cosine, cosine, -sine, sine], axis=1)
 
-    attn_out, dq, own, *far = attend(
-        where, block_mask, risk_weight, parts, kv, upstream, tables, states, far
+    attn_out, dq, own = attend(
+        where, block_mask, risk_weight, parts, kv, upstream, tables, states
     )
     slopes = lax.all_gather(dq, GROUP, axis=0, tiled=False)
     terms = gradient(where, own, near, far, slopes)

time: 165 us -> 184 us (1.12)
  waiting for transfers between devices: 33.5 us -> 50 us
  local copies, waits for them, and re-layouts: 2.49 us -> 4.81 us
    ppermute x1, waiting for transfers between devices: 11.2 us -> 29.9 us  [shards(): lax.ppermute(down, AXES, ring_pairs(-1, -1))]
    ppermute x2 -> x1, starting transfers between devices: 13.5 us -> 7.81 us  [shards(): piece = lax.ppermute(piece, AXES, home_pairs())]
    all_to_all x1, starting transfers between devices: 3.49 us -> 8.21 us  [shards(): parts = lax.all_to_all(parts, GROUP, split_axis=0, concat_axis=0)]
    ppermute x1, waiting for transfers between devices: 4.05 us -> 0.01 us  [shards(): lax.ppermute(up, AXES, ring_pairs(1, 1))]
    all_to_all x1, starting transfers between devices: 17.2 us -> 20.1 us  [shards(): lax.all_to_all(weights.reshape(16, 320, 128), SENDERS, split_axis=0, conc...]
    ppermute x2 -> x1, waiting for transfers between devices: 0.49 us -> 3.16 us  [shards(): piece = lax.ppermute(piece, AXES, home_pairs())]
    unnamed x10 -> x18, local copies, waits for them, and re-layouts: 2.4 us -> 4.72 us
  transfers between devices with their start and end apart: 10 -> 9, of which waited for: 6 -> 4; matrix products, arithmetic and copies ran while one was open for 1% -> 1% of each run, Pallas kernels for 2% -> 2%
where the time goes in v9:
time: 184 us; the launch traced here: 182 us
  blocking collectives  56.1 us (30%)
  starting transfers between devices  51.5 us (28%)
  waiting for transfers between devices  50 us (27%)
  Pallas kernels  16.6 us (9%)
  local copies, waits for them, and re-layouts  4.81 us (3%)
    all_to_all x1, blocking collectives, shards(): terms = lax.all_to_all(terms, OTHERS, split_axis=0, concat_axis=0)  34.1 us
    ppermute x1, waiting for transfers between devices, shards(): lax.ppermute(down, AXES, ring_pairs(-1, -1))  29.9 us
    all_to_all x1, starting transfers between devices, shards(): lax.all_to_all(weights.reshape(16, 320, 128), SENDERS, split_axis=0, conc...  20.1 us
    all_gather x1, blocking collectives, shards(): slopes = lax.all_gather(dq, GROUP, axis=0, tiled=False)  16.1 us
    all_to_all x1, waiting for transfers between devices, shards(): parts = lax.all_to_all(parts, GROUP, split_axis=0, concat_axis=0)  15.9 us
    all_to_all x1, starting transfers between devices, shards(): parts = lax.all_to_all(parts, GROUP, split_axis=0, concat_axis=0)  8.21 us
    ppermute x1, starting transfers between devices, shards(): piece = lax.ppermute(piece, AXES, home_pairs())  7.81 us
    ppermute x3, starting transfers between devices, swap_core(): return lax.ppermute(value, 'c', [(0, 1), (1, 0)])  6.24 us
  transfers between devices with their start and end apart: 9, of which 4 were waited for; matrix products, arithmetic and copies ran while one was open for 1% of the time, Pallas kernels for 2%

profile of v9, /device:TPU:6, one launch (start us, length us, event | category | flops | bytes accessed | tf_op | source)
XLA Modules:
  0.0 181.6 jit_solution(16240272019987585133)
XLA Ops:
  0.6 1.0 pack_weights.1
  1.7 7.8 %collective-permute-start = (bf16[2,320,128]{2,1,0:T(8,128)(2,1)S(1)}, bf16[2,320,128]{2,1,0:T(8,128)(2,1)S(1)}, u32[]{:S(2)}, u32[]{:S(2)}) collective-permute-start(bf16[2,320,128]{2,1,0:T(8,128)(2,1)S(1)} %pack_weights.1), channel_id=1, source_target_pairs={{0,0},{1,32},{2,64},{3,96},{4,128},{5,160},{6,192},{7,224},{8,256}... | collective-permute-start | bytes 491528 | tf_op jit(solution)/shard_map/ppermute | solution.py:414
  9.5 0.1 pad_add_fusion.where_ref
  9.6 3.0 %cut_states.1 = (bf16[256,1024]{1,0:T(8,128)(2,1)}, bf16[256,1024]{1,0:T(8,128)(2,1)}, bf16[256,1024]{1,0:T(8,128)(2,1)}) custom-call(s32[3]{0:T(128)S(1)} %pad_add_fusion.where_ref, bf16[256,8192]{1,0:T(8,128)(2,1)} %states_ref.5), custom_call_target="tpu_custom_call" | custom-call | tf_op jit(solution)/shard_map/cut_states/pallas_call | solution.py:139
  12.6 3.2 %collective-permute-done.piece = bf16[2,320,128]{2,1,0:T(8,128)(2,1)S(1)} collective-permute-done((bf16[2,320,128]{2,1,0:T(8,128)(2,1)S(1)}, bf16[2,320,128]{2,1,0:T(8,128)(2,1)S(1)}, u32[]{:S(2)}, u32[]{:S(2)}) %collective-permute-start) | collective-permute-done | bytes 163872 | tf_op jit(solution)/shard_map/ppermute | solution.py:414
  15.7 0.0 copy-start.6
  15.7 1.0 copy-done.6
  16.8 1.3 weight_copies.1.refs_3_
  18.0 20.1 %all-to-all-start = ((bf16[16,320,128]{2,1,0:T(8,128)(2,1)}), bf16[16,320,128]{2,1,0:T(8,128)(2,1)S(1)}, u32[]{:S(2)}, u32[]{:S(2)}) async-start(bf16[16,320,128]{2,1,0:T(8,128)(2,1)} %bitcast.5), calls=%async_computation | async-start | bytes 2621440 | tf_op jit(solution)/shard_map/all_to_all | solution.py:425
  38.1 1.9 %collective-permute-start.1 = (bf16[256,1024]{1,0:T(8,128)(2,1)}, bf16[256,1024]{1,0:T(8,128)(2,1)S(1)}, u32[]{:S(2)}, u32[]{:S(2)}) collective-permute-start(bf16[256,1024]{1,0:T(8,128)(2,1)} %get-tuple-element.14), channel_id=1, source_target_pairs={{0,56},{1,57},{2,58},{3,59},{4,60},{5,61},{6,62},{7,63},{16,0},{17... | collective-permute-start | bytes 1572872 | tf_op jit(solution)/shard_map/ppermute | solution.py:420
  40.1 5.3 %collective-permute-start.2 = (bf16[256,1024]{1,0:T(8,128)(2,1)}, bf16[256,1024]{1,0:T(8,128)(2,1)S(1)}, u32[]{:S(2)}, u32[]{:S(2)}) collective-permute-start(bf16[256,1024]{1,0:T(8,128)(2,1)} %get-tuple-element.15), channel_id=1, source_target_pairs={{0,32},{1,41},{2,34},{3,43},{4,36},{5,45},{6,38},{7,47},{16,48},{1... | collective-permute-start | bytes 1572872 | tf_op jit(solution)/shard_map/ppermute | solution.py:421
  45.4 1.9 %collective-permute-start.3 = (bf16[256,1024]{1,0:T(8,128)(2,1)}, bf16[256,1024]{1,0:T(8,128)(2,1)S(1)}, u32[]{:S(2)}, u32[]{:S(2)}) collective-permute-start(bf16[256,1024]{1,0:T(8,128)(2,1)} %get-tuple-element.16), channel_id=1, source_target_pairs={{0,16},{1,17},{2,18},{3,19},{4,20},{5,21},{6,22},{7,23},{16,32},{1... | collective-permute-start | bytes 1572872 | tf_op jit(solution)/shard_map/ppermute | solution.py:422
  47.3 29.9 %collective-permute-done.1.n1 = bf16[256,1024]{1,0:T(8,128)(2,1)S(1)} collective-permute-done((bf16[256,1024]{1,0:T(8,128)(2,1)}, bf16[256,1024]{1,0:T(8,128)(2,1)S(1)}, u32[]{:S(2)}, u32[]{:S(2)}) %collective-permute-start.1) | collective-permute-done | bytes 524320 | tf_op jit(solution)/shard_map/ppermute | solution.py:420
  77.2 1.9 %collective-permute-start.4 = (bf16[256,1024]{1,0:T(8,128)(2,1)S(1)}, bf16[256,1024]{1,0:T(8,128)(2,1)S(1)}, u32[]{:S(2)}, u32[]{:S(2)}) collective-permute-start(bf16[256,1024]{1,0:T(8,128)(2,1)S(1)} %collective-permute-done.1.n1), channel_id=1, source_target_pairs={{0,1},{1,0},{2,3},{3,2},{4,5},{5,4},{6,7},{7,6},{8,9},{9,8},{10,11... | collective-permute-start | bytes 1572872 | tf_op jit(solution)/shard_map/ppermute | solution.py:53
  79.1 0.0 collective-permute-done.2.n2
  79.1 2.4 %collective-permute-start.5 = (bf16[256,1024]{1,0:T(8,128)(2,1)S(1)}, bf16[256,1024]{1,0:T(8,128)(2,1)S(1)}, u32[]{:S(2)}, u32[]{:S(2)}) collective-permute-start(bf16[256,1024]{1,0:T(8,128)(2,1)S(1)} %collective-permute-done.2.n2), channel_id=1, source_target_pairs={{0,1},{1,0},{2,3},{3,2},{4,5},{5,4},{6,7},{7,6},{8,9},{9,8},{10,11... | collective-permute-start | bytes 1572872 | tf_op jit(solution)/shard_map/ppermute | solution.py:53
  81.6 0.0 collective-permute-done.3.n3
  81.6 1.9 %collective-permute-start.6 = (bf16[256,1024]{1,0:T(8,128)(2,1)S(1)}, bf16[256,1024]{1,0:T(8,128)(2,1)S(1)}, u32[]{:S(2)}, u32[]{:S(2)}) collective-permute-start(bf16[256,1024]{1,0:T(8,128)(2,1)S(1)} %collective-permute-done.3.n3), channel_id=1, source_target_pairs={{0,1},{1,0},{2,3},{3,2},{4,5},{5,4},{6,7},{7,6},{8,9},{9,8},{10,11... | collective-permute-start | bytes 1572872 | tf_op jit(solution)/shard_map/ppermute | solution.py:53
  83.5 0.0 collective-permute-done.4.f1
  83.5 0.0 collective-permute-done.5.f2
  83.5 0.0 copy-start
  83.5 0.8 copy-done
  84.3 1.1 collective-permute-done.6.f3
  85.4 0.0 copy-start.3
  85.4 0.8 copy-done.3
  86.2 0.0 all-to-all-done
  86.2 1.0 copy-done.1
  87.2 1.0 copy-done.4
  88.2 5.2 %project.1 = bf16[4,320,256]{2,1,0:T(8,128)(2,1)} custom-call(s32[3]{0:T(128)S(1)} %pad_add_fusion.where_ref, bf16[256,8192]{1,0:T(8,128)(2,1)} %states_ref.5, bf16[256,1024]{1,0:T(8,128)(2,1)S(1)} %collective-permute-done.1.n1, bf16[256,1024]{1,0:T(8,128)(2,1)S(1)} %collective-permute-done.2.n2, bf16[256,1024]{1,0:T(8,128)(2,1)S(1)} %collective-permute-done.3.n3, ...), custom_call_target="tpu_custom_call" | custom-call | tf_op jit(solution)/shard_map/project/pallas_call | solution.py:250
  93.5 0.0 copy-start.7
  93.5 0.0 copy-start.8
  93.5 8.2 %all-to-all-start.1 = ((bf16[4,320,256]{2,1,0:T(8,128)(2,1)}), bf16[4,320,256]{2,1,0:T(8,128)(2,1)S(1)}, u32[]{:S(2)}, u32[]{:S(2)}) async-start(bf16[4,320,256]{2,1,0:T(8,128)(2,1)} %project.1), calls=%async_computation.1 | async-start | bytes 1310720 | tf_op jit(solution)/shard_map/all_to_all | solution.py:430
  101.7 0.0 copy-done.7
  101.7 0.1 reduce_sum.19
  101.8 0.1 add_convert_fusion
  101.9 0.1 convert_element_type.15
  102.0 0.5 multiply_cosine_fusion
  102.5 0.9 pad_maximum_fusion.tables_ref
  103.4 15.9 %all-to-all-done.1.parts = bf16[4,320,256]{2,1,0:T(8,128)(2,1)S(1)} async-done(((bf16[4,320,256]{2,1,0:T(8,128)(2,1)}), bf16[4,320,256]{2,1,0:T(8,128)(2,1)S(1)}, u32[]{:S(2)}, u32[]{:S(2)}) %all-to-all-start.1) | async-done | bytes 655392 | tf_op jit(solution)/shard_map/all_to_all | solution.py:430
  119.3 5.8 %all-gather = f32[256,256]{1,0:T(8,128)S(1)} all-gather(f32[64,256]{1,0:T(8,128)S(1)} %convert_reduce_fusion), channel_id=2, replica_groups=mesh['zh'=4,'zb'=2,'yu'=2,'yb'=2,'yh'=2,'xh'=2,'xb'=2,'c'=2] {'xb','c'}, dimensions={0}, use_global_device_ids=true | all-gather | bytes 327680 | tf_op jit(solution)/shard_map/all_gather | solution.py:432
  125.1 0.0 copy-done.8
  125.1 3.4 %attend.1 = (bf16[256,256]{1,0:T(8,128)(2,1)}, bf16[256,256]{1,0:T(8,128)(2,1)S(1)}, bf16[256,2048]{1,0:T(8,128)(2,1)S(1)}) custom-call(s32[3]{0:T(128)S(1)} %pad_add_fusion.where_ref, s32[4,4]{1,0:T(4,128)S(1)} %copy-done.7, f32[4]{0:T(128)S(1)} %copy-done.8, bf16[4,320,256]{2,1,0:T(8,128)(2,1)S(1)} %all-to-all-done.1.parts, f32[4,64,256]{2,1,0:T(8,128)S(1)} %bitcast.11, ...), custom_call_target="tpu_custom_call" | custom-call | tf_op jit(solution)/shard_map/attend/pallas_call | solution.py:343
  128.5 16.1 %all-gather.1 = bf16[1024,256]{1,0:T(8,128)(2,1)S(1)} all-gather(bf16[256,256]{1,0:T(8,128)(2,1)S(1)} %get-tuple-element.19), channel_id=3, replica_groups=mesh['zh'=4,'zb'=2,'yu'=2,'yb'=2,'yh'=2,'xh'=2,'xb'=2,'c'=2] {'yu','yb'}, dimensions={0}, use_global_device_ids=true | all-gather | bytes 655360 | tf_op jit(solution)/shard_map/all_gather | solution.py:446
  144.7 0.0 copy-done.2
  144.7 0.0 copy-done.5
  144.7 1.8 gradient.1
  146.5 34.1 %all_to_all.15.terms = bf16[8,256,256]{2,1,0:T(8,128)(2,1)S(1)} all-to-all(bf16[8,256,256]{2,1,0:T(8,128)(2,1)S(1)} %gradient.1), channel_id=1, replica_groups=mesh['zh'=4,'zb'=2,'yu'=2,'yb'=2,'yh'=2,'xh'=2,'xb'=2,'c'=2] {'zh','zb'}, dimensions={0} | all-to-all | bytes 2097152 | tf_op jit(solution)/shard_map/all_to_all | solution.py:448
  180.7 0.9 add_up.1
  (8 shorter events, 0.0 us)
Async XLA Ops:
  1.7 14.1 %collective-permute-start = (bf16[2,320,128]{2,1,0:T(8,128)(2,1)S(1)}, bf16[2,320,128]{2,1,0:T(8,128)(2,1)S(1)}, u32[]{:S(2)}, u32[]{:S(2)}) collective-permute-start(bf16[2,320,128]{2,1,0:T(8,128)(2,1)S(1)} %pack_weights.1), channel_id=1, source_target_pairs={{0,0},{1,32},{2,64},{3,96},{4,128},{5,160},{6,192},{7,224},{8,256}... | collective-permute-start | bytes 491528 | tf_op jit(solution)/shard_map/ppermute | solution.py:414
  15.7 1.0 copy-start.6
  18.0 68.1 %all-to-all-start = ((bf16[16,320,128]{2,1,0:T(8,128)(2,1)}), bf16[16,320,128]{2,1,0:T(8,128)(2,1)S(1)}, u32[]{:S(2)}, u32[]{:S(2)}) async-start(bf16[16,320,128]{2,1,0:T(8,128)(2,1)} %bitcast.5), calls=%async_computation | async-start | bytes 2621440 | tf_op jit(solution)/shard_map/all_to_all | solution.py:425
  38.1 39.1 %collective-permute-start.1 = (bf16[256,1024]{1,0:T(8,128)(2,1)}, bf16[256,1024]{1,0:T(8,128)(2,1)S(1)}, u32[]{:S(2)}, u32[]{:S(2)}) collective-permute-start(bf16[256,1024]{1,0:T(8,128)(2,1)} %get-tuple-element.14), channel_id=1, source_target_pairs={{0,56},{1,57},{2,58},{3,59},{4,60},{5,61},{6,62},{7,63},{16,0},{17... | collective-permute-start | bytes 1572872 | tf_op jit(solution)/shard_map/ppermute | solution.py:420
  40.1 39.1 %collective-permute-start.2 = (bf16[256,1024]{1,0:T(8,128)(2,1)}, bf16[256,1024]{1,0:T(8,128)(2,1)S(1)}, u32[]{:S(2)}, u32[]{:S(2)}) collective-permute-start(bf16[256,1024]{1,0:T(8,128)(2,1)} %get-tuple-element.15), channel_id=1, source_target_pairs={{0,32},{1,41},{2,34},{3,43},{4,36},{5,45},{6,38},{7,47},{16,48},{1... | collective-permute-start | bytes 1572872 | tf_op jit(solution)/shard_map/ppermute | solution.py:421
  45.4 36.2 %collective-permute-start.3 = (bf16[256,1024]{1,0:T(8,128)(2,1)}, bf16[256,1024]{1,0:T(8,128)(2,1)S(1)}, u32[]{:S(2)}, u32[]{:S(2)}) collective-permute-start(bf16[256,1024]{1,0:T(8,128)(2,1)} %get-tuple-element.16), channel_id=1, source_target_pairs={{0,16},{1,17},{2,18},{3,19},{4,20},{5,21},{6,22},{7,23},{16,32},{1... | collective-permute-start | bytes 1572872 | tf_op jit(solution)/shard_map/ppermute | solution.py:422
  77.2 6.3 %collective-permute-start.4 = (bf16[256,1024]{1,0:T(8,128)(2,1)S(1)}, bf16[256,1024]{1,0:T(8,128)(2,1)S(1)}, u32[]{:S(2)}, u32[]{:S(2)}) collective-permute-start(bf16[256,1024]{1,0:T(8,128)(2,1)S(1)} %collective-permute-done.1.n1), channel_id=1, source_target_pairs={{0,1},{1,0},{2,3},{3,2},{4,5},{5,4},{6,7},{7,6},{8,9},{9,8},{10,11... | collective-permute-start | bytes 1572872 | tf_op jit(solution)/shard_map/ppermute | solution.py:53
  79.1 4.4 %collective-permute-start.5 = (bf16[256,1024]{1,0:T(8,128)(2,1)S(1)}, bf16[256,1024]{1,0:T(8,128)(2,1)S(1)}, u32[]{:S(2)}, u32[]{:S(2)}) collective-permute-start(bf16[256,1024]{1,0:T(8,128)(2,1)S(1)} %collective-permute-done.2.n2), channel_id=1, source_target_pairs={{0,1},{1,0},{2,3},{3,2},{4,5},{5,4},{6,7},{7,6},{8,9},{9,8},{10,11... | collective-permute-start | bytes 1572872 | tf_op jit(solution)/shard_map/ppermute | solution.py:53
  81.6 3.8 %collective-permute-start.6 = (bf16[256,1024]{1,0:T(8,128)(2,1)S(1)}, bf16[256,1024]{1,0:T(8,128)(2,1)S(1)}, u32[]{:S(2)}, u32[]{:S(2)}) collective-permute-start(bf16[256,1024]{1,0:T(8,128)(2,1)S(1)} %collective-permute-done.3.n3), channel_id=1, source_target_pairs={{0,1},{1,0},{2,3},{3,2},{4,5},{5,4},{6,7},{7,6},{8,9},{9,8},{10,11... | collective-permute-start | bytes 1572872 | tf_op jit(solution)/shard_map/ppermute | solution.py:53
  83.5 0.8 copy-start
  85.4 0.8 copy-start.3
  86.2 1.0 copy-start.1
  87.2 1.0 copy-start.4
  93.5 8.2 %copy-start.7 = (s32[4,4]{1,0:T(4,128)S(1)}, s32[4,4]{1,0:T(4,128)}, u32[]{:S(2)}) copy-start(s32[4,4]{1,0:T(4,128)} %mask_ref.1) | copy-start | bytes 196
  93.5 31.6 %copy-start.8 = (f32[4]{0:T(128)S(1)}, f32[4]{0:T(128)}, u32[]{:S(2)}) copy-start(f32[4]{0:T(128)} %risk_ref.1) | copy-start | bytes 52
  93.5 25.8 %all-to-all-start.1 = ((bf16[4,320,256]{2,1,0:T(8,128)(2,1)}), bf16[4,320,256]{2,1,0:T(8,128)(2,1)S(1)}, u32[]{:S(2)}, u32[]{:S(2)}) async-start(bf16[4,320,256]{2,1,0:T(8,128)(2,1)} %project.1), calls=%async_computation.1 | async-start | bytes 1310720 | tf_op jit(solution)/shard_map/all_to_all | solution.py:430
  125.1 19.6 %copy-start.2 = (bf16[256,1024]{1,0:T(8,128)(2,1)S(1)}, bf16[256,1024]{1,0:T(8,128)(2,1)}, u32[]{:S(2)}) copy-start(bf16[256,1024]{1,0:T(8,128)(2,1)} %copy-done) | copy-start | bytes 1572868
  125.1 19.6 %copy-start.5 = (bf16[256,1024]{1,0:T(8,128)(2,1)S(1)}, bf16[256,1024]{1,0:T(8,128)(2,1)}, u32[]{:S(2)}) copy-start(bf16[256,1024]{1,0:T(8,128)(2,1)} %copy-done.3) | copy-start | bytes 1572868

commit v10 on v8

--- a/solution.py
+++ b/solution.py
@@ -2,6 +2,7 @@
 
 import jax
 import jax.numpy as jnp
+import numpy as np
 from jax import lax
 from jax.experimental import pallas as pl
 from jax.experimental.pallas import tpu as pltpu
@@ -24,12 +25,19 @@
     return pltpu.CompilerParams(vmem_limit_bytes=VMEM_LIMIT)
 
 
+STEPS = ((4, 3, 6, 5), (2, 1, 0, 7))
+
+
+def resting_z(z, block):
+    return (z + STEPS[(z // 4) ^ (block // 4)][(z - block) % 4]) % 8
+
+
 def home_pairs(turn):
     pairs = []
     for d in range(32):
         for t in range(16):
             half = (d % 2) ^ turn
-            block = 4 * ((t // 2) ^ (d // 4)) + 2 * (t % 2) + half
+            block = 4 * resting_z(d // 4, t // 2) + 2 * (t % 2) + half
             pairs.append((d * 16 + t, block * 16 + d // 2))
     return pairs
 
@@ -197,28 +205,45 @@
 
 
 def project_kernel(
-    where_ref, states_ref, n1, n2, n3, f1, f2, f3, weights, out, tokens, w_q, w_kv, result, sems, out_sems
+    where_ref,
+    states_ref,
+    n1,
+    n2,
+    n3,
+    f1,
+    f2,
+    f3,
+    weights_ref,
+    out,
+    own,
+    weights,
+    w_q,
+    w_kv,
+    result,
+    sems,
+    out_sems,
 ):
     core = where_ref[0]
     arrivals = []
-    for number, far in enumerate((f1, f2, f3)):
-        place = tokens.at[number, :, pl.ds(0, 1024)]
-        arrivals.append([pltpu.make_async_copy(far, place, sems.at[8 + number])])
-    arrivals.append(own_columns(where_ref, states_ref, tokens.at[3], sems))
-    for copies in arrivals:
-        for copy in copies:
-            copy.start()
     for part in range(8):
-        block = block_of(part, core) ^ where_ref[2]
+        block = where_ref[2 + block_of(part, core)]
+        arrivals.append(
+            pltpu.make_async_copy(weights_ref.at[block], weights.at[part], sems.at[8 + part])
+        )
+    copies = own_columns(where_ref, states_ref, own, sems)
+    for copy in arrivals + copies:
+        copy.start()
+    for part in range(8):
+        arrivals[part].wait()
         for head in range(2):
             rows, cols = pl.ds(256 * part, 256), pl.ds(HEAD * head, HEAD)
-            w_q[rows, cols] = weights[block, head, :256, :]
+            w_q[rows, cols] = weights[part, head, :256, :]
             for chunk in range(2):
                 lanes = pl.ds(256 * part + 128 * chunk, 128)
                 base = 256 + 32 * chunk
-                w_kv[16 * head : 16 * head + 16, lanes] = weights[block, head, base : base + 16, :]
+                w_kv[16 * head : 16 * head + 16, lanes] = weights[part, head, base : base + 16, :]
                 w_kv[32 + 16 * head : 48 + 16 * head, lanes] = weights[
-                    block, head, base + 16 : base + 32, :
+                    part, head, base + 16 : base + 32, :
                 ]
     def product(x, rows):
         q = jnp.dot(x, w_q[rows, :], preferred_element_type=F32)
@@ -229,15 +254,14 @@
 
     low, high = pl.ds(0, 1024), pl.ds(1024, 1024)
     departures = []
-    for number, near in enumerate((n1, n2, n3, None)):
+    for number, (near, far) in enumerate(((n1, f1), (n2, f2), (n3, f3), (None, None))):
         if near is None:
-            for copy in arrivals[number]:
+            for copy in copies:
                 copy.wait()
-            q, kv = product(tokens[number], pl.ds(0, 2048))
+            q, kv = product(own[...], pl.ds(0, 2048))
         else:
             q_near, kv_near = product(near[...], low)
-            arrivals[number][0].wait()
-            q_far, kv_far = product(tokens[number, :, :1024], high)
+            q_far, kv_far = product(far[...], high)
             q, kv = q_near + q_far, kv_near + kv_far
         result[number, :256, :] = q.astype(BF16)
         result[number, 256:, :] = kv.T.astype(BF16)
@@ -254,19 +278,20 @@
     return pl.pallas_call(
         project_kernel,
         out_shape=pltpu.HBM((4, 320, 256), BF16),
-        in_specs=[in_smem(), in_hbm(), *in_vmem(3), *[in_hbm()] * 3, *in_vmem(1)],
+        in_specs=[in_smem(), in_hbm(), *in_vmem(6), in_hbm()],
         out_specs=in_hbm(),
         scratch_shapes=[
-            pltpu.VMEM((4, TOK, 2048), BF16),
+            pltpu.VMEM((TOK, 2048), BF16),
+            pltpu.VMEM((8, 2, 320, 128), BF16),
             pltpu.VMEM((2048, 256), BF16),
             pltpu.VMEM((64, 2048), BF16),
             pltpu.VMEM((4, 320, 256), BF16),
-            pltpu.SemaphoreType.DMA((11,)),
+            pltpu.SemaphoreType.DMA((16,)),
             pltpu.SemaphoreType.DMA((4,)),
         ],
         compiler_params=params(),
         name="project",
-    )(where, held(states), *near, *[held(x) for x in far], weights)
+    )(where, held(states), *near, *far, held(weights))
 
 
 def attend_kernel(
@@ -278,15 +303,9 @@
     upstream_ref,
     tables_ref,
     states_ref,
-    f1_ref,
-    f2_ref,
-    f3_ref,
     attn_out,
     dq_out,
     own,
-    f1,
-    f2,
-    f3,
     upstream,
     tables,
     sems,
@@ -294,9 +313,6 @@
     copies = [
         pltpu.make_async_copy(tables_ref, tables, sems.at[8]),
         pltpu.make_async_copy(upstream_ref, upstream, sems.at[9]),
-        pltpu.make_async_copy(f1_ref, f1, sems.at[10]),
-        pltpu.make_async_copy(f2_ref, f2, sems.at[11]),
-        pltpu.make_async_copy(f3_ref, f3, sems.at[12]),
         *own_columns(where_ref, states_ref, own, sems),
     ]
     for copy in copies:
@@ -350,19 +366,18 @@
         copy.wait()
 
 
-def attend(where, block_mask, risk_weight, parts, kv, upstream, tables, states, far):
+def attend(where, block_mask, risk_weight, parts, kv, upstream, tables, states):
     own = jax.ShapeDtypeStruct((TOK, 2048), BF16)
-    part = jax.ShapeDtypeStruct((TOK, 1024), BF16)
     square = jax.ShapeDtypeStruct((TOK, 256), BF16)
     return pl.pallas_call(
         attend_kernel,
-        out_shape=(square, square, own, part, part, part),
-        in_specs=[*[in_smem()] * 3, *in_vmem(2), *[in_hbm()] * 6],
-        out_specs=tuple(in_vmem(6)),
+        out_shape=(square, square, own),
+        in_specs=[*[in_smem()] * 3, *in_vmem(2), *[in_hbm()] * 3],
+        out_specs=tuple(in_vmem(3)),
         scratch_shapes=[
             pltpu.VMEM((TOK, 256), BF16),
             pltpu.VMEM((TOK, 2 * HEAD), F32),
-            pltpu.SemaphoreType.DMA((13,)),
+            pltpu.SemaphoreType.DMA((10,)),
         ],
         compiler_params=params(),
         name="attend",
@@ -375,7 +390,6 @@
         held(upstream),
         held(tables),
         held(states),
-        *[held(x) for x in far],
     )
 
 
@@ -422,8 +436,9 @@
 
 def shards(states, query_weight, key_matrix, value_matrix, block_mask, risk_weight, upstream):
     place = lax.axis_index(GROUP)
-    plane = lax.axis_index(("yh", "xh", "xb"))
-    where = jnp.stack([lax.axis_index("c"), place, plane]).astype(jnp.int32)
+    resting = np.array([[resting_z(z, block) for block in range(8)] for z in range(8)], np.int32)
+    resting = jnp.asarray(resting)[lax.axis_index(("yh", "xh", "xb"))]
+    where = jnp.stack([lax.axis_index("c"), place]).astype(jnp.int32)
 
     first, second = pack(where, query_weight, key_matrix.T, value_matrix.T)
     first = lax.ppermute(first, AXES, home_pairs(0))
@@ -440,7 +455,7 @@
     far = [swap_core(x) for x in near]
     weights = lax.all_to_all(weights, OTHERS, split_axis=0, concat_axis=0)
 
-    parts = project(where, states, near, far, weights)
+    parts = project(jnp.concatenate([where, resting]), states, near, far, weights)
     parts = lax.all_to_all(parts, GROUP, split_axis=0, concat_axis=0)
     kv = jnp.sum(parts[:, 256:].astype(F32), axis=0)
     kv = lax.all_gather(kv, ("xb", "c"), axis=0, tiled=False)
@@ -454,8 +469,8 @@
     cosine, sine = jnp.cos(angles), jnp.sin(angles)
     tables = jnp.concatenate([cosine, cosine, -sine, sine], axis=1)
 
-    attn_out, dq, own, *far = attend(
-        where, block_mask, risk_weight, parts, kv, upstream, tables, states, far
+    attn_out, dq, own = attend(
+        where, block_mask, risk_weight, parts, kv, upstream, tables, states
     )
     slopes = lax.all_gather(dq, GROUP, axis=0, tiled=False)
     terms = gradient(where, own, near, far, slopes)

time: 165 us -> 162 us (0.982); the launches traced: 162 us -> 161 us
  waiting for transfers between devices: 33.5 us -> 40.6 us
  starting transfers between devices: 50.5 us -> 45.1 us
  local copies, waits for them, and re-layouts: 2.49 us -> 0.8 us
    ppermute x1, waiting for transfers between devices: 0.49 us -> 6.04 us  [shards(): second = lax.ppermute(second, AXES, home_pairs(1))]
    ppermute x1, starting transfers between devices: 5.68 us -> 2.95 us  [shards(): second = lax.ppermute(second, AXES, home_pairs(1))]
    all_to_all x1, starting transfers between devices: 17.2 us -> 14.8 us  [shards(): weights = lax.all_to_all(weights, OTHERS, split_axis=0, concat_axis=0)]
    unnamed x10 -> x8, local copies, waits for them, and re-layouts: 2.4 us -> 0.02 us
  transfers between devices with their start and end apart: 10 -> 10, of which waited for: 6 -> 6; matrix products, arithmetic and copies ran while one was open for 1% -> 2% of each run, Pallas kernels for 2% -> 1%
where the time goes in v10:
time: 162 us; the launch traced here: 161 us
  blocking collectives  54.9 us (34%)
  starting transfers between devices  45.1 us (28%)
  waiting for transfers between devices  40.6 us (25%)
  Pallas kernels  17.1 us (11%)
  other arithmetic  1.81 us (1%)
    all_to_all x1, blocking collectives, shards(): terms = lax.all_to_all(terms, OTHERS, split_axis=0, concat_axis=0)  33 us
    all_gather x1, blocking collectives, shards(): slopes = lax.all_gather(dq, GROUP, axis=0, tiled=False)  16.1 us
    all_to_all x1, waiting for transfers between devices, shards(): parts = lax.all_to_all(parts, GROUP, split_axis=0, concat_axis=0)  16.1 us
    all_to_all x1, starting transfers between devices, shards(): weights = lax.all_to_all(weights, OTHERS, split_axis=0, concat_axis=0)  14.8 us
    ppermute x1, waiting for transfers between devices, shards(): lax.ppermute(down, AXES, ring_pairs(-1, -1))  10.5 us
    ppermute x1, starting transfers between devices, shards(): first = lax.ppermute(first, AXES, home_pairs(0))  7.81 us
    ppermute x3, starting transfers between devices, swap_core(): return lax.ppermute(value, 'c', [(0, 1), (1, 0)])  7.27 us
    ppermute x1, waiting for transfers between devices, shards(): second = lax.ppermute(second, AXES, home_pairs(1))  6.04 us
  transfers between devices with their start and end apart: 10, of which 6 were waited for; matrix products, arithmetic and copies ran while one was open for 2% of the time, Pallas kernels for 1%

profile of v10, /device:TPU:6, one launch (start us, length us, event | category | flops | bytes accessed | tf_op | source)
XLA Modules:
  0.0 161.1 jit_solution(8467602256846036103)
XLA Ops:
  0.6 0.1 pad_add_fusion.where_ref
  0.7 1.6 pack_weights.1
  2.3 7.8 %collective-permute-start = (bf16[320,128]{1,0:T(8,128)(2,1)S(1)}, bf16[320,128]{1,0:T(8,128)(2,1)S(1)}, u32[]{:S(2)}, u32[]{:S(2)}) collective-permute-start(bf16[320,128]{1,0:T(8,128)(2,1)S(1)} %get-tuple-element.16), channel_id=1, source_target_pairs={{0,256},{1,288},{2,320},{3,352},{4,384},{5,416},{6,192},{7,224},{8... | collective-permute-start | bytes 245768 | tf_op jit(solution)/shard_map/ppermute | solution.py:444
  10.1 3.0 %collective-permute-start.1 = (bf16[320,128]{1,0:T(8,128)(2,1)S(1)}, bf16[320,128]{1,0:T(8,128)(2,1)S(1)}, u32[]{:S(2)}, u32[]{:S(2)}) collective-permute-start(bf16[320,128]{1,0:T(8,128)(2,1)S(1)} %get-tuple-element.17), channel_id=1, source_target_pairs={{0,272},{1,304},{2,336},{3,368},{4,400},{5,432},{6,208},{7,240},{8... | collective-permute-start | bytes 245768 | tf_op jit(solution)/shard_map/ppermute | solution.py:445
  13.1 2.1 %cut_states.1 = (bf16[256,1024]{1,0:T(8,128)(2,1)S(1)}, bf16[256,1024]{1,0:T(8,128)(2,1)S(1)}, bf16[256,1024]{1,0:T(8,128)(2,1)S(1)}) custom-call(s32[2]{0:T(128)S(1)} %pad_add_fusion.where_ref, bf16[256,8192]{1,0:T(8,128)(2,1)} %states_ref.5), custom_call_target="tpu_custom_call" | custom-call | tf_op jit(solution)/shard_map/cut_states/pallas_call | solution.py:147
  15.2 0.0 collective-permute-done.first
  15.2 6.0 %collective-permute-done.1.second = bf16[320,128]{1,0:T(8,128)(2,1)S(1)} collective-permute-done((bf16[320,128]{1,0:T(8,128)(2,1)S(1)}, bf16[320,128]{1,0:T(8,128)(2,1)S(1)}, u32[]{:S(2)}, u32[]{:S(2)}) %collective-permute-start.1) | collective-permute-done | bytes 81952 | tf_op jit(solution)/shard_map/ppermute | solution.py:445
  21.3 1.8 %weight_copies.1.refs_3_ = bf16[8,2,320,128]{3,2,1,0:T(8,128)(2,1)} custom-call(s32[2]{0:T(128)S(1)} %pad_add_fusion.where_ref, bf16[320,128]{1,0:T(8,128)(2,1)S(1)} %collective-permute-done.first, bf16[320,128]{1,0:T(8,128)(2,1)S(1)} %collective-permute-done.1.second, bf16[256,1024]{1,0:T(8,128)(2,1)S(1)} %get-tuple-element.13.after.refs_0_), custom_call_target="tpu_custom_call" | custom-call | tf_op jit(solution)/shard_map/weight_copies/pallas_call | solution.py:198
  23.1 14.8 %all-to-all-start = ((bf16[8,2,320,128]{3,2,1,0:T(8,128)(2,1)}), bf16[8,2,320,128]{3,2,1,0:T(8,128)(2,1)}, u32[]{:S(2)}, u32[]{:S(2)}) async-start(bf16[8,2,320,128]{3,2,1,0:T(8,128)(2,1)} %weight_copies.1.refs_3_), calls=%async_computation | async-start | bytes 2621440 | tf_op jit(solution)/shard_map/all_to_all | solution.py:456
  37.8 1.9 %collective-permute-start.2 = (bf16[256,1024]{1,0:T(8,128)(2,1)S(1)}, bf16[256,1024]{1,0:T(8,128)(2,1)S(1)}, u32[]{:S(2)}, u32[]{:S(2)}) collective-permute-start(bf16[256,1024]{1,0:T(8,128)(2,1)S(1)} %get-tuple-element.18), channel_id=1, source_target_pairs={{0,56},{1,57},{2,58},{3,59},{4,60},{5,61},{6,62},{7,63},{16,0},{17... | collective-permute-start | bytes 1572872 | tf_op jit(solution)/shard_map/ppermute | solution.py:451
  39.8 4.9 %collective-permute-start.3 = (bf16[256,1024]{1,0:T(8,128)(2,1)S(1)}, bf16[256,1024]{1,0:T(8,128)(2,1)S(1)}, u32[]{:S(2)}, u32[]{:S(2)}) collective-permute-start(bf16[256,1024]{1,0:T(8,128)(2,1)S(1)} %get-tuple-element.19), channel_id=1, source_target_pairs={{0,32},{1,41},{2,34},{3,43},{4,36},{5,45},{6,38},{7,47},{16,48},{1... | collective-permute-start | bytes 1572872 | tf_op jit(solution)/shard_map/ppermute | solution.py:452
  44.7 1.9 %collective-permute-start.4 = (bf16[256,1024]{1,0:T(8,128)(2,1)S(1)}, bf16[256,1024]{1,0:T(8,128)(2,1)S(1)}, u32[]{:S(2)}, u32[]{:S(2)}) collective-permute-start(bf16[256,1024]{1,0:T(8,128)(2,1)S(1)} %get-tuple-element.20), channel_id=1, source_target_pairs={{0,16},{1,17},{2,18},{3,19},{4,20},{5,21},{6,22},{7,23},{16,32},{1... | collective-permute-start | bytes 1572872 | tf_op jit(solution)/shard_map/ppermute | solution.py:453
  46.6 10.5 %collective-permute-done.2.n1 = bf16[256,1024]{1,0:T(8,128)(2,1)S(1)} collective-permute-done((bf16[256,1024]{1,0:T(8,128)(2,1)S(1)}, bf16[256,1024]{1,0:T(8,128)(2,1)S(1)}, u32[]{:S(2)}, u32[]{:S(2)}) %collective-permute-start.2) | collective-permute-done | bytes 524320 | tf_op jit(solution)/shard_map/ppermute | solution.py:451
  57.1 1.9 %collective-permute-start.5 = (bf16[256,1024]{1,0:T(8,128)(2,1)S(1)}, bf16[256,1024]{1,0:T(8,128)(2,1)S(1)}, u32[]{:S(2)}, u32[]{:S(2)}) collective-permute-start(bf16[256,1024]{1,0:T(8,128)(2,1)S(1)} %collective-permute-done.2.n1), channel_id=1, source_target_pairs={{0,1},{1,0},{2,3},{3,2},{4,5},{5,4},{6,7},{7,6},{8,9},{9,8},{10,11... | collective-permute-start | bytes 1572872 | tf_op jit(solution)/shard_map/ppermute | solution.py:61
  59.0 2.7 %collective-permute-done.3.n2 = bf16[256,1024]{1,0:T(8,128)(2,1)S(1)} collective-permute-done((bf16[256,1024]{1,0:T(8,128)(2,1)S(1)}, bf16[256,1024]{1,0:T(8,128)(2,1)S(1)}, u32[]{:S(2)}, u32[]{:S(2)}) %collective-permute-start.3) | collective-permute-done | bytes 524320 | tf_op jit(solution)/shard_map/ppermute | solution.py:452
  61.8 3.5 %collective-permute-start.6 = (bf16[256,1024]{1,0:T(8,128)(2,1)S(1)}, bf16[256,1024]{1,0:T(8,128)(2,1)S(1)}, u32[]{:S(2)}, u32[]{:S(2)}) collective-permute-start(bf16[256,1024]{1,0:T(8,128)(2,1)S(1)} %collective-permute-done.3.n2), channel_id=1, source_target_pairs={{0,1},{1,0},{2,3},{3,2},{4,5},{5,4},{6,7},{7,6},{8,9},{9,8},{10,11... | collective-permute-start | bytes 1572872 | tf_op jit(solution)/shard_map/ppermute | solution.py:61
  65.2 4.2 %collective-permute-done.4.n3 = bf16[256,1024]{1,0:T(8,128)(2,1)S(1)} collective-permute-done((bf16[256,1024]{1,0:T(8,128)(2,1)S(1)}, bf16[256,1024]{1,0:T(8,128)(2,1)S(1)}, u32[]{:S(2)}, u32[]{:S(2)}) %collective-permute-start.4) | collective-permute-done | bytes 524320 | tf_op jit(solution)/shard_map/ppermute | solution.py:453
  69.4 1.9 %collective-permute-start.7 = (bf16[256,1024]{1,0:T(8,128)(2,1)S(1)}, bf16[256,1024]{1,0:T(8,128)(2,1)S(1)}, u32[]{:S(2)}, u32[]{:S(2)}) collective-permute-start(bf16[256,1024]{1,0:T(8,128)(2,1)S(1)} %collective-permute-done.4.n3), channel_id=1, source_target_pairs={{0,1},{1,0},{2,3},{3,2},{4,5},{5,4},{6,7},{7,6},{8,9},{9,8},{10,11... | collective-permute-start | bytes 1572872 | tf_op jit(solution)/shard_map/ppermute | solution.py:61
  71.3 0.7 dynamic-slice_bitcast_fusion
  72.0 0.1 pad_add_fusion.1.where_ref
  72.1 0.0 collective-permute-done.5.f1
  72.1 0.0 collective-permute-done.6.f2
  72.1 1.1 collective-permute-done.7.f3
  73.2 0.0 copy-start
  73.2 0.0 all-to-all-done.weights_ref
  73.2 5.4 %project.1 = bf16[4,320,256]{2,1,0:T(8,128)(2,1)} custom-call(s32[10]{0:T(128)S(1)} %pad_add_fusion.1.where_ref, bf16[256,8192]{1,0:T(8,128)(2,1)} %states_ref.5, bf16[256,1024]{1,0:T(8,128)(2,1)S(1)} %collective-permute-done.2.n1, bf16[256,1024]{1,0:T(8,128)(2,1)S(1)} %collective-permute-done.3.n2, bf16[256,1024]{1,0:T(8,128)(2,1)S(1)} %collective-permute-done.4.n3, ...), custom_call_target="tpu_custom_call" | custom-call | tf_op jit(solution)/shard_map/project/pallas_call | solution.py:278
  78.6 0.0 copy-done
  78.6 0.0 copy-start.2
  78.6 0.0 copy-start.3
  78.6 3.5 %all-to-all-start.1 = ((bf16[4,320,256]{2,1,0:T(8,128)(2,1)}), bf16[4,320,256]{2,1,0:T(8,128)(2,1)S(1)}, u32[]{:S(2)}, u32[]{:S(2)}) async-start(bf16[4,320,256]{2,1,0:T(8,128)(2,1)} %project.1), calls=%async_computation.1 | async-start | bytes 1310720 | tf_op jit(solution)/shard_map/all_to_all | solution.py:459
  82.1 0.0 copy-done.2
  82.1 0.1 reduce_sum.19
  82.3 0.1 add_convert_fusion
  82.3 0.1 convert_element_type.15
  82.4 0.5 multiply_cosine_fusion
  83.0 0.9 pad_maximum_fusion.tables_ref
  83.9 16.1 %all-to-all-done.1.parts = bf16[4,320,256]{2,1,0:T(8,128)(2,1)S(1)} async-done(((bf16[4,320,256]{2,1,0:T(8,128)(2,1)}), bf16[4,320,256]{2,1,0:T(8,128)(2,1)S(1)}, u32[]{:S(2)}, u32[]{:S(2)}) %all-to-all-start.1) | async-done | bytes 655392 | tf_op jit(solution)/shard_map/all_to_all | solution.py:459
  100.0 5.8 %all-gather = f32[256,256]{1,0:T(8,128)S(1)} all-gather(f32[64,256]{1,0:T(8,128)S(1)} %convert_reduce_fusion), channel_id=2, replica_groups=mesh['zh'=4,'zb'=2,'yu'=2,'yb'=2,'yh'=2,'xh'=2,'xb'=2,'c'=2] {'xb','c'}, dimensions={0}, use_global_device_ids=true | all-gather | bytes 327680 | tf_op jit(solution)/shard_map/all_gather | solution.py:461
  105.8 0.0 copy-done.3
  105.8 0.0 copy-start.1
  105.8 3.4 %attend.1 = (bf16[256,256]{1,0:T(8,128)(2,1)}, bf16[256,256]{1,0:T(8,128)(2,1)S(1)}, bf16[256,2048]{1,0:T(8,128)(2,1)S(1)}) custom-call(s32[2]{0:T(128)S(1)} %pad_add_fusion.where_ref, s32[4,4]{1,0:T(4,128)S(1)} %copy-done.2, f32[4]{0:T(128)S(1)} %copy-done.3, bf16[4,320,256]{2,1,0:T(8,128)(2,1)S(1)} %all-to-all-done.1.parts, f32[4,64,256]{2,1,0:T(8,128)S(1)} %bitcast.9, ...), custom_call_target="tpu_custom_call" | custom-call | tf_op jit(solution)/shard_map/attend/pallas_call | solution.py:372
  109.2 16.1 %all-gather.1 = bf16[1024,256]{1,0:T(8,128)(2,1)S(1)} all-gather(bf16[256,256]{1,0:T(8,128)(2,1)S(1)} %get-tuple-element.23), channel_id=3, replica_groups=mesh['zh'=4,'zb'=2,'yu'=2,'yb'=2,'yh'=2,'xh'=2,'xb'=2,'c'=2] {'yu','yb'}, dimensions={0}, use_global_device_ids=true | all-gather | bytes 655360 | tf_op jit(solution)/shard_map/all_gather | solution.py:475
  125.3 0.0 copy-done.1
  125.4 1.8 %gradient.1 = bf16[8,256,256]{2,1,0:T(8,128)(2,1)S(1)} custom-call(s32[2]{0:T(128)S(1)} %pad_add_fusion.where_ref, bf16[256,2048]{1,0:T(8,128)(2,1)S(1)} %get-tuple-element.22.own, bf16[256,1024]{1,0:T(8,128)(2,1)S(1)} %collective-permute-done.2.n1, bf16[256,1024]{1,0:T(8,128)(2,1)S(1)} %collective-permute-done.3.n2, ...), custom_call_target="tpu_custom_call" | custom-call | tf_op jit(solution)/shard_map/gradient/pallas_call | solution.py:412
  127.2 33.0 %all_to_all.15.terms = bf16[8,256,256]{2,1,0:T(8,128)(2,1)S(1)} all-to-all(bf16[8,256,256]{2,1,0:T(8,128)(2,1)S(1)} %gradient.1), channel_id=1, replica_groups=mesh['zh'=4,'zb'=2,'yu'=2,'yb'=2,'yh'=2,'xh'=2,'xb'=2,'c'=2] {'zh','zb'}, dimensions={0} | all-to-all | bytes 2097152 | tf_op jit(solution)/shard_map/all_to_all | solution.py:477
  160.2 0.9 add_up.1
  (4 shorter events, 0.0 us)
Async XLA Ops:
  2.3 12.9 %collective-permute-start = (bf16[320,128]{1,0:T(8,128)(2,1)S(1)}, bf16[320,128]{1,0:T(8,128)(2,1)S(1)}, u32[]{:S(2)}, u32[]{:S(2)}) collective-permute-start(bf16[320,128]{1,0:T(8,128)(2,1)S(1)} %get-tuple-element.16), channel_id=1, source_target_pairs={{0,256},{1,288},{2,320},{3,352},{4,384},{5,416},{6,192},{7,224},{8... | collective-permute-start | bytes 245768 | tf_op jit(solution)/shard_map/ppermute | solution.py:444
  10.1 11.1 %collective-permute-start.1 = (bf16[320,128]{1,0:T(8,128)(2,1)S(1)}, bf16[320,128]{1,0:T(8,128)(2,1)S(1)}, u32[]{:S(2)}, u32[]{:S(2)}) collective-permute-start(bf16[320,128]{1,0:T(8,128)(2,1)S(1)} %get-tuple-element.17), channel_id=1, source_target_pairs={{0,272},{1,304},{2,336},{3,368},{4,400},{5,432},{6,208},{7,240},{8... | collective-permute-start | bytes 245768 | tf_op jit(solution)/shard_map/ppermute | solution.py:445
  23.1 50.1 %all-to-all-start = ((bf16[8,2,320,128]{3,2,1,0:T(8,128)(2,1)}), bf16[8,2,320,128]{3,2,1,0:T(8,128)(2,1)}, u32[]{:S(2)}, u32[]{:S(2)}) async-start(bf16[8,2,320,128]{3,2,1,0:T(8,128)(2,1)} %weight_copies.1.refs_3_), calls=%async_computation | async-start | bytes 2621440 | tf_op jit(solution)/shard_map/all_to_all | solution.py:456
  37.8 19.3 %collective-permute-start.2 = (bf16[256,1024]{1,0:T(8,128)(2,1)S(1)}, bf16[256,1024]{1,0:T(8,128)(2,1)S(1)}, u32[]{:S(2)}, u32[]{:S(2)}) collective-permute-start(bf16[256,1024]{1,0:T(8,128)(2,1)S(1)} %get-tuple-element.18), channel_id=1, source_target_pairs={{0,56},{1,57},{2,58},{3,59},{4,60},{5,61},{6,62},{7,63},{16,0},{17... | collective-permute-start | bytes 1572872 | tf_op jit(solution)/shard_map/ppermute | solution.py:451
  39.8 22.0 %collective-permute-start.3 = (bf16[256,1024]{1,0:T(8,128)(2,1)S(1)}, bf16[256,1024]{1,0:T(8,128)(2,1)S(1)}, u32[]{:S(2)}, u32[]{:S(2)}) collective-permute-start(bf16[256,1024]{1,0:T(8,128)(2,1)S(1)} %get-tuple-element.19), channel_id=1, source_target_pairs={{0,32},{1,41},{2,34},{3,43},{4,36},{5,45},{6,38},{7,47},{16,48},{1... | collective-permute-start | bytes 1572872 | tf_op jit(solution)/shard_map/ppermute | solution.py:452
  44.7 24.7 %collective-permute-start.4 = (bf16[256,1024]{1,0:T(8,128)(2,1)S(1)}, bf16[256,1024]{1,0:T(8,128)(2,1)S(1)}, u32[]{:S(2)}, u32[]{:S(2)}) collective-permute-start(bf16[256,1024]{1,0:T(8,128)(2,1)S(1)} %get-tuple-element.20), channel_id=1, source_target_pairs={{0,16},{1,17},{2,18},{3,19},{4,20},{5,21},{6,22},{7,23},{16,32},{1... | collective-permute-start | bytes 1572872 | tf_op jit(solution)/shard_map/ppermute | solution.py:453
  57.1 15.0 %collective-permute-start.5 = (bf16[256,1024]{1,0:T(8,128)(2,1)S(1)}, bf16[256,1024]{1,0:T(8,128)(2,1)S(1)}, u32[]{:S(2)}, u32[]{:S(2)}) collective-permute-start(bf16[256,1024]{1,0:T(8,128)(2,1)S(1)} %collective-permute-done.2.n1), channel_id=1, source_target_pairs={{0,1},{1,0},{2,3},{3,2},{4,5},{5,4},{6,7},{7,6},{8,9},{9,8},{10,11... | collective-permute-start | bytes 1572872 | tf_op jit(solution)/shard_map/ppermute | solution.py:61
  61.8 10.4 %collective-permute-start.6 = (bf16[256,1024]{1,0:T(8,128)(2,1)S(1)}, bf16[256,1024]{1,0:T(8,128)(2,1)S(1)}, u32[]{:S(2)}, u32[]{:S(2)}) collective-permute-start(bf16[256,1024]{1,0:T(8,128)(2,1)S(1)} %collective-permute-done.3.n2), channel_id=1, source_target_pairs={{0,1},{1,0},{2,3},{3,2},{4,5},{5,4},{6,7},{7,6},{8,9},{9,8},{10,11... | collective-permute-start | bytes 1572872 | tf_op jit(solution)/shard_map/ppermute | solution.py:61
  69.4 3.8 %collective-permute-start.7 = (bf16[256,1024]{1,0:T(8,128)(2,1)S(1)}, bf16[256,1024]{1,0:T(8,128)(2,1)S(1)}, u32[]{:S(2)}, u32[]{:S(2)}) collective-permute-start(bf16[256,1024]{1,0:T(8,128)(2,1)S(1)} %collective-permute-done.4.n3), channel_id=1, source_target_pairs={{0,1},{1,0},{2,3},{3,2},{4,5},{5,4},{6,7},{7,6},{8,9},{9,8},{10,11... | collective-permute-start | bytes 1572872 | tf_op jit(solution)/shard_map/ppermute | solution.py:61
  73.2 5.4 %copy-start = (bf16[256,1024]{1,0:T(8,128)(2,1)}, bf16[256,1024]{1,0:T(8,128)(2,1)S(1)}, u32[]{:S(2)}) copy-start(bf16[256,1024]{1,0:T(8,128)(2,1)S(1)} %collective-permute-done.7.f3) | copy-start | bytes 1572868
  78.6 3.5 %copy-start.2 = (s32[4,4]{1,0:T(4,128)S(1)}, s32[4,4]{1,0:T(4,128)}, u32[]{:S(2)}) copy-start(s32[4,4]{1,0:T(4,128)} %mask_ref.1) | copy-start | bytes 196
  78.6 27.2 %copy-start.3 = (f32[4]{0:T(128)S(1)}, f32[4]{0:T(128)}, u32[]{:S(2)}) copy-start(f32[4]{0:T(128)} %risk_ref.1) | copy-start | bytes 52
  78.6 21.3 %all-to-all-start.1 = ((bf16[4,320,256]{2,1,0:T(8,128)(2,1)}), bf16[4,320,256]{2,1,0:T(8,128)(2,1)S(1)}, u32[]{:S(2)}, u32[]{:S(2)}) async-start(bf16[4,320,256]{2,1,0:T(8,128)(2,1)} %project.1), calls=%async_computation.1 | async-start | bytes 1310720 | tf_op jit(solution)/shard_map/all_to_all | solution.py:459
  105.8 19.6 %copy-start.1 = (bf16[256,1024]{1,0:T(8,128)(2,1)S(1)}, bf16[256,1024]{1,0:T(8,128)(2,1)}, u32[]{:S(2)}) copy-start(bf16[256,1024]{1,0:T(8,128)(2,1)} %copy-done) | copy-start | bytes 1572868

commit v11 on v10

--- a/solution.py
+++ b/solution.py
@@ -2,7 +2,6 @@
 
 import jax
 import jax.numpy as jnp
-import numpy as np
 from jax import lax
 from jax.experimental import pallas as pl
 from jax.experimental.pallas import tpu as pltpu
@@ -25,11 +24,10 @@
     return pltpu.CompilerParams(vmem_limit_bytes=VMEM_LIMIT)
 
 
-STEPS = ((4, 3, 6, 5), (2, 1, 0, 7))
-
-
 def resting_z(z, block):
-    return (z + STEPS[(z // 4) ^ (block // 4)][(z - block) % 4]) % 8
+    way = (z + 4 - block % 4) % 4
+    same = 1 - ((z // 4) ^ (block // 4))
+    return (z + 10 - way + same * (2 + 4 * (way // 2))) % 8
 
 
 def home_pairs(turn):
@@ -186,19 +184,26 @@
     return copies
 
 
-def copies_kernel(where_ref, first, second, after, out):
+def copies_kernel(where_ref, first, second, after, out, sems):
     del after
     odd = where_ref[1] % 2
+    sent = []
     for device in range(8):
-        out[device, odd] = first[...]
-        out[device, 1 - odd] = second[...]
+        for turn, piece in enumerate((first, second)):
+            copy = pltpu.make_async_copy(piece, out.at[device, odd ^ turn], sems.at[len(sent)])
+            copy.start()
+            sent.append(copy)
+    for copy in sent:
+        copy.wait()
 
 
 def copies(where, first, second, after):
     return pl.pallas_call(
         copies_kernel,
-        out_shape=jax.ShapeDtypeStruct((8, 2, 320, 128), BF16),
+        out_shape=pltpu.HBM((8, 2, 320, 128), BF16),
         in_specs=[in_smem(), *in_vmem(2), anywhere()],
+        out_specs=in_hbm(),
+        scratch_shapes=[pltpu.SemaphoreType.DMA((16,))],
         compiler_params=params(),
         name="weight_copies",
     )(where, first, second, after)
@@ -217,8 +222,7 @@
     out,
     own,
     weights,
-    w_q,
-    w_kv,
+    w_all,
     result,
     sems,
     out_sems,
@@ -226,7 +230,7 @@
     core = where_ref[0]
     arrivals = []
     for part in range(8):
-        block = where_ref[2 + block_of(part, core)]
+        block = resting_z(where_ref[2], block_of(part, core))
         arrivals.append(
             pltpu.make_async_copy(weights_ref.at[block], weights.at[part], sems.at[8 + part])
         )
@@ -235,22 +239,20 @@
         copy.start()
     for part in range(8):
         arrivals[part].wait()
+        start = 256 * part
         for head in range(2):
-            rows, cols = pl.ds(256 * part, 256), pl.ds(HEAD * head, HEAD)
-            w_q[rows, cols] = weights[part, head, :256, :]
-            for chunk in range(2):
-                lanes = pl.ds(256 * part + 128 * chunk, 128)
-                base = 256 + 32 * chunk
-                w_kv[16 * head : 16 * head + 16, lanes] = weights[part, head, base : base + 16, :]
-                w_kv[32 + 16 * head : 48 + 16 * head, lanes] = weights[
-                    part, head, base + 16 : base + 32, :
-                ]
+            w_all[start : start + 256, HEAD * head : HEAD * head + HEAD] = weights[
+                part, head, :256, :
+            ]
+        for chunk in range(2):
+            base = 256 + 32 * chunk
+            pair = [weights[part, head, base : base + 32, :] for head in range(2)]
+            columns = [pair[0][:16], pair[1][:16], pair[0][16:], pair[1][16:]]
+            rows = pl.ds(start + 128 * chunk, 128)
+            w_all[rows, 256:] = jnp.concatenate(columns, axis=0).T
+
     def product(x, rows):
-        q = jnp.dot(x, w_q[rows, :], preferred_element_type=F32)
-        kv = lax.dot_general(
-            x, w_kv[:, rows], (((1,), (1,)), ((), ())), preferred_element_type=F32
-        )
-        return q, kv
+        return jnp.dot(x, w_all[rows, :], preferred_element_type=F32)
 
     low, high = pl.ds(0, 1024), pl.ds(1024, 1024)
     departures = []
@@ -258,13 +260,11 @@
         if near is None:
             for copy in copies:
                 copy.wait()
-            q, kv = product(own[...], pl.ds(0, 2048))
+            linear = product(own[...], pl.ds(0, 2048))
         else:
-            q_near, kv_near = product(near[...], low)
-            q_far, kv_far = product(far[...], high)
-            q, kv = q_near + q_far, kv_near + kv_far
-        result[number, :256, :] = q.astype(BF16)
-        result[number, 256:, :] = kv.T.astype(BF16)
+            linear = product(near[...], low) + product(far[...], high)
+        result[number, :256, :] = linear[:, :256].astype(BF16)
+        result[number, 256:, :] = linear[:, 256:].T.astype(BF16)
         other = (where_ref[1] + number + 1) % 4
         departures.append(
             pltpu.make_async_copy(result.at[number], out.at[other], out_sems.at[number])
@@ -283,8 +283,7 @@
         scratch_shapes=[
             pltpu.VMEM((TOK, 2048), BF16),
             pltpu.VMEM((8, 2, 320, 128), BF16),
-            pltpu.VMEM((2048, 256), BF16),
-            pltpu.VMEM((64, 2048), BF16),
+            pltpu.VMEM((2048, 320), BF16),
             pltpu.VMEM((4, 320, 256), BF16),
             pltpu.SemaphoreType.DMA((16,)),
             pltpu.SemaphoreType.DMA((4,)),
@@ -302,17 +301,20 @@
     kv,
     upstream_ref,
     tables_ref,
+    turned_ref,
     states_ref,
     attn_out,
     dq_out,
     own,
     upstream,
     tables,
+    turned,
     sems,
 ):
     copies = [
         pltpu.make_async_copy(tables_ref, tables, sems.at[8]),
-        pltpu.make_async_copy(upstream_ref, upstream, sems.at[9]),
+        pltpu.make_async_copy(turned_ref, turned, sems.at[9]),
+        pltpu.make_async_copy(upstream_ref, upstream, sems.at[10]),
         *own_columns(where_ref, states_ref, own, sems),
     ]
     for copy in copies:
@@ -334,11 +336,12 @@
     risk = jnp.concatenate(risk, axis=0)
 
     copies[0].wait()
+    copies[1].wait()
     cq, sq = tables[:, :HEAD], tables[:, HEAD:]
-    ck, sk = cq[:, :64].T, sq[:, 64:].T
+    ck, sk = turned[:64], turned[64:]
     k1, k2 = k_lin[:64], k_lin[64:]
     keys = jnp.concatenate([k1 * ck - k2 * sk, k2 * ck + k1 * sk], axis=0).astype(BF16)
-    copies[1].wait()
+    copies[2].wait()
     weighted = (upstream[...].astype(F32) * risk).astype(BF16)
     for head in range(2):
         cols = pl.ds(head * HEAD, HEAD)
@@ -356,28 +359,30 @@
         pressure = jnp.dot(weighted[:, HEAD * head : HEAD * head + HEAD], values, preferred_element_type=F32)
         centre = jnp.sum(attend * pressure, axis=1, keepdims=True)
         slope = (attend * (pressure - centre)).astype(BF16)
-        dq_rot = (
-            lax.dot_general(slope, keys, (((1,), (1,)), ((), ())), preferred_element_type=F32)
+        turned_dq = (
+            lax.dot_general(keys, slope, (((1,), (1,)), ((), ())), preferred_element_type=F32)
             * scaling
         )
-        dq = dq_rot * cq - pltpu.roll(dq_rot, 64, 1) * sq
-        dq_out[cols, :] = dq.astype(BF16).T
-    for copy in copies[2:]:
+        d1, d2 = turned_dq[:64], turned_dq[64:]
+        dq_out[HEAD * head : HEAD * head + 64, :] = (d1 * ck + d2 * sk).astype(BF16)
+        dq_out[HEAD * head + 64 : HEAD * head + HEAD, :] = (d2 * ck - d1 * sk).astype(BF16)
+    for copy in copies[3:]:
         copy.wait()
 
 
-def attend(where, block_mask, risk_weight, parts, kv, upstream, tables, states):
+def attend(where, block_mask, risk_weight, parts, kv, upstream, tables, turned, states):
     own = jax.ShapeDtypeStruct((TOK, 2048), BF16)
     square = jax.ShapeDtypeStruct((TOK, 256), BF16)
     return pl.pallas_call(
         attend_kernel,
         out_shape=(square, square, own),
-        in_specs=[*[in_smem()] * 3, *in_vmem(2), *[in_hbm()] * 3],
+        in_specs=[*[in_smem()] * 3, *in_vmem(2), *[in_hbm()] * 4],
         out_specs=tuple(in_vmem(3)),
         scratch_shapes=[
             pltpu.VMEM((TOK, 256), BF16),
             pltpu.VMEM((TOK, 2 * HEAD), F32),
-            pltpu.SemaphoreType.DMA((10,)),
+            pltpu.VMEM((HEAD, TOK), F32),
+            pltpu.SemaphoreType.DMA((11,)),
         ],
         compiler_params=params(),
         name="attend",
@@ -389,6 +394,7 @@
         kv,
         held(upstream),
         held(tables),
+        held(turned),
         held(states),
     )
 
@@ -436,9 +442,8 @@
 
 def shards(states, query_weight, key_matrix, value_matrix, block_mask, risk_weight, upstream):
     place = lax.axis_index(GROUP)
-    resting = np.array([[resting_z(z, block) for block in range(8)] for z in range(8)], np.int32)
-    resting = jnp.asarray(resting)[lax.axis_index(("yh", "xh", "xb"))]
-    where = jnp.stack([lax.axis_index("c"), place]).astype(jnp.int32)
+    plane = lax.axis_index(("yh", "xh", "xb"))
+    where = jnp.stack([lax.axis_index("c"), place, plane]).astype(jnp.int32)
 
     first, second = pack(where, query_weight, key_matrix.T, value_matrix.T)
     first = lax.ppermute(first, AXES, home_pairs(0))
@@ -446,7 +451,8 @@
     outgoing = cut(where, states)
     weights = copies(where, first, second, outgoing[0])
 
-    up, two, down = gate(outgoing, weights)
+    (two,) = gate(outgoing[1:2], second)
+    up, down = gate((outgoing[0], outgoing[2]), held(weights))
     near = (
         lax.ppermute(down, AXES, ring_pairs(-1, -1)),
         lax.ppermute(two, AXES, ring_pairs(2, -2)),
@@ -455,7 +461,7 @@
     far = [swap_core(x) for x in near]
     weights = lax.all_to_all(weights, OTHERS, split_axis=0, concat_axis=0)
 
-    parts = project(jnp.concatenate([where, resting]), states, near, far, weights)
+    parts = project(where, states, near, far, weights)
     parts = lax.all_to_all(parts, GROUP, split_axis=0, concat_axis=0)
     kv = jnp.sum(parts[:, 256:].astype(F32), axis=0)
     kv = lax.all_gather(kv, ("xb", "c"), axis=0, tiled=False)
@@ -468,9 +474,10 @@
     angles = places.astype(F32)[:, None] * frequency[None, :]
     cosine, sine = jnp.cos(angles), jnp.sin(angles)
     tables = jnp.concatenate([cosine, cosine, -sine, sine], axis=1)
+    turned = jnp.concatenate([cosine.T, sine.T], axis=0)
 
     attn_out, dq, own = attend(
-        where, block_mask, risk_weight, parts, kv, upstream, tables, states
+        where, block_mask, risk_weight, parts, kv, upstream, tables, turned, states
     )
     slopes = lax.all_gather(dq, GROUP, axis=0, tiled=False)
     terms = gradient(where, own, near, far, slopes)

time: 162 us -> 161 us (level)
  waiting for transfers between devices: 40.6 us -> 36.9 us
  starting transfers between devices: 45.1 us -> 47.6 us
    ppermute x1, waiting for transfers between devices: 10.5 us -> 0.53 us  [shards(): lax.ppermute(down, AXES, ring_pairs(-1, -1))]
    ppermute x1, waiting for transfers between devices: 2.72 us -> 11 us  [shards(): lax.ppermute(two, AXES, ring_pairs(2, -2))]
    ppermute x1, starting transfers between devices: 1.92 us -> 5.78 us  [shards(): lax.ppermute(down, AXES, ring_pairs(-1, -1))]
    ppermute x1, starting transfers between devices: 4.93 us -> 2.3 us  [shards(): lax.ppermute(two, AXES, ring_pairs(2, -2))]
where the time goes in v11:
time: 161 us; the launch traced here: 160 us
  blocking collectives  54.7 us (34%)
  starting transfers between devices  47.6 us (30%)
  waiting for transfers between devices  36.9 us (23%)
  Pallas kernels  17.3 us (11%)
  other arithmetic  2.69 us (2%)
    all_to_all x1, blocking collectives, shards(): terms = lax.all_to_all(terms, OTHERS, split_axis=0, concat_axis=0)  32.8 us
    all_gather x1, blocking collectives, shards(): slopes = lax.all_gather(dq, GROUP, axis=0, tiled=False)  16.1 us
    all_to_all x1, waiting for transfers between devices, shards(): parts = lax.all_to_all(parts, GROUP, split_axis=0, concat_axis=0)  14.9 us
    all_to_all x1, starting transfers between devices, shards(): weights = lax.all_to_all(weights, OTHERS, split_axis=0, concat_axis=0)  14.8 us
    ppermute x1, waiting for transfers between devices, shards(): lax.ppermute(two, AXES, ring_pairs(2, -2))  11 us
    ppermute x1, starting transfers between devices, shards(): first = lax.ppermute(first, AXES, home_pairs(0))  7.81 us
    ppermute x3, starting transfers between devices, swap_core(): return lax.ppermute(value, 'c', [(0, 1), (1, 0)])  7.69 us
    ppermute x1, waiting for transfers between devices, shards(): second = lax.ppermute(second, AXES, home_pairs(1))  6.04 us
  transfers between devices with their start and end apart: 10, of which 6 were waited for; matrix products, arithmetic and copies ran while one was open for 2% of the time, Pallas kernels for 1%

profile of v11, /device:TPU:6, one launch (start us, length us, event | category | flops | bytes accessed | tf_op | source)
XLA Modules:
  0.0 160.2 jit_solution(5918029364136875074)
XLA Ops:
  0.6 0.1 pad_add_fusion.where_ref
  0.7 1.6 pack_weights.1
  2.3 7.8 %collective-permute-start = (bf16[320,128]{1,0:T(8,128)(2,1)S(1)}, bf16[320,128]{1,0:T(8,128)(2,1)S(1)}, u32[]{:S(2)}, u32[]{:S(2)}) collective-permute-start(bf16[320,128]{1,0:T(8,128)(2,1)S(1)} %get-tuple-element.14), channel_id=1, source_target_pairs={{0,256},{1,288},{2,320},{3,352},{4,384},{5,416},{6,192},{7,224},{8... | collective-permute-start | bytes 245768 | tf_op jit(solution)/shard_map/ppermute | solution.py:449
  10.1 3.0 %collective-permute-start.1 = (bf16[320,128]{1,0:T(8,128)(2,1)S(1)}, bf16[320,128]{1,0:T(8,128)(2,1)S(1)}, u32[]{:S(2)}, u32[]{:S(2)}) collective-permute-start(bf16[320,128]{1,0:T(8,128)(2,1)S(1)} %get-tuple-element.15), channel_id=1, source_target_pairs={{0,272},{1,304},{2,336},{3,368},{4,400},{5,432},{6,208},{7,240},{8... | collective-permute-start | bytes 245768 | tf_op jit(solution)/shard_map/ppermute | solution.py:450
  13.1 2.1 %cut_states.1 = (bf16[256,1024]{1,0:T(8,128)(2,1)S(1)}, bf16[256,1024]{1,0:T(8,128)(2,1)S(1)}, bf16[256,1024]{1,0:T(8,128)(2,1)S(1)}) custom-call(s32[3]{0:T(128)S(1)} %pad_add_fusion.where_ref, bf16[256,8192]{1,0:T(8,128)(2,1)} %states_ref.5), custom_call_target="tpu_custom_call" | custom-call | tf_op jit(solution)/shard_map/cut_states/pallas_call | solution.py:145
  15.2 0.0 collective-permute-done.first
  15.2 6.0 %collective-permute-done.1.second.refs_1_ = bf16[320,128]{1,0:T(8,128)(2,1)S(1)} collective-permute-done((bf16[320,128]{1,0:T(8,128)(2,1)S(1)}, bf16[320,128]{1,0:T(8,128)(2,1)S(1)}, u32[]{:S(2)}, u32[]{:S(2)}) %collective-permute-start.1) | collective-permute-done | bytes 81952 | tf_op jit(solution)/shard_map/ppermute | solution.py:450
  21.3 1.8 %weight_copies.1.refs_2_ = bf16[8,2,320,128]{3,2,1,0:T(8,128)(2,1)} custom-call(s32[3]{0:T(128)S(1)} %pad_add_fusion.where_ref, bf16[320,128]{1,0:T(8,128)(2,1)S(1)} %collective-permute-done.first, bf16[320,128]{1,0:T(8,128)(2,1)S(1)} %collective-permute-done.1.second.refs_1_, bf16[256,1024]{1,0:T(8,128)(2,1)S(1)} %get-tuple-element.12.after.refs_0_), custom_call_target="tpu_custom_call" | custom-call | tf_op jit(solution)/shard_map/weight_copies/pallas_call | solution.py:201
  23.0 14.8 %all-to-all-start = ((bf16[8,2,320,128]{3,2,1,0:T(8,128)(2,1)}), bf16[8,2,320,128]{3,2,1,0:T(8,128)(2,1)}, u32[]{:S(2)}, u32[]{:S(2)}) async-start(bf16[8,2,320,128]{3,2,1,0:T(8,128)(2,1)} %weight_copies.1.refs_2_), calls=%async_computation | async-start | bytes 2621440 | tf_op jit(solution)/shard_map/all_to_all | solution.py:462
  37.8 0.0 copy-start.2
  37.8 2.3 %collective-permute-start.3 = (bf16[256,1024]{1,0:T(8,128)(2,1)S(1)}, bf16[256,1024]{1,0:T(8,128)(2,1)S(1)}, u32[]{:S(2)}, u32[]{:S(2)}) collective-permute-start(bf16[256,1024]{1,0:T(8,128)(2,1)S(1)} %gate.3), channel_id=1, source_target_pairs={{0,32},{1,41},{2,34},{3,43},{4,36},{5,45},{6,38},{7,47},{16,48},{1... | collective-permute-start | bytes 1572872 | tf_op jit(solution)/shard_map/ppermute | solution.py:458
  40.1 5.8 %collective-permute-start.2 = (bf16[256,1024]{1,0:T(8,128)(2,1)S(1)}, bf16[256,1024]{1,0:T(8,128)(2,1)S(1)}, u32[]{:S(2)}, u32[]{:S(2)}) collective-permute-start(bf16[256,1024]{1,0:T(8,128)(2,1)S(1)} %get-tuple-element.16), channel_id=1, source_target_pairs={{0,56},{1,57},{2,58},{3,59},{4,60},{5,61},{6,62},{7,63},{16,0},{17... | collective-permute-start | bytes 1572872 | tf_op jit(solution)/shard_map/ppermute | solution.py:457
  45.9 1.9 %collective-permute-start.4 = (bf16[256,1024]{1,0:T(8,128)(2,1)S(1)}, bf16[256,1024]{1,0:T(8,128)(2,1)S(1)}, u32[]{:S(2)}, u32[]{:S(2)}) collective-permute-start(bf16[256,1024]{1,0:T(8,128)(2,1)S(1)} %get-tuple-element.18), channel_id=1, source_target_pairs={{0,16},{1,17},{2,18},{3,19},{4,20},{5,21},{6,22},{7,23},{16,32},{1... | collective-permute-start | bytes 1572872 | tf_op jit(solution)/shard_map/ppermute | solution.py:459
  47.9 11.0 %collective-permute-done.3.n2 = bf16[256,1024]{1,0:T(8,128)(2,1)S(1)} collective-permute-done((bf16[256,1024]{1,0:T(8,128)(2,1)S(1)}, bf16[256,1024]{1,0:T(8,128)(2,1)S(1)}, u32[]{:S(2)}, u32[]{:S(2)}) %collective-permute-start.3) | collective-permute-done | bytes 524320 | tf_op jit(solution)/shard_map/ppermute | solution.py:458
  58.8 1.9 %collective-permute-start.6 = (bf16[256,1024]{1,0:T(8,128)(2,1)S(1)}, bf16[256,1024]{1,0:T(8,128)(2,1)S(1)}, u32[]{:S(2)}, u32[]{:S(2)}) collective-permute-start(bf16[256,1024]{1,0:T(8,128)(2,1)S(1)} %collective-permute-done.3.n2), channel_id=1, source_target_pairs={{0,1},{1,0},{2,3},{3,2},{4,5},{5,4},{6,7},{7,6},{8,9},{9,8},{10,11... | collective-permute-start | bytes 1572872 | tf_op jit(solution)/shard_map/ppermute | solution.py:59
  60.7 0.5 collective-permute-done.2.n1
  61.3 3.9 %collective-permute-start.5 = (bf16[256,1024]{1,0:T(8,128)(2,1)S(1)}, bf16[256,1024]{1,0:T(8,128)(2,1)S(1)}, u32[]{:S(2)}, u32[]{:S(2)}) collective-permute-start(bf16[256,1024]{1,0:T(8,128)(2,1)S(1)} %collective-permute-done.2.n1), channel_id=1, source_target_pairs={{0,1},{1,0},{2,3},{3,2},{4,5},{5,4},{6,7},{7,6},{8,9},{9,8},{10,11... | collective-permute-start | bytes 1572872 | tf_op jit(solution)/shard_map/ppermute | solution.py:59
  65.2 2.7 %collective-permute-done.4.n3 = bf16[256,1024]{1,0:T(8,128)(2,1)S(1)} collective-permute-done((bf16[256,1024]{1,0:T(8,128)(2,1)S(1)}, bf16[256,1024]{1,0:T(8,128)(2,1)S(1)}, u32[]{:S(2)}, u32[]{:S(2)}) %collective-permute-start.4) | collective-permute-done | bytes 524320 | tf_op jit(solution)/shard_map/ppermute | solution.py:459
  67.9 1.9 %collective-permute-start.7 = (bf16[256,1024]{1,0:T(8,128)(2,1)S(1)}, bf16[256,1024]{1,0:T(8,128)(2,1)S(1)}, u32[]{:S(2)}, u32[]{:S(2)}) collective-permute-start(bf16[256,1024]{1,0:T(8,128)(2,1)S(1)} %collective-permute-done.4.n3), channel_id=1, source_target_pairs={{0,1},{1,0},{2,3},{3,2},{4,5},{5,4},{6,7},{7,6},{8,9},{9,8},{10,11... | collective-permute-start | bytes 1572872 | tf_op jit(solution)/shard_map/ppermute | solution.py:59
  69.8 0.0 copy-done.2
  69.8 0.1 reduce_sum.19
  69.9 0.0 collective-permute-done.6.f2
  69.9 0.0 collective-permute-done.5.f1
  69.9 1.7 %collective-permute-done.7.f3 = bf16[256,1024]{1,0:T(8,128)(2,1)S(1)} collective-permute-done((bf16[256,1024]{1,0:T(8,128)(2,1)S(1)}, bf16[256,1024]{1,0:T(8,128)(2,1)S(1)}, u32[]{:S(2)}, u32[]{:S(2)}) %collective-permute-start.7) | collective-permute-done | bytes 524320 | tf_op jit(solution)/shard_map/ppermute | solution.py:59
  71.7 0.0 copy-start
  71.7 0.0 all-to-all-done.weights_ref
  71.7 5.7 %project.1 = bf16[4,320,256]{2,1,0:T(8,128)(2,1)} custom-call(s32[3]{0:T(128)S(1)} %pad_add_fusion.where_ref, bf16[256,8192]{1,0:T(8,128)(2,1)} %states_ref.5, bf16[256,1024]{1,0:T(8,128)(2,1)S(1)} %collective-permute-done.2.n1, bf16[256,1024]{1,0:T(8,128)(2,1)S(1)} %collective-permute-done.3.n2, bf16[256,1024]{1,0:T(8,128)(2,1)S(1)} %collective-permute-done.4.n3, ...), custom_call_target="tpu_custom_call" | custom-call | tf_op jit(solution)/shard_map/project/pallas_call | solution.py:278
  77.3 0.0 copy-done
  77.4 4.4 %all-to-all-start.1 = ((bf16[4,320,256]{2,1,0:T(8,128)(2,1)}), bf16[4,320,256]{2,1,0:T(8,128)(2,1)S(1)}, u32[]{:S(2)}, u32[]{:S(2)}) async-start(bf16[4,320,256]{2,1,0:T(8,128)(2,1)} %project.1), calls=%async_computation.1 | async-start | bytes 1310720 | tf_op jit(solution)/shard_map/all_to_all | solution.py:465
  81.7 0.0 copy-start.3
  81.7 0.1 add_convert_fusion
  81.8 0.1 convert_element_type.15
  81.9 0.3 multiply_cosine_fusion.1
  82.2 0.7 pad_maximum_fusion.1.turned_ref
  82.9 0.5 multiply_cosine_fusion
  83.4 0.9 pad_maximum_fusion.tables_ref
  84.3 14.9 %all-to-all-done.1.parts = bf16[4,320,256]{2,1,0:T(8,128)(2,1)S(1)} async-done(((bf16[4,320,256]{2,1,0:T(8,128)(2,1)}), bf16[4,320,256]{2,1,0:T(8,128)(2,1)S(1)}, u32[]{:S(2)}, u32[]{:S(2)}) %all-to-all-start.1) | async-done | bytes 655392 | tf_op jit(solution)/shard_map/all_to_all | solution.py:465
  99.3 5.8 %all-gather = f32[256,256]{1,0:T(8,128)S(1)} all-gather(f32[64,256]{1,0:T(8,128)S(1)} %convert_reduce_fusion), channel_id=2, replica_groups=mesh['zh'=4,'zb'=2,'yu'=2,'yb'=2,'yh'=2,'xh'=2,'xb'=2,'c'=2] {'xb','c'}, dimensions={0}, use_global_device_ids=true | all-gather | bytes 327680 | tf_op jit(solution)/shard_map/all_gather | solution.py:467
  105.1 0.0 copy-done.3
  105.1 0.0 copy-start.1
  105.1 3.5 %attend.1 = (bf16[256,256]{1,0:T(8,128)(2,1)}, bf16[256,256]{1,0:T(8,128)(2,1)S(1)}, bf16[256,2048]{1,0:T(8,128)(2,1)S(1)}) custom-call(s32[3]{0:T(128)S(1)} %pad_add_fusion.where_ref, s32[4,4]{1,0:T(4,128)S(1)} %copy-done.2, f32[4]{0:T(128)S(1)} %copy-done.3, bf16[4,320,256]{2,1,0:T(8,128)(2,1)S(1)} %all-to-all-done.1.parts, f32[4,64,256]{2,1,0:T(8,128)S(1)} %bitcast.8, ...), custom_call_target="tpu_custom_call" | custom-call | tf_op jit(solution)/shard_map/attend/pallas_call | solution.py:376
  108.5 16.1 %all-gather.1 = bf16[1024,256]{1,0:T(8,128)(2,1)S(1)} all-gather(bf16[256,256]{1,0:T(8,128)(2,1)S(1)} %get-tuple-element.21), channel_id=3, replica_groups=mesh['zh'=4,'zb'=2,'yu'=2,'yb'=2,'yh'=2,'xh'=2,'xb'=2,'c'=2] {'yu','yb'}, dimensions={0}, use_global_device_ids=true | all-gather | bytes 655360 | tf_op jit(solution)/shard_map/all_gather | solution.py:482
  124.7 0.0 copy-done.1
  124.7 1.8 %gradient.1 = bf16[8,256,256]{2,1,0:T(8,128)(2,1)S(1)} custom-call(s32[3]{0:T(128)S(1)} %pad_add_fusion.where_ref, bf16[256,2048]{1,0:T(8,128)(2,1)S(1)} %get-tuple-element.20.own, bf16[256,1024]{1,0:T(8,128)(2,1)S(1)} %collective-permute-done.2.n1, bf16[256,1024]{1,0:T(8,128)(2,1)S(1)} %collective-permute-done.3.n2, ...), custom_call_target="tpu_custom_call" | custom-call | tf_op jit(solution)/shard_map/gradient/pallas_call | solution.py:418
  126.5 32.8 %all_to_all.15.terms = bf16[8,256,256]{2,1,0:T(8,128)(2,1)S(1)} all-to-all(bf16[8,256,256]{2,1,0:T(8,128)(2,1)S(1)} %gradient.1), channel_id=1, replica_groups=mesh['zh'=4,'zb'=2,'yu'=2,'yb'=2,'yh'=2,'xh'=2,'xb'=2,'c'=2] {'zh','zb'}, dimensions={0} | all-to-all | bytes 2097152 | tf_op jit(solution)/shard_map/all_to_all | solution.py:484
  159.3 0.9 add_up.1
  (5 shorter events, 0.0 us)
Async XLA Ops:
  2.3 12.9 %collective-permute-start = (bf16[320,128]{1,0:T(8,128)(2,1)S(1)}, bf16[320,128]{1,0:T(8,128)(2,1)S(1)}, u32[]{:S(2)}, u32[]{:S(2)}) collective-permute-start(bf16[320,128]{1,0:T(8,128)(2,1)S(1)} %get-tuple-element.14), channel_id=1, source_target_pairs={{0,256},{1,288},{2,320},{3,352},{4,384},{5,416},{6,192},{7,224},{8... | collective-permute-start | bytes 245768 | tf_op jit(solution)/shard_map/ppermute | solution.py:449
  10.1 11.1 %collective-permute-start.1 = (bf16[320,128]{1,0:T(8,128)(2,1)S(1)}, bf16[320,128]{1,0:T(8,128)(2,1)S(1)}, u32[]{:S(2)}, u32[]{:S(2)}) collective-permute-start(bf16[320,128]{1,0:T(8,128)(2,1)S(1)} %get-tuple-element.15), channel_id=1, source_target_pairs={{0,272},{1,304},{2,336},{3,368},{4,400},{5,432},{6,208},{7,240},{8... | collective-permute-start | bytes 245768 | tf_op jit(solution)/shard_map/ppermute | solution.py:450
  23.0 48.6 %all-to-all-start = ((bf16[8,2,320,128]{3,2,1,0:T(8,128)(2,1)}), bf16[8,2,320,128]{3,2,1,0:T(8,128)(2,1)}, u32[]{:S(2)}, u32[]{:S(2)}) async-start(bf16[8,2,320,128]{3,2,1,0:T(8,128)(2,1)} %weight_copies.1.refs_2_), calls=%async_computation | async-start | bytes 2621440 | tf_op jit(solution)/shard_map/all_to_all | solution.py:462
  37.8 32.0 %copy-start.2 = (s32[4,4]{1,0:T(4,128)S(1)}, s32[4,4]{1,0:T(4,128)}, u32[]{:S(2)}) copy-start(s32[4,4]{1,0:T(4,128)} %mask_ref.1) | copy-start | bytes 196
  37.8 21.0 %collective-permute-start.3 = (bf16[256,1024]{1,0:T(8,128)(2,1)S(1)}, bf16[256,1024]{1,0:T(8,128)(2,1)S(1)}, u32[]{:S(2)}, u32[]{:S(2)}) collective-permute-start(bf16[256,1024]{1,0:T(8,128)(2,1)S(1)} %gate.3), channel_id=1, source_target_pairs={{0,32},{1,41},{2,34},{3,43},{4,36},{5,45},{6,38},{7,47},{16,48},{1... | collective-permute-start | bytes 1572872 | tf_op jit(solution)/shard_map/ppermute | solution.py:458
  40.1 21.1 %collective-permute-start.2 = (bf16[256,1024]{1,0:T(8,128)(2,1)S(1)}, bf16[256,1024]{1,0:T(8,128)(2,1)S(1)}, u32[]{:S(2)}, u32[]{:S(2)}) collective-permute-start(bf16[256,1024]{1,0:T(8,128)(2,1)S(1)} %get-tuple-element.16), channel_id=1, source_target_pairs={{0,56},{1,57},{2,58},{3,59},{4,60},{5,61},{6,62},{7,63},{16,0},{17... | collective-permute-start | bytes 1572872 | tf_op jit(solution)/shard_map/ppermute | solution.py:457
  45.9 21.9 %collective-permute-start.4 = (bf16[256,1024]{1,0:T(8,128)(2,1)S(1)}, bf16[256,1024]{1,0:T(8,128)(2,1)S(1)}, u32[]{:S(2)}, u32[]{:S(2)}) collective-permute-start(bf16[256,1024]{1,0:T(8,128)(2,1)S(1)} %get-tuple-element.18), channel_id=1, source_target_pairs={{0,16},{1,17},{2,18},{3,19},{4,20},{5,21},{6,22},{7,23},{16,32},{1... | collective-permute-start | bytes 1572872 | tf_op jit(solution)/shard_map/ppermute | solution.py:459
  58.8 11.1 %collective-permute-start.6 = (bf16[256,1024]{1,0:T(8,128)(2,1)S(1)}, bf16[256,1024]{1,0:T(8,128)(2,1)S(1)}, u32[]{:S(2)}, u32[]{:S(2)}) collective-permute-start(bf16[256,1024]{1,0:T(8,128)(2,1)S(1)} %collective-permute-done.3.n2), channel_id=1, source_target_pairs={{0,1},{1,0},{2,3},{3,2},{4,5},{5,4},{6,7},{7,6},{8,9},{9,8},{10,11... | collective-permute-start | bytes 1572872 | tf_op jit(solution)/shard_map/ppermute | solution.py:59
  61.3 8.7 %collective-permute-start.5 = (bf16[256,1024]{1,0:T(8,128)(2,1)S(1)}, bf16[256,1024]{1,0:T(8,128)(2,1)S(1)}, u32[]{:S(2)}, u32[]{:S(2)}) collective-permute-start(bf16[256,1024]{1,0:T(8,128)(2,1)S(1)} %collective-permute-done.2.n1), channel_id=1, source_target_pairs={{0,1},{1,0},{2,3},{3,2},{4,5},{5,4},{6,7},{7,6},{8,9},{9,8},{10,11... | collective-permute-start | bytes 1572872 | tf_op jit(solution)/shard_map/ppermute | solution.py:59
  67.9 3.8 %collective-permute-start.7 = (bf16[256,1024]{1,0:T(8,128)(2,1)S(1)}, bf16[256,1024]{1,0:T(8,128)(2,1)S(1)}, u32[]{:S(2)}, u32[]{:S(2)}) collective-permute-start(bf16[256,1024]{1,0:T(8,128)(2,1)S(1)} %collective-permute-done.4.n3), channel_id=1, source_target_pairs={{0,1},{1,0},{2,3},{3,2},{4,5},{5,4},{6,7},{7,6},{8,9},{9,8},{10,11... | collective-permute-start | bytes 1572872 | tf_op jit(solution)/shard_map/ppermute | solution.py:59
  71.7 5.7 %copy-start = (bf16[256,1024]{1,0:T(8,128)(2,1)}, bf16[256,1024]{1,0:T(8,128)(2,1)S(1)}, u32[]{:S(2)}) copy-start(bf16[256,1024]{1,0:T(8,128)(2,1)S(1)} %collective-permute-done.7.f3) | copy-start | bytes 1572868
  77.4 21.9 %all-to-all-start.1 = ((bf16[4,320,256]{2,1,0:T(8,128)(2,1)}), bf16[4,320,256]{2,1,0:T(8,128)(2,1)S(1)}, u32[]{:S(2)}, u32[]{:S(2)}) async-start(bf16[4,320,256]{2,1,0:T(8,128)(2,1)} %project.1), calls=%async_computation.1 | async-start | bytes 1310720 | tf_op jit(solution)/shard_map/all_to_all | solution.py:465
  81.7 23.3 %copy-start.3 = (f32[4]{0:T(128)S(1)}, f32[4]{0:T(128)}, u32[]{:S(2)}) copy-start(f32[4]{0:T(128)} %risk_ref.1) | copy-start | bytes 52
  105.1 19.6 %copy-start.1 = (bf16[256,1024]{1,0:T(8,128)(2,1)S(1)}, bf16[256,1024]{1,0:T(8,128)(2,1)}, u32[]{:S(2)}) copy-start(bf16[256,1024]{1,0:T(8,128)(2,1)} %copy-done) | copy-start | bytes 1572868

commit v12 on v11

--- a/solution.py
+++ b/solution.py
@@ -157,7 +157,7 @@
     del refs
 
 
-def gate(parts, after):
+def gate(parts, after, cost=0):
     count = len(parts)
     return pl.pallas_call(
         gate_kernel,
@@ -165,6 +165,7 @@
         in_specs=[anywhere()] * (count + 1),
         out_specs=tuple([anywhere()] * count),
         input_output_aliases={i: i for i in range(count)},
+        cost_estimate=pl.CostEstimate(flops=cost, bytes_accessed=0, transcendentals=0),
         compiler_params=params(),
         name="gate",
     )(*parts, after)
@@ -223,6 +224,7 @@
     own,
     weights,
     w_all,
+    total,
     result,
     sems,
     out_sems,
@@ -237,7 +239,7 @@
     copies = own_columns(where_ref, states_ref, own, sems)
     for copy in arrivals + copies:
         copy.start()
-    for part in range(8):
+    def unpack(part):
         arrivals[part].wait()
         start = 256 * part
         for head in range(2):
@@ -255,14 +257,20 @@
         return jnp.dot(x, w_all[rows, :], preferred_element_type=F32)
 
     low, high = pl.ds(0, 1024), pl.ds(1024, 1024)
+    for part in range(4):
+        unpack(part)
+    for number, near in enumerate((n1, n2, n3)):
+        total[number] = product(near[...], low)
+    for part in range(4, 8):
+        unpack(part)
     departures = []
-    for number, (near, far) in enumerate(((n1, f1), (n2, f2), (n3, f3), (None, None))):
-        if near is None:
+    for number, far in enumerate((f1, f2, f3, None)):
+        if far is None:
             for copy in copies:
                 copy.wait()
             linear = product(own[...], pl.ds(0, 2048))
         else:
-            linear = product(near[...], low) + product(far[...], high)
+            linear = total[number] + product(far[...], high)
         result[number, :256, :] = linear[:, :256].astype(BF16)
         result[number, 256:, :] = linear[:, 256:].T.astype(BF16)
         other = (where_ref[1] + number + 1) % 4
@@ -284,6 +292,7 @@
             pltpu.VMEM((TOK, 2048), BF16),
             pltpu.VMEM((8, 2, 320, 128), BF16),
             pltpu.VMEM((2048, 320), BF16),
+            pltpu.VMEM((3, TOK, 320), F32),
             pltpu.VMEM((4, 320, 256), BF16),
             pltpu.SemaphoreType.DMA((16,)),
             pltpu.SemaphoreType.DMA((4,)),
@@ -315,7 +324,6 @@
         pltpu.make_async_copy(tables_ref, tables, sems.at[8]),
         pltpu.make_async_copy(turned_ref, turned, sems.at[9]),
         pltpu.make_async_copy(upstream_ref, upstream, sems.at[10]),
-        *own_columns(where_ref, states_ref, own, sems),
     ]
     for copy in copies:
         copy.start()
@@ -337,11 +345,18 @@
 
     copies[0].wait()
     copies[1].wait()
-    cq, sq = tables[:, :HEAD], tables[:, HEAD:]
+    copies[2].wait()
+    columns = own_columns(where_ref, states_ref, own, sems)
+    for copy in columns:
+        copy.start()
+    half = lax.broadcasted_iota(jnp.int32, (TOK, HEAD), 1) < HEAD // 2
+    table = tables[...]
+    turned_table = pltpu.roll(table, HEAD // 2, 1)
+    cq = jnp.where(half, table, turned_table)
+    sq = jnp.where(half, -turned_table, table)
     ck, sk = turned[:64], turned[64:]
     k1, k2 = k_lin[:64], k_lin[64:]
     keys = jnp.concatenate([k1 * ck - k2 * sk, k2 * ck + k1 * sk], axis=0).astype(BF16)
-    copies[2].wait()
     weighted = (upstream[...].astype(F32) * risk).astype(BF16)
     for head in range(2):
         cols = pl.ds(head * HEAD, HEAD)
@@ -366,7 +381,7 @@
         d1, d2 = turned_dq[:64], turned_dq[64:]
         dq_out[HEAD * head : HEAD * head + 64, :] = (d1 * ck + d2 * sk).astype(BF16)
         dq_out[HEAD * head + 64 : HEAD * head + HEAD, :] = (d2 * ck - d1 * sk).astype(BF16)
-    for copy in copies[3:]:
+    for copy in columns:
         copy.wait()
 
 
@@ -380,7 +395,7 @@
         out_specs=tuple(in_vmem(3)),
         scratch_shapes=[
             pltpu.VMEM((TOK, 256), BF16),
-            pltpu.VMEM((TOK, 2 * HEAD), F32),
+            pltpu.VMEM((TOK, HEAD), F32),
             pltpu.VMEM((HEAD, TOK), F32),
             pltpu.SemaphoreType.DMA((11,)),
         ],
@@ -451,14 +466,15 @@
     outgoing = cut(where, states)
     weights = copies(where, first, second, outgoing[0])
 
-    (two,) = gate(outgoing[1:2], second)
-    up, down = gate((outgoing[0], outgoing[2]), held(weights))
+    up, two, down = gate(outgoing, second)
     near = (
         lax.ppermute(down, AXES, ring_pairs(-1, -1)),
         lax.ppermute(two, AXES, ring_pairs(2, -2)),
         lax.ppermute(up, AXES, ring_pairs(1, 1)),
     )
     far = [swap_core(x) for x in near]
+    tokens = gate((*near, *far), where, cost=10**11)
+    near, far = tokens[:3], tokens[3:]
     weights = lax.all_to_all(weights, OTHERS, split_axis=0, concat_axis=0)
 
     parts = project(where, states, near, far, weights)
@@ -473,7 +489,7 @@
     )
     angles = places.astype(F32)[:, None] * frequency[None, :]
     cosine, sine = jnp.cos(angles), jnp.sin(angles)
-    tables = jnp.concatenate([cosine, cosine, -sine, sine], axis=1)
+    tables = jnp.concatenate([cosine, sine], axis=1)
     turned = jnp.concatenate([cosine.T, sine.T], axis=0)
 
     attn_out, dq, own = attend(

time: 161 us -> 191 us (1.19)
  waiting for transfers between devices: 36.9 us -> 70.3 us
  blocking collectives: 54.7 us -> 50.9 us
    all_to_all x1, waiting for transfers between devices: 0.01 us -> 35.1 us  [shards(): weights = lax.all_to_all(weights, OTHERS, split_axis=0, concat_axis=0)]
    ppermute x1, waiting for transfers between devices: 0.01 us -> 6.16 us  [shards(): first = lax.ppermute(first, AXES, home_pairs(0))]
    ppermute x1, waiting for transfers between devices: 6.04 us -> 0.01 us  [shards(): second = lax.ppermute(second, AXES, home_pairs(1))]
    ppermute x1, starting transfers between devices: 2.95 us -> 8.82 us  [shards(): second = lax.ppermute(second, AXES, home_pairs(1))]
    ppermute x1, starting transfers between devices: 7.81 us -> 1.94 us  [shards(): first = lax.ppermute(first, AXES, home_pairs(0))]
    ppermute x1, waiting for transfers between devices: 11 us -> 5.29 us  [shards(): lax.ppermute(two, AXES, ring_pairs(2, -2))]
    ppermute x3, starting transfers between devices: 7.69 us -> 13.3 us  [swap_core(): return lax.ppermute(value, 'c', [(0, 1), (1, 0)])]
    all_to_all x1, starting transfers between devices: 14.8 us -> 10.2 us  [shards(): weights = lax.all_to_all(weights, OTHERS, split_axis=0, concat_axis=0)]
  transfers between devices with their start and end apart: 10 -> 10, of which waited for: 6 -> 6; matrix products, arithmetic and copies ran while one was open for 2% -> 1% of each run, Pallas kernels for 1% -> 1%
where the time goes in v12:
time: 191 us
  waiting for transfers between devices  70.3 us (37%)
  blocking collectives  50.9 us (27%)
  starting transfers between devices  47.9 us (25%)
  Pallas kernels  17.9 us (9%)
  other arithmetic  2.57 us (1%)
    all_to_all x1, waiting for transfers between devices, shards(): weights = lax.all_to_all(weights, OTHERS, split_axis=0, concat_axis=0)  35.1 us
    all_to_all x1, blocking collectives, shards(): terms = lax.all_to_all(terms, OTHERS, split_axis=0, concat_axis=0)  28.9 us
    all_gather x1, blocking collectives, shards(): slopes = lax.all_gather(dq, GROUP, axis=0, tiled=False)  16.1 us
    all_to_all x1, waiting for transfers between devices, shards(): parts = lax.all_to_all(parts, GROUP, split_axis=0, concat_axis=0)  15.3 us
    ppermute x3, starting transfers between devices, swap_core(): return lax.ppermute(value, 'c', [(0, 1), (1, 0)])  13.3 us
    all_to_all x1, starting transfers between devices, shards(): weights = lax.all_to_all(weights, OTHERS, split_axis=0, concat_axis=0)  10.2 us
    ppermute x1, starting transfers between devices, shards(): second = lax.ppermute(second, AXES, home_pairs(1))  8.82 us
    ppermute x1, waiting for transfers between devices, shards(): first = lax.ppermute(first, AXES, home_pairs(0))  6.16 us
  transfers between devices with their start and end apart: 10, of which 6 were waited for; matrix products, arithmetic and copies ran while one was open for 1% of the time, Pallas kernels for 1%

profile of v12, /device:TPU:6, one launch (start us, length us, event | category | flops | bytes accessed | tf_op | source)
XLA Modules:
  0.0 190.6 jit_solution(885899967449924474)
XLA Ops:
  0.6 0.1 pad_add_fusion.where_ref.refs_6_
  0.7 1.6 pack_weights.1
  2.3 8.8 %collective-permute-start = (bf16[320,128]{1,0:T(8,128)(2,1)S(1)}, bf16[320,128]{1,0:T(8,128)(2,1)S(1)}, u32[]{:S(2)}, u32[]{:S(2)}) collective-permute-start(bf16[320,128]{1,0:T(8,128)(2,1)S(1)} %get-tuple-element.22), channel_id=1, source_target_pairs={{0,272},{1,304},{2,336},{3,368},{4,400},{5,432},{6,208},{7,240},{8... | collective-permute-start | bytes 245768 | tf_op jit(solution)/shard_map/ppermute | solution.py:465
  11.1 1.9 %collective-permute-start.7 = (bf16[320,128]{1,0:T(8,128)(2,1)S(1)}, bf16[320,128]{1,0:T(8,128)(2,1)S(1)}, u32[]{:S(2)}, u32[]{:S(2)}) collective-permute-start(bf16[320,128]{1,0:T(8,128)(2,1)S(1)} %get-tuple-element.32), channel_id=1, source_target_pairs={{0,256},{1,288},{2,320},{3,352},{4,384},{5,416},{6,192},{7,224},{8... | collective-permute-start | bytes 245768 | tf_op jit(solution)/shard_map/ppermute | solution.py:464
  13.1 2.1 %cut_states.1 = (bf16[256,1024]{1,0:T(8,128)(2,1)S(1)}, bf16[256,1024]{1,0:T(8,128)(2,1)S(1)}, bf16[256,1024]{1,0:T(8,128)(2,1)S(1)}) custom-call(s32[3]{0:T(128)S(1)} %pad_add_fusion.where_ref.refs_6_, bf16[256,8192]{1,0:T(8,128)(2,1)} %states_ref.5), custom_call_target="tpu_custom_call" | custom-call | tf_op jit(solution)/shard_map/cut_states/pallas_call | solution.py:145
  15.2 0.0 collective-permute-done.refs_3_.second
  15.2 6.2 %collective-permute-done.7.first = bf16[320,128]{1,0:T(8,128)(2,1)S(1)} collective-permute-done((bf16[320,128]{1,0:T(8,128)(2,1)S(1)}, bf16[320,128]{1,0:T(8,128)(2,1)S(1)}, u32[]{:S(2)}, u32[]{:S(2)}) %collective-permute-start.7) | collective-permute-done | bytes 81952 | tf_op jit(solution)/shard_map/ppermute | solution.py:464
  21.4 1.8 weight_copies.1
  23.2 0.0 copy-start.2
  23.2 3.8 %collective-permute-start.1 = (bf16[256,1024]{1,0:T(8,128)(2,1)S(1)}, bf16[256,1024]{1,0:T(8,128)(2,1)S(1)}, u32[]{:S(2)}, u32[]{:S(2)}) collective-permute-start(bf16[256,1024]{1,0:T(8,128)(2,1)S(1)} %get-tuple-element.23), channel_id=1, source_target_pairs={{0,56},{1,57},{2,58},{3,59},{4,60},{5,61},{6,62},{7,63},{16,0},{17... | collective-permute-start | bytes 1572872 | tf_op jit(solution)/shard_map/ppermute | solution.py:471
  26.9 2.5 %collective-permute-start.2 = (bf16[256,1024]{1,0:T(8,128)(2,1)S(1)}, bf16[256,1024]{1,0:T(8,128)(2,1)S(1)}, u32[]{:S(2)}, u32[]{:S(2)}) collective-permute-start(bf16[256,1024]{1,0:T(8,128)(2,1)S(1)} %get-tuple-element.24), channel_id=1, source_target_pairs={{0,32},{1,41},{2,34},{3,43},{4,36},{5,45},{6,38},{7,47},{16,48},{1... | collective-permute-start | bytes 1572872 | tf_op jit(solution)/shard_map/ppermute | solution.py:472
  29.5 3.9 %collective-permute-start.3 = (bf16[256,1024]{1,0:T(8,128)(2,1)S(1)}, bf16[256,1024]{1,0:T(8,128)(2,1)S(1)}, u32[]{:S(2)}, u32[]{:S(2)}) collective-permute-start(bf16[256,1024]{1,0:T(8,128)(2,1)S(1)} %get-tuple-element.25), channel_id=1, source_target_pairs={{0,16},{1,17},{2,18},{3,19},{4,20},{5,21},{6,22},{7,23},{16,32},{1... | collective-permute-start | bytes 1572872 | tf_op jit(solution)/shard_map/ppermute | solution.py:473
  33.4 4.0 %collective-permute-done.1.refs_0_ = bf16[256,1024]{1,0:T(8,128)(2,1)S(1)} collective-permute-done((bf16[256,1024]{1,0:T(8,128)(2,1)S(1)}, bf16[256,1024]{1,0:T(8,128)(2,1)S(1)}, u32[]{:S(2)}, u32[]{:S(2)}) %collective-permute-start.1) | collective-permute-done | bytes 524320 | tf_op jit(solution)/shard_map/ppermute | solution.py:471
  37.4 9.5 %collective-permute-start.4 = (bf16[256,1024]{1,0:T(8,128)(2,1)S(1)}, bf16[256,1024]{1,0:T(8,128)(2,1)S(1)}, u32[]{:S(2)}, u32[]{:S(2)}) collective-permute-start(bf16[256,1024]{1,0:T(8,128)(2,1)S(1)} %collective-permute-done.1.refs_0_), channel_id=1, source_target_pairs={{0,1},{1,0},{2,3},{3,2},{4,5},{5,4},{6,7},{7,6},{8,9},{9,8},{10,11... | collective-permute-start | bytes 1572872 | tf_op jit(solution)/shard_map/ppermute | solution.py:59
  46.9 5.3 %collective-permute-done.2.refs_1_ = bf16[256,1024]{1,0:T(8,128)(2,1)S(1)} collective-permute-done((bf16[256,1024]{1,0:T(8,128)(2,1)S(1)}, bf16[256,1024]{1,0:T(8,128)(2,1)S(1)}, u32[]{:S(2)}, u32[]{:S(2)}) %collective-permute-start.2) | collective-permute-done | bytes 524320 | tf_op jit(solution)/shard_map/ppermute | solution.py:472
  52.2 1.9 %collective-permute-start.5 = (bf16[256,1024]{1,0:T(8,128)(2,1)S(1)}, bf16[256,1024]{1,0:T(8,128)(2,1)S(1)}, u32[]{:S(2)}, u32[]{:S(2)}) collective-permute-start(bf16[256,1024]{1,0:T(8,128)(2,1)S(1)} %collective-permute-done.2.refs_1_), channel_id=1, source_target_pairs={{0,1},{1,0},{2,3},{3,2},{4,5},{5,4},{6,7},{7,6},{8,9},{9,8},{10,11... | collective-permute-start | bytes 1572872 | tf_op jit(solution)/shard_map/ppermute | solution.py:59
  54.1 4.5 %collective-permute-done.3.refs_2_ = bf16[256,1024]{1,0:T(8,128)(2,1)S(1)} collective-permute-done((bf16[256,1024]{1,0:T(8,128)(2,1)S(1)}, bf16[256,1024]{1,0:T(8,128)(2,1)S(1)}, u32[]{:S(2)}, u32[]{:S(2)}) %collective-permute-start.3) | collective-permute-done | bytes 524320 | tf_op jit(solution)/shard_map/ppermute | solution.py:473
  58.5 1.9 %collective-permute-start.6 = (bf16[256,1024]{1,0:T(8,128)(2,1)S(1)}, bf16[256,1024]{1,0:T(8,128)(2,1)S(1)}, u32[]{:S(2)}, u32[]{:S(2)}) collective-permute-start(bf16[256,1024]{1,0:T(8,128)(2,1)S(1)} %collective-permute-done.3.refs_2_), channel_id=1, source_target_pairs={{0,1},{1,0},{2,3},{3,2},{4,5},{5,4},{6,7},{7,6},{8,9},{9,8},{10,11... | collective-permute-start | bytes 1572872 | tf_op jit(solution)/shard_map/ppermute | solution.py:59
  60.5 0.0 copy-done.2
  60.5 0.1 reduce_sum.19
  60.6 10.2 %all-to-all-start = ((bf16[8,2,320,128]{3,2,1,0:T(8,128)(2,1)}), bf16[8,2,320,128]{3,2,1,0:T(8,128)(2,1)}, u32[]{:S(2)}, u32[]{:S(2)}) async-start(bf16[8,2,320,128]{3,2,1,0:T(8,128)(2,1)} %weight_copies.1), calls=%async_computation | async-start | bytes 2621440 | tf_op jit(solution)/shard_map/all_to_all | solution.py:478
  70.8 0.0 collective-permute-done.4.refs_3_
  70.8 0.0 collective-permute-done.5.refs_4_
  70.8 0.0 collective-permute-done.6.refs_5_
  70.8 0.0 copy-start
  70.8 35.1 %all-to-all-done.weights_ref = bf16[8,2,320,128]{3,2,1,0:T(8,128)(2,1)} async-done(((bf16[8,2,320,128]{3,2,1,0:T(8,128)(2,1)}), bf16[8,2,320,128]{3,2,1,0:T(8,128)(2,1)}, u32[]{:S(2)}, u32[]{:S(2)}) %all-to-all-start) | async-done | bytes 1310752 | tf_op jit(solution)/shard_map/all_to_all | solution.py:478
  105.9 5.7 %project.1 = bf16[4,320,256]{2,1,0:T(8,128)(2,1)} custom-call(s32[3]{0:T(128)S(1)} %pad_add_fusion.where_ref.refs_6_, bf16[256,8192]{1,0:T(8,128)(2,1)} %states_ref.5, bf16[256,1024]{1,0:T(8,128)(2,1)S(1)} %get-tuple-element.26.n1, bf16[256,1024]{1,0:T(8,128)(2,1)S(1)} %get-tuple-element.27.n2, bf16[256,1024]{1,0:T(8,128)(2,1)S(1)} %get-tuple-element.28.n3, ...), custom_call_target="tpu_custom_call" | custom-call | tf_op jit(solution)/shard_map/project/pallas_call | solution.py:286
  111.6 0.0 copy-done
  111.6 0.0 copy-start.3
  111.6 3.5 %all-to-all-start.1 = ((bf16[4,320,256]{2,1,0:T(8,128)(2,1)}), bf16[4,320,256]{2,1,0:T(8,128)(2,1)S(1)}, u32[]{:S(2)}, u32[]{:S(2)}) async-start(bf16[4,320,256]{2,1,0:T(8,128)(2,1)} %project.1), calls=%async_computation.1 | async-start | bytes 1310720 | tf_op jit(solution)/shard_map/all_to_all | solution.py:481
  115.1 0.1 add_convert_fusion
  115.2 0.1 convert_element_type.15
  115.3 0.5 multiply_cosine_fusion
  115.8 0.8 pad_maximum_fusion.tables_ref
  116.6 0.3 multiply_cosine_fusion.1
  116.9 0.7 pad_maximum_fusion.1.turned_ref
  117.5 15.3 %all-to-all-done.1.parts = bf16[4,320,256]{2,1,0:T(8,128)(2,1)S(1)} async-done(((bf16[4,320,256]{2,1,0:T(8,128)(2,1)}), bf16[4,320,256]{2,1,0:T(8,128)(2,1)S(1)}, u32[]{:S(2)}, u32[]{:S(2)}) %all-to-all-start.1) | async-done | bytes 655392 | tf_op jit(solution)/shard_map/all_to_all | solution.py:481
  132.9 5.8 %all-gather = f32[256,256]{1,0:T(8,128)S(1)} all-gather(f32[64,256]{1,0:T(8,128)S(1)} %convert_reduce_fusion), channel_id=2, replica_groups=mesh['zh'=4,'zb'=2,'yu'=2,'yb'=2,'yh'=2,'xh'=2,'xb'=2,'c'=2] {'xb','c'}, dimensions={0}, use_global_device_ids=true | all-gather | bytes 327680 | tf_op jit(solution)/shard_map/all_gather | solution.py:483
  138.7 0.0 copy-done.3
  138.7 0.0 copy-start.1
  138.7 4.0 %attend.1 = (bf16[256,256]{1,0:T(8,128)(2,1)}, bf16[256,256]{1,0:T(8,128)(2,1)S(1)}, bf16[256,2048]{1,0:T(8,128)(2,1)S(1)}) custom-call(s32[3]{0:T(128)S(1)} %pad_add_fusion.where_ref.refs_6_, s32[4,4]{1,0:T(4,128)S(1)} %copy-done.2, f32[4]{0:T(128)S(1)} %copy-done.3, bf16[4,320,256]{2,1,0:T(8,128)(2,1)S(1)} %all-to-all-done.1.parts, ...), custom_call_target="tpu_custom_call" | custom-call | tf_op jit(solution)/shard_map/attend/pallas_call | solution.py:391
  142.7 16.1 %all-gather.1 = bf16[1024,256]{1,0:T(8,128)(2,1)S(1)} all-gather(bf16[256,256]{1,0:T(8,128)(2,1)S(1)} %get-tuple-element.35), channel_id=3, replica_groups=mesh['zh'=4,'zb'=2,'yu'=2,'yb'=2,'yh'=2,'xh'=2,'xb'=2,'c'=2] {'yu','yb'}, dimensions={0}, use_global_device_ids=true | all-gather | bytes 655360 | tf_op jit(solution)/shard_map/all_gather | solution.py:498
  158.9 0.0 copy-done.1
  158.9 1.8 gradient.1
  160.7 28.9 %all_to_all.15.terms = bf16[8,256,256]{2,1,0:T(8,128)(2,1)S(1)} all-to-all(bf16[8,256,256]{2,1,0:T(8,128)(2,1)S(1)} %gradient.1), channel_id=1, replica_groups=mesh['zh'=4,'zb'=2,'yu'=2,'yb'=2,'yh'=2,'xh'=2,'xb'=2,'c'=2] {'zh','zb'}, dimensions={0} | all-to-all | bytes 2097152 | tf_op jit(solution)/shard_map/all_to_all | solution.py:500
  189.7 0.9 add_up.1
  (5 shorter events, 0.0 us)
Async XLA Ops:
  2.3 12.9 %collective-permute-start = (bf16[320,128]{1,0:T(8,128)(2,1)S(1)}, bf16[320,128]{1,0:T(8,128)(2,1)S(1)}, u32[]{:S(2)}, u32[]{:S(2)}) collective-permute-start(bf16[320,128]{1,0:T(8,128)(2,1)S(1)} %get-tuple-element.22), channel_id=1, source_target_pairs={{0,272},{1,304},{2,336},{3,368},{4,400},{5,432},{6,208},{7,240},{8... | collective-permute-start | bytes 245768 | tf_op jit(solution)/shard_map/ppermute | solution.py:465
  11.1 10.2 %collective-permute-start.7 = (bf16[320,128]{1,0:T(8,128)(2,1)S(1)}, bf16[320,128]{1,0:T(8,128)(2,1)S(1)}, u32[]{:S(2)}, u32[]{:S(2)}) collective-permute-start(bf16[320,128]{1,0:T(8,128)(2,1)S(1)} %get-tuple-element.32), channel_id=1, source_target_pairs={{0,256},{1,288},{2,320},{3,352},{4,384},{5,416},{6,192},{7,224},{8... | collective-permute-start | bytes 245768 | tf_op jit(solution)/shard_map/ppermute | solution.py:464
  23.2 37.3 %copy-start.2 = (s32[4,4]{1,0:T(4,128)S(1)}, s32[4,4]{1,0:T(4,128)}, u32[]{:S(2)}) copy-start(s32[4,4]{1,0:T(4,128)} %mask_ref.1) | copy-start | bytes 196
  23.2 14.2 %collective-permute-start.1 = (bf16[256,1024]{1,0:T(8,128)(2,1)S(1)}, bf16[256,1024]{1,0:T(8,128)(2,1)S(1)}, u32[]{:S(2)}, u32[]{:S(2)}) collective-permute-start(bf16[256,1024]{1,0:T(8,128)(2,1)S(1)} %get-tuple-element.23), channel_id=1, source_target_pairs={{0,56},{1,57},{2,58},{3,59},{4,60},{5,61},{6,62},{7,63},{16,0},{17... | collective-permute-start | bytes 1572872 | tf_op jit(solution)/shard_map/ppermute | solution.py:471
  26.9 25.2 %collective-permute-start.2 = (bf16[256,1024]{1,0:T(8,128)(2,1)S(1)}, bf16[256,1024]{1,0:T(8,128)(2,1)S(1)}, u32[]{:S(2)}, u32[]{:S(2)}) collective-permute-start(bf16[256,1024]{1,0:T(8,128)(2,1)S(1)} %get-tuple-element.24), channel_id=1, source_target_pairs={{0,32},{1,41},{2,34},{3,43},{4,36},{5,45},{6,38},{7,47},{16,48},{1... | collective-permute-start | bytes 1572872 | tf_op jit(solution)/shard_map/ppermute | solution.py:472
  29.5 29.1 %collective-permute-start.3 = (bf16[256,1024]{1,0:T(8,128)(2,1)S(1)}, bf16[256,1024]{1,0:T(8,128)(2,1)S(1)}, u32[]{:S(2)}, u32[]{:S(2)}) collective-permute-start(bf16[256,1024]{1,0:T(8,128)(2,1)S(1)} %get-tuple-element.25), channel_id=1, source_target_pairs={{0,16},{1,17},{2,18},{3,19},{4,20},{5,21},{6,22},{7,23},{16,32},{1... | collective-permute-start | bytes 1572872 | tf_op jit(solution)/shard_map/ppermute | solution.py:473
  37.4 33.4 %collective-permute-start.4 = (bf16[256,1024]{1,0:T(8,128)(2,1)S(1)}, bf16[256,1024]{1,0:T(8,128)(2,1)S(1)}, u32[]{:S(2)}, u32[]{:S(2)}) collective-permute-start(bf16[256,1024]{1,0:T(8,128)(2,1)S(1)} %collective-permute-done.1.refs_0_), channel_id=1, source_target_pairs={{0,1},{1,0},{2,3},{3,2},{4,5},{5,4},{6,7},{7,6},{8,9},{9,8},{10,11... | collective-permute-start | bytes 1572872 | tf_op jit(solution)/shard_map/ppermute | solution.py:59
  52.2 18.6 %collective-permute-start.5 = (bf16[256,1024]{1,0:T(8,128)(2,1)S(1)}, bf16[256,1024]{1,0:T(8,128)(2,1)S(1)}, u32[]{:S(2)}, u32[]{:S(2)}) collective-permute-start(bf16[256,1024]{1,0:T(8,128)(2,1)S(1)} %collective-permute-done.2.refs_1_), channel_id=1, source_target_pairs={{0,1},{1,0},{2,3},{3,2},{4,5},{5,4},{6,7},{7,6},{8,9},{9,8},{10,11... | collective-permute-start | bytes 1572872 | tf_op jit(solution)/shard_map/ppermute | solution.py:59
  58.5 12.2 %collective-permute-start.6 = (bf16[256,1024]{1,0:T(8,128)(2,1)S(1)}, bf16[256,1024]{1,0:T(8,128)(2,1)S(1)}, u32[]{:S(2)}, u32[]{:S(2)}) collective-permute-start(bf16[256,1024]{1,0:T(8,128)(2,1)S(1)} %collective-permute-done.3.refs_2_), channel_id=1, source_target_pairs={{0,1},{1,0},{2,3},{3,2},{4,5},{5,4},{6,7},{7,6},{8,9},{9,8},{10,11... | collective-permute-start | bytes 1572872 | tf_op jit(solution)/shard_map/ppermute | solution.py:59
  60.6 45.3 %all-to-all-start = ((bf16[8,2,320,128]{3,2,1,0:T(8,128)(2,1)}), bf16[8,2,320,128]{3,2,1,0:T(8,128)(2,1)}, u32[]{:S(2)}, u32[]{:S(2)}) async-start(bf16[8,2,320,128]{3,2,1,0:T(8,128)(2,1)} %weight_copies.1), calls=%async_computation | async-start | bytes 2621440 | tf_op jit(solution)/shard_map/all_to_all | solution.py:478
  70.8 40.8 %copy-start = (bf16[256,1024]{1,0:T(8,128)(2,1)}, bf16[256,1024]{1,0:T(8,128)(2,1)S(1)}, u32[]{:S(2)}) copy-start(bf16[256,1024]{1,0:T(8,128)(2,1)S(1)} %get-tuple-element.31.f3) | copy-start | bytes 1572868
  111.6 27.1 %copy-start.3 = (f32[4]{0:T(128)S(1)}, f32[4]{0:T(128)}, u32[]{:S(2)}) copy-start(f32[4]{0:T(128)} %risk_ref.1) | copy-start | bytes 52
  111.6 21.3 %all-to-all-start.1 = ((bf16[4,320,256]{2,1,0:T(8,128)(2,1)}), bf16[4,320,256]{2,1,0:T(8,128)(2,1)S(1)}, u32[]{:S(2)}, u32[]{:S(2)}) async-start(bf16[4,320,256]{2,1,0:T(8,128)(2,1)} %project.1), calls=%async_computation.1 | async-start | bytes 1310720 | tf_op jit(solution)/shard_map/all_to_all | solution.py:481
  138.7 20.2 %copy-start.1 = (bf16[256,1024]{1,0:T(8,128)(2,1)S(1)}, bf16[256,1024]{1,0:T(8,128)(2,1)}, u32[]{:S(2)}) copy-start(bf16[256,1024]{1,0:T(8,128)(2,1)} %copy-done) | copy-start | bytes 1572868

commit v13 on v11

--- a/solution.py
+++ b/solution.py
@@ -1,3 +1,4 @@
+import functools
 import math
 
 import jax
@@ -87,7 +88,8 @@
     return pl.BlockSpec(memory_space=pl.ANY)
 
 
-def pack_kernel(where_ref, query, key_t, value_t, first, second, sems):
+def pack_kernel(where_ref, query, key_t, value_t, after, first, second, sems):
+    del after
     odd = where_ref[1] % 2
     copies = []
 
@@ -108,25 +110,26 @@
         each.wait()
 
 
-def pack(where, query, key_t, value_t):
+def pack(where, query, key_t, value_t, after):
     part = jax.ShapeDtypeStruct((320, 128), BF16)
     return pl.pallas_call(
         pack_kernel,
         out_shape=(part, part),
-        in_specs=[in_smem(), in_hbm(), in_hbm(), in_hbm()],
+        in_specs=[in_smem(), in_hbm(), in_hbm(), in_hbm(), anywhere()],
         out_specs=tuple(in_vmem(2)),
         scratch_shapes=[pltpu.SemaphoreType.DMA((10,))],
         compiler_params=params(),
         name="pack_weights",
-    )(where, held(query), held(key_t), held(value_t))
-
-
-def cut_kernel(where_ref, states_ref, up_ref, two_ref, down_ref, sems):
+    )(where, held(query), held(key_t), held(value_t), after)
+
+
+def cut_kernel(ways, where_ref, states_ref, *refs):
     core, place = where_ref[0], where_ref[1]
+    outs, sems = refs[:-1], refs[-1]
     copies = []
-    for number, out in enumerate((up_ref, two_ref, down_ref)):
+    for way, out in zip(ways, outs):
         for part in range(4):
-            start = column_of(block_of(part, core), (place + number + 1) % 4)
+            start = column_of(block_of(part, core), (place + way) % 4)
             copies.append(
                 pltpu.make_async_copy(
                     states_ref.at[:, pl.ds(start, 256)],
@@ -140,14 +143,14 @@
         copy.wait()
 
 
-def cut(where, states):
+def cut(where, states, ways):
     part = jax.ShapeDtypeStruct((TOK, 1024), BF16)
     return pl.pallas_call(
-        cut_kernel,
-        out_shape=(part, part, part),
+        functools.partial(cut_kernel, ways),
+        out_shape=(part,) * len(ways),
         in_specs=[in_smem(), in_hbm()],
-        out_specs=tuple(in_vmem(3)),
-        scratch_shapes=[pltpu.SemaphoreType.DMA((12,))],
+        out_specs=tuple(in_vmem(len(ways))),
+        scratch_shapes=[pltpu.SemaphoreType.DMA((4 * len(ways),))],
         compiler_params=params(),
         name="cut_states",
     )(where, held(states))
@@ -212,41 +215,39 @@
 def project_kernel(
     where_ref,
     states_ref,
+    n2,
+    f2,
     n1,
-    n2,
     n3,
     f1,
-    f2,
     f3,
-    weights_ref,
+    weights,
     out,
     own,
-    weights,
+    joined,
     w_all,
     result,
     sems,
     out_sems,
 ):
     core = where_ref[0]
-    arrivals = []
+    copies = own_columns(where_ref, states_ref, own, sems)
+    first = [
+        pltpu.make_async_copy(n2, joined.at[:, pl.ds(0, 1024)], sems.at[8]),
+        pltpu.make_async_copy(f2, joined.at[:, pl.ds(1024, 1024)], sems.at[9]),
+    ]
+    for copy in first + copies:
+        copy.start()
     for part in range(8):
         block = resting_z(where_ref[2], block_of(part, core))
-        arrivals.append(
-            pltpu.make_async_copy(weights_ref.at[block], weights.at[part], sems.at[8 + part])
-        )
-    copies = own_columns(where_ref, states_ref, own, sems)
-    for copy in arrivals + copies:
-        copy.start()
-    for part in range(8):
-        arrivals[part].wait()
         start = 256 * part
         for head in range(2):
             w_all[start : start + 256, HEAD * head : HEAD * head + HEAD] = weights[
-                part, head, :256, :
+                block, head, :256, :
             ]
         for chunk in range(2):
             base = 256 + 32 * chunk
-            pair = [weights[part, head, base : base + 32, :] for head in range(2)]
+            pair = [weights[block, head, base : base + 32, :] for head in range(2)]
             columns = [pair[0][:16], pair[1][:16], pair[0][16:], pair[1][16:]]
             rows = pl.ds(start + 128 * chunk, 128)
             w_all[rows, 256:] = jnp.concatenate(columns, axis=0).T
@@ -256,13 +257,15 @@
 
     low, high = pl.ds(0, 1024), pl.ds(1024, 1024)
     departures = []
-    for number, (near, far) in enumerate(((n1, f1), (n2, f2), (n3, f3), (None, None))):
-        if near is None:
-            for copy in copies:
+    for number in (0, 2, 1, 3):
+        if number % 2 == 0:
+            near, far = ((n1, f1), (n3, f3))[number // 2]
+            linear = product(near[...], low) + product(far[...], high)
+        else:
+            tokens, arrivals = ((joined, first), (own, copies))[number // 3]
+            for copy in arrivals:
                 copy.wait()
-            linear = product(own[...], pl.ds(0, 2048))
-        else:
-            linear = product(near[...], low) + product(far[...], high)
+            linear = product(tokens[...], pl.ds(0, 2048))
         result[number, :256, :] = linear[:, :256].astype(BF16)
         result[number, 256:, :] = linear[:, 256:].T.astype(BF16)
         other = (where_ref[1] + number + 1) % 4
@@ -278,19 +281,19 @@
     return pl.pallas_call(
         project_kernel,
         out_shape=pltpu.HBM((4, 320, 256), BF16),
-        in_specs=[in_smem(), in_hbm(), *in_vmem(6), in_hbm()],
+        in_specs=[in_smem(), *[in_hbm()] * 3, *in_vmem(5)],
         out_specs=in_hbm(),
         scratch_shapes=[
             pltpu.VMEM((TOK, 2048), BF16),
-            pltpu.VMEM((8, 2, 320, 128), BF16),
+            pltpu.VMEM((TOK, 2048), BF16),
             pltpu.VMEM((2048, 320), BF16),
             pltpu.VMEM((4, 320, 256), BF16),
-            pltpu.SemaphoreType.DMA((16,)),
+            pltpu.SemaphoreType.DMA((10,)),
             pltpu.SemaphoreType.DMA((4,)),
         ],
         compiler_params=params(),
         name="project",
-    )(where, held(states), *near, *far, held(weights))
+    )(where, held(states), held(near[1]), held(far[1]), *near[::2], *far[::2], weights)
 
 
 def attend_kernel(
@@ -337,7 +340,11 @@
 
     copies[0].wait()
     copies[1].wait()
-    cq, sq = tables[:, :HEAD], tables[:, HEAD:]
+    half = lax.broadcasted_iota(jnp.int32, (TOK, HEAD), 1) < HEAD // 2
+    table = tables[...]
+    turned_table = pltpu.roll(table, HEAD // 2, 1)
+    cq = jnp.where(half, table, turned_table)
+    sq = jnp.where(half, -turned_table, table)
     ck, sk = turned[:64], turned[64:]
     k1, k2 = k_lin[:64], k_lin[64:]
     keys = jnp.concatenate([k1 * ck - k2 * sk, k2 * ck + k1 * sk], axis=0).astype(BF16)
@@ -351,7 +358,7 @@
         queries = ((q_lin * cq + pltpu.roll(q_lin, 64, 1) * sq) * scaling).astype(BF16)
         scores = jnp.dot(queries, keys, preferred_element_type=F32)
         raised = jnp.where(seen, jnp.exp(scores), 0.0)
-        attend = raised / jnp.sum(raised, axis=1, keepdims=True)
+        attend = raised * (1.0 / jnp.sum(raised, axis=1, keepdims=True))
         mixed = lax.dot_general(
             attend.astype(BF16), values, (((1,), (1,)), ((), ())), preferred_element_type=F32
         )
@@ -380,7 +387,7 @@
         out_specs=tuple(in_vmem(3)),
         scratch_shapes=[
             pltpu.VMEM((TOK, 256), BF16),
-            pltpu.VMEM((TOK, 2 * HEAD), F32),
+            pltpu.VMEM((TOK, HEAD), F32),
             pltpu.VMEM((HEAD, TOK), F32),
             pltpu.SemaphoreType.DMA((11,)),
         ],
@@ -445,19 +452,19 @@
     plane = lax.axis_index(("yh", "xh", "xb"))
     where = jnp.stack([lax.axis_index("c"), place, plane]).astype(jnp.int32)
 
-    first, second = pack(where, query_weight, key_matrix.T, value_matrix.T)
+    (two,) = cut(where, states, (2,))
+    n2 = lax.ppermute(two, AXES, ring_pairs(2, -2))
+
+    first, second = pack(where, query_weight, key_matrix.T, value_matrix.T, two)
     first = lax.ppermute(first, AXES, home_pairs(0))
     second = lax.ppermute(second, AXES, home_pairs(1))
-    outgoing = cut(where, states)
+    outgoing = cut(where, states, (1, 3))
     weights = copies(where, first, second, outgoing[0])
 
-    (two,) = gate(outgoing[1:2], second)
-    up, down = gate((outgoing[0], outgoing[2]), held(weights))
-    near = (
-        lax.ppermute(down, AXES, ring_pairs(-1, -1)),
-        lax.ppermute(two, AXES, ring_pairs(2, -2)),
-        lax.ppermute(up, AXES, ring_pairs(1, 1)),
-    )
+    up, down = gate(outgoing, held(weights))
+    n1 = lax.ppermute(down, AXES, ring_pairs(-1, -1))
+    n3 = lax.ppermute(up, AXES, ring_pairs(1, 1))
+    near = (n1, n2, n3)
     far = [swap_core(x) for x in near]
     weights = lax.all_to_all(weights, OTHERS, split_axis=0, concat_axis=0)
 
@@ -473,7 +480,7 @@
     )
     angles = places.astype(F32)[:, None] * frequency[None, :]
     cosine, sine = jnp.cos(angles), jnp.sin(angles)
-    tables = jnp.concatenate([cosine, cosine, -sine, sine], axis=1)
+    tables = jnp.concatenate([cosine, sine], axis=1)
     turned = jnp.concatenate([cosine.T, sine.T], axis=0)
 
     attn_out, dq, own = attend(

time: 161 us -> 163 us (1.012)
  Pallas kernels: 17.3 us -> 20 us
    pallas_call x1 -> x2, Pallas kernels: 2.12 us -> 4.4 us  [cut(): pl.pallas_call(functools.partial(cut_kernel, ways), out_shape=(part,) * l...]
  transfers between devices with their start and end apart: 10 -> 10, of which waited for: 6 -> 6; matrix products, arithmetic and copies ran while one was open for 2% -> 2% of each run, Pallas kernels for 1% -> 2%
where the time goes in v13:
time: 163 us; the launch traced here: 162 us
  blocking collectives  55 us (34%)
  starting transfers between devices  47.2 us (29%)
  waiting for transfers between devices  35.9 us (22%)
  Pallas kernels  20 us (12%)
  other arithmetic  2.57 us (2%)
    all_to_all x1, blocking collectives, shards(): terms = lax.all_to_all(terms, OTHERS, split_axis=0, concat_axis=0)  33.1 us
    all_gather x1, blocking collectives, shards(): slopes = lax.all_gather(dq, GROUP, axis=0, tiled=False)  16.1 us
    all_to_all x1, waiting for transfers between devices, shards(): parts = lax.all_to_all(parts, GROUP, split_axis=0, concat_axis=0)  15.1 us
    all_to_all x1, starting transfers between devices, shards(): weights = lax.all_to_all(weights, OTHERS, split_axis=0, concat_axis=0)  14.8 us
    ppermute x1, waiting for transfers between devices, shards(): n2 = lax.ppermute(two, AXES, ring_pairs(2, -2))  9.31 us
    ppermute x1, starting transfers between devices, shards(): first = lax.ppermute(first, AXES, home_pairs(0))  7.81 us
    ppermute x3, starting transfers between devices, swap_core(): return lax.ppermute(value, 'c', [(0, 1), (1, 0)])  7.58 us
    all_gather x1, blocking collectives, shards(): kv = lax.all_gather(kv, ('xb', 'c'), axis=0, tiled=False)  5.79 us
  transfers between devices with their start and end apart: 10, of which 6 were waited for; matrix products, arithmetic and copies ran while one was open for 2% of the time, Pallas kernels for 2%

profile of v13, /device:TPU:6, one launch (start us, length us, event | category | flops | bytes accessed | tf_op | source)
XLA Modules:
  0.0 162.5 jit_solution(11212324050501569808)
XLA Ops:
  0.6 0.1 pad_add_fusion.where_ref
  0.7 1.7 %cut_states.2.after = bf16[256,1024]{1,0:T(8,128)(2,1)S(1)} custom-call(s32[3]{0:T(128)S(1)} %pad_add_fusion.where_ref, bf16[256,8192]{1,0:T(8,128)(2,1)} %states_ref.7), custom_call_target="tpu_custom_call" | custom-call | tf_op jit(solution)/shard_map/cut_states/pallas_call | solution.py:148
  2.4 1.6 pack_weights.1
  4.0 7.8 %collective-permute-start.2 = (bf16[320,128]{1,0:T(8,128)(2,1)S(1)}, bf16[320,128]{1,0:T(8,128)(2,1)S(1)}, u32[]{:S(2)}, u32[]{:S(2)}) collective-permute-start(bf16[320,128]{1,0:T(8,128)(2,1)S(1)} %get-tuple-element.13), channel_id=1, source_target_pairs={{0,256},{1,288},{2,320},{3,352},{4,384},{5,416},{6,192},{7,224},{8... | collective-permute-start | bytes 245768 | tf_op jit(solution)/shard_map/ppermute | solution.py:459
  11.8 3.0 %collective-permute-start.3 = (bf16[320,128]{1,0:T(8,128)(2,1)S(1)}, bf16[320,128]{1,0:T(8,128)(2,1)S(1)}, u32[]{:S(2)}, u32[]{:S(2)}) collective-permute-start(bf16[320,128]{1,0:T(8,128)(2,1)S(1)} %get-tuple-element.14), channel_id=1, source_target_pairs={{0,272},{1,304},{2,336},{3,368},{4,400},{5,432},{6,208},{7,240},{8... | collective-permute-start | bytes 245768 | tf_op jit(solution)/shard_map/ppermute | solution.py:460
  14.8 2.7 %cut_states.3 = (bf16[256,1024]{1,0:T(8,128)(2,1)S(1)}, bf16[256,1024]{1,0:T(8,128)(2,1)}) custom-call(s32[3]{0:T(128)S(1)} %pad_add_fusion.where_ref, bf16[256,8192]{1,0:T(8,128)(2,1)} %states_ref.7), custom_call_target="tpu_custom_call" | custom-call | tf_op jit(solution)/shard_map/cut_states/pallas_call | solution.py:148
  17.5 0.0 collective-permute-done.2.first
  17.5 5.5 %collective-permute-done.3.second = bf16[320,128]{1,0:T(8,128)(2,1)S(1)} collective-permute-done((bf16[320,128]{1,0:T(8,128)(2,1)S(1)}, bf16[320,128]{1,0:T(8,128)(2,1)S(1)}, u32[]{:S(2)}, u32[]{:S(2)}) %collective-permute-start.3) | collective-permute-done | bytes 81952 | tf_op jit(solution)/shard_map/ppermute | solution.py:460
  23.0 1.8 %weight_copies.1.refs_2_ = bf16[8,2,320,128]{3,2,1,0:T(8,128)(2,1)} custom-call(s32[3]{0:T(128)S(1)} %pad_add_fusion.where_ref, bf16[320,128]{1,0:T(8,128)(2,1)S(1)} %collective-permute-done.2.first, bf16[320,128]{1,0:T(8,128)(2,1)S(1)} %collective-permute-done.3.second, bf16[256,1024]{1,0:T(8,128)(2,1)S(1)} %get-tuple-element.11.after.refs_0_), custom_call_target="tpu_custom_call" | custom-call | tf_op jit(solution)/shard_map/weight_copies/pallas_call | solution.py:204
  24.7 14.8 %all-to-all-start = ((bf16[8,2,320,128]{3,2,1,0:T(8,128)(2,1)}), bf16[8,2,320,128]{3,2,1,0:T(8,128)(2,1)S(1)}, u32[]{:S(2)}, u32[]{:S(2)}) async-start(bf16[8,2,320,128]{3,2,1,0:T(8,128)(2,1)} %weight_copies.1.refs_2_), calls=%async_computation | async-start | bytes 2621440 | tf_op jit(solution)/shard_map/all_to_all | solution.py:469
  39.5 2.3 %collective-permute-start = (bf16[256,1024]{1,0:T(8,128)(2,1)S(1)}, bf16[256,1024]{1,0:T(8,128)(2,1)S(1)}, u32[]{:S(2)}, u32[]{:S(2)}) collective-permute-start(bf16[256,1024]{1,0:T(8,128)(2,1)S(1)} %cut_states.2.after), channel_id=1, source_target_pairs={{0,32},{1,41},{2,34},{3,43},{4,36},{5,45},{6,38},{7,47},{16,48},{1... | collective-permute-start | bytes 1572872 | tf_op jit(solution)/shard_map/ppermute | solution.py:456
  41.8 0.0 copy-start.4
  41.8 0.8 copy-done.4
  42.7 5.7 %collective-permute-start.4 = (bf16[256,1024]{1,0:T(8,128)(2,1)}, bf16[256,1024]{1,0:T(8,128)(2,1)S(1)}, u32[]{:S(2)}, u32[]{:S(2)}) collective-permute-start(bf16[256,1024]{1,0:T(8,128)(2,1)} %get-tuple-element.15), channel_id=1, source_target_pairs={{0,56},{1,57},{2,58},{3,59},{4,60},{5,61},{6,62},{7,63},{16,0},{17... | collective-permute-start | bytes 1572872 | tf_op jit(solution)/shard_map/ppermute | solution.py:465
  48.4 1.9 %collective-permute-start.5 = (bf16[256,1024]{1,0:T(8,128)(2,1)}, bf16[256,1024]{1,0:T(8,128)(2,1)S(1)}, u32[]{:S(2)}, u32[]{:S(2)}) collective-permute-start(bf16[256,1024]{1,0:T(8,128)(2,1)} %copy-done.4), channel_id=1, source_target_pairs={{0,16},{1,17},{2,18},{3,19},{4,20},{5,21},{6,22},{7,23},{16,32},{1... | collective-permute-start | bytes 1572872 | tf_op jit(solution)/shard_map/ppermute | solution.py:466
  50.3 9.3 %collective-permute-done.n2 = bf16[256,1024]{1,0:T(8,128)(2,1)S(1)} collective-permute-done((bf16[256,1024]{1,0:T(8,128)(2,1)S(1)}, bf16[256,1024]{1,0:T(8,128)(2,1)S(1)}, u32[]{:S(2)}, u32[]{:S(2)}) %collective-permute-start) | collective-permute-done | bytes 524320 | tf_op jit(solution)/shard_map/ppermute | solution.py:456
  59.6 1.9 %collective-permute-start.1 = (bf16[256,1024]{1,0:T(8,128)(2,1)S(1)}, bf16[256,1024]{1,0:T(8,128)(2,1)S(1)}, u32[]{:S(2)}, u32[]{:S(2)}) collective-permute-start(bf16[256,1024]{1,0:T(8,128)(2,1)S(1)} %collective-permute-done.n2), channel_id=1, source_target_pairs={{0,1},{1,0},{2,3},{3,2},{4,5},{5,4},{6,7},{7,6},{8,9},{9,8},{10,11... | collective-permute-start | bytes 1572872 | tf_op jit(solution)/shard_map/ppermute | solution.py:60
  61.6 1.5 collective-permute-done.4.n1
  63.1 3.8 %collective-permute-start.6 = (bf16[256,1024]{1,0:T(8,128)(2,1)S(1)}, bf16[256,1024]{1,0:T(8,128)(2,1)}, u32[]{:S(2)}, u32[]{:S(2)}) collective-permute-start(bf16[256,1024]{1,0:T(8,128)(2,1)S(1)} %collective-permute-done.4.n1), channel_id=1, source_target_pairs={{0,1},{1,0},{2,3},{3,2},{4,5},{5,4},{6,7},{7,6},{8,9},{9,8},{10,11... | collective-permute-start | bytes 1572872 | tf_op jit(solution)/shard_map/ppermute | solution.py:60
  66.8 2.7 %collective-permute-done.5.n3 = bf16[256,1024]{1,0:T(8,128)(2,1)S(1)} collective-permute-done((bf16[256,1024]{1,0:T(8,128)(2,1)}, bf16[256,1024]{1,0:T(8,128)(2,1)S(1)}, u32[]{:S(2)}, u32[]{:S(2)}) %collective-permute-start.5) | collective-permute-done | bytes 524320 | tf_op jit(solution)/shard_map/ppermute | solution.py:466
  69.6 1.9 %collective-permute-start.7 = (bf16[256,1024]{1,0:T(8,128)(2,1)S(1)}, bf16[256,1024]{1,0:T(8,128)(2,1)}, u32[]{:S(2)}, u32[]{:S(2)}) collective-permute-start(bf16[256,1024]{1,0:T(8,128)(2,1)S(1)} %collective-permute-done.5.n3), channel_id=1, source_target_pairs={{0,1},{1,0},{2,3},{3,2},{4,5},{5,4},{6,7},{7,6},{8,9},{9,8},{10,11... | collective-permute-start | bytes 1572872 | tf_op jit(solution)/shard_map/ppermute | solution.py:60
  71.5 0.0 copy-done.5
  71.5 0.1 reduce_sum.19
  71.6 0.0 collective-permute-done.1.f2
  71.6 0.0 copy-start.2
  71.6 0.0 collective-permute-done.6.f1
  71.6 1.8 %collective-permute-done.7.f3 = bf16[256,1024]{1,0:T(8,128)(2,1)} collective-permute-done((bf16[256,1024]{1,0:T(8,128)(2,1)S(1)}, bf16[256,1024]{1,0:T(8,128)(2,1)}, u32[]{:S(2)}, u32[]{:S(2)}) %collective-permute-start.7) | collective-permute-done | bytes 524320 | tf_op jit(solution)/shard_map/ppermute | solution.py:60
  73.5 0.0 all-to-all-done.weights
  73.5 0.0 copy-done
  73.5 0.0 copy-done.2
  73.5 5.4 %project.1 = bf16[4,320,256]{2,1,0:T(8,128)(2,1)} custom-call(s32[3]{0:T(128)S(1)} %pad_add_fusion.where_ref, bf16[256,8192]{1,0:T(8,128)(2,1)} %states_ref.7, bf16[256,1024]{1,0:T(8,128)(2,1)} %copy-done, bf16[256,1024]{1,0:T(8,128)(2,1)} %copy-done.2, bf16[256,1024]{1,0:T(8,128)(2,1)S(1)} %collective-permute-done.4.n1, ...), custom_call_target="tpu_custom_call" | custom-call | tf_op jit(solution)/shard_map/project/pallas_call | solution.py:281
  78.9 0.0 copy-start.6
  78.9 4.1 %all-to-all-start.1 = ((bf16[4,320,256]{2,1,0:T(8,128)(2,1)}), bf16[4,320,256]{2,1,0:T(8,128)(2,1)S(1)}, u32[]{:S(2)}, u32[]{:S(2)}) async-start(bf16[4,320,256]{2,1,0:T(8,128)(2,1)} %project.1), calls=%async_computation.1 | async-start | bytes 1310720 | tf_op jit(solution)/shard_map/all_to_all | solution.py:472
  83.0 0.1 add_convert_fusion
  83.1 0.1 convert_element_type.15
  83.2 0.3 multiply_cosine_fusion.1
  83.5 0.7 pad_maximum_fusion.1.turned_ref
  84.2 0.5 multiply_cosine_fusion
  84.7 0.8 pad_maximum_fusion.tables_ref
  85.5 15.1 %all-to-all-done.1.parts = bf16[4,320,256]{2,1,0:T(8,128)(2,1)S(1)} async-done(((bf16[4,320,256]{2,1,0:T(8,128)(2,1)}), bf16[4,320,256]{2,1,0:T(8,128)(2,1)S(1)}, u32[]{:S(2)}, u32[]{:S(2)}) %all-to-all-start.1) | async-done | bytes 655392 | tf_op jit(solution)/shard_map/all_to_all | solution.py:472
  100.6 5.8 %all-gather = f32[256,256]{1,0:T(8,128)S(1)} all-gather(f32[64,256]{1,0:T(8,128)S(1)} %convert_reduce_fusion), channel_id=2, replica_groups=mesh['zh'=4,'zb'=2,'yu'=2,'yb'=2,'yh'=2,'xh'=2,'xb'=2,'c'=2] {'xb','c'}, dimensions={0}, use_global_device_ids=true | all-gather | bytes 327680 | tf_op jit(solution)/shard_map/all_gather | solution.py:474
  106.3 0.0 copy-done.6
  106.3 3.5 %attend.1 = (bf16[256,256]{1,0:T(8,128)(2,1)}, bf16[256,256]{1,0:T(8,128)(2,1)S(1)}, bf16[256,2048]{1,0:T(8,128)(2,1)S(1)}) custom-call(s32[3]{0:T(128)S(1)} %pad_add_fusion.where_ref, s32[4,4]{1,0:T(4,128)S(1)} %copy-done.5, f32[4]{0:T(128)S(1)} %copy-done.6, bf16[4,320,256]{2,1,0:T(8,128)(2,1)S(1)} %all-to-all-done.1.parts, f32[4,64,256]{2,1,0:T(8,128)S(1)} %bitcast.8, ...), custom_call_target="tpu_custom_call" | custom-call | tf_op jit(solution)/shard_map/attend/pallas_call | solution.py:383
  109.8 16.1 %all-gather.1 = bf16[1024,256]{1,0:T(8,128)(2,1)S(1)} all-gather(bf16[256,256]{1,0:T(8,128)(2,1)S(1)} %get-tuple-element.19), channel_id=3, replica_groups=mesh['zh'=4,'zb'=2,'yu'=2,'yb'=2,'yh'=2,'xh'=2,'xb'=2,'c'=2] {'yu','yb'}, dimensions={0}, use_global_device_ids=true | all-gather | bytes 655360 | tf_op jit(solution)/shard_map/all_gather | solution.py:489
  126.0 0.0 copy-done.3
  126.0 2.5 %gradient.1 = bf16[8,256,256]{2,1,0:T(8,128)(2,1)S(1)} custom-call(s32[3]{0:T(128)S(1)} %pad_add_fusion.where_ref, bf16[256,2048]{1,0:T(8,128)(2,1)S(1)} %get-tuple-element.18.own, bf16[256,1024]{1,0:T(8,128)(2,1)S(1)} %collective-permute-done.4.n1, bf16[256,1024]{1,0:T(8,128)(2,1)S(1)} %copy-done.1, bf16[256,1024]{1,0:T(8,128)(2,1)S(1)} %collective-permute-done.5.n3, ...), custom_call_target="tpu_custom_call" | custom-call | tf_op jit(solution)/shard_map/gradient/pallas_call | solution.py:425
  128.5 33.1 %all_to_all.15.terms = bf16[8,256,256]{2,1,0:T(8,128)(2,1)S(1)} all-to-all(bf16[8,256,256]{2,1,0:T(8,128)(2,1)S(1)} %gradient.1), channel_id=1, replica_groups=mesh['zh'=4,'zb'=2,'yu'=2,'yb'=2,'yh'=2,'xh'=2,'xb'=2,'c'=2] {'zh','zb'}, dimensions={0} | all-to-all | bytes 2097152 | tf_op jit(solution)/shard_map/all_to_all | solution.py:491
  161.6 0.9 add_up.1
  (9 shorter events, 0.0 us)
Async XLA Ops:
  4.0 13.5 %collective-permute-start.2 = (bf16[320,128]{1,0:T(8,128)(2,1)S(1)}, bf16[320,128]{1,0:T(8,128)(2,1)S(1)}, u32[]{:S(2)}, u32[]{:S(2)}) collective-permute-start(bf16[320,128]{1,0:T(8,128)(2,1)S(1)} %get-tuple-element.13), channel_id=1, source_target_pairs={{0,256},{1,288},{2,320},{3,352},{4,384},{5,416},{6,192},{7,224},{8... | collective-permute-start | bytes 245768 | tf_op jit(solution)/shard_map/ppermute | solution.py:459
  11.8 11.1 %collective-permute-start.3 = (bf16[320,128]{1,0:T(8,128)(2,1)S(1)}, bf16[320,128]{1,0:T(8,128)(2,1)S(1)}, u32[]{:S(2)}, u32[]{:S(2)}) collective-permute-start(bf16[320,128]{1,0:T(8,128)(2,1)S(1)} %get-tuple-element.14), channel_id=1, source_target_pairs={{0,272},{1,304},{2,336},{3,368},{4,400},{5,432},{6,208},{7,240},{8... | collective-permute-start | bytes 245768 | tf_op jit(solution)/shard_map/ppermute | solution.py:460
  24.7 48.7 %all-to-all-start = ((bf16[8,2,320,128]{3,2,1,0:T(8,128)(2,1)}), bf16[8,2,320,128]{3,2,1,0:T(8,128)(2,1)S(1)}, u32[]{:S(2)}, u32[]{:S(2)}) async-start(bf16[8,2,320,128]{3,2,1,0:T(8,128)(2,1)} %weight_copies.1.refs_2_), calls=%async_computation | async-start | bytes 2621440 | tf_op jit(solution)/shard_map/all_to_all | solution.py:469
  39.5 32.0 %copy-start.5 = (s32[4,4]{1,0:T(4,128)S(1)}, s32[4,4]{1,0:T(4,128)}, u32[]{:S(2)}) copy-start(s32[4,4]{1,0:T(4,128)} %mask_ref.1) | copy-start | bytes 196
  39.5 20.1 %collective-permute-start = (bf16[256,1024]{1,0:T(8,128)(2,1)S(1)}, bf16[256,1024]{1,0:T(8,128)(2,1)S(1)}, u32[]{:S(2)}, u32[]{:S(2)}) collective-permute-start(bf16[256,1024]{1,0:T(8,128)(2,1)S(1)} %cut_states.2.after), channel_id=1, source_target_pairs={{0,32},{1,41},{2,34},{3,43},{4,36},{5,45},{6,38},{7,47},{16,48},{1... | collective-permute-start | bytes 1572872 | tf_op jit(solution)/shard_map/ppermute | solution.py:456
  41.8 0.8 copy-start.4
  42.7 20.4 %collective-permute-start.4 = (bf16[256,1024]{1,0:T(8,128)(2,1)}, bf16[256,1024]{1,0:T(8,128)(2,1)S(1)}, u32[]{:S(2)}, u32[]{:S(2)}) collective-permute-start(bf16[256,1024]{1,0:T(8,128)(2,1)} %get-tuple-element.15), channel_id=1, source_target_pairs={{0,56},{1,57},{2,58},{3,59},{4,60},{5,61},{6,62},{7,63},{16,0},{17... | collective-permute-start | bytes 1572872 | tf_op jit(solution)/shard_map/ppermute | solution.py:465
  48.4 21.2 %collective-permute-start.5 = (bf16[256,1024]{1,0:T(8,128)(2,1)}, bf16[256,1024]{1,0:T(8,128)(2,1)S(1)}, u32[]{:S(2)}, u32[]{:S(2)}) collective-permute-start(bf16[256,1024]{1,0:T(8,128)(2,1)} %copy-done.4), channel_id=1, source_target_pairs={{0,16},{1,17},{2,18},{3,19},{4,20},{5,21},{6,22},{7,23},{16,32},{1... | collective-permute-start | bytes 1572872 | tf_op jit(solution)/shard_map/ppermute | solution.py:466
  59.6 13.8 %copy-start = (bf16[256,1024]{1,0:T(8,128)(2,1)}, bf16[256,1024]{1,0:T(8,128)(2,1)S(1)}, u32[]{:S(2)}) copy-start(bf16[256,1024]{1,0:T(8,128)(2,1)S(1)} %collective-permute-done.n2) | copy-start | bytes 1572868
  59.6 12.0 %collective-permute-start.1 = (bf16[256,1024]{1,0:T(8,128)(2,1)S(1)}, bf16[256,1024]{1,0:T(8,128)(2,1)S(1)}, u32[]{:S(2)}, u32[]{:S(2)}) collective-permute-start(bf16[256,1024]{1,0:T(8,128)(2,1)S(1)} %collective-permute-done.n2), channel_id=1, source_target_pairs={{0,1},{1,0},{2,3},{3,2},{4,5},{5,4},{6,7},{7,6},{8,9},{9,8},{10,11... | collective-permute-start | bytes 1572872 | tf_op jit(solution)/shard_map/ppermute | solution.py:60
  63.1 8.6 %collective-permute-start.6 = (bf16[256,1024]{1,0:T(8,128)(2,1)S(1)}, bf16[256,1024]{1,0:T(8,128)(2,1)}, u32[]{:S(2)}, u32[]{:S(2)}) collective-permute-start(bf16[256,1024]{1,0:T(8,128)(2,1)S(1)} %collective-permute-done.4.n1), channel_id=1, source_target_pairs={{0,1},{1,0},{2,3},{3,2},{4,5},{5,4},{6,7},{7,6},{8,9},{9,8},{10,11... | collective-permute-start | bytes 1572872 | tf_op jit(solution)/shard_map/ppermute | solution.py:60
  69.6 3.9 %collective-permute-start.7 = (bf16[256,1024]{1,0:T(8,128)(2,1)S(1)}, bf16[256,1024]{1,0:T(8,128)(2,1)}, u32[]{:S(2)}, u32[]{:S(2)}) collective-permute-start(bf16[256,1024]{1,0:T(8,128)(2,1)S(1)} %collective-permute-done.5.n3), channel_id=1, source_target_pairs={{0,1},{1,0},{2,3},{3,2},{4,5},{5,4},{6,7},{7,6},{8,9},{9,8},{10,11... | collective-permute-start | bytes 1572872 | tf_op jit(solution)/shard_map/ppermute | solution.py:60
  71.6 1.9 %copy-start.2 = (bf16[256,1024]{1,0:T(8,128)(2,1)}, bf16[256,1024]{1,0:T(8,128)(2,1)S(1)}, u32[]{:S(2)}) copy-start(bf16[256,1024]{1,0:T(8,128)(2,1)S(1)} %collective-permute-done.1.f2) | copy-start | bytes 1572868
  78.9 27.4 %copy-start.6 = (f32[4]{0:T(128)S(1)}, f32[4]{0:T(128)}, u32[]{:S(2)}) copy-start(f32[4]{0:T(128)} %risk_ref.1) | copy-start | bytes 52
  78.9 21.6 %all-to-all-start.1 = ((bf16[4,320,256]{2,1,0:T(8,128)(2,1)}), bf16[4,320,256]{2,1,0:T(8,128)(2,1)S(1)}, u32[]{:S(2)}, u32[]{:S(2)}) async-start(bf16[4,320,256]{2,1,0:T(8,128)(2,1)} %project.1), calls=%async_computation.1 | async-start | bytes 1310720 | tf_op jit(solution)/shard_map/all_to_all | solution.py:472
  106.3 19.7 %copy-start.1 = (bf16[256,1024]{1,0:T(8,128)(2,1)S(1)}, bf16[256,1024]{1,0:T(8,128)(2,1)}, u32[]{:S(2)}) copy-start(bf16[256,1024]{1,0:T(8,128)(2,1)} %copy-done) | copy-start | bytes 1572868
  106.3 19.7 %copy-start.3 = (bf16[256,1024]{1,0:T(8,128)(2,1)S(1)}, bf16[256,1024]{1,0:T(8,128)(2,1)}, u32[]{:S(2)}) copy-start(bf16[256,1024]{1,0:T(8,128)(2,1)} %copy-done.2) | copy-start | bytes 1572868

commit v14 on v13

--- a/solution.py
+++ b/solution.py
@@ -187,8 +187,8 @@
     return copies
 
 
-def copies_kernel(where_ref, first, second, after, out, sems):
-    del after
+def copies_kernel(where_ref, first, second, after, later, out, sems):
+    del after, later
     odd = where_ref[1] % 2
     sent = []
     for device in range(8):
@@ -200,16 +200,16 @@
         copy.wait()
 
 
-def copies(where, first, second, after):
+def copies(where, first, second, after, later):
     return pl.pallas_call(
         copies_kernel,
         out_shape=pltpu.HBM((8, 2, 320, 128), BF16),
-        in_specs=[in_smem(), *in_vmem(2), anywhere()],
+        in_specs=[in_smem(), *in_vmem(2), anywhere(), anywhere()],
         out_specs=in_hbm(),
         scratch_shapes=[pltpu.SemaphoreType.DMA((16,))],
         compiler_params=params(),
         name="weight_copies",
-    )(where, first, second, after)
+    )(where, first, second, after, later)
 
 
 def project_kernel(
@@ -225,7 +225,8 @@
     out,
     own,
     joined,
-    w_all,
+    w_q,
+    w_kv,
     result,
     sems,
     out_sems,
@@ -242,32 +243,38 @@
         block = resting_z(where_ref[2], block_of(part, core))
         start = 256 * part
         for head in range(2):
-            w_all[start : start + 256, HEAD * head : HEAD * head + HEAD] = weights[
-                block, head, :256, :
-            ]
-        for chunk in range(2):
-            base = 256 + 32 * chunk
-            pair = [weights[block, head, base : base + 32, :] for head in range(2)]
-            columns = [pair[0][:16], pair[1][:16], pair[0][16:], pair[1][16:]]
-            rows = pl.ds(start + 128 * chunk, 128)
-            w_all[rows, 256:] = jnp.concatenate(columns, axis=0).T
+            rows, cols = pl.ds(start, 256), pl.ds(HEAD * head, HEAD)
+            w_q[rows, cols] = weights[block, head, :256, :]
+            for chunk in range(2):
+                lanes = pl.ds(start + 128 * chunk, 128)
+                base = 256 + 32 * chunk
+                w_kv[16 * head : 16 * head + 16, lanes] = weights[block, head, base : base + 16, :]
+                w_kv[32 + 16 * head : 48 + 16 * head, lanes] = weights[
+                    block, head, base + 16 : base + 32, :
+                ]
 
     def product(x, rows):
-        return jnp.dot(x, w_all[rows, :], preferred_element_type=F32)
+        q = jnp.dot(x, w_q[rows, :], preferred_element_type=F32)
+        kv = lax.dot_general(
+            x, w_kv[:, rows], (((1,), (1,)), ((), ())), preferred_element_type=F32
+        )
+        return q, kv
 
     low, high = pl.ds(0, 1024), pl.ds(1024, 1024)
     departures = []
     for number in (0, 2, 1, 3):
         if number % 2 == 0:
             near, far = ((n1, f1), (n3, f3))[number // 2]
-            linear = product(near[...], low) + product(far[...], high)
+            q_near, kv_near = product(near[...], low)
+            q_far, kv_far = product(far[...], high)
+            q, kv = q_near + q_far, kv_near + kv_far
         else:
             tokens, arrivals = ((joined, first), (own, copies))[number // 3]
             for copy in arrivals:
                 copy.wait()
-            linear = product(tokens[...], pl.ds(0, 2048))
-        result[number, :256, :] = linear[:, :256].astype(BF16)
-        result[number, 256:, :] = linear[:, 256:].T.astype(BF16)
+            q, kv = product(tokens[...], pl.ds(0, 2048))
+        result[number, :256, :] = q.astype(BF16)
+        result[number, 256:, :] = kv.T.astype(BF16)
         other = (where_ref[1] + number + 1) % 4
         departures.append(
             pltpu.make_async_copy(result.at[number], out.at[other], out_sems.at[number])
@@ -286,7 +293,8 @@
         scratch_shapes=[
             pltpu.VMEM((TOK, 2048), BF16),
             pltpu.VMEM((TOK, 2048), BF16),
-            pltpu.VMEM((2048, 320), BF16),
+            pltpu.VMEM((2048, 256), BF16),
+            pltpu.VMEM((64, 2048), BF16),
             pltpu.VMEM((4, 320, 256), BF16),
             pltpu.SemaphoreType.DMA((10,)),
             pltpu.SemaphoreType.DMA((4,)),
@@ -306,9 +314,13 @@
     tables_ref,
     turned_ref,
     states_ref,
+    n2_ref,
+    f2_ref,
     attn_out,
     dq_out,
     own,
+    n2,
+    f2,
     upstream,
     tables,
     turned,
@@ -319,6 +331,8 @@
         pltpu.make_async_copy(turned_ref, turned, sems.at[9]),
         pltpu.make_async_copy(upstream_ref, upstream, sems.at[10]),
         *own_columns(where_ref, states_ref, own, sems),
+        pltpu.make_async_copy(n2_ref, n2, sems.at[11]),
+        pltpu.make_async_copy(f2_ref, f2, sems.at[12]),
     ]
     for copy in copies:
         copy.start()
@@ -377,19 +391,20 @@
         copy.wait()
 
 
-def attend(where, block_mask, risk_weight, parts, kv, upstream, tables, turned, states):
+def attend(where, block_mask, risk_weight, parts, kv, upstream, tables, turned, states, n2, f2):
     own = jax.ShapeDtypeStruct((TOK, 2048), BF16)
+    part = jax.ShapeDtypeStruct((TOK, 1024), BF16)
     square = jax.ShapeDtypeStruct((TOK, 256), BF16)
     return pl.pallas_call(
         attend_kernel,
-        out_shape=(square, square, own),
-        in_specs=[*[in_smem()] * 3, *in_vmem(2), *[in_hbm()] * 4],
-        out_specs=tuple(in_vmem(3)),
+        out_shape=(square, square, own, part, part),
+        in_specs=[*[in_smem()] * 3, *in_vmem(2), *[in_hbm()] * 6],
+        out_specs=tuple(in_vmem(5)),
         scratch_shapes=[
             pltpu.VMEM((TOK, 256), BF16),
             pltpu.VMEM((TOK, HEAD), F32),
             pltpu.VMEM((HEAD, TOK), F32),
-            pltpu.SemaphoreType.DMA((11,)),
+            pltpu.SemaphoreType.DMA((13,)),
         ],
         compiler_params=params(),
         name="attend",
@@ -403,6 +418,8 @@
         held(tables),
         held(turned),
         held(states),
+        held(n2),
+        held(f2),
     )
 
 
@@ -459,7 +476,7 @@
     first = lax.ppermute(first, AXES, home_pairs(0))
     second = lax.ppermute(second, AXES, home_pairs(1))
     outgoing = cut(where, states, (1, 3))
-    weights = copies(where, first, second, outgoing[0])
+    weights = copies(where, first, second, outgoing[0], n2)
 
     up, down = gate(outgoing, held(weights))
     n1 = lax.ppermute(down, AXES, ring_pairs(-1, -1))
@@ -483,9 +500,10 @@
     tables = jnp.concatenate([cosine, sine], axis=1)
     turned = jnp.concatenate([cosine.T, sine.T], axis=0)
 
-    attn_out, dq, own = attend(
-        where, block_mask, risk_weight, parts, kv, upstream, tables, turned, states
+    attn_out, dq, own, n2, f2 = attend(
+        where, block_mask, risk_weight, parts, kv, upstream, tables, turned, states, n2, far[1]
     )
+    near, far = (n1, n2, n3), (far[0], f2, far[2])
     slopes = lax.all_gather(dq, GROUP, axis=0, tiled=False)
     terms = gradient(where, own, near, far, slopes)
     terms = lax.all_to_all(terms, OTHERS, split_axis=0, concat_axis=0)

time: 163 us -> 163 us (level)
  waiting for transfers between devices: 35.9 us -> 42.4 us
  blocking collectives: 55 us -> 50.9 us
  starting transfers between devices: 47.2 us -> 44.8 us
    all_to_all x1, waiting for transfers between devices: 0.01 us -> 11.8 us  [shards(): weights = lax.all_to_all(weights, OTHERS, split_axis=0, concat_axis=0)]
    ppermute x1, waiting for transfers between devices: 9.31 us -> 0.01 us  [shards(): n2 = lax.ppermute(two, AXES, ring_pairs(2, -2))]
    ppermute x1, waiting for transfers between devices: 1.5 us -> 5.98 us  [shards(): n1 = lax.ppermute(down, AXES, ring_pairs(-1, -1))]
    all_to_all x1, blocking collectives: 33.1 us -> 28.9 us  [shards(): terms = lax.all_to_all(terms, OTHERS, split_axis=0, concat_axis=0)]
    ppermute x1, starting transfers between devices: 5.75 us -> 2.99 us  [shards(): n1 = lax.ppermute(down, AXES, ring_pairs(-1, -1))]
    ppermute x1, starting transfers between devices: 2.3 us -> 4.5 us  [shards(): n2 = lax.ppermute(two, AXES, ring_pairs(2, -2))]
    ppermute x3, starting transfers between devices: 7.58 us -> 5.74 us  [swap_core(): return lax.ppermute(value, 'c', [(0, 1), (1, 0)])]
  transfers between devices with their start and end apart: 10 -> 10, of which waited for: 6 -> 6; matrix products, arithmetic and copies ran while one was open for 2% -> 2% of each run, Pallas kernels for 2% -> 3%
where the time goes in v14:
time: 163 us; the launch traced here: 162 us
  blocking collectives  50.9 us (31%)
  starting transfers between devices  44.8 us (27%)
  waiting for transfers between devices  42.4 us (26%)
  Pallas kernels  20.2 us (12%)
  other arithmetic  2.58 us (2%)
    all_to_all x1, blocking collectives, shards(): terms = lax.all_to_all(terms, OTHERS, split_axis=0, concat_axis=0)  28.9 us
    all_gather x1, blocking collectives, shards(): slopes = lax.all_gather(dq, GROUP, axis=0, tiled=False)  16.1 us
    all_to_all x1, waiting for transfers between devices, shards(): parts = lax.all_to_all(parts, GROUP, split_axis=0, concat_axis=0)  15.3 us
    all_to_all x1, starting transfers between devices, shards(): weights = lax.all_to_all(weights, OTHERS, split_axis=0, concat_axis=0)  14.4 us
    all_to_all x1, waiting for transfers between devices, shards(): weights = lax.all_to_all(weights, OTHERS, split_axis=0, concat_axis=0)  11.8 us
    ppermute x1, starting transfers between devices, shards(): first = lax.ppermute(first, AXES, home_pairs(0))  7.81 us
    ppermute x1, waiting for transfers between devices, shards(): second = lax.ppermute(second, AXES, home_pairs(1))  6.12 us
    ppermute x1, waiting for transfers between devices, shards(): n1 = lax.ppermute(down, AXES, ring_pairs(-1, -1))  5.98 us
  transfers between devices with their start and end apart: 10, of which 6 were waited for; matrix products, arithmetic and copies ran while one was open for 2% of the time, Pallas kernels for 3%

profile of v14, /device:TPU:6, one launch (start us, length us, event | category | flops | bytes accessed | tf_op | source)
XLA Modules:
  0.0 161.8 jit_solution(295180706974112476)
XLA Ops:
  0.6 0.1 pad_add_fusion.where_ref
  0.7 1.7 %cut_states.2.after = bf16[256,1024]{1,0:T(8,128)(2,1)S(1)} custom-call(s32[3]{0:T(128)S(1)} %pad_add_fusion.where_ref, bf16[256,8192]{1,0:T(8,128)(2,1)} %states_ref.7), custom_call_target="tpu_custom_call" | custom-call | tf_op jit(solution)/shard_map/cut_states/pallas_call | solution.py:148
  2.4 4.5 %collective-permute-start = (bf16[256,1024]{1,0:T(8,128)(2,1)S(1)}, bf16[256,1024]{1,0:T(8,128)(2,1)S(1)}, u32[]{:S(2)}, u32[]{:S(2)}) collective-permute-start(bf16[256,1024]{1,0:T(8,128)(2,1)S(1)} %cut_states.2.after), channel_id=1, source_target_pairs={{0,32},{1,41},{2,34},{3,43},{4,36},{5,45},{6,38},{7,47},{16,48},{1... | collective-permute-start | bytes 1572872 | tf_op jit(solution)/shard_map/ppermute | solution.py:473
  6.9 1.6 pack_weights.1
  8.5 7.8 %collective-permute-start.2 = (bf16[320,128]{1,0:T(8,128)(2,1)S(1)}, bf16[320,128]{1,0:T(8,128)(2,1)S(1)}, u32[]{:S(2)}, u32[]{:S(2)}) collective-permute-start(bf16[320,128]{1,0:T(8,128)(2,1)S(1)} %get-tuple-element.15), channel_id=1, source_target_pairs={{0,256},{1,288},{2,320},{3,352},{4,384},{5,416},{6,192},{7,224},{8... | collective-permute-start | bytes 245768 | tf_op jit(solution)/shard_map/ppermute | solution.py:476
  16.3 3.0 %collective-permute-start.3 = (bf16[320,128]{1,0:T(8,128)(2,1)S(1)}, bf16[320,128]{1,0:T(8,128)(2,1)S(1)}, u32[]{:S(2)}, u32[]{:S(2)}) collective-permute-start(bf16[320,128]{1,0:T(8,128)(2,1)S(1)} %get-tuple-element.16), channel_id=1, source_target_pairs={{0,272},{1,304},{2,336},{3,368},{4,400},{5,432},{6,208},{7,240},{8... | collective-permute-start | bytes 245768 | tf_op jit(solution)/shard_map/ppermute | solution.py:477
  19.3 2.7 %cut_states.3 = (bf16[256,1024]{1,0:T(8,128)(2,1)}, bf16[256,1024]{1,0:T(8,128)(2,1)S(1)}) custom-call(s32[3]{0:T(128)S(1)} %pad_add_fusion.where_ref, bf16[256,8192]{1,0:T(8,128)(2,1)} %states_ref.7), custom_call_target="tpu_custom_call" | custom-call | tf_op jit(solution)/shard_map/cut_states/pallas_call | solution.py:148
  22.0 0.0 collective-permute-done.2.first
  22.0 6.1 %collective-permute-done.3.second = bf16[320,128]{1,0:T(8,128)(2,1)S(1)} collective-permute-done((bf16[320,128]{1,0:T(8,128)(2,1)S(1)}, bf16[320,128]{1,0:T(8,128)(2,1)S(1)}, u32[]{:S(2)}, u32[]{:S(2)}) %collective-permute-start.3) | collective-permute-done | bytes 81952 | tf_op jit(solution)/shard_map/ppermute | solution.py:477
  28.2 0.0 collective-permute-done.later.n2.n2_ref
  28.2 0.0 copy-start
  28.2 1.8 %weight_copies.1.refs_2_ = bf16[8,2,320,128]{3,2,1,0:T(8,128)(2,1)} custom-call(s32[3]{0:T(128)S(1)} %pad_add_fusion.where_ref, bf16[320,128]{1,0:T(8,128)(2,1)S(1)} %collective-permute-done.2.first, bf16[320,128]{1,0:T(8,128)(2,1)S(1)} %collective-permute-done.3.second, bf16[256,1024]{1,0:T(8,128)(2,1)} %get-tuple-element.13.after.refs_0_, ...), custom_call_target="tpu_custom_call" | custom-call | tf_op jit(solution)/shard_map/weight_copies/pallas_call | solution.py:204
  29.9 14.4 %all-to-all-start = ((bf16[8,2,320,128]{3,2,1,0:T(8,128)(2,1)}), bf16[8,2,320,128]{3,2,1,0:T(8,128)(2,1)S(1)}, u32[]{:S(2)}, u32[]{:S(2)}) async-start(bf16[8,2,320,128]{3,2,1,0:T(8,128)(2,1)} %weight_copies.1.refs_2_), calls=%async_computation | async-start | bytes 2621440 | tf_op jit(solution)/shard_map/all_to_all | solution.py:486
  44.4 0.0 copy-start.1
  44.4 3.0 %collective-permute-start.4 = (bf16[256,1024]{1,0:T(8,128)(2,1)S(1)}, bf16[256,1024]{1,0:T(8,128)(2,1)S(1)}, u32[]{:S(2)}, u32[]{:S(2)}) collective-permute-start(bf16[256,1024]{1,0:T(8,128)(2,1)S(1)} %get-tuple-element.17), channel_id=1, source_target_pairs={{0,56},{1,57},{2,58},{3,59},{4,60},{5,61},{6,62},{7,63},{16,0},{17... | collective-permute-start | bytes 1572872 | tf_op jit(solution)/shard_map/ppermute | solution.py:482
  47.4 2.9 %collective-permute-start.5 = (bf16[256,1024]{1,0:T(8,128)(2,1)}, bf16[256,1024]{1,0:T(8,128)(2,1)S(1)}, u32[]{:S(2)}, u32[]{:S(2)}) collective-permute-start(bf16[256,1024]{1,0:T(8,128)(2,1)} %get-tuple-element.18), channel_id=1, source_target_pairs={{0,16},{1,17},{2,18},{3,19},{4,20},{5,21},{6,22},{7,23},{16,32},{1... | collective-permute-start | bytes 1572872 | tf_op jit(solution)/shard_map/ppermute | solution.py:483
  50.2 0.0 copy-done
  50.2 1.9 %collective-permute-start.1 = (bf16[256,1024]{1,0:T(8,128)(2,1)S(1)}, bf16[256,1024]{1,0:T(8,128)(2,1)}, u32[]{:S(2)}, u32[]{:S(2)}) collective-permute-start(bf16[256,1024]{1,0:T(8,128)(2,1)S(1)} %collective-permute-done.later.n2.n2_ref), channel_id=1, source_target_pairs={{0,1},{1,0},{2,3},{3,2},{4,5},{5,4},{6,7},{7,6},{8,9},{9,8},{10,11... | collective-permute-start | bytes 1572872 | tf_op jit(solution)/shard_map/ppermute | solution.py:60
  52.2 6.0 %collective-permute-done.4.n1 = bf16[256,1024]{1,0:T(8,128)(2,1)S(1)} collective-permute-done((bf16[256,1024]{1,0:T(8,128)(2,1)S(1)}, bf16[256,1024]{1,0:T(8,128)(2,1)S(1)}, u32[]{:S(2)}, u32[]{:S(2)}) %collective-permute-start.4) | collective-permute-done | bytes 524320 | tf_op jit(solution)/shard_map/ppermute | solution.py:482
  58.1 1.9 %collective-permute-start.6 = (bf16[256,1024]{1,0:T(8,128)(2,1)S(1)}, bf16[256,1024]{1,0:T(8,128)(2,1)S(1)}, u32[]{:S(2)}, u32[]{:S(2)}) collective-permute-start(bf16[256,1024]{1,0:T(8,128)(2,1)S(1)} %collective-permute-done.4.n1), channel_id=1, source_target_pairs={{0,1},{1,0},{2,3},{3,2},{4,5},{5,4},{6,7},{7,6},{8,9},{9,8},{10,11... | collective-permute-start | bytes 1572872 | tf_op jit(solution)/shard_map/ppermute | solution.py:60
  60.1 1.4 collective-permute-done.5.n3
  61.5 1.9 %collective-permute-start.7 = (bf16[256,1024]{1,0:T(8,128)(2,1)S(1)}, bf16[256,1024]{1,0:T(8,128)(2,1)}, u32[]{:S(2)}, u32[]{:S(2)}) collective-permute-start(bf16[256,1024]{1,0:T(8,128)(2,1)S(1)} %collective-permute-done.5.n3), channel_id=1, source_target_pairs={{0,1},{1,0},{2,3},{3,2},{4,5},{5,4},{6,7},{7,6},{8,9},{9,8},{10,11... | collective-permute-start | bytes 1572872 | tf_op jit(solution)/shard_map/ppermute | solution.py:60
  63.4 0.0 copy-done.1
  63.4 0.1 reduce_sum.19
  63.6 0.0 collective-permute-done.1.f2.f2_ref
  63.6 0.0 collective-permute-done.6.f1
  63.6 1.9 %collective-permute-done.7.f3 = bf16[256,1024]{1,0:T(8,128)(2,1)} collective-permute-done((bf16[256,1024]{1,0:T(8,128)(2,1)S(1)}, bf16[256,1024]{1,0:T(8,128)(2,1)}, u32[]{:S(2)}, u32[]{:S(2)}) %collective-permute-start.7) | collective-permute-done | bytes 524320 | tf_op jit(solution)/shard_map/ppermute | solution.py:60
  65.4 11.8 %all-to-all-done.weights = bf16[8,2,320,128]{3,2,1,0:T(8,128)(2,1)S(1)} async-done(((bf16[8,2,320,128]{3,2,1,0:T(8,128)(2,1)}), bf16[8,2,320,128]{3,2,1,0:T(8,128)(2,1)S(1)}, u32[]{:S(2)}, u32[]{:S(2)}) %all-to-all-start) | async-done | bytes 1310752 | tf_op jit(solution)/shard_map/all_to_all | solution.py:486
  77.2 5.7 %project.1 = bf16[4,320,256]{2,1,0:T(8,128)(2,1)} custom-call(s32[3]{0:T(128)S(1)} %pad_add_fusion.where_ref, bf16[256,8192]{1,0:T(8,128)(2,1)} %states_ref.7, bf16[256,1024]{1,0:T(8,128)(2,1)} %copy-done, bf16[256,1024]{1,0:T(8,128)(2,1)} %collective-permute-done.1.f2.f2_ref, bf16[256,1024]{1,0:T(8,128)(2,1)S(1)} %collective-permute-done.4.n1, ...), custom_call_target="tpu_custom_call" | custom-call | tf_op jit(solution)/shard_map/project/pallas_call | solution.py:288
  82.9 0.0 copy-start.2
  82.9 3.5 %all-to-all-start.1 = ((bf16[4,320,256]{2,1,0:T(8,128)(2,1)}), bf16[4,320,256]{2,1,0:T(8,128)(2,1)S(1)}, u32[]{:S(2)}, u32[]{:S(2)}) async-start(bf16[4,320,256]{2,1,0:T(8,128)(2,1)} %project.1), calls=%async_computation.1 | async-start | bytes 1310720 | tf_op jit(solution)/shard_map/all_to_all | solution.py:489
  86.4 0.1 add_convert_fusion
  86.5 0.1 convert_element_type.15
  86.6 0.3 multiply_cosine_fusion.1
  86.9 0.7 pad_maximum_fusion.1.turned_ref
  87.6 0.5 multiply_cosine_fusion
  88.1 0.8 pad_maximum_fusion.tables_ref
  88.9 15.3 %all-to-all-done.1.parts = bf16[4,320,256]{2,1,0:T(8,128)(2,1)S(1)} async-done(((bf16[4,320,256]{2,1,0:T(8,128)(2,1)}), bf16[4,320,256]{2,1,0:T(8,128)(2,1)S(1)}, u32[]{:S(2)}, u32[]{:S(2)}) %all-to-all-start.1) | async-done | bytes 655392 | tf_op jit(solution)/shard_map/all_to_all | solution.py:489
  104.1 5.8 %all-gather = f32[256,256]{1,0:T(8,128)S(1)} all-gather(f32[64,256]{1,0:T(8,128)S(1)} %convert_reduce_fusion), channel_id=2, replica_groups=mesh['zh'=4,'zb'=2,'yu'=2,'yb'=2,'yh'=2,'xh'=2,'xb'=2,'c'=2] {'xb','c'}, dimensions={0}, use_global_device_ids=true | all-gather | bytes 327680 | tf_op jit(solution)/shard_map/all_gather | solution.py:491
  109.9 0.0 copy-done.2
  109.9 3.5 %attend.1 = (bf16[256,256]{1,0:T(8,128)(2,1)}, bf16[256,256]{1,0:T(8,128)(2,1)S(1)}, bf16[256,2048]{1,0:T(8,128)(2,1)S(1)}, bf16[256,1024]{1,0:T(8,128)(2,1)S(1)}, bf16[256,1024]{1,0:T(8,128)(2,1)S(1)}) custom-call(s32[3]{0:T(128)S(1)} %pad_add_fusion.where_ref, s32[4,4]{1,0:T(4,128)S(1)} %copy-done.1, f32[4]{0:T(128)S(1)} %copy-done.2, ...), custom_call_target="tpu_custom_call" | custom-call | tf_op jit(solution)/shard_map/attend/pallas_call | solution.py:398
  113.5 16.1 %all-gather.1 = bf16[1024,256]{1,0:T(8,128)(2,1)S(1)} all-gather(bf16[256,256]{1,0:T(8,128)(2,1)S(1)} %get-tuple-element.23), channel_id=3, replica_groups=mesh['zh'=4,'zb'=2,'yu'=2,'yb'=2,'yh'=2,'xh'=2,'xb'=2,'c'=2] {'yu','yb'}, dimensions={0}, use_global_device_ids=true | all-gather | bytes 655360 | tf_op jit(solution)/shard_map/all_gather | solution.py:507
  129.6 2.3 %gradient.1 = bf16[8,256,256]{2,1,0:T(8,128)(2,1)S(1)} custom-call(s32[3]{0:T(128)S(1)} %pad_add_fusion.where_ref, bf16[256,2048]{1,0:T(8,128)(2,1)S(1)} %get-tuple-element.20.own, bf16[256,1024]{1,0:T(8,128)(2,1)S(1)} %collective-permute-done.4.n1, bf16[256,1024]{1,0:T(8,128)(2,1)S(1)} %get-tuple-element.21.n2, ...), custom_call_target="tpu_custom_call" | custom-call | tf_op jit(solution)/shard_map/gradient/pallas_call | solution.py:442
  131.9 28.9 %all_to_all.15.terms = bf16[8,256,256]{2,1,0:T(8,128)(2,1)S(1)} all-to-all(bf16[8,256,256]{2,1,0:T(8,128)(2,1)S(1)} %gradient.1), channel_id=1, replica_groups=mesh['zh'=4,'zb'=2,'yu'=2,'yb'=2,'yh'=2,'xh'=2,'xb'=2,'c'=2] {'zh','zb'}, dimensions={0} | all-to-all | bytes 2097152 | tf_op jit(solution)/shard_map/all_to_all | solution.py:509
  160.9 0.9 add_up.1
  (4 shorter events, 0.0 us)
Async XLA Ops:
  2.4 25.7 %collective-permute-start = (bf16[256,1024]{1,0:T(8,128)(2,1)S(1)}, bf16[256,1024]{1,0:T(8,128)(2,1)S(1)}, u32[]{:S(2)}, u32[]{:S(2)}) collective-permute-start(bf16[256,1024]{1,0:T(8,128)(2,1)S(1)} %cut_states.2.after), channel_id=1, source_target_pairs={{0,32},{1,41},{2,34},{3,43},{4,36},{5,45},{6,38},{7,47},{16,48},{1... | collective-permute-start | bytes 1572872 | tf_op jit(solution)/shard_map/ppermute | solution.py:473
  8.5 13.5 %collective-permute-start.2 = (bf16[320,128]{1,0:T(8,128)(2,1)S(1)}, bf16[320,128]{1,0:T(8,128)(2,1)S(1)}, u32[]{:S(2)}, u32[]{:S(2)}) collective-permute-start(bf16[320,128]{1,0:T(8,128)(2,1)S(1)} %get-tuple-element.15), channel_id=1, source_target_pairs={{0,256},{1,288},{2,320},{3,352},{4,384},{5,416},{6,192},{7,224},{8... | collective-permute-start | bytes 245768 | tf_op jit(solution)/shard_map/ppermute | solution.py:476
  16.3 11.8 %collective-permute-start.3 = (bf16[320,128]{1,0:T(8,128)(2,1)S(1)}, bf16[320,128]{1,0:T(8,128)(2,1)S(1)}, u32[]{:S(2)}, u32[]{:S(2)}) collective-permute-start(bf16[320,128]{1,0:T(8,128)(2,1)S(1)} %get-tuple-element.16), channel_id=1, source_target_pairs={{0,272},{1,304},{2,336},{3,368},{4,400},{5,432},{6,208},{7,240},{8... | collective-permute-start | bytes 245768 | tf_op jit(solution)/shard_map/ppermute | solution.py:477
  28.2 22.1 %copy-start = (bf16[256,1024]{1,0:T(8,128)(2,1)}, bf16[256,1024]{1,0:T(8,128)(2,1)S(1)}, u32[]{:S(2)}) copy-start(bf16[256,1024]{1,0:T(8,128)(2,1)S(1)} %collective-permute-done.later.n2.n2_ref) | copy-start | bytes 1572868
  29.9 47.3 %all-to-all-start = ((bf16[8,2,320,128]{3,2,1,0:T(8,128)(2,1)}), bf16[8,2,320,128]{3,2,1,0:T(8,128)(2,1)S(1)}, u32[]{:S(2)}, u32[]{:S(2)}) async-start(bf16[8,2,320,128]{3,2,1,0:T(8,128)(2,1)} %weight_copies.1.refs_2_), calls=%async_computation | async-start | bytes 2621440 | tf_op jit(solution)/shard_map/all_to_all | solution.py:486
  44.4 19.1 %copy-start.1 = (s32[4,4]{1,0:T(4,128)S(1)}, s32[4,4]{1,0:T(4,128)}, u32[]{:S(2)}) copy-start(s32[4,4]{1,0:T(4,128)} %mask_ref.1) | copy-start | bytes 196
  44.4 13.8 %collective-permute-start.4 = (bf16[256,1024]{1,0:T(8,128)(2,1)S(1)}, bf16[256,1024]{1,0:T(8,128)(2,1)S(1)}, u32[]{:S(2)}, u32[]{:S(2)}) collective-permute-start(bf16[256,1024]{1,0:T(8,128)(2,1)S(1)} %get-tuple-element.17), channel_id=1, source_target_pairs={{0,56},{1,57},{2,58},{3,59},{4,60},{5,61},{6,62},{7,63},{16,0},{17... | collective-permute-start | bytes 1572872 | tf_op jit(solution)/shard_map/ppermute | solution.py:482
  47.4 14.1 %collective-permute-start.5 = (bf16[256,1024]{1,0:T(8,128)(2,1)}, bf16[256,1024]{1,0:T(8,128)(2,1)S(1)}, u32[]{:S(2)}, u32[]{:S(2)}) collective-permute-start(bf16[256,1024]{1,0:T(8,128)(2,1)} %get-tuple-element.18), channel_id=1, source_target_pairs={{0,16},{1,17},{2,18},{3,19},{4,20},{5,21},{6,22},{7,23},{16,32},{1... | collective-permute-start | bytes 1572872 | tf_op jit(solution)/shard_map/ppermute | solution.py:483
  50.2 13.3 %collective-permute-start.1 = (bf16[256,1024]{1,0:T(8,128)(2,1)S(1)}, bf16[256,1024]{1,0:T(8,128)(2,1)}, u32[]{:S(2)}, u32[]{:S(2)}) collective-permute-start(bf16[256,1024]{1,0:T(8,128)(2,1)S(1)} %collective-permute-done.later.n2.n2_ref), channel_id=1, source_target_pairs={{0,1},{1,0},{2,3},{3,2},{4,5},{5,4},{6,7},{7,6},{8,9},{9,8},{10,11... | collective-permute-start | bytes 1572872 | tf_op jit(solution)/shard_map/ppermute | solution.py:60
  58.1 5.4 %collective-permute-start.6 = (bf16[256,1024]{1,0:T(8,128)(2,1)S(1)}, bf16[256,1024]{1,0:T(8,128)(2,1)S(1)}, u32[]{:S(2)}, u32[]{:S(2)}) collective-permute-start(bf16[256,1024]{1,0:T(8,128)(2,1)S(1)} %collective-permute-done.4.n1), channel_id=1, source_target_pairs={{0,1},{1,0},{2,3},{3,2},{4,5},{5,4},{6,7},{7,6},{8,9},{9,8},{10,11... | collective-permute-start | bytes 1572872 | tf_op jit(solution)/shard_map/ppermute | solution.py:60
  61.5 3.9 %collective-permute-start.7 = (bf16[256,1024]{1,0:T(8,128)(2,1)S(1)}, bf16[256,1024]{1,0:T(8,128)(2,1)}, u32[]{:S(2)}, u32[]{:S(2)}) collective-permute-start(bf16[256,1024]{1,0:T(8,128)(2,1)S(1)} %collective-permute-done.5.n3), channel_id=1, source_target_pairs={{0,1},{1,0},{2,3},{3,2},{4,5},{5,4},{6,7},{7,6},{8,9},{9,8},{10,11... | collective-permute-start | bytes 1572872 | tf_op jit(solution)/shard_map/ppermute | solution.py:60
  82.9 27.0 %copy-start.2 = (f32[4]{0:T(128)S(1)}, f32[4]{0:T(128)}, u32[]{:S(2)}) copy-start(f32[4]{0:T(128)} %risk_ref.1) | copy-start | bytes 52
  82.9 21.2 %all-to-all-start.1 = ((bf16[4,320,256]{2,1,0:T(8,128)(2,1)}), bf16[4,320,256]{2,1,0:T(8,128)(2,1)S(1)}, u32[]{:S(2)}, u32[]{:S(2)}) async-start(bf16[4,320,256]{2,1,0:T(8,128)(2,1)} %project.1), calls=%async_computation.1 | async-start | bytes 1310720 | tf_op jit(solution)/shard_map/all_to_all | solution.py:489

commit v15 on v11

--- a/solution.py
+++ b/solution.py
@@ -87,25 +87,25 @@
     return pl.BlockSpec(memory_space=pl.ANY)
 
 
-def pack_kernel(where_ref, query, key_t, value_t, first, second, sems):
+def pack_kernel(where_ref, query_ref, key_ref, value_ref, first, second, query, key_t, value_t, sems):
     odd = where_ref[1] % 2
-    copies = []
-
-    def copy(source, target):
-        copies.append(pltpu.make_async_copy(source, target, sems.at[len(copies)]))
-        copies[-1].start()
-
+    copies = [
+        pltpu.make_async_copy(query_ref, query, sems.at[0]),
+        pltpu.make_async_copy(key_ref, key_t, sems.at[1]),
+        pltpu.make_async_copy(value_ref, value_t, sems.at[2]),
+    ]
+    for copy in copies:
+        copy.start()
+    for copy in copies:
+        copy.wait()
     for turn, out in enumerate((first, second)):
         half = odd ^ turn
-        rows = pl.ds(pl.multiple_of(256 * half, 256), 256)
-        copy(query.at[rows, :], out.at[pl.ds(0, 256), :])
+        out[:256, :] = query[pl.ds(pl.multiple_of(256 * half, 256), 256), :]
         for chunk in range(2):
             lanes = pl.ds(pl.multiple_of(256 * half + 128 * chunk, 128), 128)
             base = 256 + 32 * chunk
-            copy(key_t.at[:, lanes], out.at[pl.ds(base, 16), :])
-            copy(value_t.at[:, lanes], out.at[pl.ds(base + 16, 16), :])
-    for each in copies:
-        each.wait()
+            out[base : base + 16, :] = key_t[:, lanes]
+            out[base + 16 : base + 32, :] = value_t[:, lanes]
 
 
 def pack(where, query, key_t, value_t):
@@ -115,15 +115,20 @@
         out_shape=(part, part),
         in_specs=[in_smem(), in_hbm(), in_hbm(), in_hbm()],
         out_specs=tuple(in_vmem(2)),
-        scratch_shapes=[pltpu.SemaphoreType.DMA((10,))],
+        scratch_shapes=[
+            pltpu.VMEM((512, 128), BF16),
+            pltpu.VMEM((16, 512), BF16),
+            pltpu.VMEM((16, 512), BF16),
+            pltpu.SemaphoreType.DMA((3,)),
+        ],
         compiler_params=params(),
         name="pack_weights",
     )(where, held(query), held(key_t), held(value_t))
 
 
-def cut_kernel(where_ref, states_ref, up_ref, two_ref, down_ref, sems):
+def cut_kernel(where_ref, states_ref, up_ref, two_ref, down_ref, own_ref, own, sems):
     core, place = where_ref[0], where_ref[1]
-    copies = []
+    copies = own_columns(where_ref, states_ref, own, sems)
     for number, out in enumerate((up_ref, two_ref, down_ref)):
         for part in range(4):
             start = column_of(block_of(part, core), (place + number + 1) % 4)
@@ -136,18 +141,23 @@
             )
     for copy in copies:
         copy.start()
-    for copy in copies:
+    for copy in copies[:8]:
         copy.wait()
+    keep = pltpu.make_async_copy(own, own_ref, sems.at[20])
+    keep.start()
+    for copy in copies[8:]:
+        copy.wait()
+    keep.wait()
 
 
 def cut(where, states):
     part = jax.ShapeDtypeStruct((TOK, 1024), BF16)
     return pl.pallas_call(
         cut_kernel,
-        out_shape=(part, part, part),
+        out_shape=(part, part, part, pltpu.HBM((TOK, 2048), BF16)),
         in_specs=[in_smem(), in_hbm()],
-        out_specs=tuple(in_vmem(3)),
-        scratch_shapes=[pltpu.SemaphoreType.DMA((12,))],
+        out_specs=(*in_vmem(3), in_hbm()),
+        scratch_shapes=[pltpu.VMEM((TOK, 2048), BF16), pltpu.SemaphoreType.DMA((21,))],
         compiler_params=params(),
         name="cut_states",
     )(where, held(states))
@@ -184,15 +194,14 @@
     return copies
 
 
-def copies_kernel(where_ref, first, second, after, out, sems):
+def copies_kernel(where_ref, first, second, after, out, piece, sems):
     del after
     odd = where_ref[1] % 2
-    sent = []
-    for device in range(8):
-        for turn, piece in enumerate((first, second)):
-            copy = pltpu.make_async_copy(piece, out.at[device, odd ^ turn], sems.at[len(sent)])
-            copy.start()
-            sent.append(copy)
+    piece[odd] = first[...]
+    piece[1 - odd] = second[...]
+    sent = [pltpu.make_async_copy(piece, out.at[i], sems.at[i]) for i in range(8)]
+    for copy in sent:
+        copy.start()
     for copy in sent:
         copy.wait()
 
@@ -203,7 +212,7 @@
         out_shape=pltpu.HBM((8, 2, 320, 128), BF16),
         in_specs=[in_smem(), *in_vmem(2), anywhere()],
         out_specs=in_hbm(),
-        scratch_shapes=[pltpu.SemaphoreType.DMA((16,))],
+        scratch_shapes=[pltpu.VMEM((2, 320, 128), BF16), pltpu.SemaphoreType.DMA((8,))],
         compiler_params=params(),
         name="weight_copies",
     )(where, first, second, after)
@@ -211,7 +220,7 @@
 
 def project_kernel(
     where_ref,
-    states_ref,
+    own_ref,
     n1,
     n2,
     n3,
@@ -222,7 +231,8 @@
     out,
     own,
     weights,
-    w_all,
+    w_q,
+    w_kv,
     result,
     sems,
     out_sems,
@@ -234,25 +244,29 @@
         arrivals.append(
             pltpu.make_async_copy(weights_ref.at[block], weights.at[part], sems.at[8 + part])
         )
-    copies = own_columns(where_ref, states_ref, own, sems)
+    copies = [pltpu.make_async_copy(own_ref, own, sems.at[0])]
     for copy in arrivals + copies:
         copy.start()
     for part in range(8):
         arrivals[part].wait()
         start = 256 * part
         for head in range(2):
-            w_all[start : start + 256, HEAD * head : HEAD * head + HEAD] = weights[
-                part, head, :256, :
-            ]
-        for chunk in range(2):
-            base = 256 + 32 * chunk
-            pair = [weights[part, head, base : base + 32, :] for head in range(2)]
-            columns = [pair[0][:16], pair[1][:16], pair[0][16:], pair[1][16:]]
-            rows = pl.ds(start + 128 * chunk, 128)
-            w_all[rows, 256:] = jnp.concatenate(columns, axis=0).T
+            rows, cols = pl.ds(start, 256), pl.ds(HEAD * head, HEAD)
+            w_q[rows, cols] = weights[part, head, :256, :]
+            for chunk in range(2):
+                lanes = pl.ds(start + 128 * chunk, 128)
+                base = 256 + 32 * chunk
+                w_kv[16 * head : 16 * head + 16, lanes] = weights[part, head, base : base + 16, :]
+                w_kv[32 + 16 * head : 48 + 16 * head, lanes] = weights[
+                    part, head, base + 16 : base + 32, :
+                ]
 
     def product(x, rows):
-        return jnp.dot(x, w_all[rows, :], preferred_element_type=F32)
+        q = jnp.dot(x, w_q[rows, :], preferred_element_type=F32)
+        kv = lax.dot_general(
+            x, w_kv[:, rows], (((1,), (1,)), ((), ())), preferred_element_type=F32
+        )
+        return q, kv
 
     low, high = pl.ds(0, 1024), pl.ds(1024, 1024)
     departures = []
@@ -260,11 +274,13 @@
         if near is None:
             for copy in copies:
                 copy.wait()
-            linear = product(own[...], pl.ds(0, 2048))
+            q, kv = product(own[...], pl.ds(0, 2048))
         else:
-            linear = product(near[...], low) + product(far[...], high)
-        result[number, :256, :] = linear[:, :256].astype(BF16)
-        result[number, 256:, :] = linear[:, 256:].T.astype(BF16)
+            q_near, kv_near = product(near[...], low)
+            q_far, kv_far = product(far[...], high)
+            q, kv = q_near + q_far, kv_near + kv_far
+        result[number, :256, :] = q.astype(BF16)
+        result[number, 256:, :] = kv.T.astype(BF16)
         other = (where_ref[1] + number + 1) % 4
         departures.append(
             pltpu.make_async_copy(result.at[number], out.at[other], out_sems.at[number])
@@ -274,7 +290,7 @@
         copy.wait()
 
 
-def project(where, states, near, far, weights):
+def project(where, own, near, far, weights):
     return pl.pallas_call(
         project_kernel,
         out_shape=pltpu.HBM((4, 320, 256), BF16),
@@ -283,18 +299,18 @@
         scratch_shapes=[
             pltpu.VMEM((TOK, 2048), BF16),
             pltpu.VMEM((8, 2, 320, 128), BF16),
-            pltpu.VMEM((2048, 320), BF16),
+            pltpu.VMEM((2048, 256), BF16),
+            pltpu.VMEM((64, 2048), BF16),
             pltpu.VMEM((4, 320, 256), BF16),
             pltpu.SemaphoreType.DMA((16,)),
             pltpu.SemaphoreType.DMA((4,)),
         ],
         compiler_params=params(),
         name="project",
-    )(where, held(states), *near, *far, held(weights))
+    )(where, held(own), *near, *far, held(weights))
 
 
 def attend_kernel(
-    where_ref,
     mask_ref,
     risk_ref,
     parts,
@@ -302,7 +318,7 @@
     upstream_ref,
     tables_ref,
     turned_ref,
-    states_ref,
+    own_ref,
     attn_out,
     dq_out,
     own,
@@ -315,13 +331,13 @@
         pltpu.make_async_copy(tables_ref, tables, sems.at[8]),
         pltpu.make_async_copy(turned_ref, turned, sems.at[9]),
         pltpu.make_async_copy(upstream_ref, upstream, sems.at[10]),
-        *own_columns(where_ref, states_ref, own, sems),
+        pltpu.make_async_copy(own_ref, own, sems.at[0]),
     ]
     for copy in copies:
         copy.start()
     scaling = 1.0 / math.sqrt(HEAD)
-    k_lin = jnp.concatenate([kv[s, :32, :] for s in range(4)], axis=0)
-    values = jnp.concatenate([kv[s, 32:, :] for s in range(4)], axis=0).astype(BF16)
+    k_lin = jnp.concatenate([kv[s, :32, :] for s in range(4)], axis=0).astype(F32)
+    values = jnp.concatenate([kv[s, 32:, :] for s in range(4)], axis=0)
 
     row = lax.broadcasted_iota(jnp.int32, (BS, TOK), 0)
     column = lax.broadcasted_iota(jnp.int32, (BS, TOK), 1)
@@ -337,7 +353,11 @@
 
     copies[0].wait()
     copies[1].wait()
-    cq, sq = tables[:, :HEAD], tables[:, HEAD:]
+    half = lax.broadcasted_iota(jnp.int32, (TOK, HEAD), 1) < HEAD // 2
+    table = tables[...]
+    turned_table = pltpu.roll(table, HEAD // 2, 1)
+    cq = jnp.where(half, table, turned_table)
+    sq = jnp.where(half, -turned_table, table)
     ck, sk = turned[:64], turned[64:]
     k1, k2 = k_lin[:64], k_lin[64:]
     keys = jnp.concatenate([k1 * ck - k2 * sk, k2 * ck + k1 * sk], axis=0).astype(BF16)
@@ -351,7 +371,7 @@
         queries = ((q_lin * cq + pltpu.roll(q_lin, 64, 1) * sq) * scaling).astype(BF16)
         scores = jnp.dot(queries, keys, preferred_element_type=F32)
         raised = jnp.where(seen, jnp.exp(scores), 0.0)
-        attend = raised / jnp.sum(raised, axis=1, keepdims=True)
+        attend = raised * (1.0 / jnp.sum(raised, axis=1, keepdims=True))
         mixed = lax.dot_general(
             attend.astype(BF16), values, (((1,), (1,)), ((), ())), preferred_element_type=F32
         )
@@ -370,24 +390,23 @@
         copy.wait()
 
 
-def attend(where, block_mask, risk_weight, parts, kv, upstream, tables, turned, states):
-    own = jax.ShapeDtypeStruct((TOK, 2048), BF16)
+def attend(block_mask, risk_weight, parts, kv, upstream, tables, turned, own):
+    whole = jax.ShapeDtypeStruct((TOK, 2048), BF16)
     square = jax.ShapeDtypeStruct((TOK, 256), BF16)
     return pl.pallas_call(
         attend_kernel,
-        out_shape=(square, square, own),
-        in_specs=[*[in_smem()] * 3, *in_vmem(2), *[in_hbm()] * 4],
+        out_shape=(square, square, whole),
+        in_specs=[*[in_smem()] * 2, *in_vmem(2), *[in_hbm()] * 4],
         out_specs=tuple(in_vmem(3)),
         scratch_shapes=[
             pltpu.VMEM((TOK, 256), BF16),
-            pltpu.VMEM((TOK, 2 * HEAD), F32),
+            pltpu.VMEM((TOK, HEAD), F32),
             pltpu.VMEM((HEAD, TOK), F32),
             pltpu.SemaphoreType.DMA((11,)),
         ],
         compiler_params=params(),
         name="attend",
     )(
-        where,
         block_mask,
         risk_weight,
         parts,
@@ -395,7 +414,7 @@
         held(upstream),
         held(tables),
         held(turned),
-        held(states),
+        held(own),
     )
 
 
@@ -448,7 +467,7 @@
     first, second = pack(where, query_weight, key_matrix.T, value_matrix.T)
     first = lax.ppermute(first, AXES, home_pairs(0))
     second = lax.ppermute(second, AXES, home_pairs(1))
-    outgoing = cut(where, states)
+    *outgoing, own = cut(where, states)
     weights = copies(where, first, second, outgoing[0])
 
     (two,) = gate(outgoing[1:2], second)
@@ -461,9 +480,9 @@
     far = [swap_core(x) for x in near]
     weights = lax.all_to_all(weights, OTHERS, split_axis=0, concat_axis=0)
 
-    parts = project(where, states, near, far, weights)
+    parts = project(where, own, near, far, weights)
     parts = lax.all_to_all(parts, GROUP, split_axis=0, concat_axis=0)
-    kv = jnp.sum(parts[:, 256:].astype(F32), axis=0)
+    kv = jnp.sum(parts[:, 256:].astype(F32), axis=0).astype(BF16)
     kv = lax.all_gather(kv, ("xb", "c"), axis=0, tiled=False)
 
     depths = jnp.sum(block_mask, axis=1) - 1
@@ -473,11 +492,11 @@
     )
     angles = places.astype(F32)[:, None] * frequency[None, :]
     cosine, sine = jnp.cos(angles), jnp.sin(angles)
-    tables = jnp.concatenate([cosine, cosine, -sine, sine], axis=1)
+    tables = jnp.concatenate([cosine, sine], axis=1)
     turned = jnp.concatenate([cosine.T, sine.T], axis=0)
 
     attn_out, dq, own = attend(
-        where, block_mask, risk_weight, parts, kv, upstream, tables, turned, states
+        block_mask, risk_weight, parts, kv, upstream, tables, turned, own
     )
     slopes = lax.all_gather(dq, GROUP, axis=0, tiled=False)
     terms = gradient(where, own, near, far, slopes)

time: 161 us -> 160 us (level)
  transfers between devices with their start and end apart: 10 -> 10, of which waited for: 6 -> 6; matrix products, arithmetic and copies ran while one was open for 2% -> 2% of each run, Pallas kernels for 1% -> 2%
where the time goes in v15:
time: 160 us
  blocking collectives  54.4 us (34%)
  starting transfers between devices  47.6 us (30%)
  waiting for transfers between devices  36.2 us (23%)
  Pallas kernels  17.9 us (11%)
  other arithmetic  2.57 us (2%)
    all_to_all x1, blocking collectives, shards(): terms = lax.all_to_all(terms, OTHERS, split_axis=0, concat_axis=0)  32.8 us
    all_gather x1, blocking collectives, shards(): slopes = lax.all_gather(dq, GROUP, axis=0, tiled=False)  16.1 us
    all_to_all x1, waiting for transfers between devices, shards(): parts = lax.all_to_all(parts, GROUP, split_axis=0, concat_axis=0)  15.1 us
    all_to_all x1, starting transfers between devices, shards(): weights = lax.all_to_all(weights, OTHERS, split_axis=0, concat_axis=0)  14.8 us
    ppermute x1, waiting for transfers between devices, shards(): lax.ppermute(two, AXES, ring_pairs(2, -2))  11 us
    ppermute x1, starting transfers between devices, shards(): first = lax.ppermute(first, AXES, home_pairs(0))  7.81 us
    ppermute x3, starting transfers between devices, swap_core(): return lax.ppermute(value, 'c', [(0, 1), (1, 0)])  7.72 us
    ppermute x1, starting transfers between devices, shards(): lax.ppermute(down, AXES, ring_pairs(-1, -1))  5.77 us
  transfers between devices with their start and end apart: 10, of which 6 were waited for; matrix products, arithmetic and copies ran while one was open for 2% of the time, Pallas kernels for 2%

profile of v15, /device:TPU:6, one launch (start us, length us, event | category | flops | bytes accessed | tf_op | source)
XLA Modules:
  0.0 159.5 jit_solution(10539718041573553307)
XLA Ops:
  0.6 0.1 pad_add_fusion.where_ref
  0.7 1.5 pack_weights.1
  2.2 7.8 %collective-permute-start = (bf16[320,128]{1,0:T(8,128)(2,1)S(1)}, bf16[320,128]{1,0:T(8,128)(2,1)S(1)}, u32[]{:S(2)}, u32[]{:S(2)}) collective-permute-start(bf16[320,128]{1,0:T(8,128)(2,1)S(1)} %get-tuple-element.16), channel_id=1, source_target_pairs={{0,256},{1,288},{2,320},{3,352},{4,384},{5,416},{6,192},{7,224},{8... | collective-permute-start | bytes 245768 | tf_op jit(solution)/shard_map/ppermute | solution.py:468
  10.0 3.0 %collective-permute-start.1 = (bf16[320,128]{1,0:T(8,128)(2,1)S(1)}, bf16[320,128]{1,0:T(8,128)(2,1)S(1)}, u32[]{:S(2)}, u32[]{:S(2)}) collective-permute-start(bf16[320,128]{1,0:T(8,128)(2,1)S(1)} %get-tuple-element.17), channel_id=1, source_target_pairs={{0,272},{1,304},{2,336},{3,368},{4,400},{5,432},{6,208},{7,240},{8... | collective-permute-start | bytes 245768 | tf_op jit(solution)/shard_map/ppermute | solution.py:469
  13.0 3.0 %cut_states.1 = (bf16[256,1024]{1,0:T(8,128)(2,1)S(1)}, bf16[256,1024]{1,0:T(8,128)(2,1)S(1)}, bf16[256,1024]{1,0:T(8,128)(2,1)S(1)}, bf16[256,2048]{1,0:T(8,128)(2,1)}) custom-call(s32[3]{0:T(128)S(1)} %pad_add_fusion.where_ref, bf16[256,8192]{1,0:T(8,128)(2,1)} %states_ref.1), custom_call_target="tpu_custom_call" | custom-call | tf_op jit(solution)/shard_map/cut_states/pallas_call | solution.py:155
  16.0 0.0 collective-permute-done.first
  16.0 5.2 %collective-permute-done.1.second.refs_1_ = bf16[320,128]{1,0:T(8,128)(2,1)S(1)} collective-permute-done((bf16[320,128]{1,0:T(8,128)(2,1)S(1)}, bf16[320,128]{1,0:T(8,128)(2,1)S(1)}, u32[]{:S(2)}, u32[]{:S(2)}) %collective-permute-start.1) | collective-permute-done | bytes 81952 | tf_op jit(solution)/shard_map/ppermute | solution.py:469
  21.2 1.7 %weight_copies.1.refs_2_ = bf16[8,2,320,128]{3,2,1,0:T(8,128)(2,1)} custom-call(s32[3]{0:T(128)S(1)} %pad_add_fusion.where_ref, bf16[320,128]{1,0:T(8,128)(2,1)S(1)} %collective-permute-done.first, bf16[320,128]{1,0:T(8,128)(2,1)S(1)} %collective-permute-done.1.second.refs_1_, bf16[256,1024]{1,0:T(8,128)(2,1)S(1)} %get-tuple-element.14.after.refs_0_), custom_call_target="tpu_custom_call" | custom-call | tf_op jit(solution)/shard_map/weight_copies/pallas_call | solution.py:210
  22.9 14.8 %all-to-all-start = ((bf16[8,2,320,128]{3,2,1,0:T(8,128)(2,1)}), bf16[8,2,320,128]{3,2,1,0:T(8,128)(2,1)}, u32[]{:S(2)}, u32[]{:S(2)}) async-start(bf16[8,2,320,128]{3,2,1,0:T(8,128)(2,1)} %weight_copies.1.refs_2_), calls=%async_computation | async-start | bytes 2621440 | tf_op jit(solution)/shard_map/all_to_all | solution.py:481
  37.7 0.0 copy-start.2
  37.7 2.3 %collective-permute-start.3 = (bf16[256,1024]{1,0:T(8,128)(2,1)S(1)}, bf16[256,1024]{1,0:T(8,128)(2,1)S(1)}, u32[]{:S(2)}, u32[]{:S(2)}) collective-permute-start(bf16[256,1024]{1,0:T(8,128)(2,1)S(1)} %gate.3), channel_id=1, source_target_pairs={{0,32},{1,41},{2,34},{3,43},{4,36},{5,45},{6,38},{7,47},{16,48},{1... | collective-permute-start | bytes 1572872 | tf_op jit(solution)/shard_map/ppermute | solution.py:477
  40.0 5.8 %collective-permute-start.2 = (bf16[256,1024]{1,0:T(8,128)(2,1)S(1)}, bf16[256,1024]{1,0:T(8,128)(2,1)S(1)}, u32[]{:S(2)}, u32[]{:S(2)}) collective-permute-start(bf16[256,1024]{1,0:T(8,128)(2,1)S(1)} %get-tuple-element.18), channel_id=1, source_target_pairs={{0,56},{1,57},{2,58},{3,59},{4,60},{5,61},{6,62},{7,63},{16,0},{17... | collective-permute-start | bytes 1572872 | tf_op jit(solution)/shard_map/ppermute | solution.py:476
  45.8 1.9 %collective-permute-start.4 = (bf16[256,1024]{1,0:T(8,128)(2,1)S(1)}, bf16[256,1024]{1,0:T(8,128)(2,1)S(1)}, u32[]{:S(2)}, u32[]{:S(2)}) collective-permute-start(bf16[256,1024]{1,0:T(8,128)(2,1)S(1)} %get-tuple-element.20), channel_id=1, source_target_pairs={{0,16},{1,17},{2,18},{3,19},{4,20},{5,21},{6,22},{7,23},{16,32},{1... | collective-permute-start | bytes 1572872 | tf_op jit(solution)/shard_map/ppermute | solution.py:478
  47.7 11.0 %collective-permute-done.3.n2 = bf16[256,1024]{1,0:T(8,128)(2,1)S(1)} collective-permute-done((bf16[256,1024]{1,0:T(8,128)(2,1)S(1)}, bf16[256,1024]{1,0:T(8,128)(2,1)S(1)}, u32[]{:S(2)}, u32[]{:S(2)}) %collective-permute-start.3) | collective-permute-done | bytes 524320 | tf_op jit(solution)/shard_map/ppermute | solution.py:477
  58.7 1.9 %collective-permute-start.6 = (bf16[256,1024]{1,0:T(8,128)(2,1)S(1)}, bf16[256,1024]{1,0:T(8,128)(2,1)S(1)}, u32[]{:S(2)}, u32[]{:S(2)}) collective-permute-start(bf16[256,1024]{1,0:T(8,128)(2,1)S(1)} %collective-permute-done.3.n2), channel_id=1, source_target_pairs={{0,1},{1,0},{2,3},{3,2},{4,5},{5,4},{6,7},{7,6},{8,9},{9,8},{10,11... | collective-permute-start | bytes 1572872 | tf_op jit(solution)/shard_map/ppermute | solution.py:59
  60.6 0.5 collective-permute-done.2.n1
  61.1 3.9 %collective-permute-start.5 = (bf16[256,1024]{1,0:T(8,128)(2,1)S(1)}, bf16[256,1024]{1,0:T(8,128)(2,1)S(1)}, u32[]{:S(2)}, u32[]{:S(2)}) collective-permute-start(bf16[256,1024]{1,0:T(8,128)(2,1)S(1)} %collective-permute-done.2.n1), channel_id=1, source_target_pairs={{0,1},{1,0},{2,3},{3,2},{4,5},{5,4},{6,7},{7,6},{8,9},{9,8},{10,11... | collective-permute-start | bytes 1572872 | tf_op jit(solution)/shard_map/ppermute | solution.py:59
  65.0 2.7 %collective-permute-done.4.n3 = bf16[256,1024]{1,0:T(8,128)(2,1)S(1)} collective-permute-done((bf16[256,1024]{1,0:T(8,128)(2,1)S(1)}, bf16[256,1024]{1,0:T(8,128)(2,1)S(1)}, u32[]{:S(2)}, u32[]{:S(2)}) %collective-permute-start.4) | collective-permute-done | bytes 524320 | tf_op jit(solution)/shard_map/ppermute | solution.py:478
  67.7 1.9 %collective-permute-start.7 = (bf16[256,1024]{1,0:T(8,128)(2,1)S(1)}, bf16[256,1024]{1,0:T(8,128)(2,1)S(1)}, u32[]{:S(2)}, u32[]{:S(2)}) collective-permute-start(bf16[256,1024]{1,0:T(8,128)(2,1)S(1)} %collective-permute-done.4.n3), channel_id=1, source_target_pairs={{0,1},{1,0},{2,3},{3,2},{4,5},{5,4},{6,7},{7,6},{8,9},{9,8},{10,11... | collective-permute-start | bytes 1572872 | tf_op jit(solution)/shard_map/ppermute | solution.py:59
  69.6 0.0 copy-done.2
  69.6 0.1 reduce_sum.22
  69.8 0.0 collective-permute-done.6.f2
  69.8 0.0 collective-permute-done.5.f1
  69.8 1.7 %collective-permute-done.7.f3 = bf16[256,1024]{1,0:T(8,128)(2,1)S(1)} collective-permute-done((bf16[256,1024]{1,0:T(8,128)(2,1)S(1)}, bf16[256,1024]{1,0:T(8,128)(2,1)S(1)}, u32[]{:S(2)}, u32[]{:S(2)}) %collective-permute-start.7) | collective-permute-done | bytes 524320 | tf_op jit(solution)/shard_map/ppermute | solution.py:59
  71.5 0.0 copy-start
  71.5 0.0 all-to-all-done.weights_ref
  71.5 5.5 %project.1 = bf16[4,320,256]{2,1,0:T(8,128)(2,1)} custom-call(s32[3]{0:T(128)S(1)} %pad_add_fusion.where_ref, bf16[256,2048]{1,0:T(8,128)(2,1)} %get-tuple-element.13.own_ref, bf16[256,1024]{1,0:T(8,128)(2,1)S(1)} %collective-permute-done.2.n1, bf16[256,1024]{1,0:T(8,128)(2,1)S(1)} %collective-permute-done.3.n2, ...), custom_call_target="tpu_custom_call" | custom-call | tf_op jit(solution)/shard_map/project/pallas_call | solution.py:294
  77.0 0.0 copy-done
  77.0 0.0 copy-start.3
  77.0 4.4 %all-to-all-start.1 = ((bf16[4,320,256]{2,1,0:T(8,128)(2,1)}), bf16[4,320,256]{2,1,0:T(8,128)(2,1)S(1)}, u32[]{:S(2)}, u32[]{:S(2)}) async-start(bf16[4,320,256]{2,1,0:T(8,128)(2,1)} %project.1), calls=%async_computation.1 | async-start | bytes 1310720 | tf_op jit(solution)/shard_map/all_to_all | solution.py:484
  81.4 0.1 add_convert_fusion
  81.4 0.1 convert_element_type.13
  81.5 0.3 multiply_cosine_fusion.1
  81.9 0.7 pad_maximum_fusion.1.turned_ref
  82.5 0.5 multiply_cosine_fusion
  83.1 0.8 pad_maximum_fusion.tables_ref
  83.8 15.1 %all-to-all-done.1.parts = bf16[4,320,256]{2,1,0:T(8,128)(2,1)S(1)} async-done(((bf16[4,320,256]{2,1,0:T(8,128)(2,1)}), bf16[4,320,256]{2,1,0:T(8,128)(2,1)S(1)}, u32[]{:S(2)}, u32[]{:S(2)}) %all-to-all-start.1) | async-done | bytes 655392 | tf_op jit(solution)/shard_map/all_to_all | solution.py:484
  98.9 5.4 %all-gather = bf16[256,256]{1,0:T(8,128)(2,1)S(1)} all-gather(bf16[64,256]{1,0:T(8,128)(2,1)S(1)} %slice_reduce_fusion), channel_id=2, replica_groups=mesh['zh'=4,'zb'=2,'yu'=2,'yb'=2,'yh'=2,'xh'=2,'xb'=2,'c'=2] {'xb','c'}, dimensions={0}, use_global_device_ids=true | all-gather | bytes 163840 | tf_op jit(solution)/shard_map/all_gather | solution.py:486
  104.3 0.0 copy-done.3
  104.3 0.0 copy-start.1
  104.3 3.5 %attend.1 = (bf16[256,256]{1,0:T(8,128)(2,1)}, bf16[256,256]{1,0:T(8,128)(2,1)S(1)}, bf16[256,2048]{1,0:T(8,128)(2,1)S(1)}) custom-call(s32[4,4]{1,0:T(4,128)S(1)} %copy-done.2, f32[4]{0:T(128)S(1)} %copy-done.3, bf16[4,320,256]{2,1,0:T(8,128)(2,1)S(1)} %all-to-all-done.1.parts, bf16[4,64,256]{2,1,0:T(8,128)(2,1)S(1)} %bitcast.8, ...), custom_call_target="tpu_custom_call" | custom-call | tf_op jit(solution)/shard_map/attend/pallas_call | solution.py:396
  107.8 16.1 %all-gather.1 = bf16[1024,256]{1,0:T(8,128)(2,1)S(1)} all-gather(bf16[256,256]{1,0:T(8,128)(2,1)S(1)} %get-tuple-element.23), channel_id=3, replica_groups=mesh['zh'=4,'zb'=2,'yu'=2,'yb'=2,'yh'=2,'xh'=2,'xb'=2,'c'=2] {'yu','yb'}, dimensions={0}, use_global_device_ids=true | all-gather | bytes 655360 | tf_op jit(solution)/shard_map/all_gather | solution.py:501
  124.0 0.0 copy-done.1
  124.0 1.8 %gradient.1 = bf16[8,256,256]{2,1,0:T(8,128)(2,1)S(1)} custom-call(s32[3]{0:T(128)S(1)} %pad_add_fusion.where_ref, bf16[256,2048]{1,0:T(8,128)(2,1)S(1)} %get-tuple-element.22.own, bf16[256,1024]{1,0:T(8,128)(2,1)S(1)} %collective-permute-done.2.n1, bf16[256,1024]{1,0:T(8,128)(2,1)S(1)} %collective-permute-done.3.n2, ...), custom_call_target="tpu_custom_call" | custom-call | tf_op jit(solution)/shard_map/gradient/pallas_call | solution.py:437
  125.8 32.8 %all_to_all.15.terms = bf16[8,256,256]{2,1,0:T(8,128)(2,1)S(1)} all-to-all(bf16[8,256,256]{2,1,0:T(8,128)(2,1)S(1)} %gradient.1), channel_id=1, replica_groups=mesh['zh'=4,'zb'=2,'yu'=2,'yb'=2,'yh'=2,'xh'=2,'xb'=2,'c'=2] {'zh','zb'}, dimensions={0} | all-to-all | bytes 2097152 | tf_op jit(solution)/shard_map/all_to_all | solution.py:503
  158.6 0.9 add_up.1
  (5 shorter events, 0.0 us)
Async XLA Ops:
  2.2 13.8 %collective-permute-start = (bf16[320,128]{1,0:T(8,128)(2,1)S(1)}, bf16[320,128]{1,0:T(8,128)(2,1)S(1)}, u32[]{:S(2)}, u32[]{:S(2)}) collective-permute-start(bf16[320,128]{1,0:T(8,128)(2,1)S(1)} %get-tuple-element.16), channel_id=1, source_target_pairs={{0,256},{1,288},{2,320},{3,352},{4,384},{5,416},{6,192},{7,224},{8... | collective-permute-start | bytes 245768 | tf_op jit(solution)/shard_map/ppermute | solution.py:468
  10.0 11.1 %collective-permute-start.1 = (bf16[320,128]{1,0:T(8,128)(2,1)S(1)}, bf16[320,128]{1,0:T(8,128)(2,1)S(1)}, u32[]{:S(2)}, u32[]{:S(2)}) collective-permute-start(bf16[320,128]{1,0:T(8,128)(2,1)S(1)} %get-tuple-element.17), channel_id=1, source_target_pairs={{0,272},{1,304},{2,336},{3,368},{4,400},{5,432},{6,208},{7,240},{8... | collective-permute-start | bytes 245768 | tf_op jit(solution)/shard_map/ppermute | solution.py:469
  22.9 48.6 %all-to-all-start = ((bf16[8,2,320,128]{3,2,1,0:T(8,128)(2,1)}), bf16[8,2,320,128]{3,2,1,0:T(8,128)(2,1)}, u32[]{:S(2)}, u32[]{:S(2)}) async-start(bf16[8,2,320,128]{3,2,1,0:T(8,128)(2,1)} %weight_copies.1.refs_2_), calls=%async_computation | async-start | bytes 2621440 | tf_op jit(solution)/shard_map/all_to_all | solution.py:481
  37.7 32.0 %copy-start.2 = (s32[4,4]{1,0:T(4,128)S(1)}, s32[4,4]{1,0:T(4,128)}, u32[]{:S(2)}) copy-start(s32[4,4]{1,0:T(4,128)} %mask_ref.1) | copy-start | bytes 196
  37.7 21.0 %collective-permute-start.3 = (bf16[256,1024]{1,0:T(8,128)(2,1)S(1)}, bf16[256,1024]{1,0:T(8,128)(2,1)S(1)}, u32[]{:S(2)}, u32[]{:S(2)}) collective-permute-start(bf16[256,1024]{1,0:T(8,128)(2,1)S(1)} %gate.3), channel_id=1, source_target_pairs={{0,32},{1,41},{2,34},{3,43},{4,36},{5,45},{6,38},{7,47},{16,48},{1... | collective-permute-start | bytes 1572872 | tf_op jit(solution)/shard_map/ppermute | solution.py:477
  40.0 21.1 %collective-permute-start.2 = (bf16[256,1024]{1,0:T(8,128)(2,1)S(1)}, bf16[256,1024]{1,0:T(8,128)(2,1)S(1)}, u32[]{:S(2)}, u32[]{:S(2)}) collective-permute-start(bf16[256,1024]{1,0:T(8,128)(2,1)S(1)} %get-tuple-element.18), channel_id=1, source_target_pairs={{0,56},{1,57},{2,58},{3,59},{4,60},{5,61},{6,62},{7,63},{16,0},{17... | collective-permute-start | bytes 1572872 | tf_op jit(solution)/shard_map/ppermute | solution.py:476
  45.8 21.9 %collective-permute-start.4 = (bf16[256,1024]{1,0:T(8,128)(2,1)S(1)}, bf16[256,1024]{1,0:T(8,128)(2,1)S(1)}, u32[]{:S(2)}, u32[]{:S(2)}) collective-permute-start(bf16[256,1024]{1,0:T(8,128)(2,1)S(1)} %get-tuple-element.20), channel_id=1, source_target_pairs={{0,16},{1,17},{2,18},{3,19},{4,20},{5,21},{6,22},{7,23},{16,32},{1... | collective-permute-start | bytes 1572872 | tf_op jit(solution)/shard_map/ppermute | solution.py:478
  58.7 11.1 %collective-permute-start.6 = (bf16[256,1024]{1,0:T(8,128)(2,1)S(1)}, bf16[256,1024]{1,0:T(8,128)(2,1)S(1)}, u32[]{:S(2)}, u32[]{:S(2)}) collective-permute-start(bf16[256,1024]{1,0:T(8,128)(2,1)S(1)} %collective-permute-done.3.n2), channel_id=1, source_target_pairs={{0,1},{1,0},{2,3},{3,2},{4,5},{5,4},{6,7},{7,6},{8,9},{9,8},{10,11... | collective-permute-start | bytes 1572872 | tf_op jit(solution)/shard_map/ppermute | solution.py:59
  61.1 8.7 %collective-permute-start.5 = (bf16[256,1024]{1,0:T(8,128)(2,1)S(1)}, bf16[256,1024]{1,0:T(8,128)(2,1)S(1)}, u32[]{:S(2)}, u32[]{:S(2)}) collective-permute-start(bf16[256,1024]{1,0:T(8,128)(2,1)S(1)} %collective-permute-done.2.n1), channel_id=1, source_target_pairs={{0,1},{1,0},{2,3},{3,2},{4,5},{5,4},{6,7},{7,6},{8,9},{9,8},{10,11... | collective-permute-start | bytes 1572872 | tf_op jit(solution)/shard_map/ppermute | solution.py:59
  67.7 3.8 %collective-permute-start.7 = (bf16[256,1024]{1,0:T(8,128)(2,1)S(1)}, bf16[256,1024]{1,0:T(8,128)(2,1)S(1)}, u32[]{:S(2)}, u32[]{:S(2)}) collective-permute-start(bf16[256,1024]{1,0:T(8,128)(2,1)S(1)} %collective-permute-done.4.n3), channel_id=1, source_target_pairs={{0,1},{1,0},{2,3},{3,2},{4,5},{5,4},{6,7},{7,6},{8,9},{9,8},{10,11... | collective-permute-start | bytes 1572872 | tf_op jit(solution)/shard_map/ppermute | solution.py:59
  71.5 5.5 %copy-start = (bf16[256,1024]{1,0:T(8,128)(2,1)}, bf16[256,1024]{1,0:T(8,128)(2,1)S(1)}, u32[]{:S(2)}) copy-start(bf16[256,1024]{1,0:T(8,128)(2,1)S(1)} %collective-permute-done.7.f3) | copy-start | bytes 1572868
  77.0 27.3 %copy-start.3 = (f32[4]{0:T(128)S(1)}, f32[4]{0:T(128)}, u32[]{:S(2)}) copy-start(f32[4]{0:T(128)} %risk_ref.1) | copy-start | bytes 52
  77.0 21.9 %all-to-all-start.1 = ((bf16[4,320,256]{2,1,0:T(8,128)(2,1)}), bf16[4,320,256]{2,1,0:T(8,128)(2,1)S(1)}, u32[]{:S(2)}, u32[]{:S(2)}) async-start(bf16[4,320,256]{2,1,0:T(8,128)(2,1)} %project.1), calls=%async_computation.1 | async-start | bytes 1310720 | tf_op jit(solution)/shard_map/all_to_all | solution.py:484
  104.3 19.6 %copy-start.1 = (bf16[256,1024]{1,0:T(8,128)(2,1)S(1)}, bf16[256,1024]{1,0:T(8,128)(2,1)}, u32[]{:S(2)}) copy-start(bf16[256,1024]{1,0:T(8,128)(2,1)} %copy-done) | copy-start | bytes 1572868

commit v16 on v15

--- a/solution.py
+++ b/solution.py
@@ -167,17 +167,18 @@
     del refs
 
 
-def gate(parts, after):
+def gate(parts, *after, cost=0):
     count = len(parts)
     return pl.pallas_call(
         gate_kernel,
         out_shape=tuple(jax.ShapeDtypeStruct(x.shape, x.dtype) for x in parts),
-        in_specs=[anywhere()] * (count + 1),
+        in_specs=[anywhere()] * (count + len(after)),
         out_specs=tuple([anywhere()] * count),
         input_output_aliases={i: i for i in range(count)},
+        cost_estimate=pl.CostEstimate(flops=cost, bytes_accessed=0, transcendentals=0),
         compiler_params=params(),
         name="gate",
-    )(*parts, after)
+    )(*parts, *after)
 
 
 def own_columns(where_ref, states_ref, own, sems):
@@ -470,7 +471,7 @@
     *outgoing, own = cut(where, states)
     weights = copies(where, first, second, outgoing[0])
 
-    (two,) = gate(outgoing[1:2], second)
+    (two,) = gate(outgoing[1:2], first, second)
     up, down = gate((outgoing[0], outgoing[2]), held(weights))
     near = (
         lax.ppermute(down, AXES, ring_pairs(-1, -1)),
@@ -478,6 +479,8 @@
         lax.ppermute(up, AXES, ring_pairs(1, 1)),
     )
     far = [swap_core(x) for x in near]
+    n2, f2 = gate((near[1], far[1]), where, cost=16 * 10**9)
+    near, far = (near[0], n2, near[2]), (far[0], f2, far[2])
     weights = lax.all_to_all(weights, OTHERS, split_axis=0, concat_axis=0)
 
     parts = project(where, own, near, far, weights)

time: 160 us -> 159 us (level)
  blocking collectives: 54.4 us -> 50.5 us
  waiting for transfers between devices: 36.2 us -> 38.9 us
  starting transfers between devices: 47.6 us -> 45.9 us
    all_to_all x1, waiting for transfers between devices: 0.01 us -> 11.3 us  [shards(): weights = lax.all_to_all(weights, OTHERS, split_axis=0, concat_axis=0)]
    ppermute x1, waiting for transfers between devices: 11 us -> 0.01 us  [shards(): lax.ppermute(two, AXES, ring_pairs(2, -2))]
    ppermute x1, waiting for transfers between devices: 0.47 us -> 4.45 us  [shards(): lax.ppermute(down, AXES, ring_pairs(-1, -1))]
    all_to_all x1, blocking collectives: 32.8 us -> 28.9 us  [shards(): terms = lax.all_to_all(terms, OTHERS, split_axis=0, concat_axis=0)]
    ppermute x3, starting transfers between devices: 7.72 us -> 5.74 us  [swap_core(): return lax.ppermute(value, 'c', [(0, 1), (1, 0)])]
  transfers between devices with their start and end apart: 10 -> 10, of which waited for: 6 -> 6; matrix products, arithmetic and copies ran while one was open for 2% -> 2% of each run, Pallas kernels for 2% -> 3%
where the time goes in v16:
time: 159 us; the launch traced here: 158 us
  blocking collectives  50.5 us (32%)
  starting transfers between devices  45.9 us (29%)
  waiting for transfers between devices  38.9 us (24%)
  Pallas kernels  18.7 us (12%)
  other arithmetic  2.57 us (2%)
    all_to_all x1, blocking collectives, shards(): terms = lax.all_to_all(terms, OTHERS, split_axis=0, concat_axis=0)  28.9 us
    all_gather x1, blocking collectives, shards(): slopes = lax.all_gather(dq, GROUP, axis=0, tiled=False)  16.1 us
    all_to_all x1, waiting for transfers between devices, shards(): parts = lax.all_to_all(parts, GROUP, split_axis=0, concat_axis=0)  15 us
    all_to_all x1, starting transfers between devices, shards(): weights = lax.all_to_all(weights, OTHERS, split_axis=0, concat_axis=0)  13.4 us
    all_to_all x1, waiting for transfers between devices, shards(): weights = lax.all_to_all(weights, OTHERS, split_axis=0, concat_axis=0)  11.3 us
    ppermute x1, starting transfers between devices, shards(): first = lax.ppermute(first, AXES, home_pairs(0))  7.81 us
    ppermute x1, starting transfers between devices, shards(): lax.ppermute(down, AXES, ring_pairs(-1, -1))  5.77 us
    ppermute x3, starting transfers between devices, swap_core(): return lax.ppermute(value, 'c', [(0, 1), (1, 0)])  5.74 us
  transfers between devices with their start and end apart: 10, of which 6 were waited for; matrix products, arithmetic and copies ran while one was open for 2% of the time, Pallas kernels for 3%

profile of v16, /device:TPU:6, one launch (start us, length us, event | category | flops | bytes accessed | tf_op | source)
XLA Modules:
  0.0 157.5 jit_solution(4768716893865794595)
XLA Ops:
  0.6 0.1 pad_add_fusion.where_ref.refs_2_
  0.7 1.5 pack_weights.1
  2.2 7.8 %collective-permute-start = (bf16[320,128]{1,0:T(8,128)(2,1)S(1)}, bf16[320,128]{1,0:T(8,128)(2,1)S(1)}, u32[]{:S(2)}, u32[]{:S(2)}) collective-permute-start(bf16[320,128]{1,0:T(8,128)(2,1)S(1)} %get-tuple-element.18), channel_id=1, source_target_pairs={{0,256},{1,288},{2,320},{3,352},{4,384},{5,416},{6,192},{7,224},{8... | collective-permute-start | bytes 245768 | tf_op jit(solution)/shard_map/ppermute | solution.py:469
  10.0 3.0 %collective-permute-start.1 = (bf16[320,128]{1,0:T(8,128)(2,1)S(1)}, bf16[320,128]{1,0:T(8,128)(2,1)S(1)}, u32[]{:S(2)}, u32[]{:S(2)}) collective-permute-start(bf16[320,128]{1,0:T(8,128)(2,1)S(1)} %get-tuple-element.19), channel_id=1, source_target_pairs={{0,272},{1,304},{2,336},{3,368},{4,400},{5,432},{6,208},{7,240},{8... | collective-permute-start | bytes 245768 | tf_op jit(solution)/shard_map/ppermute | solution.py:470
  13.0 3.8 %cut_states.1 = (bf16[256,1024]{1,0:T(8,128)(2,1)S(1)}, bf16[256,1024]{1,0:T(8,128)(2,1)S(1)}, bf16[256,1024]{1,0:T(8,128)(2,1)}, bf16[256,2048]{1,0:T(8,128)(2,1)}) custom-call(s32[3]{0:T(128)S(1)} %pad_add_fusion.where_ref.refs_2_, bf16[256,8192]{1,0:T(8,128)(2,1)} %states_ref.1), custom_call_target="tpu_custom_call" | custom-call | tf_op jit(solution)/shard_map/cut_states/pallas_call | solution.py:155
  16.8 0.0 collective-permute-done.first.refs_1_
  16.8 4.4 %collective-permute-done.1.second.refs_2_ = bf16[320,128]{1,0:T(8,128)(2,1)S(1)} collective-permute-done((bf16[320,128]{1,0:T(8,128)(2,1)S(1)}, bf16[320,128]{1,0:T(8,128)(2,1)S(1)}, u32[]{:S(2)}, u32[]{:S(2)}) %collective-permute-start.1) | collective-permute-done | bytes 81952 | tf_op jit(solution)/shard_map/ppermute | solution.py:470
  21.2 3.7 %collective-permute-start.3 = (bf16[256,1024]{1,0:T(8,128)(2,1)S(1)}, bf16[256,1024]{1,0:T(8,128)(2,1)S(1)}, u32[]{:S(2)}, u32[]{:S(2)}) collective-permute-start(bf16[256,1024]{1,0:T(8,128)(2,1)S(1)} %gate.4), channel_id=1, source_target_pairs={{0,32},{1,41},{2,34},{3,43},{4,36},{5,45},{6,38},{7,47},{16,48},{1... | collective-permute-start | bytes 1572872 | tf_op jit(solution)/shard_map/ppermute | solution.py:478
  24.8 1.7 %weight_copies.1.refs_2_ = bf16[8,2,320,128]{3,2,1,0:T(8,128)(2,1)} custom-call(s32[3]{0:T(128)S(1)} %pad_add_fusion.where_ref.refs_2_, bf16[320,128]{1,0:T(8,128)(2,1)S(1)} %collective-permute-done.first.refs_1_, bf16[320,128]{1,0:T(8,128)(2,1)S(1)} %collective-permute-done.1.second.refs_2_, bf16[256,1024]{1,0:T(8,128)(2,1)S(1)} %get-tuple-element.16.after.refs_0_), custom_call_target="tpu_custom_call" | custom-call | tf_op jit(solution)/shard_map/weight_copies/pallas_call | solution.py:211
  26.6 13.4 %all-to-all-start = ((bf16[8,2,320,128]{3,2,1,0:T(8,128)(2,1)}), bf16[8,2,320,128]{3,2,1,0:T(8,128)(2,1)}, u32[]{:S(2)}, u32[]{:S(2)}) async-start(bf16[8,2,320,128]{3,2,1,0:T(8,128)(2,1)} %weight_copies.1.refs_2_), calls=%async_computation | async-start | bytes 2621440 | tf_op jit(solution)/shard_map/all_to_all | solution.py:484
  40.0 0.0 copy-start.2
  40.0 5.8 %collective-permute-start.2 = (bf16[256,1024]{1,0:T(8,128)(2,1)}, bf16[256,1024]{1,0:T(8,128)(2,1)S(1)}, u32[]{:S(2)}, u32[]{:S(2)}) collective-permute-start(bf16[256,1024]{1,0:T(8,128)(2,1)} %get-tuple-element.20), channel_id=1, source_target_pairs={{0,56},{1,57},{2,58},{3,59},{4,60},{5,61},{6,62},{7,63},{16,0},{17... | collective-permute-start | bytes 1572872 | tf_op jit(solution)/shard_map/ppermute | solution.py:477
  45.7 1.9 %collective-permute-start.5 = (bf16[256,1024]{1,0:T(8,128)(2,1)S(1)}, bf16[256,1024]{1,0:T(8,128)(2,1)S(1)}, u32[]{:S(2)}, u32[]{:S(2)}) collective-permute-start(bf16[256,1024]{1,0:T(8,128)(2,1)S(1)} %get-tuple-element.23), channel_id=1, source_target_pairs={{0,16},{1,17},{2,18},{3,19},{4,20},{5,21},{6,22},{7,23},{16,32},{1... | collective-permute-start | bytes 1572872 | tf_op jit(solution)/shard_map/ppermute | solution.py:479
  47.7 0.0 collective-permute-done.3.refs_0_
  47.7 1.9 %collective-permute-start.4 = (bf16[256,1024]{1,0:T(8,128)(2,1)S(1)}, bf16[256,1024]{1,0:T(8,128)(2,1)S(1)}, u32[]{:S(2)}, u32[]{:S(2)}) collective-permute-start(bf16[256,1024]{1,0:T(8,128)(2,1)S(1)} %collective-permute-done.3.refs_0_), channel_id=1, source_target_pairs={{0,1},{1,0},{2,3},{3,2},{4,5},{5,4},{6,7},{7,6},{8,9},{9,8},{10,11... | collective-permute-start | bytes 1572872 | tf_op jit(solution)/shard_map/ppermute | solution.py:59
  49.6 0.0 copy-done.2
  49.6 0.1 reduce_sum.22
  49.8 4.4 %collective-permute-done.2.n1 = bf16[256,1024]{1,0:T(8,128)(2,1)S(1)} collective-permute-done((bf16[256,1024]{1,0:T(8,128)(2,1)}, bf16[256,1024]{1,0:T(8,128)(2,1)S(1)}, u32[]{:S(2)}, u32[]{:S(2)}) %collective-permute-start.2) | collective-permute-done | bytes 524320 | tf_op jit(solution)/shard_map/ppermute | solution.py:477
  54.2 1.9 %collective-permute-start.6 = (bf16[256,1024]{1,0:T(8,128)(2,1)S(1)}, bf16[256,1024]{1,0:T(8,128)(2,1)S(1)}, u32[]{:S(2)}, u32[]{:S(2)}) collective-permute-start(bf16[256,1024]{1,0:T(8,128)(2,1)S(1)} %collective-permute-done.2.n1), channel_id=1, source_target_pairs={{0,1},{1,0},{2,3},{3,2},{4,5},{5,4},{6,7},{7,6},{8,9},{9,8},{10,11... | collective-permute-start | bytes 1572872 | tf_op jit(solution)/shard_map/ppermute | solution.py:59
  56.1 1.9 %collective-permute-done.5.n3 = bf16[256,1024]{1,0:T(8,128)(2,1)S(1)} collective-permute-done((bf16[256,1024]{1,0:T(8,128)(2,1)S(1)}, bf16[256,1024]{1,0:T(8,128)(2,1)S(1)}, u32[]{:S(2)}, u32[]{:S(2)}) %collective-permute-start.5) | collective-permute-done | bytes 524320 | tf_op jit(solution)/shard_map/ppermute | solution.py:479
  58.0 1.9 %collective-permute-start.7 = (bf16[256,1024]{1,0:T(8,128)(2,1)S(1)}, bf16[256,1024]{1,0:T(8,128)(2,1)S(1)}, u32[]{:S(2)}, u32[]{:S(2)}) collective-permute-start(bf16[256,1024]{1,0:T(8,128)(2,1)S(1)} %collective-permute-done.5.n3), channel_id=1, source_target_pairs={{0,1},{1,0},{2,3},{3,2},{4,5},{5,4},{6,7},{7,6},{8,9},{9,8},{10,11... | collective-permute-start | bytes 1572872 | tf_op jit(solution)/shard_map/ppermute | solution.py:59
  60.0 0.0 collective-permute-done.4.refs_1_
  60.0 0.0 copy-start
  60.0 0.0 collective-permute-done.6.f1
  60.0 1.8 %collective-permute-done.7.f3 = bf16[256,1024]{1,0:T(8,128)(2,1)S(1)} collective-permute-done((bf16[256,1024]{1,0:T(8,128)(2,1)S(1)}, bf16[256,1024]{1,0:T(8,128)(2,1)S(1)}, u32[]{:S(2)}, u32[]{:S(2)}) %collective-permute-start.7) | collective-permute-done | bytes 524320 | tf_op jit(solution)/shard_map/ppermute | solution.py:59
  61.8 11.3 %all-to-all-done.weights_ref = bf16[8,2,320,128]{3,2,1,0:T(8,128)(2,1)} async-done(((bf16[8,2,320,128]{3,2,1,0:T(8,128)(2,1)}), bf16[8,2,320,128]{3,2,1,0:T(8,128)(2,1)}, u32[]{:S(2)}, u32[]{:S(2)}) %all-to-all-start) | async-done | bytes 1310752 | tf_op jit(solution)/shard_map/all_to_all | solution.py:484
  73.1 5.5 %project.1 = bf16[4,320,256]{2,1,0:T(8,128)(2,1)} custom-call(s32[3]{0:T(128)S(1)} %pad_add_fusion.where_ref.refs_2_, bf16[256,2048]{1,0:T(8,128)(2,1)} %get-tuple-element.15.own_ref, bf16[256,1024]{1,0:T(8,128)(2,1)S(1)} %collective-permute-done.2.n1, bf16[256,1024]{1,0:T(8,128)(2,1)S(1)} %get-tuple-element.22.n2, ...), custom_call_target="tpu_custom_call" | custom-call | tf_op jit(solution)/shard_map/project/pallas_call | solution.py:295
  78.6 0.0 copy-done
  78.6 0.0 copy-start.3
  78.6 4.6 %all-to-all-start.1 = ((bf16[4,320,256]{2,1,0:T(8,128)(2,1)}), bf16[4,320,256]{2,1,0:T(8,128)(2,1)S(1)}, u32[]{:S(2)}, u32[]{:S(2)}) async-start(bf16[4,320,256]{2,1,0:T(8,128)(2,1)} %project.1), calls=%async_computation.1 | async-start | bytes 1310720 | tf_op jit(solution)/shard_map/all_to_all | solution.py:487
  83.3 0.1 add_convert_fusion
  83.3 0.1 convert_element_type.13
  83.4 0.3 multiply_cosine_fusion.1
  83.8 0.7 pad_maximum_fusion.1.turned_ref
  84.4 0.5 multiply_cosine_fusion
  85.0 0.8 pad_maximum_fusion.tables_ref
  85.7 15.0 %all-to-all-done.1.parts = bf16[4,320,256]{2,1,0:T(8,128)(2,1)S(1)} async-done(((bf16[4,320,256]{2,1,0:T(8,128)(2,1)}), bf16[4,320,256]{2,1,0:T(8,128)(2,1)S(1)}, u32[]{:S(2)}, u32[]{:S(2)}) %all-to-all-start.1) | async-done | bytes 655392 | tf_op jit(solution)/shard_map/all_to_all | solution.py:487
  100.8 5.4 %all-gather = bf16[256,256]{1,0:T(8,128)(2,1)S(1)} all-gather(bf16[64,256]{1,0:T(8,128)(2,1)S(1)} %slice_reduce_fusion), channel_id=2, replica_groups=mesh['zh'=4,'zb'=2,'yu'=2,'yb'=2,'yh'=2,'xh'=2,'xb'=2,'c'=2] {'xb','c'}, dimensions={0}, use_global_device_ids=true | all-gather | bytes 163840 | tf_op jit(solution)/shard_map/all_gather | solution.py:489
  106.2 0.0 copy-done.3
  106.2 0.0 copy-start.1
  106.2 3.5 %attend.1 = (bf16[256,256]{1,0:T(8,128)(2,1)}, bf16[256,256]{1,0:T(8,128)(2,1)S(1)}, bf16[256,2048]{1,0:T(8,128)(2,1)S(1)}) custom-call(s32[4,4]{1,0:T(4,128)S(1)} %copy-done.2, f32[4]{0:T(128)S(1)} %copy-done.3, bf16[4,320,256]{2,1,0:T(8,128)(2,1)S(1)} %all-to-all-done.1.parts, bf16[4,64,256]{2,1,0:T(8,128)(2,1)S(1)} %bitcast.8, ...), custom_call_target="tpu_custom_call" | custom-call | tf_op jit(solution)/shard_map/attend/pallas_call | solution.py:397
  109.7 16.1 %all-gather.1 = bf16[1024,256]{1,0:T(8,128)(2,1)S(1)} all-gather(bf16[256,256]{1,0:T(8,128)(2,1)S(1)} %get-tuple-element.27), channel_id=3, replica_groups=mesh['zh'=4,'zb'=2,'yu'=2,'yb'=2,'yh'=2,'xh'=2,'xb'=2,'c'=2] {'yu','yb'}, dimensions={0}, use_global_device_ids=true | all-gather | bytes 655360 | tf_op jit(solution)/shard_map/all_gather | solution.py:504
  125.8 0.0 copy-done.1
  125.8 1.8 %gradient.1 = bf16[8,256,256]{2,1,0:T(8,128)(2,1)S(1)} custom-call(s32[3]{0:T(128)S(1)} %pad_add_fusion.where_ref.refs_2_, bf16[256,2048]{1,0:T(8,128)(2,1)S(1)} %get-tuple-element.26.own, bf16[256,1024]{1,0:T(8,128)(2,1)S(1)} %collective-permute-done.2.n1, bf16[256,1024]{1,0:T(8,128)(2,1)S(1)} %get-tuple-element.22.n2, ...), custom_call_target="tpu_custom_call" | custom-call | tf_op jit(solution)/shard_map/gradient/pallas_call | solution.py:438
  127.7 28.9 %all_to_all.15.terms = bf16[8,256,256]{2,1,0:T(8,128)(2,1)S(1)} all-to-all(bf16[8,256,256]{2,1,0:T(8,128)(2,1)S(1)} %gradient.1), channel_id=1, replica_groups=mesh['zh'=4,'zb'=2,'yu'=2,'yb'=2,'yh'=2,'xh'=2,'xb'=2,'c'=2] {'zh','zb'}, dimensions={0} | all-to-all | bytes 2097152 | tf_op jit(solution)/shard_map/all_to_all | solution.py:506
  156.6 0.9 add_up.1
  (6 shorter events, 0.0 us)
Async XLA Ops:
  2.2 14.6 %collective-permute-start = (bf16[320,128]{1,0:T(8,128)(2,1)S(1)}, bf16[320,128]{1,0:T(8,128)(2,1)S(1)}, u32[]{:S(2)}, u32[]{:S(2)}) collective-permute-start(bf16[320,128]{1,0:T(8,128)(2,1)S(1)} %get-tuple-element.18), channel_id=1, source_target_pairs={{0,256},{1,288},{2,320},{3,352},{4,384},{5,416},{6,192},{7,224},{8... | collective-permute-start | bytes 245768 | tf_op jit(solution)/shard_map/ppermute | solution.py:469
  10.0 11.1 %collective-permute-start.1 = (bf16[320,128]{1,0:T(8,128)(2,1)S(1)}, bf16[320,128]{1,0:T(8,128)(2,1)S(1)}, u32[]{:S(2)}, u32[]{:S(2)}) collective-permute-start(bf16[320,128]{1,0:T(8,128)(2,1)S(1)} %get-tuple-element.19), channel_id=1, source_target_pairs={{0,272},{1,304},{2,336},{3,368},{4,400},{5,432},{6,208},{7,240},{8... | collective-permute-start | bytes 245768 | tf_op jit(solution)/shard_map/ppermute | solution.py:470
  21.2 26.5 %collective-permute-start.3 = (bf16[256,1024]{1,0:T(8,128)(2,1)S(1)}, bf16[256,1024]{1,0:T(8,128)(2,1)S(1)}, u32[]{:S(2)}, u32[]{:S(2)}) collective-permute-start(bf16[256,1024]{1,0:T(8,128)(2,1)S(1)} %gate.4), channel_id=1, source_target_pairs={{0,32},{1,41},{2,34},{3,43},{4,36},{5,45},{6,38},{7,47},{16,48},{1... | collective-permute-start | bytes 1572872 | tf_op jit(solution)/shard_map/ppermute | solution.py:478
  26.6 46.6 %all-to-all-start = ((bf16[8,2,320,128]{3,2,1,0:T(8,128)(2,1)}), bf16[8,2,320,128]{3,2,1,0:T(8,128)(2,1)}, u32[]{:S(2)}, u32[]{:S(2)}) async-start(bf16[8,2,320,128]{3,2,1,0:T(8,128)(2,1)} %weight_copies.1.refs_2_), calls=%async_computation | async-start | bytes 2621440 | tf_op jit(solution)/shard_map/all_to_all | solution.py:484
  40.0 9.7 %copy-start.2 = (s32[4,4]{1,0:T(4,128)S(1)}, s32[4,4]{1,0:T(4,128)}, u32[]{:S(2)}) copy-start(s32[4,4]{1,0:T(4,128)} %mask_ref.1) | copy-start | bytes 196
  40.0 14.2 %collective-permute-start.2 = (bf16[256,1024]{1,0:T(8,128)(2,1)}, bf16[256,1024]{1,0:T(8,128)(2,1)S(1)}, u32[]{:S(2)}, u32[]{:S(2)}) collective-permute-start(bf16[256,1024]{1,0:T(8,128)(2,1)} %get-tuple-element.20), channel_id=1, source_target_pairs={{0,56},{1,57},{2,58},{3,59},{4,60},{5,61},{6,62},{7,63},{16,0},{17... | collective-permute-start | bytes 1572872 | tf_op jit(solution)/shard_map/ppermute | solution.py:477
  45.7 12.3 %collective-permute-start.5 = (bf16[256,1024]{1,0:T(8,128)(2,1)S(1)}, bf16[256,1024]{1,0:T(8,128)(2,1)S(1)}, u32[]{:S(2)}, u32[]{:S(2)}) collective-permute-start(bf16[256,1024]{1,0:T(8,128)(2,1)S(1)} %get-tuple-element.23), channel_id=1, source_target_pairs={{0,16},{1,17},{2,18},{3,19},{4,20},{5,21},{6,22},{7,23},{16,32},{1... | collective-permute-start | bytes 1572872 | tf_op jit(solution)/shard_map/ppermute | solution.py:479
  47.7 12.3 %collective-permute-start.4 = (bf16[256,1024]{1,0:T(8,128)(2,1)S(1)}, bf16[256,1024]{1,0:T(8,128)(2,1)S(1)}, u32[]{:S(2)}, u32[]{:S(2)}) collective-permute-start(bf16[256,1024]{1,0:T(8,128)(2,1)S(1)} %collective-permute-done.3.refs_0_), channel_id=1, source_target_pairs={{0,1},{1,0},{2,3},{3,2},{4,5},{5,4},{6,7},{7,6},{8,9},{9,8},{10,11... | collective-permute-start | bytes 1572872 | tf_op jit(solution)/shard_map/ppermute | solution.py:59
  54.2 5.8 %collective-permute-start.6 = (bf16[256,1024]{1,0:T(8,128)(2,1)S(1)}, bf16[256,1024]{1,0:T(8,128)(2,1)S(1)}, u32[]{:S(2)}, u32[]{:S(2)}) collective-permute-start(bf16[256,1024]{1,0:T(8,128)(2,1)S(1)} %collective-permute-done.2.n1), channel_id=1, source_target_pairs={{0,1},{1,0},{2,3},{3,2},{4,5},{5,4},{6,7},{7,6},{8,9},{9,8},{10,11... | collective-permute-start | bytes 1572872 | tf_op jit(solution)/shard_map/ppermute | solution.py:59
  58.0 3.8 %collective-permute-start.7 = (bf16[256,1024]{1,0:T(8,128)(2,1)S(1)}, bf16[256,1024]{1,0:T(8,128)(2,1)S(1)}, u32[]{:S(2)}, u32[]{:S(2)}) collective-permute-start(bf16[256,1024]{1,0:T(8,128)(2,1)S(1)} %collective-permute-done.5.n3), channel_id=1, source_target_pairs={{0,1},{1,0},{2,3},{3,2},{4,5},{5,4},{6,7},{7,6},{8,9},{9,8},{10,11... | collective-permute-start | bytes 1572872 | tf_op jit(solution)/shard_map/ppermute | solution.py:59
  60.0 18.6 %copy-start = (bf16[256,1024]{1,0:T(8,128)(2,1)}, bf16[256,1024]{1,0:T(8,128)(2,1)S(1)}, u32[]{:S(2)}) copy-start(bf16[256,1024]{1,0:T(8,128)(2,1)S(1)} %get-tuple-element.24.f2) | copy-start | bytes 1572868
  78.6 27.6 %copy-start.3 = (f32[4]{0:T(128)S(1)}, f32[4]{0:T(128)}, u32[]{:S(2)}) copy-start(f32[4]{0:T(128)} %risk_ref.1) | copy-start | bytes 52
  78.6 22.1 %all-to-all-start.1 = ((bf16[4,320,256]{2,1,0:T(8,128)(2,1)}), bf16[4,320,256]{2,1,0:T(8,128)(2,1)S(1)}, u32[]{:S(2)}, u32[]{:S(2)}) async-start(bf16[4,320,256]{2,1,0:T(8,128)(2,1)} %project.1), calls=%async_computation.1 | async-start | bytes 1310720 | tf_op jit(solution)/shard_map/all_to_all | solution.py:487
  106.2 19.6 %copy-start.1 = (bf16[256,1024]{1,0:T(8,128)(2,1)S(1)}, bf16[256,1024]{1,0:T(8,128)(2,1)}, u32[]{:S(2)}) copy-start(bf16[256,1024]{1,0:T(8,128)(2,1)} %copy-done) | copy-start | bytes 1572868

commit v17 on v16

--- a/solution.py
+++ b/solution.py
@@ -471,7 +471,7 @@
     *outgoing, own = cut(where, states)
     weights = copies(where, first, second, outgoing[0])
 
-    (two,) = gate(outgoing[1:2], first, second)
+    (two,) = gate(outgoing[1:2], held(weights))
     up, down = gate((outgoing[0], outgoing[2]), held(weights))
     near = (
         lax.ppermute(down, AXES, ring_pairs(-1, -1)),

time: 159 us -> 159 us (level)
  transfers between devices with their start and end apart: 10 -> 10, of which waited for: 6 -> 6; matrix products, arithmetic and copies ran while one was open for 2% -> 2% of each run, Pallas kernels for 3% -> 2%
where the time goes in v17:
time: 159 us; the launch traced here: 158 us
  blocking collectives  50.5 us (32%)
  starting transfers between devices  45.9 us (29%)
  waiting for transfers between devices  39.7 us (25%)
  Pallas kernels  17.8 us (11%)
  other arithmetic  2.57 us (2%)
    all_to_all x1, blocking collectives, shards(): terms = lax.all_to_all(terms, OTHERS, split_axis=0, concat_axis=0)  28.9 us
    all_gather x1, blocking collectives, shards(): slopes = lax.all_gather(dq, GROUP, axis=0, tiled=False)  16.1 us
    all_to_all x1, waiting for transfers between devices, shards(): parts = lax.all_to_all(parts, GROUP, split_axis=0, concat_axis=0)  15 us
    all_to_all x1, starting transfers between devices, shards(): weights = lax.all_to_all(weights, OTHERS, split_axis=0, concat_axis=0)  13.4 us
    all_to_all x1, waiting for transfers between devices, shards(): weights = lax.all_to_all(weights, OTHERS, split_axis=0, concat_axis=0)  11.3 us
    ppermute x1, starting transfers between devices, shards(): first = lax.ppermute(first, AXES, home_pairs(0))  7.81 us
    ppermute x1, starting transfers between devices, shards(): lax.ppermute(down, AXES, ring_pairs(-1, -1))  5.77 us
    ppermute x3, starting transfers between devices, swap_core(): return lax.ppermute(value, 'c', [(0, 1), (1, 0)])  5.74 us
  transfers between devices with their start and end apart: 10, of which 6 were waited for; matrix products, arithmetic and copies ran while one was open for 2% of the time, Pallas kernels for 2%

profile of v17, /device:TPU:6, one launch (start us, length us, event | category | flops | bytes accessed | tf_op | source)
XLA Modules:
  0.0 157.5 jit_solution(1711599025702183727)
XLA Ops:
  0.6 0.1 pad_add_fusion.where_ref.refs_2_
  0.7 1.5 pack_weights.1
  2.2 7.8 %collective-permute-start = (bf16[320,128]{1,0:T(8,128)(2,1)S(1)}, bf16[320,128]{1,0:T(8,128)(2,1)S(1)}, u32[]{:S(2)}, u32[]{:S(2)}) collective-permute-start(bf16[320,128]{1,0:T(8,128)(2,1)S(1)} %get-tuple-element.18), channel_id=1, source_target_pairs={{0,256},{1,288},{2,320},{3,352},{4,384},{5,416},{6,192},{7,224},{8... | collective-permute-start | bytes 245768 | tf_op jit(solution)/shard_map/ppermute | solution.py:469
  10.0 3.0 %collective-permute-start.1 = (bf16[320,128]{1,0:T(8,128)(2,1)S(1)}, bf16[320,128]{1,0:T(8,128)(2,1)S(1)}, u32[]{:S(2)}, u32[]{:S(2)}) collective-permute-start(bf16[320,128]{1,0:T(8,128)(2,1)S(1)} %get-tuple-element.19), channel_id=1, source_target_pairs={{0,272},{1,304},{2,336},{3,368},{4,400},{5,432},{6,208},{7,240},{8... | collective-permute-start | bytes 245768 | tf_op jit(solution)/shard_map/ppermute | solution.py:470
  13.0 3.0 %cut_states.1 = (bf16[256,1024]{1,0:T(8,128)(2,1)S(1)}, bf16[256,1024]{1,0:T(8,128)(2,1)S(1)}, bf16[256,1024]{1,0:T(8,128)(2,1)S(1)}, bf16[256,2048]{1,0:T(8,128)(2,1)}) custom-call(s32[3]{0:T(128)S(1)} %pad_add_fusion.where_ref.refs_2_, bf16[256,8192]{1,0:T(8,128)(2,1)} %states_ref.1), custom_call_target="tpu_custom_call" | custom-call | tf_op jit(solution)/shard_map/cut_states/pallas_call | solution.py:155
  16.0 0.0 collective-permute-done.first
  16.0 5.2 %collective-permute-done.1.second = bf16[320,128]{1,0:T(8,128)(2,1)S(1)} collective-permute-done((bf16[320,128]{1,0:T(8,128)(2,1)S(1)}, bf16[320,128]{1,0:T(8,128)(2,1)S(1)}, u32[]{:S(2)}, u32[]{:S(2)}) %collective-permute-start.1) | collective-permute-done | bytes 81952 | tf_op jit(solution)/shard_map/ppermute | solution.py:470
  21.2 1.7 %weight_copies.1.refs_2_.refs_1_ = bf16[8,2,320,128]{3,2,1,0:T(8,128)(2,1)} custom-call(s32[3]{0:T(128)S(1)} %pad_add_fusion.where_ref.refs_2_, bf16[320,128]{1,0:T(8,128)(2,1)S(1)} %collective-permute-done.first, bf16[320,128]{1,0:T(8,128)(2,1)S(1)} %collective-permute-done.1.second, bf16[256,1024]{1,0:T(8,128)(2,1)S(1)} %get-tuple-element.16.after.refs_0_), custom_call_target="tpu_custom_call" | custom-call | tf_op jit(solution)/shard_map/weight_copies/pallas_call | solution.py:211
  22.9 3.7 %collective-permute-start.3 = (bf16[256,1024]{1,0:T(8,128)(2,1)S(1)}, bf16[256,1024]{1,0:T(8,128)(2,1)S(1)}, u32[]{:S(2)}, u32[]{:S(2)}) collective-permute-start(bf16[256,1024]{1,0:T(8,128)(2,1)S(1)} %gate.4), channel_id=1, source_target_pairs={{0,32},{1,41},{2,34},{3,43},{4,36},{5,45},{6,38},{7,47},{16,48},{1... | collective-permute-start | bytes 1572872 | tf_op jit(solution)/shard_map/ppermute | solution.py:478
  26.6 13.4 %all-to-all-start = ((bf16[8,2,320,128]{3,2,1,0:T(8,128)(2,1)}), bf16[8,2,320,128]{3,2,1,0:T(8,128)(2,1)}, u32[]{:S(2)}, u32[]{:S(2)}) async-start(bf16[8,2,320,128]{3,2,1,0:T(8,128)(2,1)} %weight_copies.1.refs_2_.refs_1_), calls=%async_computation | async-start | bytes 2621440 | tf_op jit(solution)/shard_map/all_to_all | solution.py:484
  40.0 0.0 copy-start.2
  40.0 5.8 %collective-permute-start.2 = (bf16[256,1024]{1,0:T(8,128)(2,1)S(1)}, bf16[256,1024]{1,0:T(8,128)(2,1)S(1)}, u32[]{:S(2)}, u32[]{:S(2)}) collective-permute-start(bf16[256,1024]{1,0:T(8,128)(2,1)S(1)} %get-tuple-element.20), channel_id=1, source_target_pairs={{0,56},{1,57},{2,58},{3,59},{4,60},{5,61},{6,62},{7,63},{16,0},{17... | collective-permute-start | bytes 1572872 | tf_op jit(solution)/shard_map/ppermute | solution.py:477
  45.8 1.9 %collective-permute-start.5 = (bf16[256,1024]{1,0:T(8,128)(2,1)S(1)}, bf16[256,1024]{1,0:T(8,128)(2,1)S(1)}, u32[]{:S(2)}, u32[]{:S(2)}) collective-permute-start(bf16[256,1024]{1,0:T(8,128)(2,1)S(1)} %get-tuple-element.23), channel_id=1, source_target_pairs={{0,16},{1,17},{2,18},{3,19},{4,20},{5,21},{6,22},{7,23},{16,32},{1... | collective-permute-start | bytes 1572872 | tf_op jit(solution)/shard_map/ppermute | solution.py:479
  47.7 0.0 collective-permute-done.3.refs_0_
  47.7 1.9 %collective-permute-start.4 = (bf16[256,1024]{1,0:T(8,128)(2,1)S(1)}, bf16[256,1024]{1,0:T(8,128)(2,1)S(1)}, u32[]{:S(2)}, u32[]{:S(2)}) collective-permute-start(bf16[256,1024]{1,0:T(8,128)(2,1)S(1)} %collective-permute-done.3.refs_0_), channel_id=1, source_target_pairs={{0,1},{1,0},{2,3},{3,2},{4,5},{5,4},{6,7},{7,6},{8,9},{9,8},{10,11... | collective-permute-start | bytes 1572872 | tf_op jit(solution)/shard_map/ppermute | solution.py:59
  49.6 0.0 copy-done.2
  49.6 0.1 reduce_sum.22
  49.8 4.9 %collective-permute-done.2.n1 = bf16[256,1024]{1,0:T(8,128)(2,1)S(1)} collective-permute-done((bf16[256,1024]{1,0:T(8,128)(2,1)S(1)}, bf16[256,1024]{1,0:T(8,128)(2,1)S(1)}, u32[]{:S(2)}, u32[]{:S(2)}) %collective-permute-start.2) | collective-permute-done | bytes 524320 | tf_op jit(solution)/shard_map/ppermute | solution.py:477
  54.6 1.9 %collective-permute-start.6 = (bf16[256,1024]{1,0:T(8,128)(2,1)S(1)}, bf16[256,1024]{1,0:T(8,128)(2,1)S(1)}, u32[]{:S(2)}, u32[]{:S(2)}) collective-permute-start(bf16[256,1024]{1,0:T(8,128)(2,1)S(1)} %collective-permute-done.2.n1), channel_id=1, source_target_pairs={{0,1},{1,0},{2,3},{3,2},{4,5},{5,4},{6,7},{7,6},{8,9},{9,8},{10,11... | collective-permute-start | bytes 1572872 | tf_op jit(solution)/shard_map/ppermute | solution.py:59
  56.6 1.5 collective-permute-done.5.n3
  58.1 1.9 %collective-permute-start.7 = (bf16[256,1024]{1,0:T(8,128)(2,1)S(1)}, bf16[256,1024]{1,0:T(8,128)(2,1)S(1)}, u32[]{:S(2)}, u32[]{:S(2)}) collective-permute-start(bf16[256,1024]{1,0:T(8,128)(2,1)S(1)} %collective-permute-done.5.n3), channel_id=1, source_target_pairs={{0,1},{1,0},{2,3},{3,2},{4,5},{5,4},{6,7},{7,6},{8,9},{9,8},{10,11... | collective-permute-start | bytes 1572872 | tf_op jit(solution)/shard_map/ppermute | solution.py:59
  60.0 0.0 collective-permute-done.4.refs_1_
  60.0 0.0 copy-start
  60.0 0.0 collective-permute-done.6.f1
  60.0 1.8 %collective-permute-done.7.f3 = bf16[256,1024]{1,0:T(8,128)(2,1)S(1)} collective-permute-done((bf16[256,1024]{1,0:T(8,128)(2,1)S(1)}, bf16[256,1024]{1,0:T(8,128)(2,1)S(1)}, u32[]{:S(2)}, u32[]{:S(2)}) %collective-permute-start.7) | collective-permute-done | bytes 524320 | tf_op jit(solution)/shard_map/ppermute | solution.py:59
  61.8 11.3 %all-to-all-done.weights_ref = bf16[8,2,320,128]{3,2,1,0:T(8,128)(2,1)} async-done(((bf16[8,2,320,128]{3,2,1,0:T(8,128)(2,1)}), bf16[8,2,320,128]{3,2,1,0:T(8,128)(2,1)}, u32[]{:S(2)}, u32[]{:S(2)}) %all-to-all-start) | async-done | bytes 1310752 | tf_op jit(solution)/shard_map/all_to_all | solution.py:484
  73.2 5.5 %project.1 = bf16[4,320,256]{2,1,0:T(8,128)(2,1)} custom-call(s32[3]{0:T(128)S(1)} %pad_add_fusion.where_ref.refs_2_, bf16[256,2048]{1,0:T(8,128)(2,1)} %get-tuple-element.15.own_ref, bf16[256,1024]{1,0:T(8,128)(2,1)S(1)} %collective-permute-done.2.n1, bf16[256,1024]{1,0:T(8,128)(2,1)S(1)} %get-tuple-element.22.n2, ...), custom_call_target="tpu_custom_call" | custom-call | tf_op jit(solution)/shard_map/project/pallas_call | solution.py:295
  78.6 0.0 copy-done
  78.6 0.0 copy-start.3
  78.7 4.6 %all-to-all-start.1 = ((bf16[4,320,256]{2,1,0:T(8,128)(2,1)}), bf16[4,320,256]{2,1,0:T(8,128)(2,1)S(1)}, u32[]{:S(2)}, u32[]{:S(2)}) async-start(bf16[4,320,256]{2,1,0:T(8,128)(2,1)} %project.1), calls=%async_computation.1 | async-start | bytes 1310720 | tf_op jit(solution)/shard_map/all_to_all | solution.py:487
  83.3 0.1 add_convert_fusion
  83.4 0.1 convert_element_type.13
  83.5 0.3 multiply_cosine_fusion.1
  83.8 0.7 pad_maximum_fusion.1.turned_ref
  84.4 0.5 multiply_cosine_fusion
  85.0 0.8 pad_maximum_fusion.tables_ref
  85.7 15.0 %all-to-all-done.1.parts = bf16[4,320,256]{2,1,0:T(8,128)(2,1)S(1)} async-done(((bf16[4,320,256]{2,1,0:T(8,128)(2,1)}), bf16[4,320,256]{2,1,0:T(8,128)(2,1)S(1)}, u32[]{:S(2)}, u32[]{:S(2)}) %all-to-all-start.1) | async-done | bytes 655392 | tf_op jit(solution)/shard_map/all_to_all | solution.py:487
  100.8 5.4 %all-gather = bf16[256,256]{1,0:T(8,128)(2,1)S(1)} all-gather(bf16[64,256]{1,0:T(8,128)(2,1)S(1)} %slice_reduce_fusion), channel_id=2, replica_groups=mesh['zh'=4,'zb'=2,'yu'=2,'yb'=2,'yh'=2,'xh'=2,'xb'=2,'c'=2] {'xb','c'}, dimensions={0}, use_global_device_ids=true | all-gather | bytes 163840 | tf_op jit(solution)/shard_map/all_gather | solution.py:489
  106.2 0.0 copy-done.3
  106.2 0.0 copy-start.1
  106.2 3.5 %attend.1 = (bf16[256,256]{1,0:T(8,128)(2,1)}, bf16[256,256]{1,0:T(8,128)(2,1)S(1)}, bf16[256,2048]{1,0:T(8,128)(2,1)S(1)}) custom-call(s32[4,4]{1,0:T(4,128)S(1)} %copy-done.2, f32[4]{0:T(128)S(1)} %copy-done.3, bf16[4,320,256]{2,1,0:T(8,128)(2,1)S(1)} %all-to-all-done.1.parts, bf16[4,64,256]{2,1,0:T(8,128)(2,1)S(1)} %bitcast.8, ...), custom_call_target="tpu_custom_call" | custom-call | tf_op jit(solution)/shard_map/attend/pallas_call | solution.py:397
  109.7 16.1 %all-gather.1 = bf16[1024,256]{1,0:T(8,128)(2,1)S(1)} all-gather(bf16[256,256]{1,0:T(8,128)(2,1)S(1)} %get-tuple-element.27), channel_id=3, replica_groups=mesh['zh'=4,'zb'=2,'yu'=2,'yb'=2,'yh'=2,'xh'=2,'xb'=2,'c'=2] {'yu','yb'}, dimensions={0}, use_global_device_ids=true | all-gather | bytes 655360 | tf_op jit(solution)/shard_map/all_gather | solution.py:504
  125.8 0.0 copy-done.1
  125.8 1.8 %gradient.1 = bf16[8,256,256]{2,1,0:T(8,128)(2,1)S(1)} custom-call(s32[3]{0:T(128)S(1)} %pad_add_fusion.where_ref.refs_2_, bf16[256,2048]{1,0:T(8,128)(2,1)S(1)} %get-tuple-element.26.own, bf16[256,1024]{1,0:T(8,128)(2,1)S(1)} %collective-permute-done.2.n1, bf16[256,1024]{1,0:T(8,128)(2,1)S(1)} %get-tuple-element.22.n2, ...), custom_call_target="tpu_custom_call" | custom-call | tf_op jit(solution)/shard_map/gradient/pallas_call | solution.py:438
  127.7 28.9 %all_to_all.15.terms = bf16[8,256,256]{2,1,0:T(8,128)(2,1)S(1)} all-to-all(bf16[8,256,256]{2,1,0:T(8,128)(2,1)S(1)} %gradient.1), channel_id=1, replica_groups=mesh['zh'=4,'zb'=2,'yu'=2,'yb'=2,'yh'=2,'xh'=2,'xb'=2,'c'=2] {'zh','zb'}, dimensions={0} | all-to-all | bytes 2097152 | tf_op jit(solution)/shard_map/all_to_all | solution.py:506
  156.6 0.9 add_up.1
  (6 shorter events, 0.0 us)
Async XLA Ops:
  2.2 13.8 %collective-permute-start = (bf16[320,128]{1,0:T(8,128)(2,1)S(1)}, bf16[320,128]{1,0:T(8,128)(2,1)S(1)}, u32[]{:S(2)}, u32[]{:S(2)}) collective-permute-start(bf16[320,128]{1,0:T(8,128)(2,1)S(1)} %get-tuple-element.18), channel_id=1, source_target_pairs={{0,256},{1,288},{2,320},{3,352},{4,384},{5,416},{6,192},{7,224},{8... | collective-permute-start | bytes 245768 | tf_op jit(solution)/shard_map/ppermute | solution.py:469
  10.0 11.1 %collective-permute-start.1 = (bf16[320,128]{1,0:T(8,128)(2,1)S(1)}, bf16[320,128]{1,0:T(8,128)(2,1)S(1)}, u32[]{:S(2)}, u32[]{:S(2)}) collective-permute-start(bf16[320,128]{1,0:T(8,128)(2,1)S(1)} %get-tuple-element.19), channel_id=1, source_target_pairs={{0,272},{1,304},{2,336},{3,368},{4,400},{5,432},{6,208},{7,240},{8... | collective-permute-start | bytes 245768 | tf_op jit(solution)/shard_map/ppermute | solution.py:470
  22.9 24.8 %collective-permute-start.3 = (bf16[256,1024]{1,0:T(8,128)(2,1)S(1)}, bf16[256,1024]{1,0:T(8,128)(2,1)S(1)}, u32[]{:S(2)}, u32[]{:S(2)}) collective-permute-start(bf16[256,1024]{1,0:T(8,128)(2,1)S(1)} %gate.4), channel_id=1, source_target_pairs={{0,32},{1,41},{2,34},{3,43},{4,36},{5,45},{6,38},{7,47},{16,48},{1... | collective-permute-start | bytes 1572872 | tf_op jit(solution)/shard_map/ppermute | solution.py:478
  26.6 46.6 %all-to-all-start = ((bf16[8,2,320,128]{3,2,1,0:T(8,128)(2,1)}), bf16[8,2,320,128]{3,2,1,0:T(8,128)(2,1)}, u32[]{:S(2)}, u32[]{:S(2)}) async-start(bf16[8,2,320,128]{3,2,1,0:T(8,128)(2,1)} %weight_copies.1.refs_2_.refs_1_), calls=%async_computation | async-start | bytes 2621440 | tf_op jit(solution)/shard_map/all_to_all | solution.py:484
  40.0 9.7 %copy-start.2 = (s32[4,4]{1,0:T(4,128)S(1)}, s32[4,4]{1,0:T(4,128)}, u32[]{:S(2)}) copy-start(s32[4,4]{1,0:T(4,128)} %mask_ref.1) | copy-start | bytes 196
  40.0 14.6 %collective-permute-start.2 = (bf16[256,1024]{1,0:T(8,128)(2,1)S(1)}, bf16[256,1024]{1,0:T(8,128)(2,1)S(1)}, u32[]{:S(2)}, u32[]{:S(2)}) collective-permute-start(bf16[256,1024]{1,0:T(8,128)(2,1)S(1)} %get-tuple-element.20), channel_id=1, source_target_pairs={{0,56},{1,57},{2,58},{3,59},{4,60},{5,61},{6,62},{7,63},{16,0},{17... | collective-permute-start | bytes 1572872 | tf_op jit(solution)/shard_map/ppermute | solution.py:477
  45.8 12.3 %collective-permute-start.5 = (bf16[256,1024]{1,0:T(8,128)(2,1)S(1)}, bf16[256,1024]{1,0:T(8,128)(2,1)S(1)}, u32[]{:S(2)}, u32[]{:S(2)}) collective-permute-start(bf16[256,1024]{1,0:T(8,128)(2,1)S(1)} %get-tuple-element.23), channel_id=1, source_target_pairs={{0,16},{1,17},{2,18},{3,19},{4,20},{5,21},{6,22},{7,23},{16,32},{1... | collective-permute-start | bytes 1572872 | tf_op jit(solution)/shard_map/ppermute | solution.py:479
  47.7 12.3 %collective-permute-start.4 = (bf16[256,1024]{1,0:T(8,128)(2,1)S(1)}, bf16[256,1024]{1,0:T(8,128)(2,1)S(1)}, u32[]{:S(2)}, u32[]{:S(2)}) collective-permute-start(bf16[256,1024]{1,0:T(8,128)(2,1)S(1)} %collective-permute-done.3.refs_0_), channel_id=1, source_target_pairs={{0,1},{1,0},{2,3},{3,2},{4,5},{5,4},{6,7},{7,6},{8,9},{9,8},{10,11... | collective-permute-start | bytes 1572872 | tf_op jit(solution)/shard_map/ppermute | solution.py:59
  54.6 5.4 %collective-permute-start.6 = (bf16[256,1024]{1,0:T(8,128)(2,1)S(1)}, bf16[256,1024]{1,0:T(8,128)(2,1)S(1)}, u32[]{:S(2)}, u32[]{:S(2)}) collective-permute-start(bf16[256,1024]{1,0:T(8,128)(2,1)S(1)} %collective-permute-done.2.n1), channel_id=1, source_target_pairs={{0,1},{1,0},{2,3},{3,2},{4,5},{5,4},{6,7},{7,6},{8,9},{9,8},{10,11... | collective-permute-start | bytes 1572872 | tf_op jit(solution)/shard_map/ppermute | solution.py:59
  58.1 3.8 %collective-permute-start.7 = (bf16[256,1024]{1,0:T(8,128)(2,1)S(1)}, bf16[256,1024]{1,0:T(8,128)(2,1)S(1)}, u32[]{:S(2)}, u32[]{:S(2)}) collective-permute-start(bf16[256,1024]{1,0:T(8,128)(2,1)S(1)} %collective-permute-done.5.n3), channel_id=1, source_target_pairs={{0,1},{1,0},{2,3},{3,2},{4,5},{5,4},{6,7},{7,6},{8,9},{9,8},{10,11... | collective-permute-start | bytes 1572872 | tf_op jit(solution)/shard_map/ppermute | solution.py:59
  60.0 18.6 %copy-start = (bf16[256,1024]{1,0:T(8,128)(2,1)}, bf16[256,1024]{1,0:T(8,128)(2,1)S(1)}, u32[]{:S(2)}) copy-start(bf16[256,1024]{1,0:T(8,128)(2,1)S(1)} %get-tuple-element.24.f2) | copy-start | bytes 1572868
  78.6 27.6 %copy-start.3 = (f32[4]{0:T(128)S(1)}, f32[4]{0:T(128)}, u32[]{:S(2)}) copy-start(f32[4]{0:T(128)} %risk_ref.1) | copy-start | bytes 52
  78.7 22.1 %all-to-all-start.1 = ((bf16[4,320,256]{2,1,0:T(8,128)(2,1)}), bf16[4,320,256]{2,1,0:T(8,128)(2,1)S(1)}, u32[]{:S(2)}, u32[]{:S(2)}) async-start(bf16[4,320,256]{2,1,0:T(8,128)(2,1)} %project.1), calls=%async_computation.1 | async-start | bytes 1310720 | tf_op jit(solution)/shard_map/all_to_all | solution.py:487
  106.2 19.6 %copy-start.1 = (bf16[256,1024]{1,0:T(8,128)(2,1)S(1)}, bf16[256,1024]{1,0:T(8,128)(2,1)}, u32[]{:S(2)}) copy-start(bf16[256,1024]{1,0:T(8,128)(2,1)} %copy-done) | copy-start | bytes 1572868

commit v18 on v16

--- a/solution.py
+++ b/solution.py
@@ -248,7 +248,7 @@
     copies = [pltpu.make_async_copy(own_ref, own, sems.at[0])]
     for copy in arrivals + copies:
         copy.start()
-    for part in range(8):
+    def unpack(part):
         arrivals[part].wait()
         start = 256 * part
         for head in range(2):
@@ -270,6 +270,11 @@
         return q, kv
 
     low, high = pl.ds(0, 1024), pl.ds(1024, 1024)
+    for part in range(4):
+        unpack(part)
+    begun = [product(near[...], low) for near in (n1, n2, n3)]
+    for part in range(4, 8):
+        unpack(part)
     departures = []
     for number, (near, far) in enumerate(((n1, f1), (n2, f2), (n3, f3), (None, None))):
         if near is None:
@@ -277,7 +282,7 @@
                 copy.wait()
             q, kv = product(own[...], pl.ds(0, 2048))
         else:
-            q_near, kv_near = product(near[...], low)
+            q_near, kv_near = begun[number]
             q_far, kv_far = product(far[...], high)
             q, kv = q_near + q_far, kv_near + kv_far
         result[number, :256, :] = q.astype(BF16)

time: 159 us -> 159 us (level)
  no operation moved by 1% of the time
where the time goes in v18:
time: 159 us; the launch traced here: 157 us
  blocking collectives  50.5 us (32%)
  starting transfers between devices  45.9 us (29%)
  waiting for transfers between devices  38.9 us (24%)
  Pallas kernels  18.6 us (12%)
  other arithmetic  2.57 us (2%)
    all_to_all x1, blocking collectives, shards(): terms = lax.all_to_all(terms, OTHERS, split_axis=0, concat_axis=0)  29 us
    all_gather x1, blocking collectives, shards(): slopes = lax.all_gather(dq, GROUP, axis=0, tiled=False)  16.1 us
    all_to_all x1, waiting for transfers between devices, shards(): parts = lax.all_to_all(parts, GROUP, split_axis=0, concat_axis=0)  15 us
    all_to_all x1, starting transfers between devices, shards(): weights = lax.all_to_all(weights, OTHERS, split_axis=0, concat_axis=0)  13.4 us
    all_to_all x1, waiting for transfers between devices, shards(): weights = lax.all_to_all(weights, OTHERS, split_axis=0, concat_axis=0)  11.3 us
    ppermute x1, starting transfers between devices, shards(): first = lax.ppermute(first, AXES, home_pairs(0))  7.81 us
    ppermute x1, starting transfers between devices, shards(): lax.ppermute(down, AXES, ring_pairs(-1, -1))  5.77 us
    ppermute x3, starting transfers between devices, swap_core(): return lax.ppermute(value, 'c', [(0, 1), (1, 0)])  5.74 us
  transfers between devices with their start and end apart: 10, of which 6 were waited for; matrix products, arithmetic and copies ran while one was open for 2% of the time, Pallas kernels for 3%

profile of v18, /device:TPU:6, one launch (start us, length us, event | category | flops | bytes accessed | tf_op | source)
XLA Modules:
  0.0 157.5 jit_solution(81889248119877795)
XLA Ops:
  0.6 0.1 pad_add_fusion.where_ref.refs_2_
  0.7 1.5 pack_weights.1
  2.2 7.8 %collective-permute-start = (bf16[320,128]{1,0:T(8,128)(2,1)S(1)}, bf16[320,128]{1,0:T(8,128)(2,1)S(1)}, u32[]{:S(2)}, u32[]{:S(2)}) collective-permute-start(bf16[320,128]{1,0:T(8,128)(2,1)S(1)} %get-tuple-element.18), channel_id=1, source_target_pairs={{0,256},{1,288},{2,320},{3,352},{4,384},{5,416},{6,192},{7,224},{8... | collective-permute-start | bytes 245768 | tf_op jit(solution)/shard_map/ppermute | solution.py:474
  10.0 3.0 %collective-permute-start.1 = (bf16[320,128]{1,0:T(8,128)(2,1)S(1)}, bf16[320,128]{1,0:T(8,128)(2,1)S(1)}, u32[]{:S(2)}, u32[]{:S(2)}) collective-permute-start(bf16[320,128]{1,0:T(8,128)(2,1)S(1)} %get-tuple-element.19), channel_id=1, source_target_pairs={{0,272},{1,304},{2,336},{3,368},{4,400},{5,432},{6,208},{7,240},{8... | collective-permute-start | bytes 245768 | tf_op jit(solution)/shard_map/ppermute | solution.py:475
  13.0 3.8 %cut_states.1 = (bf16[256,1024]{1,0:T(8,128)(2,1)S(1)}, bf16[256,1024]{1,0:T(8,128)(2,1)S(1)}, bf16[256,1024]{1,0:T(8,128)(2,1)}, bf16[256,2048]{1,0:T(8,128)(2,1)}) custom-call(s32[3]{0:T(128)S(1)} %pad_add_fusion.where_ref.refs_2_, bf16[256,8192]{1,0:T(8,128)(2,1)} %states_ref.1), custom_call_target="tpu_custom_call" | custom-call | tf_op jit(solution)/shard_map/cut_states/pallas_call | solution.py:155
  16.8 0.0 collective-permute-done.first.refs_1_
  16.8 4.4 %collective-permute-done.1.second.refs_2_ = bf16[320,128]{1,0:T(8,128)(2,1)S(1)} collective-permute-done((bf16[320,128]{1,0:T(8,128)(2,1)S(1)}, bf16[320,128]{1,0:T(8,128)(2,1)S(1)}, u32[]{:S(2)}, u32[]{:S(2)}) %collective-permute-start.1) | collective-permute-done | bytes 81952 | tf_op jit(solution)/shard_map/ppermute | solution.py:475
  21.2 3.7 %collective-permute-start.3 = (bf16[256,1024]{1,0:T(8,128)(2,1)S(1)}, bf16[256,1024]{1,0:T(8,128)(2,1)S(1)}, u32[]{:S(2)}, u32[]{:S(2)}) collective-permute-start(bf16[256,1024]{1,0:T(8,128)(2,1)S(1)} %gate.4), channel_id=1, source_target_pairs={{0,32},{1,41},{2,34},{3,43},{4,36},{5,45},{6,38},{7,47},{16,48},{1... | collective-permute-start | bytes 1572872 | tf_op jit(solution)/shard_map/ppermute | solution.py:483
  24.8 1.7 %weight_copies.1.refs_2_ = bf16[8,2,320,128]{3,2,1,0:T(8,128)(2,1)} custom-call(s32[3]{0:T(128)S(1)} %pad_add_fusion.where_ref.refs_2_, bf16[320,128]{1,0:T(8,128)(2,1)S(1)} %collective-permute-done.first.refs_1_, bf16[320,128]{1,0:T(8,128)(2,1)S(1)} %collective-permute-done.1.second.refs_2_, bf16[256,1024]{1,0:T(8,128)(2,1)S(1)} %get-tuple-element.16.after.refs_0_), custom_call_target="tpu_custom_call" | custom-call | tf_op jit(solution)/shard_map/weight_copies/pallas_call | solution.py:211
  26.6 13.4 %all-to-all-start = ((bf16[8,2,320,128]{3,2,1,0:T(8,128)(2,1)}), bf16[8,2,320,128]{3,2,1,0:T(8,128)(2,1)}, u32[]{:S(2)}, u32[]{:S(2)}) async-start(bf16[8,2,320,128]{3,2,1,0:T(8,128)(2,1)} %weight_copies.1.refs_2_), calls=%async_computation | async-start | bytes 2621440 | tf_op jit(solution)/shard_map/all_to_all | solution.py:489
  40.0 0.0 copy-start.2
  40.0 5.8 %collective-permute-start.2 = (bf16[256,1024]{1,0:T(8,128)(2,1)}, bf16[256,1024]{1,0:T(8,128)(2,1)S(1)}, u32[]{:S(2)}, u32[]{:S(2)}) collective-permute-start(bf16[256,1024]{1,0:T(8,128)(2,1)} %get-tuple-element.20), channel_id=1, source_target_pairs={{0,56},{1,57},{2,58},{3,59},{4,60},{5,61},{6,62},{7,63},{16,0},{17... | collective-permute-start | bytes 1572872 | tf_op jit(solution)/shard_map/ppermute | solution.py:482
  45.7 1.9 %collective-permute-start.5 = (bf16[256,1024]{1,0:T(8,128)(2,1)S(1)}, bf16[256,1024]{1,0:T(8,128)(2,1)S(1)}, u32[]{:S(2)}, u32[]{:S(2)}) collective-permute-start(bf16[256,1024]{1,0:T(8,128)(2,1)S(1)} %get-tuple-element.23), channel_id=1, source_target_pairs={{0,16},{1,17},{2,18},{3,19},{4,20},{5,21},{6,22},{7,23},{16,32},{1... | collective-permute-start | bytes 1572872 | tf_op jit(solution)/shard_map/ppermute | solution.py:484
  47.7 0.0 collective-permute-done.3.refs_0_
  47.7 1.9 %collective-permute-start.4 = (bf16[256,1024]{1,0:T(8,128)(2,1)S(1)}, bf16[256,1024]{1,0:T(8,128)(2,1)S(1)}, u32[]{:S(2)}, u32[]{:S(2)}) collective-permute-start(bf16[256,1024]{1,0:T(8,128)(2,1)S(1)} %collective-permute-done.3.refs_0_), channel_id=1, source_target_pairs={{0,1},{1,0},{2,3},{3,2},{4,5},{5,4},{6,7},{7,6},{8,9},{9,8},{10,11... | collective-permute-start | bytes 1572872 | tf_op jit(solution)/shard_map/ppermute | solution.py:59
  49.6 0.0 copy-done.2
  49.6 0.1 reduce_sum.22
  49.8 4.4 %collective-permute-done.2.n1 = bf16[256,1024]{1,0:T(8,128)(2,1)S(1)} collective-permute-done((bf16[256,1024]{1,0:T(8,128)(2,1)}, bf16[256,1024]{1,0:T(8,128)(2,1)S(1)}, u32[]{:S(2)}, u32[]{:S(2)}) %collective-permute-start.2) | collective-permute-done | bytes 524320 | tf_op jit(solution)/shard_map/ppermute | solution.py:482
  54.2 1.9 %collective-permute-start.6 = (bf16[256,1024]{1,0:T(8,128)(2,1)S(1)}, bf16[256,1024]{1,0:T(8,128)(2,1)S(1)}, u32[]{:S(2)}, u32[]{:S(2)}) collective-permute-start(bf16[256,1024]{1,0:T(8,128)(2,1)S(1)} %collective-permute-done.2.n1), channel_id=1, source_target_pairs={{0,1},{1,0},{2,3},{3,2},{4,5},{5,4},{6,7},{7,6},{8,9},{9,8},{10,11... | collective-permute-start | bytes 1572872 | tf_op jit(solution)/shard_map/ppermute | solution.py:59
  56.1 1.9 %collective-permute-done.5.n3 = bf16[256,1024]{1,0:T(8,128)(2,1)S(1)} collective-permute-done((bf16[256,1024]{1,0:T(8,128)(2,1)S(1)}, bf16[256,1024]{1,0:T(8,128)(2,1)S(1)}, u32[]{:S(2)}, u32[]{:S(2)}) %collective-permute-start.5) | collective-permute-done | bytes 524320 | tf_op jit(solution)/shard_map/ppermute | solution.py:484
  58.0 1.9 %collective-permute-start.7 = (bf16[256,1024]{1,0:T(8,128)(2,1)S(1)}, bf16[256,1024]{1,0:T(8,128)(2,1)S(1)}, u32[]{:S(2)}, u32[]{:S(2)}) collective-permute-start(bf16[256,1024]{1,0:T(8,128)(2,1)S(1)} %collective-permute-done.5.n3), channel_id=1, source_target_pairs={{0,1},{1,0},{2,3},{3,2},{4,5},{5,4},{6,7},{7,6},{8,9},{9,8},{10,11... | collective-permute-start | bytes 1572872 | tf_op jit(solution)/shard_map/ppermute | solution.py:59
  60.0 0.0 collective-permute-done.4.refs_1_
  60.0 0.0 copy-start
  60.0 0.0 collective-permute-done.6.f1
  60.0 1.8 %collective-permute-done.7.f3 = bf16[256,1024]{1,0:T(8,128)(2,1)S(1)} collective-permute-done((bf16[256,1024]{1,0:T(8,128)(2,1)S(1)}, bf16[256,1024]{1,0:T(8,128)(2,1)S(1)}, u32[]{:S(2)}, u32[]{:S(2)}) %collective-permute-start.7) | collective-permute-done | bytes 524320 | tf_op jit(solution)/shard_map/ppermute | solution.py:59
  61.8 11.3 %all-to-all-done.weights_ref = bf16[8,2,320,128]{3,2,1,0:T(8,128)(2,1)} async-done(((bf16[8,2,320,128]{3,2,1,0:T(8,128)(2,1)}), bf16[8,2,320,128]{3,2,1,0:T(8,128)(2,1)}, u32[]{:S(2)}, u32[]{:S(2)}) %all-to-all-start) | async-done | bytes 1310752 | tf_op jit(solution)/shard_map/all_to_all | solution.py:489
  73.1 5.4 %project.1 = bf16[4,320,256]{2,1,0:T(8,128)(2,1)} custom-call(s32[3]{0:T(128)S(1)} %pad_add_fusion.where_ref.refs_2_, bf16[256,2048]{1,0:T(8,128)(2,1)} %get-tuple-element.15.own_ref, bf16[256,1024]{1,0:T(8,128)(2,1)S(1)} %collective-permute-done.2.n1, bf16[256,1024]{1,0:T(8,128)(2,1)S(1)} %get-tuple-element.22.n2, ...), custom_call_target="tpu_custom_call" | custom-call | tf_op jit(solution)/shard_map/project/pallas_call | solution.py:300
  78.6 0.0 copy-done
  78.6 0.0 copy-start.3
  78.6 4.6 %all-to-all-start.1 = ((bf16[4,320,256]{2,1,0:T(8,128)(2,1)}), bf16[4,320,256]{2,1,0:T(8,128)(2,1)S(1)}, u32[]{:S(2)}, u32[]{:S(2)}) async-start(bf16[4,320,256]{2,1,0:T(8,128)(2,1)} %project.1), calls=%async_computation.1 | async-start | bytes 1310720 | tf_op jit(solution)/shard_map/all_to_all | solution.py:492
  83.2 0.1 add_convert_fusion
  83.3 0.1 convert_element_type.13
  83.4 0.3 multiply_cosine_fusion.1
  83.7 0.7 pad_maximum_fusion.1.turned_ref
  84.4 0.5 multiply_cosine_fusion
  84.9 0.8 pad_maximum_fusion.tables_ref
  85.7 15.0 %all-to-all-done.1.parts = bf16[4,320,256]{2,1,0:T(8,128)(2,1)S(1)} async-done(((bf16[4,320,256]{2,1,0:T(8,128)(2,1)}), bf16[4,320,256]{2,1,0:T(8,128)(2,1)S(1)}, u32[]{:S(2)}, u32[]{:S(2)}) %all-to-all-start.1) | async-done | bytes 655392 | tf_op jit(solution)/shard_map/all_to_all | solution.py:492
  100.7 5.4 %all-gather = bf16[256,256]{1,0:T(8,128)(2,1)S(1)} all-gather(bf16[64,256]{1,0:T(8,128)(2,1)S(1)} %slice_reduce_fusion), channel_id=2, replica_groups=mesh['zh'=4,'zb'=2,'yu'=2,'yb'=2,'yh'=2,'xh'=2,'xb'=2,'c'=2] {'xb','c'}, dimensions={0}, use_global_device_ids=true | all-gather | bytes 163840 | tf_op jit(solution)/shard_map/all_gather | solution.py:494
  106.2 0.0 copy-done.3
  106.2 0.0 copy-start.1
  106.2 3.5 %attend.1 = (bf16[256,256]{1,0:T(8,128)(2,1)}, bf16[256,256]{1,0:T(8,128)(2,1)S(1)}, bf16[256,2048]{1,0:T(8,128)(2,1)S(1)}) custom-call(s32[4,4]{1,0:T(4,128)S(1)} %copy-done.2, f32[4]{0:T(128)S(1)} %copy-done.3, bf16[4,320,256]{2,1,0:T(8,128)(2,1)S(1)} %all-to-all-done.1.parts, bf16[4,64,256]{2,1,0:T(8,128)(2,1)S(1)} %bitcast.8, ...), custom_call_target="tpu_custom_call" | custom-call | tf_op jit(solution)/shard_map/attend/pallas_call | solution.py:402
  109.7 16.1 %all-gather.1 = bf16[1024,256]{1,0:T(8,128)(2,1)S(1)} all-gather(bf16[256,256]{1,0:T(8,128)(2,1)S(1)} %get-tuple-element.27), channel_id=3, replica_groups=mesh['zh'=4,'zb'=2,'yu'=2,'yb'=2,'yh'=2,'xh'=2,'xb'=2,'c'=2] {'yu','yb'}, dimensions={0}, use_global_device_ids=true | all-gather | bytes 655360 | tf_op jit(solution)/shard_map/all_gather | solution.py:509
  125.8 0.0 copy-done.1
  125.8 1.8 %gradient.1 = bf16[8,256,256]{2,1,0:T(8,128)(2,1)S(1)} custom-call(s32[3]{0:T(128)S(1)} %pad_add_fusion.where_ref.refs_2_, bf16[256,2048]{1,0:T(8,128)(2,1)S(1)} %get-tuple-element.26.own, bf16[256,1024]{1,0:T(8,128)(2,1)S(1)} %collective-permute-done.2.n1, bf16[256,1024]{1,0:T(8,128)(2,1)S(1)} %get-tuple-element.22.n2, ...), custom_call_target="tpu_custom_call" | custom-call | tf_op jit(solution)/shard_map/gradient/pallas_call | solution.py:443
  127.6 29.0 %all_to_all.15.terms = bf16[8,256,256]{2,1,0:T(8,128)(2,1)S(1)} all-to-all(bf16[8,256,256]{2,1,0:T(8,128)(2,1)S(1)} %gradient.1), channel_id=1, replica_groups=mesh['zh'=4,'zb'=2,'yu'=2,'yb'=2,'yh'=2,'xh'=2,'xb'=2,'c'=2] {'zh','zb'}, dimensions={0} | all-to-all | bytes 2097152 | tf_op jit(solution)/shard_map/all_to_all | solution.py:511
  156.6 0.9 add_up.1
  (6 shorter events, 0.0 us)
Async XLA Ops:
  2.2 14.6 %collective-permute-start = (bf16[320,128]{1,0:T(8,128)(2,1)S(1)}, bf16[320,128]{1,0:T(8,128)(2,1)S(1)}, u32[]{:S(2)}, u32[]{:S(2)}) collective-permute-start(bf16[320,128]{1,0:T(8,128)(2,1)S(1)} %get-tuple-element.18), channel_id=1, source_target_pairs={{0,256},{1,288},{2,320},{3,352},{4,384},{5,416},{6,192},{7,224},{8... | collective-permute-start | bytes 245768 | tf_op jit(solution)/shard_map/ppermute | solution.py:474
  10.0 11.1 %collective-permute-start.1 = (bf16[320,128]{1,0:T(8,128)(2,1)S(1)}, bf16[320,128]{1,0:T(8,128)(2,1)S(1)}, u32[]{:S(2)}, u32[]{:S(2)}) collective-permute-start(bf16[320,128]{1,0:T(8,128)(2,1)S(1)} %get-tuple-element.19), channel_id=1, source_target_pairs={{0,272},{1,304},{2,336},{3,368},{4,400},{5,432},{6,208},{7,240},{8... | collective-permute-start | bytes 245768 | tf_op jit(solution)/shard_map/ppermute | solution.py:475
  21.2 26.5 %collective-permute-start.3 = (bf16[256,1024]{1,0:T(8,128)(2,1)S(1)}, bf16[256,1024]{1,0:T(8,128)(2,1)S(1)}, u32[]{:S(2)}, u32[]{:S(2)}) collective-permute-start(bf16[256,1024]{1,0:T(8,128)(2,1)S(1)} %gate.4), channel_id=1, source_target_pairs={{0,32},{1,41},{2,34},{3,43},{4,36},{5,45},{6,38},{7,47},{16,48},{1... | collective-permute-start | bytes 1572872 | tf_op jit(solution)/shard_map/ppermute | solution.py:483
  26.6 46.6 %all-to-all-start = ((bf16[8,2,320,128]{3,2,1,0:T(8,128)(2,1)}), bf16[8,2,320,128]{3,2,1,0:T(8,128)(2,1)}, u32[]{:S(2)}, u32[]{:S(2)}) async-start(bf16[8,2,320,128]{3,2,1,0:T(8,128)(2,1)} %weight_copies.1.refs_2_), calls=%async_computation | async-start | bytes 2621440 | tf_op jit(solution)/shard_map/all_to_all | solution.py:489
  40.0 9.7 %copy-start.2 = (s32[4,4]{1,0:T(4,128)S(1)}, s32[4,4]{1,0:T(4,128)}, u32[]{:S(2)}) copy-start(s32[4,4]{1,0:T(4,128)} %mask_ref.1) | copy-start | bytes 196
  40.0 14.2 %collective-permute-start.2 = (bf16[256,1024]{1,0:T(8,128)(2,1)}, bf16[256,1024]{1,0:T(8,128)(2,1)S(1)}, u32[]{:S(2)}, u32[]{:S(2)}) collective-permute-start(bf16[256,1024]{1,0:T(8,128)(2,1)} %get-tuple-element.20), channel_id=1, source_target_pairs={{0,56},{1,57},{2,58},{3,59},{4,60},{5,61},{6,62},{7,63},{16,0},{17... | collective-permute-start | bytes 1572872 | tf_op jit(solution)/shard_map/ppermute | solution.py:482
  45.7 12.3 %collective-permute-start.5 = (bf16[256,1024]{1,0:T(8,128)(2,1)S(1)}, bf16[256,1024]{1,0:T(8,128)(2,1)S(1)}, u32[]{:S(2)}, u32[]{:S(2)}) collective-permute-start(bf16[256,1024]{1,0:T(8,128)(2,1)S(1)} %get-tuple-element.23), channel_id=1, source_target_pairs={{0,16},{1,17},{2,18},{3,19},{4,20},{5,21},{6,22},{7,23},{16,32},{1... | collective-permute-start | bytes 1572872 | tf_op jit(solution)/shard_map/ppermute | solution.py:484
  47.7 12.3 %collective-permute-start.4 = (bf16[256,1024]{1,0:T(8,128)(2,1)S(1)}, bf16[256,1024]{1,0:T(8,128)(2,1)S(1)}, u32[]{:S(2)}, u32[]{:S(2)}) collective-permute-start(bf16[256,1024]{1,0:T(8,128)(2,1)S(1)} %collective-permute-done.3.refs_0_), channel_id=1, source_target_pairs={{0,1},{1,0},{2,3},{3,2},{4,5},{5,4},{6,7},{7,6},{8,9},{9,8},{10,11... | collective-permute-start | bytes 1572872 | tf_op jit(solution)/shard_map/ppermute | solution.py:59
  54.2 5.8 %collective-permute-start.6 = (bf16[256,1024]{1,0:T(8,128)(2,1)S(1)}, bf16[256,1024]{1,0:T(8,128)(2,1)S(1)}, u32[]{:S(2)}, u32[]{:S(2)}) collective-permute-start(bf16[256,1024]{1,0:T(8,128)(2,1)S(1)} %collective-permute-done.2.n1), channel_id=1, source_target_pairs={{0,1},{1,0},{2,3},{3,2},{4,5},{5,4},{6,7},{7,6},{8,9},{9,8},{10,11... | collective-permute-start | bytes 1572872 | tf_op jit(solution)/shard_map/ppermute | solution.py:59
  58.0 3.8 %collective-permute-start.7 = (bf16[256,1024]{1,0:T(8,128)(2,1)S(1)}, bf16[256,1024]{1,0:T(8,128)(2,1)S(1)}, u32[]{:S(2)}, u32[]{:S(2)}) collective-permute-start(bf16[256,1024]{1,0:T(8,128)(2,1)S(1)} %collective-permute-done.5.n3), channel_id=1, source_target_pairs={{0,1},{1,0},{2,3},{3,2},{4,5},{5,4},{6,7},{7,6},{8,9},{9,8},{10,11... | collective-permute-start | bytes 1572872 | tf_op jit(solution)/shard_map/ppermute | solution.py:59
  60.0 18.6 %copy-start = (bf16[256,1024]{1,0:T(8,128)(2,1)}, bf16[256,1024]{1,0:T(8,128)(2,1)S(1)}, u32[]{:S(2)}) copy-start(bf16[256,1024]{1,0:T(8,128)(2,1)S(1)} %get-tuple-element.24.f2) | copy-start | bytes 1572868
  78.6 27.6 %copy-start.3 = (f32[4]{0:T(128)S(1)}, f32[4]{0:T(128)}, u32[]{:S(2)}) copy-start(f32[4]{0:T(128)} %risk_ref.1) | copy-start | bytes 52
  78.6 22.1 %all-to-all-start.1 = ((bf16[4,320,256]{2,1,0:T(8,128)(2,1)}), bf16[4,320,256]{2,1,0:T(8,128)(2,1)S(1)}, u32[]{:S(2)}, u32[]{:S(2)}) async-start(bf16[4,320,256]{2,1,0:T(8,128)(2,1)} %project.1), calls=%async_computation.1 | async-start | bytes 1310720 | tf_op jit(solution)/shard_map/all_to_all | solution.py:492
  106.2 19.6 %copy-start.1 = (bf16[256,1024]{1,0:T(8,128)(2,1)S(1)}, bf16[256,1024]{1,0:T(8,128)(2,1)}, u32[]{:S(2)}) copy-start(bf16[256,1024]{1,0:T(8,128)(2,1)} %copy-done) | copy-start | bytes 1572868
